TPU v7x, 256 devices: a whole 4x4x8 slice. The times are simulated.
256 devices in a mesh: problem: 16 (over x, y_hi, core), sample: 16 (over y_lo, z).
Axes of the slice: x: 4, y: 4 (y_hi: 2, y_lo: 2; y = y_hi * 2 + y_lo), z: 8, core: 2. Of those that a mesh axis runs over, the one named last changes fastest.
Arguments:
- queries: bfloat16 [256, 256, 1024], P(('problem', 'sample')), parts along dimension 0, may hold values from -6 to 6
- resp_keys: bfloat16 [256, 256, 128], P(('problem', 'sample')), parts along dimension 0, may hold values from -6 to 6
- resp_values: bfloat16 [256, 256, 128], P(('problem', 'sample')), parts along dimension 0, may hold values from -6 to 6
- prompt_keys: bfloat16 [32768, 128], P(('problem', 'sample')), parts along dimension 0, may hold values from -6 to 6
- prompt_values: bfloat16 [32768, 128], P(('problem', 'sample')), parts along dimension 0, may hold values from -6 to 6
- grad_out: bfloat16 [256, 256, 1024], P(('problem', 'sample')), parts along dimension 0, may hold values from -24 to 24
- lengths: int32 [256], P(('problem', 'sample')), parts along dimension 0, may hold values from 64 to 256
- rewards: int32 [256], P(('problem', 'sample')), parts along dimension 0, may hold values from 0 to 16
Outputs:
- grad_queries: float32 [256, 256, 1024], P(('problem', 'sample')), parts along dimension 0
- grad_resp_keys: float32 [256, 256, 128], P(('problem', 'sample')), parts along dimension 0
- grad_resp_values: float32 [256, 256, 128], P(('problem', 'sample')), parts along dimension 0
- grad_prompt_keys: float32 [32768, 128], P(('problem', 'sample')), parts along dimension 0
- grad_prompt_values: float32 [32768, 128], P(('problem', 'sample')), parts along dimension 0
There are 16 independent parts, one for each index of `problem`. A program takes and returns all parts, laid end to end along the dimension named above; each array names one. Nothing has to cross between parts.
All inputs are finite; a program needn't handle non-finite values.
Results may differ from a plain program's by a relative error of at most 0.007.
Values may be sent and summed in bfloat16 or wider, within the bound.
No kernel may reach another device: no remote copies, remote signals or barrier semaphores. Data moves between devices by JAX's collectives and lax.ppermute only.
A program may use at most 64 MiB of HBM per device.

v0:
```python
import math

import jax
import jax.numpy as jnp
from jax import lax
from jax.sharding import PartitionSpec as P


def contract_last(left, right):
    return lax.dot_general(
        left, right, (((1,), (1,)), ((), ())), preferred_element_type=jnp.float32
    )


def contract_first(left, right):
    return lax.dot_general(
        left, right, (((0,), (0,)), ((), ())), preferred_element_type=jnp.float32
    )


def shards(queries, resp_keys, resp_values, prompt_keys, prompt_values, grad_out, lengths, rewards):
    head_width = resp_keys.shape[2]
    resp_len = queries.shape[1]
    head_count = queries.shape[2] // head_width
    query_count = resp_len * head_count
    score_scale = 1.0 / math.sqrt(head_width)
    query_rows = queries.reshape(query_count, head_width)
    own_keys = resp_keys.reshape(resp_len, head_width)
    own_values = resp_values.reshape(resp_len, head_width)
    position = lax.broadcasted_iota(jnp.int32, (query_count, 1), 0) // head_count
    cotangent = jnp.where(
        position < lengths[0],
        grad_out.reshape(query_count, head_width),
        jnp.zeros((), jnp.bfloat16),
    )
    reward_total = lax.psum(jnp.sum(rewards.astype(jnp.float32)), "sample")
    advantage = rewards[0].astype(jnp.float32) - reward_total / lax.axis_size("sample")
    gathered_keys, gathered_values = (
        lax.all_gather(prompt_keys, "sample", axis=0, tiled=True),
        lax.all_gather(prompt_values, "sample", axis=0, tiled=True),
    )
    prompt_len = gathered_keys.shape[0]
    row_block = math.gcd(query_count, 512)
    block_count = query_count // row_block
    query_blocks = query_rows.reshape(block_count, row_block, head_width)
    cot_blocks = cotangent.reshape(block_count, row_block, head_width)
    block_ids = jnp.arange(block_count, dtype=jnp.int32)

    def block_pass(carried, inputs):
        own_kg, own_vg, prompt_kg, prompt_vg = carried
        q_blk, c_blk, block_id = inputs
        rows_pos = (
            block_id * row_block + lax.broadcasted_iota(jnp.int32, (row_block, 1), 0)
        ) // head_count
        allowed = lax.broadcasted_iota(jnp.int32, (1, resp_len), 1) <= rows_pos
        prompt_scores = contract_last(q_blk, gathered_keys) * score_scale
        own_scores = jnp.where(allowed, contract_last(q_blk, own_keys) * score_scale, -jnp.inf)
        row_max = jnp.maximum(jnp.max(prompt_scores, axis=1), jnp.max(own_scores, axis=1))
        row_sum = jnp.sum(jnp.exp(prompt_scores - row_max[:, None]), axis=1) + jnp.sum(
            jnp.exp(own_scores - row_max[:, None]), axis=1
        )
        logsum = row_max + jnp.log(row_sum)
        prompt_attn = jnp.exp(prompt_scores - logsum[:, None])
        own_attn = jnp.exp(own_scores - logsum[:, None])
        prompt_round = prompt_attn.astype(jnp.bfloat16)
        own_round = own_attn.astype(jnp.bfloat16)
        attended = jnp.dot(
            prompt_round, gathered_values, preferred_element_type=jnp.float32
        ) + jnp.dot(own_round, own_values, preferred_element_type=jnp.float32)
        row_delta = jnp.sum(c_blk.astype(jnp.float32) * attended, axis=1)
        own_sg = (own_attn * (contract_last(c_blk, own_values) - row_delta[:, None])).astype(
            jnp.bfloat16
        )
        prompt_sg = (
            prompt_attn * (contract_last(c_blk, gathered_values) - row_delta[:, None])
        ).astype(jnp.bfloat16)
        q_grad = jnp.dot(own_sg, own_keys, preferred_element_type=jnp.float32) + jnp.dot(
            prompt_sg, gathered_keys, preferred_element_type=jnp.float32
        )
        own_kg = own_kg + contract_first(own_sg, q_blk) * score_scale
        own_vg = own_vg + contract_first(own_round, c_blk)
        prompt_kg = prompt_kg + contract_first(prompt_sg, q_blk) * score_scale
        prompt_vg = prompt_vg + contract_first(prompt_round, c_blk)
        return ((own_kg, own_vg, prompt_kg, prompt_vg), (q_grad, logsum, row_delta))

    own_zero = jnp.zeros((resp_len, head_width), jnp.float32)
    prompt_zero = jnp.zeros((prompt_len, head_width), jnp.float32)
    (own_key_grad, own_value_grad, prompt_kg, prompt_vg), (q_parts, logsum_parts, delta_parts) = (
        lax.scan(
            block_pass,
            (own_zero, own_zero, prompt_zero, prompt_zero),
            (query_blocks, cot_blocks, block_ids),
        )
    )
    query_grad = q_parts.reshape(query_count, head_width)
    prompt_key_grad, prompt_value_grad = (
        lax.psum_scatter(advantage * prompt_kg, "sample", scatter_dimension=0, tiled=True),
        lax.psum_scatter(advantage * prompt_vg, "sample", scatter_dimension=0, tiled=True),
    )
    grad_queries = (advantage * score_scale * query_grad).reshape(
        1, resp_len, head_count * head_width
    )
    grad_resp_keys = (advantage * own_key_grad).reshape(1, resp_len, head_width)
    grad_resp_values = (advantage * own_value_grad).reshape(1, resp_len, head_width)
    return (grad_queries, grad_resp_keys, grad_resp_values, prompt_key_grad, prompt_value_grad)


def solution(mesh):
    return jax.shard_map(
        shards,
        mesh=mesh,
        in_specs=(
            P(("problem", "sample"), None, None),
            P(("problem", "sample"), None, None),
            P(("problem", "sample"), None, None),
            P(("problem", "sample"), None),
            P(("problem", "sample"), None),
            P(("problem", "sample"), None, None),
            P(("problem", "sample")),
            P(("problem", "sample")),
        ),
        out_specs=(
            P(("problem", "sample"), None, None),
            P(("problem", "sample"), None, None),
            P(("problem", "sample"), None, None),
            P(("problem", "sample"), None),
            P(("problem", "sample"), None),
        ),
        check_vma=False,
    )
```

profile of v0, /device:TPU:2, one launch (start us, length us, event | category | flops | bytes accessed | tf_op | source)
XLA Modules:
  0.0 323.0 jit_solution(1718611311900414192)
XLA Ops:
  7.9 38.8 %psum.7 = f32[]{:T(128)} all-reduce(f32[]{:T(128)} %bitcast), channel_id=1, replica_groups=mesh['problem'=16,'sample'=16] {'sample'}, use_global_device_ids=true, to_apply=%region_0.1 | all-reduce | flops 1 | bytes 8 | tf_op jit(solution)/shard_map/psum | solution.py:36
  48.0 2.1 reshape_reshape.3
  50.1 32.6 %all_gather.6 = bf16[2048,128]{1,0:T(8,128)(2,1)S(1)} all-gather(bf16[128,128]{1,0:T(8,128)(2,1)} %param.13), channel_id=1, replica_groups=mesh['problem'=16,'sample'=16] {'sample'}, dimensions={0}, use_global_device_ids=true | all-gather | bytes 557056 | tf_op jit(solution)/shard_map/all_gather | solution.py:39
  82.7 34.8 %all_gather.7 = bf16[2048,128]{1,0:T(8,128)(2,1)S(1)} all-gather(bf16[128,128]{1,0:T(8,128)(2,1)} %param.14), channel_id=1, replica_groups=mesh['problem'=16,'sample'=16] {'sample'}, dimensions={0}, use_global_device_ids=true | all-gather | bytes 557056 | tf_op jit(solution)/shard_map/all_gather | solution.py:40
  117.5 2.1 reshape.153
  119.6 2.2 broadcast_select_fusion
  121.8 54.6 %while.21 = (s32[]{:T(128)}, f32[256,128]{1,0:T(8,128)}, f32[256,128]{1,0:T(8,128)}, f32[2048,128]{1,0:T(8,128)S(1)}, f32[2048,128]{1,0:T(8,128)S(1)}, /*index=5...) while((s32[]{:T(128)}, f32[256,128]{1,0:T(8,128)}, ...), condition=%wide.region_7.8_spmd.clone, body=%wide.region_1.7_spmd.clone.sunk | while | flops 1832360960 | bytes 45007204 | solution.py:89
  124.1 1.1 fusion.104
  125.3 1.7 multiply_reduce_fusion.2
  130.4 1.4 convolution_add_fusion.7
  131.8 1.1 multiply_convert_fusion.2
  132.9 1.5 fusion.111
  137.8 1.2 fusion.104
  139.0 1.7 multiply_reduce_fusion.2
  144.0 1.4 convolution_add_fusion.7
  145.5 1.1 multiply_convert_fusion.2
  146.6 1.5 fusion.111
  148.1 1.1 fusion.109
  151.4 1.2 fusion.104
  152.6 1.7 multiply_reduce_fusion.2
  157.7 1.4 convolution_add_fusion.7
  159.1 1.1 multiply_convert_fusion.2
  160.3 1.5 fusion.111
  165.1 1.2 fusion.104
  166.3 1.7 multiply_reduce_fusion.2
  171.3 1.4 convolution_add_fusion.7
  172.8 1.1 multiply_convert_fusion.2
  173.9 1.5 fusion.111
  176.5 1.1 broadcast_multiply_fusion
  178.8 1.1 mul.93
  180.7 64.6 %reduce-scatter.5.cloned.1.call-done = f32[128,128]{1,0:T(8,128)} async-done(((f32[2048,128]{1,0:T(8,128)}), f32[128,128]{1,0:T(8,128)}) %reduce-scatter.5.cloned.1.call-update) | async-done | bytes 65552 | tf_op jit(solution)/shard_map/reduce_scatter | solution.py:98
  245.2 71.0 %reduce-scatter.3.cloned.1.call-done = f32[128,128]{1,0:T(8,128)} async-done(((f32[2048,128]{1,0:T(8,128)}), f32[128,128]{1,0:T(8,128)}) %reduce-scatter.3.cloned.1.call-update) | async-done | bytes 65552 | tf_op jit(solution)/shard_map/reduce_scatter | solution.py:97
  (123 shorter events, 24.7 us)
Async XLA Ops:
  7.2 114.7 %copy-start.1 = (bf16[1,256,128]{2,1,0:T(8,128)(2,1)S(1)}, bf16[1,256,128]{2,1,0:T(8,128)(2,1)}, u32[]{:S(2)}) copy-start(bf16[1,256,128]{2,1,0:T(8,128)(2,1)} %param.12) | copy-start | bytes 196612
  7.2 114.6 %copy-start.8 = (bf16[1,256,128]{2,1,0:T(8,128)(2,1)S(1)}, bf16[1,256,128]{2,1,0:T(8,128)(2,1)}, u32[]{:S(2)}) copy-start(bf16[1,256,128]{2,1,0:T(8,128)(2,1)} %param.11) | copy-start | bytes 196612
  7.2 238.0 %reduce-scatter.5.cloned.1.call-start = ((), (), s32[]{:S(2)}) async-start(), calls=%async_computation.3 | async-start | bytes 1114112 | tf_op jit(solution)/shard_map/reduce_scatter | solution.py:98
  125.3 2.7 copy-start.2
  128.0 1.8 copy-start
  128.0 1.9 copy-start.5
  128.3 3.5 %copy-start.3 = (f32[256,128]{1,0:T(8,128)}, f32[256,128]{1,0:T(8,128)S(1)}, u32[]{:S(2)}) copy-start(f32[256,128]{1,0:T(8,128)S(1)} %convolution_add_fusion.6) | copy-start | bytes 393220 | tf_op jit(solution)/shard_map/while
  130.1 2.8 copy-start.6
  138.9 2.7 copy-start.2
  141.6 1.8 copy-start
  141.6 1.9 copy-start.5
  141.9 3.5 %copy-start.3 = (f32[256,128]{1,0:T(8,128)}, f32[256,128]{1,0:T(8,128)S(1)}, u32[]{:S(2)}) copy-start(f32[256,128]{1,0:T(8,128)S(1)} %convolution_add_fusion.6) | copy-start | bytes 393220 | tf_op jit(solution)/shard_map/while
  143.8 2.8 copy-start.6
  152.6 2.7 copy-start.2
  155.3 1.8 copy-start
  155.3 1.9 copy-start.5
  155.6 3.5 %copy-start.3 = (f32[256,128]{1,0:T(8,128)}, f32[256,128]{1,0:T(8,128)S(1)}, u32[]{:S(2)}) copy-start(f32[256,128]{1,0:T(8,128)S(1)} %convolution_add_fusion.6) | copy-start | bytes 393220 | tf_op jit(solution)/shard_map/while
  157.4 2.8 copy-start.6
  166.3 2.7 copy-start.2
  168.9 1.8 copy-start
  168.9 1.9 copy-start.5
  169.2 3.5 %copy-start.3 = (f32[256,128]{1,0:T(8,128)}, f32[256,128]{1,0:T(8,128)S(1)}, u32[]{:S(2)}) copy-start(f32[256,128]{1,0:T(8,128)S(1)} %convolution_add_fusion.6) | copy-start | bytes 393220 | tf_op jit(solution)/shard_map/while
  171.1 2.8 copy-start.6
  176.5 2.3 copy-start.9
  177.6 2.4 copy-start.4
  177.6 2.4 copy-start.7
  177.6 138.6 %reduce-scatter.3.cloned.1.call-start = ((), (), s32[]{:S(2)}) async-start(), calls=%async_computation.2 | async-start | bytes 1114112 | tf_op jit(solution)/shard_map/reduce_scatter | solution.py:97
Sparse Core Ops, SparseCore 0:
  177.7 67.4 reduce-scatter.4
  248.5 67.6 reduce-scatter.2
where the time goes:
time: 324 us; the launch traced here: 323 us
  waiting for transfers between devices  136 us (42%)
  blocking collectives  106 us (33%)
  matrix products  40.8 us (13%)
  between operations  16.1 us (5%)
  local copies, waits for them, and re-layouts  11.9 us (4%)
  other arithmetic  9 us (3%)
  loops' own time  3.35 us (1%)
    reduce_scatter x1, waiting for transfers between devices, shards(): lax.psum_scatter(advantage * prompt_kg, 'sample', scatter_dimension=0, ti...  71 us
    reduce_scatter x1, waiting for transfers between devices, shards(): lax.psum_scatter(advantage * prompt_vg, 'sample', scatter_dimension=0, ti...  64.6 us
    psum x1, blocking collectives, shards(): reward_total = lax.psum(jnp.sum(rewards.astype(jnp.float32)), 'sample')  38.8 us
    all_gather x1, blocking collectives, shards(): lax.all_gather(prompt_values, 'sample', axis=0, tiled=True)  34.8 us
    all_gather x1, blocking collectives, shards(): lax.all_gather(prompt_keys, 'sample', axis=0, tiled=True)  32.6 us
    dot_general x16, matrix products, contract_last(): lax.dot_general(left, right, (((1,), (1,)), ((), ())), preferred_element_...  17 us
    dot_general x16, matrix products, contract_first(): lax.dot_general(left, right, (((0,), (0,)), ((), ())), preferred_element_...  11.9 us
    dynamic_slice x12, local copies, waits for them, and re-layouts, shards(): lax.scan(block_pass, (own_zero, own_zero, prompt_zero, prompt_zero), (que...  6.48 us
  transfers between devices with their start and end apart: 2, of which 2 were waited for; matrix products, arithmetic and copies ran while one was open for 1% of the time, Pallas kernels for 0%

commit v1 on v0

v1 whole, which is shorter than its diff:
```python
import functools
import math

import jax
import jax.numpy as jnp
from jax import lax
from jax.experimental import pallas as pl
from jax.experimental.pallas import tpu as pltpu
from jax.sharding import PartitionSpec as P

F32 = jnp.float32
BF16 = jnp.bfloat16
CHUNK = 256


def dot_nn(left, right):
    return lax.dot_general(left, right, (((1,), (0,)), ((), ())), preferred_element_type=F32)


def dot_nt(left, right):
    return lax.dot_general(left, right, (((1,), (1,)), ((), ())), preferred_element_type=F32)


def fold_rows(values, combine):
    parts = [values[i : i + 8] for i in range(0, values.shape[0], 8)]
    while len(parts) > 1:
        parts = [
            combine(parts[i], parts[i + 1]) if i + 1 < len(parts) else parts[i]
            for i in range(0, len(parts), 2)
        ]
    return parts[0]


def attention_kernel(
    heads, owners, share, len_ref, q_ref, c_ref, g_ref, rk_ref, rv_ref,
    dq_ref, drk_ref, drv_ref, dp_ref,
    k_all, v_all, k_t, dk_acc, dv_acc, s0, s1, g0, g1, g2, e0, e1,
):
    resp, width = rk_ref.shape[1], rk_ref.shape[2]
    prompt = owners * share
    keys = prompt + resp
    chunks = keys // CHUNK
    scale = 1.0 / math.sqrt(width)
    rate = scale * math.log2(math.e)
    s_buf, g_buf, e_buf = (s0, s1), (g0, g1, g2), (e0, e1)

    for owner in range(owners):
        rows = pl.ds(owner * share, share)
        k_all[rows, :] = g_ref[owner, :share, :]
        v_all[rows, :] = g_ref[owner, share : 2 * share, :]
    k_all[prompt:, :] = rk_ref[0]
    v_all[prompt:, :] = rv_ref[0]
    for j in range(chunks):
        span = slice(j * CHUNK, (j + 1) * CHUNK)
        k_t[:, span] = k_all[span, :].T

    total = jnp.zeros((1, width), F32)
    for owner in range(owners):
        total = total + g_ref[owner, 2 * share : 2 * share + 16, :].astype(F32)[:1]
    me = lax.axis_index("sample")
    mine = g_ref[me, 2 * share : 2 * share + 16, :].astype(F32)[:1]
    advantage = mine - total / owners

    live = lax.broadcasted_iota(jnp.int32, (resp, width), 0) < len_ref[0]
    allowed = lax.broadcasted_iota(jnp.int32, (CHUNK, resp), 0) <= lax.broadcasted_iota(
        jnp.int32, (CHUNK, resp), 1
    )

    def query_rows(h):
        return q_ref[0, :, h * width : (h + 1) * width]

    def cotangent(h):
        return jnp.where(live, c_ref[0, :, h * width : (h + 1) * width], jnp.zeros((), BF16))

    peak, inv, delta = {}, {}, {}
    for t in range(heads + 2):
        one, two, three = t, t - 1, t - 2
        do1, do2, do3 = one < heads, 0 <= two < heads, 0 <= three
        if do1:
            q1, c1 = query_rows(one), cotangent(one)
            top = None
        if do2:
            level = peak[two] * rate
            mass = mixed = None
        if do3:
            q3, c3 = query_rows(three), cotangent(three)
            dq_t = jnp.zeros((width, resp), F32)
        for j in range(chunks):
            span = slice(j * CHUNK, (j + 1) * CHUNK)
            if do1:
                s = dot_nt(k_all[span, :], q1)
                if j == chunks - 1:
                    s = jnp.where(allowed, s, -jnp.inf)
                s_buf[one % 2][span, :] = s
                part = fold_rows(s, jnp.maximum)
                top = part if top is None else jnp.maximum(top, part)
                g_buf[one % 3][span, :] = dot_nt(v_all[span, :], c1)
            if do2:
                e = jnp.exp2(s_buf[two % 2][span, :] * rate - level)
                e_buf[two % 2][span, :] = e
                part = fold_rows(e, jnp.add)
                mass = part if mass is None else mass + part
                part = fold_rows(e * g_buf[two % 3][span, :], jnp.add)
                mixed = part if mixed is None else mixed + part
            if do3:
                p = e_buf[three % 2][span, :] * inv[three]
                ds = (p * (g_buf[three % 3][span, :] - delta[three])).astype(BF16)
                dv = dot_nn(p.astype(BF16), c3)
                dk = dot_nn(ds, q3)
                if three == 0:
                    dv_acc[span, :] = dv
                    dk_acc[span, :] = dk
                else:
                    dv_acc[span, :] += dv
                    dk_acc[span, :] += dk
                dq_t = dq_t + dot_nn(k_t[:, span], ds)
        if do1:
            peak[one] = jnp.max(top, axis=0, keepdims=True)
        if do2:
            inv[two] = 1.0 / jnp.sum(mass, axis=0, keepdims=True)
            delta[two] = jnp.sum(mixed, axis=0, keepdims=True) * inv[two]
        if do3:
            dq_ref[0, :, three * width : (three + 1) * width] = dq_t.T * (advantage * scale)

    drk_ref[0] = dk_acc[prompt:, :] * (advantage * scale)
    drv_ref[0] = dv_acc[prompt:, :] * advantage
    for owner in range(owners):
        rows = pl.ds(owner * share, share)
        dp_ref[owner, :share, :] = (dk_acc[rows, :] * (advantage * scale)).astype(BF16)
        dp_ref[owner, share:, :] = (dv_acc[rows, :] * advantage).astype(BF16)


def attention_grads(lengths, queries, grad_out, gathered, resp_keys, resp_values):
    owners = gathered.shape[0]
    resp, width = resp_keys.shape[1:]
    heads = queries.shape[2] // width
    share = (gathered.shape[1] - 16) // 2
    keys = owners * share + resp
    vmem = pl.BlockSpec(memory_space=pltpu.VMEM)
    products = 5 * 2 * heads * resp * keys * width
    return pl.pallas_call(
        functools.partial(attention_kernel, heads, owners, share),
        out_shape=(
            jax.ShapeDtypeStruct(queries.shape, F32),
            jax.ShapeDtypeStruct(resp_keys.shape, F32),
            jax.ShapeDtypeStruct(resp_values.shape, F32),
            jax.ShapeDtypeStruct((owners, 2 * share, width), BF16),
        ),
        in_specs=[pl.BlockSpec(memory_space=pltpu.SMEM)] + [vmem] * 5,
        out_specs=(vmem,) * 4,
        scratch_shapes=[
            pltpu.VMEM((keys, width), BF16),
            pltpu.VMEM((keys, width), BF16),
            pltpu.VMEM((width, keys), BF16),
            pltpu.VMEM((keys, width), F32),
            pltpu.VMEM((keys, width), F32),
        ]
        + [pltpu.VMEM((keys, resp), F32)] * 7,
        compiler_params=pltpu.CompilerParams(vmem_limit_bytes=48 * 1024 * 1024),
        cost_estimate=pl.CostEstimate(
            flops=products, bytes_accessed=8 * 1024 * 1024, transcendentals=heads * resp * keys
        ),
        name="attention_grads",
    )(lengths, queries, grad_out, gathered, resp_keys, resp_values)


def shards(queries, resp_keys, resp_values, prompt_keys, prompt_values, grad_out, lengths, rewards):
    share, width = prompt_keys.shape
    reward_rows = jnp.broadcast_to(rewards.astype(BF16)[:, None], (16, width))
    packed = jnp.concatenate([prompt_keys, prompt_values, reward_rows], axis=0)
    gathered = lax.all_gather(packed, "sample", axis=0, tiled=False)
    grad_queries, grad_resp_keys, grad_resp_values, parts = attention_grads(
        lengths, queries, grad_out, gathered, resp_keys, resp_values
    )
    received = lax.all_to_all(parts, "sample", split_axis=0, concat_axis=0, tiled=True)
    summed = jnp.sum(received.astype(F32), axis=0)
    return grad_queries, grad_resp_keys, grad_resp_values, summed[:share], summed[share:]


def solution(mesh):
    whole = P(("problem", "sample"), None, None)
    rows = P(("problem", "sample"), None)
    one = P(("problem", "sample"))
    return jax.shard_map(
        shards,
        mesh=mesh,
        in_specs=(whole, whole, whole, rows, rows, whole, one, one),
        out_specs=(whole, whole, whole, rows, rows),
        check_vma=False,
    )
```

time: 324 us -> 139 us (0.43)
  blocking collectives: 106 us -> 21.8 us
  waiting for transfers between devices: 136 us -> 72.9 us
  matrix products: 40.8 us -> 0 us
  Pallas kernels: 0 us -> 21.4 us
  other arithmetic: 9 us -> 1.65 us
  local copies, waits for them, and re-layouts: 11.9 us -> 5.68 us
  loops' own time: 3.35 us -> 0 us
    reduce_scatter x2 -> x0, waiting for transfers between devices: 136 us -> none  [the longest x1 71 us: shards(): lax.psum_scatter(advantage * prompt_kg, 'sample', scatter_dimension=0, ti...]
    all_gather x0 -> x1, waiting for transfers between devices: none -> 72.8 us  [shards(): gathered = lax.all_gather(packed, 'sample', axis=0, tiled=False)]
    all_gather x2 -> x0, blocking collectives: 67.4 us -> none  [the longest x1 34.8 us: shards(): lax.all_gather(prompt_values, 'sample', axis=0, tiled=True)]
    dot_general x48 -> x0, matrix products: 40.8 us -> none  [the longest x16 17 us: contract_last(): lax.dot_general(left, right, (((1,), (1,)), ((), ())), preferred_element_...]
    psum x1 -> x0, blocking collectives: 38.8 us -> none  [shards(): reward_total = lax.psum(jnp.sum(rewards.astype(jnp.float32)), 'sample')]
    all_to_all x0 -> x1, blocking collectives: none -> 21.8 us  [shards(): lax.all_to_all(parts, 'sample', split_axis=0, concat_axis=0, tiled=True)]
    pallas_call x0 -> x1, Pallas kernels: none -> 21.4 us  [attention_grads(): pl.pallas_call(functools.partial(attention_kernel, heads, owners, share),...]
    dynamic_slice x12 -> x0, local copies, waits for them, and re-layouts: 6.48 us -> none  [shards(): lax.scan(block_pass, (own_zero, own_zero, prompt_zero, prompt_zero), (que...]
  transfers between devices with their start and end apart: 2 -> 1, of which waited for: 2 -> 1; matrix products, arithmetic and copies ran while one was open for 1% -> 0% of each run, Pallas kernels for 0% -> 0%
where the time goes in v1:
time: 139 us
  waiting for transfers between devices  72.9 us (52%)
  blocking collectives  21.8 us (16%)
  Pallas kernels  21.4 us (15%)
  between operations  15.3 us (11%)
  local copies, waits for them, and re-layouts  5.68 us (4%)
  other arithmetic  1.65 us (1%)
    all_gather x1, waiting for transfers between devices, shards(): gathered = lax.all_gather(packed, 'sample', axis=0, tiled=False)  72.8 us
    all_to_all x1, blocking collectives, shards(): lax.all_to_all(parts, 'sample', split_axis=0, concat_axis=0, tiled=True)  21.8 us
    pallas_call x1, Pallas kernels, attention_grads(): pl.pallas_call(functools.partial(attention_kernel, heads, owners, share),...  21.4 us
    unnamed x10, local copies, waits for them, and re-layouts  5.01 us
  transfers between devices with their start and end apart: 1, of which 1 were waited for; matrix products, arithmetic and copies ran while one was open for 0% of the time, Pallas kernels for 0%

profile of v1, /device:TPU:2, one launch (start us, length us, event | category | flops | bytes accessed | tf_op | source)
XLA Modules:
  0.0 138.8 jit_solution(902962694296099107)
XLA Ops:
  7.2 0.0 all-gather.3.cloned.1.call-start
  7.9 1.5 %maximum_maximum_fusion = bf16[272,128]{1,0:T(8,128)(2,1)} fusion(bf16[128,128]{1,0:T(8,128)(2,1)} %param.12, bf16[128,128]{1,0:T(8,128)(2,1)} %param.11, bf16[272]{0:T(512)(128)(2,1)S(1)} %pad.2.clone), kind=kLoop, calls=%fused_computation.1 | loop fusion | flops 208896 | bytes 135712 | tf_op jit(solution)/shard_map/concatenate | solution.py:170
  9.4 0.0 all-gather.3.cloned.1.call-update
  10.1 72.8 %all-gather.3.cloned.1.call-done = bf16[4352,128]{1,0:T(8,128)(2,1)} async-done(((bf16[272,128]{1,0:T(8,128)(2,1)}), bf16[4352,128]{1,0:T(8,128)(2,1)}) %all-gather.3.cloned.1.call-update) | async-done | bytes 1114128 | tf_op jit(solution)/shard_map/all_gather | solution.py:171
  82.9 0.0 copy-start
  82.9 1.2 copy-done
  84.2 0.0 copy-start.1
  84.2 1.0 copy-done.1
  85.2 0.0 copy-start.2
  85.2 1.0 copy-done.2
  86.2 0.0 copy-start.3
  86.3 0.8 copy-done.3
  87.1 0.0 copy-start.4
  87.1 0.8 copy-done.4
  87.9 21.4 %attention_grads.1 = (f32[1,256,1024]{2,1,0:T(8,128)}, f32[1,256,128]{2,1,0:T(8,128)}, f32[1,256,128]{2,1,0:T(8,128)}, bf16[16,256,128]{2,1,0:T(8,128)(2,1)S(1)}) custom-call(s32[1]{0:T(128)S(6)} %copy.13.len_ref, bf16[1,256,1024]{2,1,0:T(8,128)(2,1)S(1)} %copy-done.1, bf16[1,256,1024]{2,1,0:T(8,128)(2,1)S(1)} %copy-done.2, ...), custom_call_target="tpu_custom_call" | custom-call | flops 6039797760 | bytes 8388608 | tf_op jit(solution)/shard_map/attention_grads/pallas_call | solution.py:141
  109.3 21.8 %all_to_all.5 = bf16[16,256,128]{2,1,0:T(8,128)(2,1)S(1)} all-to-all(bf16[16,256,128]{2,1,0:T(8,128)(2,1)S(1)} %get-tuple-element.12), channel_id=1, replica_groups=mesh['problem'=16,'sample'=16] {'sample'}, dimensions={0} | all-to-all | bytes 2097152 | tf_op jit(solution)/shard_map/all_to_all | solution.py:175
  131.2 0.1 convert_reduce_fusion
  131.3 0.7 fusion
  (2 shorter events, 0.0 us)
Async XLA Ops:
  7.2 75.8 %all-gather.3.cloned.1.call-start = ((), (), s32[]{:S(2)}) async-start(), calls=%async_computation.1 | async-start | bytes 1183744 | tf_op jit(solution)/shard_map/all_gather | solution.py:171
  82.9 1.2 copy-start
  84.2 1.0 copy-start.1
  85.2 1.0 copy-start.2
  86.2 0.8 copy-start.3
  87.1 0.8 copy-start.4
Sparse Core Ops, SparseCore 0:
  10.4 72.5 all-gather.2

commit v2 on v1

v2 whole, which is shorter than its diff:
```python
import functools
import math

import jax
import jax.numpy as jnp
from jax import lax
from jax.experimental import pallas as pl
from jax.experimental.pallas import tpu as pltpu
from jax.sharding import PartitionSpec as P

F32 = jnp.float32
BF16 = jnp.bfloat16
PAD = 16
PIECES = 3
SLICE = 64


def dot_nn(left, right):
    return lax.dot_general(left, right, (((1,), (0,)), ((), ())), preferred_element_type=F32)


def dot_nt(left, right):
    return lax.dot_general(left, right, (((1,), (1,)), ((), ())), preferred_element_type=F32)


def fold_rows(values, combine):
    parts = [values[i : i + 8] for i in range(0, values.shape[0], 8)]
    while len(parts) > 1:
        parts = [
            combine(parts[i], parts[i + 1]) if i + 1 < len(parts) else parts[i]
            for i in range(0, len(parts), 2)
        ]
    return parts[0]


def attention_kernel(
    heads, owners, share, len_ref, pay_ref, q_hbm, c_hbm, g_hbm, rk_hbm, rv_hbm,
    dq_ref, drk_ref, drv_ref, dp_ref,
    q_rows, c_rows, k_all, v_all, pay, k_t, dk_acc, dv_acc,
    s0, s1, g0, g1, e0, e1, p0, p1, ds0, ds1, q_sems, c_sems, sems,
):
    resp, width = rk_hbm.shape[1], rk_hbm.shape[2]
    prompt = owners * share
    keys = prompt + resp
    piece = keys // PIECES
    per_piece = piece // share
    scale = 1.0 / math.sqrt(width)
    rate = scale * math.log2(math.e)
    s_buf, g_buf, e_buf = (s0, s1), (g0, g1), (e0, e1)
    p_buf, ds_buf = (p0, p1), (ds0, ds1)

    def head_rows(h):
        return pl.ds(h * resp, resp)

    bring_q, bring_c = [], []
    for h in range(heads):
        lanes = pl.ds(h * width, width)
        bring_q.append(
            pltpu.make_async_copy(q_hbm.at[0, :, lanes], q_rows.at[head_rows(h), :], q_sems.at[h])
        )
        bring_c.append(
            pltpu.make_async_copy(c_hbm.at[0, :, lanes], c_rows.at[head_rows(h), :], c_sems.at[h])
        )
    owned = resp // share
    moves = [
        (g_hbm.at[:, pl.ds(0, share), :], k_all.at[pl.ds(0, owners)]),
        (g_hbm.at[:, pl.ds(share, share), :], v_all.at[pl.ds(0, owners)]),
        (g_hbm.at[:, pl.ds(2 * share, PAD), :], pay),
    ]
    for i in range(owned):
        rows = pl.ds(i * share, share)
        moves.append((rk_hbm.at[0, rows, :], k_all.at[owners + i]))
        moves.append((rv_hbm.at[0, rows, :], v_all.at[owners + i]))
    bring = [pltpu.make_async_copy(src, dst, sems.at[i]) for i, (src, dst) in enumerate(moves)]
    bring_q[0].start()
    bring_c[0].start()
    for copy in bring:
        copy.start()
    for h in range(1, heads):
        bring_q[h].start()
        bring_c[h].start()
    for copy in bring:
        copy.wait()

    total = jnp.zeros((1, width), F32)
    for owner in range(owners):
        total = total + pay[owner].astype(F32)[:1]
    advantage = pay_ref[0].astype(F32) - total / owners

    live = lax.broadcasted_iota(jnp.int32, (resp, width), 0) < len_ref[0]
    key_at = lax.broadcasted_iota(jnp.int32, (SLICE, resp), 0)
    query_at = lax.broadcasted_iota(jnp.int32, (SLICE, resp), 1)

    def rows_of(ref, i):
        return ref[i * per_piece : (i + 1) * per_piece].reshape(piece, width)

    peaks, rescale, delta = {}, {}, {}
    for t in range(heads + 1):
        one, two = t, t - 1
        do1, do2 = one < heads, two >= 0
        if do1:
            bring_q[one].wait()
            bring_c[one].wait()
            rows = head_rows(one)
            q1 = q_rows[rows, :]
            c1 = jnp.where(live, c_rows[rows, :], jnp.zeros((), BF16))
            c_rows[rows, :] = c1
            mass = mixed = peak = None
            levels = []
        if do2:
            pair = (two // 2) % 2
            half = slice((two % 2) * resp, (two % 2 + 1) * resp)
            dq_t = None
        for i in range(PIECES):
            first = i * piece
            span = slice(first, first + piece)
            if t == 0:
                k_t[:, span] = rows_of(k_all, i).T
            if do1:
                s_now, g_now, e_now = s_buf[i % 2], g_buf[one % 2], e_buf[one % 2]
                s_now[...] = dot_nt(rows_of(k_all, i), q1)
                g_now[span, :] = dot_nt(rows_of(v_all, i), c1)
                top = None
                for at in range(0, piece, SLICE):
                    s = s_now[at : at + SLICE, :]
                    if first + at >= prompt:
                        s = jnp.where(key_at + (first + at - prompt) <= query_at, s, -jnp.inf)
                    part = fold_rows(s, jnp.maximum)
                    top = part if top is None else jnp.maximum(top, part)
                top = jnp.max(top, axis=0, keepdims=True)
                if peak is None:
                    peak = top
                    levels.append(peak * rate)
                else:
                    peak = jnp.maximum(peak, top)
                    levels.append(peak * rate)
                    weight = jnp.exp2(levels[-2] - levels[-1])
                    mass, mixed = mass * weight, mixed * weight
                for at in range(0, piece, SLICE):
                    e = jnp.exp2(s_now[at : at + SLICE, :] * rate - levels[-1])
                    if first + at >= prompt:
                        e = jnp.where(key_at + (first + at - prompt) <= query_at, e, 0.0)
                    e_now[first + at : first + at + SLICE, :] = e
                    part = fold_rows(e, jnp.add)
                    mass = part if mass is None else mass + part
                    part = fold_rows(e * g_now[first + at : first + at + SLICE, :], jnp.add)
                    mixed = part if mixed is None else mixed + part
            if do2:
                factor, shift = rescale[two][i], delta[two]
                for at in range(first, first + piece, SLICE):
                    here = slice(at, at + SLICE)
                    p = e_buf[two % 2][here, :] * factor
                    p_buf[pair][here, half] = p.astype(BF16)
                    ds_buf[pair][here, half] = (p * (g_buf[two % 2][here, :] - shift)).astype(BF16)
                part = dot_nn(k_t[:, span], ds_buf[pair][span, half])
                dq_t = part if dq_t is None else dq_t + part
                if two % 2 == 1:
                    both = slice((two - 1) * resp, (two + 1) * resp)
                    dk = dot_nn(ds_buf[pair][span, :], q_rows[both, :])
                    dv = dot_nn(p_buf[pair][span, :], c_rows[both, :])
                    if two > 1:
                        dk = dk_acc[span, :] + dk
                        dv = dv_acc[span, :] + dv
                    if two < heads - 1:
                        dk_acc[span, :] = dk
                        dv_acc[span, :] = dv
                    else:
                        dk = dk * (advantage * scale)
                        dv = dv * advantage
                        for sub in range(per_piece):
                            owner = i * per_piece + sub
                            part = slice(sub * share, (sub + 1) * share)
                            if owner < owners:
                                dp_ref[owner, :share, :] = dk[part].astype(BF16)
                                dp_ref[owner, share:, :] = dv[part].astype(BF16)
                            else:
                                rows = slice((owner - owners) * share, (owner - owners + 1) * share)
                                drk_ref[0, rows, :] = dk[part]
                                drv_ref[0, rows, :] = dv[part]
        if do1:
            inv = 1.0 / jnp.sum(mass, axis=0, keepdims=True)
            delta[one] = jnp.sum(mixed, axis=0, keepdims=True) * inv
            rescale[one] = [jnp.exp2(level - levels[-1]) * inv for level in levels]
        if do2:
            dq_ref[0, :, two * width : (two + 1) * width] = dq_t.T * (advantage * scale)


def attention_grads(lengths, rewards, queries, grad_out, gathered, resp_keys, resp_values):
    owners = gathered.shape[0]
    resp, width = resp_keys.shape[1:]
    heads = queries.shape[2] // width
    share = (gathered.shape[1] - PAD) // 2
    keys = owners * share + resp
    piece = keys // PIECES
    vmem = pl.BlockSpec(memory_space=pltpu.VMEM)
    smem = pl.BlockSpec(memory_space=pltpu.SMEM)
    return pl.pallas_call(
        functools.partial(attention_kernel, heads, owners, share),
        out_shape=(
            jax.ShapeDtypeStruct(queries.shape, F32),
            jax.ShapeDtypeStruct(resp_keys.shape, F32),
            jax.ShapeDtypeStruct(resp_values.shape, F32),
            jax.ShapeDtypeStruct((owners, 2 * share, width), BF16),
        ),
        in_specs=[smem] * 2 + [pl.BlockSpec(memory_space=pl.ANY)] * 5,
        out_specs=(vmem,) * 4,
        scratch_shapes=[
            pltpu.VMEM((heads * resp, width), BF16),
            pltpu.VMEM((heads * resp, width), BF16),
            pltpu.VMEM((keys // share, share, width), BF16),
            pltpu.VMEM((keys // share, share, width), BF16),
            pltpu.VMEM((owners, PAD, width), BF16),
            pltpu.VMEM((width, keys), BF16),
            pltpu.VMEM((keys, width), F32),
            pltpu.VMEM((keys, width), F32),
        ]
        + [pltpu.VMEM((piece, resp), F32)] * 2
        + [pltpu.VMEM((keys, resp), F32)] * 4
        + [pltpu.VMEM((keys, 2 * resp), BF16)] * 4
        + [
            pltpu.SemaphoreType.DMA((heads,)),
            pltpu.SemaphoreType.DMA((heads,)),
            pltpu.SemaphoreType.DMA((3 + 2 * (resp // share),)),
        ],
        compiler_params=pltpu.CompilerParams(vmem_limit_bytes=48 * 1024 * 1024),
        cost_estimate=pl.CostEstimate(
            flops=10 * heads * resp * keys * width,
            bytes_accessed=4 * 1024 * 1024,
            transcendentals=heads * resp * keys,
        ),
        name="attention_grads",
    )(lengths, rewards, queries, grad_out, gathered, resp_keys, resp_values)


def shards(queries, resp_keys, resp_values, prompt_keys, prompt_values, grad_out, lengths, rewards):
    share, width = prompt_keys.shape
    owners = lax.axis_size("sample")
    reward_rows = jnp.broadcast_to(rewards.astype(BF16)[:, None], (PAD, width))
    packed = jnp.concatenate([prompt_keys, prompt_values, reward_rows], axis=0)
    copies = jnp.broadcast_to(packed[None], (owners,) + packed.shape)
    gathered = lax.all_to_all(copies, "sample", split_axis=0, concat_axis=0, tiled=True)
    grad_queries, grad_resp_keys, grad_resp_values, parts = attention_grads(
        lengths, rewards, queries, grad_out, gathered, resp_keys, resp_values
    )
    received = lax.all_to_all(parts, "sample", split_axis=0, concat_axis=0, tiled=True)
    summed = jnp.sum(received.astype(F32), axis=0)
    return grad_queries, grad_resp_keys, grad_resp_values, summed[:share], summed[share:]


def solution(mesh):
    whole = P(("problem", "sample"), None, None)
    rows = P(("problem", "sample"), None)
    one = P(("problem", "sample"))
    return jax.shard_map(
        shards,
        mesh=mesh,
        in_specs=(whole, whole, whole, rows, rows, whole, one, one),
        out_specs=(whole, whole, whole, rows, rows),
        check_vma=False,
    )
```

time: 139 us -> 92.2 us (0.66)
  waiting for transfers between devices: 72.9 us -> 27.8 us
  between operations: 15.3 us -> 1.99 us
  starting transfers between devices: 0.04 us -> 9.73 us
  blocking collectives: 21.8 us -> 31.1 us
  local copies, waits for them, and re-layouts: 5.68 us -> 1.82 us
  Pallas kernels: 21.4 us -> 18.4 us
    all_gather x1 -> x0, waiting for transfers between devices: 72.8 us -> none  [shards(): gathered = lax.all_gather(packed, 'sample', axis=0, tiled=False)]
    all_to_all x0 -> x1, waiting for transfers between devices: none -> 27.8 us  [shards(): lax.all_to_all(copies, 'sample', split_axis=0, concat_axis=0, tiled=True)]
    all_to_all x0 -> x1, starting transfers between devices: none -> 9.73 us  [shards(): lax.all_to_all(copies, 'sample', split_axis=0, concat_axis=0, tiled=True)]
    all_to_all x1, blocking collectives: 21.8 us -> 31.1 us  [shards(): lax.all_to_all(parts, 'sample', split_axis=0, concat_axis=0, tiled=True)]
    unnamed x10 -> x8, local copies, waits for them, and re-layouts: 5.01 us -> 0.01 us
    pallas_call x1, Pallas kernels: 21.4 us -> 18.4 us  [attention_grads(): pl.pallas_call(functools.partial(attention_kernel, heads, owners, share),...]
where the time goes in v2:
time: 92.2 us; the launch traced here: 91.9 us
  blocking collectives  31.1 us (34%)
  waiting for transfers between devices  27.8 us (30%)
  Pallas kernels  18.4 us (20%)
  starting transfers between devices  9.73 us (11%)
  between operations  1.99 us (2%)
  local copies, waits for them, and re-layouts  1.82 us (2%)
  other arithmetic  1.02 us (1%)
    all_to_all x1, blocking collectives, shards(): lax.all_to_all(parts, 'sample', split_axis=0, concat_axis=0, tiled=True)  31.1 us
    all_to_all x1, waiting for transfers between devices, shards(): lax.all_to_all(copies, 'sample', split_axis=0, concat_axis=0, tiled=True)  27.8 us
    pallas_call x1, Pallas kernels, attention_grads(): pl.pallas_call(functools.partial(attention_kernel, heads, owners, share),...  18.4 us
    all_to_all x1, starting transfers between devices, shards(): lax.all_to_all(copies, 'sample', split_axis=0, concat_axis=0, tiled=True)  9.73 us
  transfers between devices with their start and end apart: 1, of which 1 were waited for; matrix products, arithmetic and copies ran while one was open for 0% of the time, Pallas kernels for 0%

profile of v2, /device:TPU:2, one launch (start us, length us, event | category | flops | bytes accessed | tf_op | source)
XLA Modules:
  0.0 91.9 jit_solution(14701806670818133662)
XLA Ops:
  1.3 0.9 maximum_maximum_fusion
  2.2 1.1 %broadcast_in_dim.16 = bf16[16,272,128]{2,1,0:T(8,128)(2,1)} broadcast(bf16[272,128]{1,0:T(8,128)(2,1)S(1)} %maximum_maximum_fusion), dimensions={1,2} | broadcast | bytes 1183744 | tf_op jit(solution)/shard_map/broadcast_in_dim | solution.py:240
  3.3 0.0 copy-start
  3.3 0.0 copy-start.1
  3.3 0.0 copy-start.2
  3.3 0.0 copy-start.3
  3.3 9.7 %all-to-all-start = ((bf16[16,272,128]{2,1,0:T(8,128)(2,1)}), bf16[16,272,128]{2,1,0:T(8,128)(2,1)S(1)}, u32[]{:S(2)}, u32[]{:S(2)}) async-start(bf16[16,272,128]{2,1,0:T(8,128)(2,1)} %broadcast_in_dim.16), calls=%async_computation | async-start | bytes 2228224 | tf_op jit(solution)/shard_map/all_to_all | solution.py:241
  13.7 27.8 %all-to-all-done.g_hbm = bf16[16,272,128]{2,1,0:T(8,128)(2,1)S(1)} async-done(((bf16[16,272,128]{2,1,0:T(8,128)(2,1)}), bf16[16,272,128]{2,1,0:T(8,128)(2,1)S(1)}, u32[]{:S(2)}, u32[]{:S(2)}) %all-to-all-start) | async-done | bytes 1114144 | tf_op jit(solution)/shard_map/all_to_all | solution.py:241
  41.5 0.0 copy-done
  41.5 0.0 copy-done.1
  41.5 0.0 copy-done.2
  41.5 0.0 copy-done.3
  41.5 18.4 %attention_grads.1 = (f32[1,256,1024]{2,1,0:T(8,128)}, f32[1,256,128]{2,1,0:T(8,128)}, f32[1,256,128]{2,1,0:T(8,128)}, bf16[16,256,128]{2,1,0:T(8,128)(2,1)S(1)}) custom-call(s32[1]{0:T(128)S(6)} %copy.13.len_ref, s32[1]{0:T(128)S(6)} %copy.14.pay_ref, bf16[1,256,1024]{2,1,0:T(8,128)(2,1)S(1)} %copy-done, bf16[1,256,1024]{2,1,0:T(8,128)(2,1)S(1)} %copy-done.1, ...), custom_call_target="tpu_custom_call" | custom-call | flops 6039797760 | bytes 4194304 | tf_op jit(solution)/shard_map/attention_grads/pallas_call | solution.py:197
  60.0 31.1 %all_to_all.10 = bf16[16,256,128]{2,1,0:T(8,128)(2,1)S(1)} all-to-all(bf16[16,256,128]{2,1,0:T(8,128)(2,1)S(1)} %get-tuple-element.12), channel_id=1, replica_groups=mesh['problem'=16,'sample'=16] {'sample'}, dimensions={0} | all-to-all | bytes 2097152 | tf_op jit(solution)/shard_map/all_to_all | solution.py:245
  91.1 0.1 convert_reduce_fusion
  91.2 0.7 fusion
  (2 shorter events, 0.0 us)
Async XLA Ops:
  3.3 38.2 %copy-start = (bf16[1,256,1024]{2,1,0:T(8,128)(2,1)S(1)}, bf16[1,256,1024]{2,1,0:T(8,128)(2,1)}, u32[]{:S(2)}) copy-start(bf16[1,256,1024]{2,1,0:T(8,128)(2,1)} %q_hbm.1) | copy-start | bytes 1572868
  3.3 38.2 %copy-start.1 = (bf16[1,256,1024]{2,1,0:T(8,128)(2,1)S(1)}, bf16[1,256,1024]{2,1,0:T(8,128)(2,1)}, u32[]{:S(2)}) copy-start(bf16[1,256,1024]{2,1,0:T(8,128)(2,1)} %c_hbm.1) | copy-start | bytes 1572868
  3.3 38.2 %copy-start.2 = (bf16[1,256,128]{2,1,0:T(8,128)(2,1)S(1)}, bf16[1,256,128]{2,1,0:T(8,128)(2,1)}, u32[]{:S(2)}) copy-start(bf16[1,256,128]{2,1,0:T(8,128)(2,1)} %rk_hbm.1) | copy-start | bytes 196612
  3.3 38.2 %copy-start.3 = (bf16[1,256,128]{2,1,0:T(8,128)(2,1)S(1)}, bf16[1,256,128]{2,1,0:T(8,128)(2,1)}, u32[]{:S(2)}) copy-start(bf16[1,256,128]{2,1,0:T(8,128)(2,1)} %rv_hbm.1) | copy-start | bytes 196612
  3.3 38.2 %all-to-all-start = ((bf16[16,272,128]{2,1,0:T(8,128)(2,1)}), bf16[16,272,128]{2,1,0:T(8,128)(2,1)S(1)}, u32[]{:S(2)}, u32[]{:S(2)}) async-start(bf16[16,272,128]{2,1,0:T(8,128)(2,1)} %broadcast_in_dim.16), calls=%async_computation | async-start | bytes 2228224 | tf_op jit(solution)/shard_map/all_to_all | solution.py:241

commit v3 on v1

v3 whole, which is shorter than its diff:
```python
import functools
import math

import jax
import jax.numpy as jnp
from jax import lax
from jax.experimental import pallas as pl
from jax.experimental.pallas import tpu as pltpu
from jax.sharding import PartitionSpec as P

F32 = jnp.float32
BF16 = jnp.bfloat16
PAD = 16
RING = 8
SLICE = 64

VMEM_SPEC = pl.BlockSpec(memory_space=pltpu.VMEM)
SMEM_SPEC = pl.BlockSpec(memory_space=pltpu.SMEM)
ANY_SPEC = pl.BlockSpec(memory_space=pl.ANY)


def dot_nn(left, right):
    return lax.dot_general(left, right, (((1,), (0,)), ((), ())), preferred_element_type=F32)


def dot_nt(left, right):
    return lax.dot_general(left, right, (((1,), (1,)), ((), ())), preferred_element_type=F32)


def fold_rows(values, combine):
    parts = [values[i : i + 8] for i in range(0, values.shape[0], 8)]
    while len(parts) > 1:
        parts = [
            combine(parts[i], parts[i + 1]) if i + 1 < len(parts) else parts[i]
            for i in range(0, len(parts), 2)
        ]
    return parts[0]


def pack_places(blocks, share):
    size = 2 * share + PAD
    return [(ref, at) for ref in blocks for at in range(0, ref.shape[0], size)]


def load_rows(blocks, own, k_all, v_all, share):
    places = pack_places(blocks, share)
    for i, (ref, at) in enumerate(places):
        k_all[i * share : (i + 1) * share, :] = ref[at : at + share, :]
        v_all[i * share : (i + 1) * share, :] = ref[at + share : at + 2 * share, :]
    if own:
        k_all[len(places) * share :, :] = own[0][0]
        v_all[len(places) * share :, :] = own[1][0]
    return len(places) * share


def own_mask(at, resp):
    key_at = lax.broadcasted_iota(jnp.int32, (SLICE, resp), 0) + at
    return key_at <= lax.broadcasted_iota(jnp.int32, (SLICE, resp), 1)


def forward_kernel(heads, share, count, opening, *refs):
    refs, scratch = refs[:-6], refs[-6:]
    k_all, v_all, s0, s1, g0, g1 = scratch
    if opening:
        len_ref, q_ref, c_ref = refs[:3]
        blocks, own = refs[3 : 3 + count], refs[3 + count : 5 + count]
        out_ref, q_rows, c_rows = refs[5 + count :]
    else:
        q_rows, c_rows = refs[:2]
        blocks, own, out_ref = refs[2 : 2 + count], (), refs[-1]
    width, resp = q_rows.shape[1], q_rows.shape[0] // heads
    rate = math.log2(math.e) / math.sqrt(width)
    s_buf, g_buf = (s0, s1), (g0, g1)
    prompt = load_rows(blocks, own, k_all, v_all, share)
    keys = k_all.shape[0]
    if opening:
        live = lax.broadcasted_iota(jnp.int32, (resp, width), 0) < len_ref[0]

    for t in range(heads + 1):
        if t < heads:
            rows = slice(t * resp, (t + 1) * resp)
            if opening:
                lanes = slice(t * width, (t + 1) * width)
                q_rows[rows, :] = q_ref[0, :, lanes]
                c_rows[rows, :] = jnp.where(live, c_ref[0, :, lanes], jnp.zeros((), BF16))
            s_buf[t % 2][...] = dot_nt(k_all[...], q_rows[rows, :])
            g_buf[t % 2][...] = dot_nt(v_all[...], c_rows[rows, :])
        if t > 0:
            h = t - 1
            s_now, g_now = s_buf[h % 2], g_buf[h % 2]
            top = mass = mixed = None
            for at in range(0, keys, SLICE):
                s = s_now[at : at + SLICE, :]
                if at >= prompt:
                    s = jnp.where(own_mask(at - prompt, resp), s, -jnp.inf)
                part = fold_rows(s, jnp.maximum)
                top = part if top is None else jnp.maximum(top, part)
            top = jnp.max(top, axis=0, keepdims=True)
            level = top * rate
            for at in range(0, keys, SLICE):
                e = jnp.exp2(s_now[at : at + SLICE, :] * rate - level)
                if at >= prompt:
                    e = jnp.where(own_mask(at - prompt, resp), e, 0.0)
                part = fold_rows(e, jnp.add)
                mass = part if mass is None else mass + part
                part = fold_rows(e * g_now[at : at + SLICE, :], jnp.add)
                mixed = part if mixed is None else mixed + part
            out_ref[h : h + 1, :] = top
            out_ref[heads + h : heads + h + 1, :] = jnp.sum(mass, axis=0, keepdims=True)
            out_ref[2 * heads + h : 2 * heads + h + 1, :] = jnp.sum(mixed, axis=0, keepdims=True)
    paid = jnp.zeros((1, width), F32)
    for ref, at in pack_places(blocks, share):
        paid = paid + ref[at + 2 * share : at + 2 * share + PAD, :].astype(F32)[:1]
    out_ref[3 * heads :, :] = jnp.broadcast_to(jnp.max(paid), (heads, resp))


def backward_kernel(heads, share, owners, count, stats, after, more, last, *refs):
    refs, scratch = refs[:-7], refs[-7:]
    k_all, v_all, k_t, s_now, g_now, p_all, ds_all = scratch
    pay_ref, q_rows, c_rows = refs[:3]
    refs = refs[3:]
    stat_refs, refs = refs[:stats], refs[stats:]
    blocks, refs = refs[:count], refs[count:]
    own, refs = (refs[:2], refs[2:]) if last else ((), refs)
    prior, refs = (refs[0], refs[1:]) if more else (None, refs)
    refs = refs[after:]
    dq_ref, refs = refs[0], refs[1:]
    part_refs, own_out = refs[:count], refs[count:]
    width, resp = q_rows.shape[1], q_rows.shape[0] // heads
    scale = 1.0 / math.sqrt(width)
    rate = scale * math.log2(math.e)
    prompt = load_rows(blocks, own, k_all, v_all, share)
    keys = k_all.shape[0]

    peaks = [ref[:heads, :] for ref in stat_refs]
    peak = functools.reduce(jnp.maximum, peaks)
    mass, mixed, paid = 0.0, 0.0, 0.0
    for ref, local in zip(stat_refs, peaks):
        weight = jnp.exp2((local - peak) * rate)
        mass = mass + ref[heads : 2 * heads, :] * weight
        mixed = mixed + ref[2 * heads : 3 * heads, :] * weight
        paid = paid + ref[3 * heads :, :]
    level = peak * rate + jnp.log2(mass)
    delta = mixed / mass
    advantage = (pay_ref[0].astype(F32) - paid / owners)[:1, :width]

    for at in range(0, keys, share):
        k_t[:, at : at + share] = k_all[at : at + share, :].T
    half = heads // 2
    dk = dv = None
    for h in range(heads):
        rows = slice(h * resp, (h + 1) * resp)
        s_now[h % 2] = dot_nt(k_all[...], q_rows[rows, :])
        g_now[h % 2] = dot_nt(v_all[...], c_rows[rows, :])
        for at in range(0, keys, SLICE):
            here = slice(at, at + SLICE)
            p = jnp.exp2(s_now[h % 2, here, :] * rate - level[h : h + 1])
            if at >= prompt:
                p = jnp.where(own_mask(at - prompt, resp), p, 0.0)
            p_all[here, rows] = p.astype(BF16)
            ds_all[here, rows] = (p * (g_now[h % 2, here, :] - delta[h : h + 1])).astype(BF16)
        lanes = slice(h * width, (h + 1) * width)
        dq = dot_nn(k_t[...], ds_all[:, rows])
        if more:
            dq = dq + prior[lanes, :]
        if last:
            dq_ref[0, :, lanes] = dq.T * (advantage * scale)
        else:
            dq_ref[lanes, :] = dq
        if h % half == half - 1:
            block = slice((h + 1 - half) * resp, (h + 1) * resp)
            dk_part = dot_nn(ds_all[:, block], q_rows[block, :])
            dv_part = dot_nn(p_all[:, block], c_rows[block, :])
            dk = dk_part if dk is None else dk + dk_part
            dv = dv_part if dv is None else dv + dv_part
    dk, dv = dk * (advantage * scale), dv * advantage
    at = 0
    for ref in part_refs:
        for base in range(0, ref.shape[0], 2 * share):
            ref[base : base + share, :] = dk[at : at + share].astype(ref.dtype)
            ref[base + share : base + 2 * share, :] = dv[at : at + share].astype(ref.dtype)
            at += share
    if last:
        own_out[0][0] = dk[prompt:]
        own_out[1][0] = dv[prompt:]


def count_keys(blocks, share, own):
    return share * sum(b.shape[0] // (2 * share + PAD) for b in blocks) + (
        own[0].shape[1] if own else 0
    )


def forward_stats(heads, share, blocks, rows=(), opening=()):
    if opening:
        lengths, queries, grad_out, *own = opening
        resp, width = queries.shape[1], queries.shape[2] // heads
        operands = (lengths, queries, grad_out, *blocks, *own)
        specs = [SMEM_SPEC] + [VMEM_SPEC] * (len(operands) - 1)
    else:
        own = ()
        resp, width = rows[0].shape[0] // heads, rows[0].shape[1]
        operands = (*rows, *blocks)
        specs = [VMEM_SPEC] * len(operands)
    keys = count_keys(blocks, share, own)
    outs = [jax.ShapeDtypeStruct((4 * heads, resp), F32)]
    if opening:
        outs += [jax.ShapeDtypeStruct((heads * resp, width), BF16)] * 2
    return pl.pallas_call(
        functools.partial(forward_kernel, heads, share, len(blocks), bool(opening)),
        out_shape=tuple(outs),
        in_specs=specs,
        out_specs=(VMEM_SPEC,) * len(outs),
        scratch_shapes=[pltpu.VMEM((keys, width), BF16)] * 2 + [pltpu.VMEM((keys, resp), F32)] * 4,
        compiler_params=pltpu.CompilerParams(vmem_limit_bytes=24 * 1024 * 1024),
        cost_estimate=pl.CostEstimate(
            flops=12 * heads * resp * keys * width,
            bytes_accessed=1024 * 1024,
            transcendentals=heads * resp * keys,
        ),
        name="forward_stats",
    )(*operands)


def backward_grads(rewards, rows, stats, blocks, dtypes, owners, heads, share, own, prior, after):
    resp, width = rows[0].shape[0] // heads, rows[0].shape[1]
    last, more = bool(own), prior is not None
    keys = count_keys(blocks, share, own)
    dq_shape = (1, resp, heads * width) if last else (heads * width, resp)
    outs = [jax.ShapeDtypeStruct(dq_shape, F32)]
    for block, dtype in zip(blocks, dtypes):
        packs = block.shape[0] // (2 * share + PAD)
        outs.append(jax.ShapeDtypeStruct((packs * 2 * share, width), dtype))
    outs += [jax.ShapeDtypeStruct((1, resp, width), F32)] * len(own)
    operands = (*rows, *stats, *blocks, *own, *((prior,) if more else ()))
    return pl.pallas_call(
        functools.partial(
            backward_kernel, heads, share, owners, len(blocks), len(stats), len(after), more, last
        ),
        out_shape=tuple(outs),
        in_specs=[SMEM_SPEC] + [VMEM_SPEC] * len(operands) + [ANY_SPEC] * len(after),
        out_specs=(VMEM_SPEC,) * len(outs),
        scratch_shapes=[pltpu.VMEM((keys, width), BF16)] * 2
        + [pltpu.VMEM((width, keys), BF16)]
        + [pltpu.VMEM((2, keys, resp), F32)] * 2
        + [pltpu.VMEM((keys, heads * resp), BF16)] * 2,
        compiler_params=pltpu.CompilerParams(vmem_limit_bytes=24 * 1024 * 1024),
        cost_estimate=pl.CostEstimate(
            flops=30 * heads * resp * keys * width,
            bytes_accessed=2 * 1024 * 1024,
            transcendentals=heads * resp * keys,
        ),
        name="backward_grads",
    )(rewards, *operands, *after)


def send(block, plane, step):
    pairs = [
        (y * RING + z, (y + plane) % 2 * RING + (z + step) % RING)
        for y in range(2)
        for z in range(RING)
    ]
    return lax.ppermute(block, "sample", pairs)


def shards(queries, resp_keys, resp_values, prompt_keys, prompt_values, grad_out, lengths, rewards):
    share, width = prompt_keys.shape
    heads = queries.shape[2] // width
    owners = lax.axis_size("sample")
    reward_rows = jnp.broadcast_to(rewards.astype(BF16)[:, None], (PAD, width))
    packed = jnp.concatenate([prompt_keys, prompt_values, reward_rows], axis=0)

    swapped = send(packed, 1, 0)
    pairs = {0: jnp.concatenate([packed, swapped], axis=0)}
    for step in (1, 2, 3, 4):
        pairs[step] = send(pairs[step - 1], 0, 1)
        if step < 4:
            pairs[RING - step] = send(pairs[(RING - step + 1) % RING], 0, -1)

    own = (resp_keys, resp_values)
    first, *rows = forward_stats(
        heads, share, [packed], opening=(lengths, queries, grad_out, *own)
    )
    stats = [first]
    for blocks in ([swapped], [pairs[1], pairs[7]], [pairs[2], pairs[6]], [pairs[3], pairs[5]], [pairs[4]]):
        stats += forward_stats(heads, share, blocks, rows)

    back = functools.partial(
        backward_grads, rewards, rows, stats, owners=owners, heads=heads, share=share
    )

    def add(received, part):
        return (received.astype(F32) + part).astype(BF16)

    dq, down = back([pairs[4]], [BF16], own=(), prior=None, after=())
    dq, part, up = back([pairs[3], pairs[5]], [F32, BF16], own=(), prior=dq, after=())
    down = add(send(down, 0, -1), part)
    for step in (2, 1):
        dq, part_down, part_up = back(
            [pairs[step], pairs[RING - step]], [F32, F32], own=(), prior=dq, after=(down, up)
        )
        down = add(send(down, 0, -1), part_down)
        up = add(send(up, 0, 1), part_up)
    grad_queries, mine, grad_resp_keys, grad_resp_values = back(
        [pairs[0]], [F32], own=own, prior=dq, after=(down, up)
    )
    mine = mine + send(down, 0, -1).astype(F32) + send(up, 0, 1).astype(F32)
    total = mine[: 2 * share] + send(mine[2 * share :].astype(BF16), 1, 0).astype(F32)
    return grad_queries, grad_resp_keys, grad_resp_values, total[:share], total[share:]


def solution(mesh):
    whole = P(("problem", "sample"), None, None)
    rows = P(("problem", "sample"), None)
    one = P(("problem", "sample"))
    return jax.shard_map(
        shards,
        mesh=mesh,
        in_specs=(whole, whole, whole, rows, rows, whole, one, one),
        out_specs=(whole, whole, whole, rows, rows),
        check_vma=False,
    )
```

time: 139 us -> 71.1 us (0.51)
  waiting for transfers between devices: 72.9 us -> 12.1 us
  starting transfers between devices: 0.04 us -> 26.3 us
  blocking collectives: 21.8 us -> 0 us
  between operations: 15.3 us -> 2.14 us
  Pallas kernels: 21.4 us -> 26.4 us
  local copies, waits for them, and re-layouts: 5.68 us -> 2.78 us
    all_gather x1 -> x0, waiting for transfers between devices: 72.8 us -> none  [shards(): gathered = lax.all_gather(packed, 'sample', axis=0, tiled=False)]
    ppermute x0 -> x16, starting transfers between devices: none -> 26.3 us  [send(): return lax.ppermute(block, 'sample', pairs)]
    all_to_all x1 -> x0, blocking collectives: 21.8 us -> none  [shards(): lax.all_to_all(parts, 'sample', split_axis=0, concat_axis=0, tiled=True)]
    ppermute x0 -> x16, waiting for transfers between devices: none -> 12.1 us  [send(): return lax.ppermute(block, 'sample', pairs)]
    pallas_call x1 -> x11, Pallas kernels: 21.4 us -> 26.4 us  [the longest x5 18 us: backward_grads(): pl.pallas_call(functools.partial(backward_kernel, heads, share, owners, l...]
    unnamed x10 -> x12, local copies, waits for them, and re-layouts: 5.01 us -> 2.11 us
  transfers between devices with their start and end apart: 1 -> 16, of which waited for: 1 -> 7; matrix products, arithmetic and copies ran while one was open for 0% -> 0% of each run, Pallas kernels for 0% -> 32%
where the time goes in v3:
time: 71.1 us; the launch traced here: 70.9 us
  Pallas kernels  26.4 us (37%)
  starting transfers between devices  26.3 us (37%)
  waiting for transfers between devices  12.1 us (17%)
  local copies, waits for them, and re-layouts  2.78 us (4%)
  between operations  2.14 us (3%)
  other arithmetic  1.06 us (1%)
    ppermute x16, starting transfers between devices, send(): return lax.ppermute(block, 'sample', pairs)  26.3 us
    pallas_call x5, Pallas kernels, backward_grads(): pl.pallas_call(functools.partial(backward_kernel, heads, share, owners, l...  18 us
    ppermute x16, waiting for transfers between devices, send(): return lax.ppermute(block, 'sample', pairs)  12.1 us
    pallas_call x6, Pallas kernels, forward_stats(): pl.pallas_call(functools.partial(forward_kernel, heads, share, len(blocks...  8.46 us
    unnamed x12, local copies, waits for them, and re-layouts  2.11 us
  transfers between devices with their start and end apart: 16, of which 7 were waited for; matrix products, arithmetic and copies ran while one was open for 0% of the time, Pallas kernels for 32%

profile of v3, /device:TPU:2, one launch (start us, length us, event | category | flops | bytes accessed | tf_op | source)
XLA Modules:
  0.0 70.9 jit_solution(5671058085642474468)
XLA Ops:
  1.3 0.8 %pad_maximum_fusion.1.refs_3_ = bf16[272,128]{1,0:T(8,128)(2,1)S(1)} fusion(bf16[16,128]{1,0:T(8,128)(2,1)S(1)} %broadcast_in_dim.9, bf16[128,128]{1,0:T(8,128)(2,1)} %param.12, bf16[128,128]{1,0:T(8,128)(2,1)} %param.11), kind=kLoop, calls=%fused_computation.9 | loop fusion | flops 208896 | bytes 139264 | tf_op jit(solution)/shard_map/concatenate | solution.py:271
  2.1 1.6 %collective-permute-start = (bf16[272,128]{1,0:T(8,128)(2,1)S(1)}, bf16[272,128]{1,0:T(8,128)(2,1)S(1)}, u32[]{:S(2)}, u32[]{:S(2)}) collective-permute-start(bf16[272,128]{1,0:T(8,128)(2,1)S(1)} %pad_maximum_fusion.1.refs_3_), channel_id=1, source_target_pairs={{0,8},{1,9},{2,10},{3,11},{4,12},{5,13},{6,14},{7,15},{8,0},{9,1},... | collective-permute-start | bytes 208904 | tf_op jit(solution)/shard_map/ppermute | solution.py:263
  4.4 2.1 %collective-permute-done.refs_2_ = bf16[272,128]{1,0:T(8,128)(2,1)S(1)} collective-permute-done((bf16[272,128]{1,0:T(8,128)(2,1)S(1)}, bf16[272,128]{1,0:T(8,128)(2,1)S(1)}, u32[]{:S(2)}, u32[]{:S(2)}) %collective-permute-start) | collective-permute-done | bytes 69664 | tf_op jit(solution)/shard_map/ppermute | solution.py:263
  6.5 2.0 %collective-permute-start.1 = (bf16[544,128]{1,0:T(8,128)(2,1)S(1)}, bf16[544,128]{1,0:T(8,128)(2,1)S(1)}, u32[]{:S(2)}, u32[]{:S(2)}) collective-permute-start(bf16[544,128]{1,0:T(8,128)(2,1)S(1)} %pad_maximum_fusion.refs_9_), channel_id=1, source_target_pairs={{0,1},{1,2},{2,3},{3,4},{4,5},{5,6},{6,7},{7,0},{8,9},{9,10},{10,1... | collective-permute-start | bytes 417800 | tf_op jit(solution)/shard_map/ppermute | solution.py:263
  8.5 4.0 %collective-permute-start.2 = (bf16[544,128]{1,0:T(8,128)(2,1)S(1)}, bf16[544,128]{1,0:T(8,128)(2,1)S(1)}, u32[]{:S(2)}, u32[]{:S(2)}) collective-permute-start(bf16[544,128]{1,0:T(8,128)(2,1)S(1)} %pad_maximum_fusion.refs_9_), channel_id=1, source_target_pairs={{0,7},{1,0},{2,1},{3,2},{4,3},{5,4},{6,5},{7,6},{8,15},{9,8},{10,9... | collective-permute-start | bytes 417800 | tf_op jit(solution)/shard_map/ppermute | solution.py:263
  12.5 1.0 %copy-done = bf16[1,256,1024]{2,1,0:T(8,128)(2,1)S(1)} copy-done((bf16[1,256,1024]{2,1,0:T(8,128)(2,1)S(1)}, bf16[1,256,1024]{2,1,0:T(8,128)(2,1)}, u32[]{:S(2)}) %copy-start) | copy-done | bytes 524312
  13.6 1.0 %copy-done.1 = bf16[1,256,1024]{2,1,0:T(8,128)(2,1)S(1)} copy-done((bf16[1,256,1024]{2,1,0:T(8,128)(2,1)S(1)}, bf16[1,256,1024]{2,1,0:T(8,128)(2,1)}, u32[]{:S(2)}) %copy-start.1) | copy-done | bytes 524312
  14.6 1.4 %forward_stats.6 = (f32[32,256]{1,0:T(8,128)S(1)}, bf16[2048,128]{1,0:T(8,128)(2,1)S(1)}, bf16[2048,128]{1,0:T(8,128)(2,1)S(1)}) custom-call(s32[1]{0:T(128)S(6)} %copy.13.refs_0_, bf16[1,256,1024]{2,1,0:T(8,128)(2,1)S(1)} %copy-done, bf16[1,256,1024]{2,1,0:T(8,128)(2,1)S(1)} %copy-done.1, bf16[272,128]{1,0:T(8,128)(2,1)S(1)} %pad_maximum_fusion.1.refs_3_, ...), custom_call_target="tpu_custom_call" | custom-call | flops 1207959552 | bytes 1048576 | tf_op jit(solution)/shard_map/forward_stats/pallas_call | solution.py:209
  16.0 0.6 forward_stats.7.refs_4_
  16.7 3.2 %collective-permute-start.4 = (bf16[544,128]{1,0:T(8,128)(2,1)S(1)}, bf16[544,128]{1,0:T(8,128)(2,1)S(1)}, u32[]{:S(2)}, u32[]{:S(2)}) collective-permute-start(bf16[544,128]{1,0:T(8,128)(2,1)S(1)} %collective-permute-done.2.refs_3_.refs_10_), channel_id=1, source_target_pairs={{0,7},{1,0},{2,1},{3,2},{4,3},{5,4},{6,5},{7,6},{8,15},{9,8},{10,9... | collective-permute-start | bytes 417800 | tf_op jit(solution)/shard_map/ppermute | solution.py:263
  19.9 1.8 %forward_stats.8.refs_5_ = f32[32,256]{1,0:T(8,128)S(1)} custom-call(bf16[2048,128]{1,0:T(8,128)(2,1)S(1)} %get-tuple-element.23.refs_0_.refs_1_, bf16[2048,128]{1,0:T(8,128)(2,1)S(1)} %get-tuple-element.24.refs_1_.refs_2_, bf16[544,128]{1,0:T(8,128)(2,1)S(1)} %collective-permute-done.1.refs_2_.refs_9_, ...), custom_call_target="tpu_custom_call" | custom-call | flops 1610612736 | bytes 1048576 | tf_op jit(solution)/shard_map/forward_stats/pallas_call | solution.py:209
  21.8 1.2 %collective-permute-done.3.refs_2_.refs_9_ = bf16[544,128]{1,0:T(8,128)(2,1)S(1)} collective-permute-done((bf16[544,128]{1,0:T(8,128)(2,1)S(1)}, bf16[544,128]{1,0:T(8,128)(2,1)S(1)}, u32[]{:S(2)}, u32[]{:S(2)}) %collective-permute-start.3) | collective-permute-done | bytes 139296 | tf_op jit(solution)/shard_map/ppermute | solution.py:263
  23.0 3.2 %collective-permute-start.6 = (bf16[544,128]{1,0:T(8,128)(2,1)S(1)}, bf16[544,128]{1,0:T(8,128)(2,1)S(1)}, u32[]{:S(2)}, u32[]{:S(2)}) collective-permute-start(bf16[544,128]{1,0:T(8,128)(2,1)S(1)} %collective-permute-done.4.refs_3_.refs_10_), channel_id=1, source_target_pairs={{0,7},{1,0},{2,1},{3,2},{4,3},{5,4},{6,5},{7,6},{8,15},{9,8},{10,9... | collective-permute-start | bytes 417800 | tf_op jit(solution)/shard_map/ppermute | solution.py:263
  26.2 1.8 %forward_stats.9.refs_6_ = f32[32,256]{1,0:T(8,128)S(1)} custom-call(bf16[2048,128]{1,0:T(8,128)(2,1)S(1)} %get-tuple-element.23.refs_0_.refs_1_, bf16[2048,128]{1,0:T(8,128)(2,1)S(1)} %get-tuple-element.24.refs_1_.refs_2_, bf16[544,128]{1,0:T(8,128)(2,1)S(1)} %collective-permute-done.3.refs_2_.refs_9_, ...), custom_call_target="tpu_custom_call" | custom-call | flops 1610612736 | bytes 1048576 | tf_op jit(solution)/shard_map/forward_stats/pallas_call | solution.py:209
  28.0 1.2 %collective-permute-done.5.refs_2_.refs_9_ = bf16[544,128]{1,0:T(8,128)(2,1)S(1)} collective-permute-done((bf16[544,128]{1,0:T(8,128)(2,1)S(1)}, bf16[544,128]{1,0:T(8,128)(2,1)S(1)}, u32[]{:S(2)}, u32[]{:S(2)}) %collective-permute-start.5) | collective-permute-done | bytes 139296 | tf_op jit(solution)/shard_map/ppermute | solution.py:263
  29.3 1.8 %forward_stats.10.refs_7_ = f32[32,256]{1,0:T(8,128)S(1)} custom-call(bf16[2048,128]{1,0:T(8,128)(2,1)S(1)} %get-tuple-element.23.refs_0_.refs_1_, bf16[2048,128]{1,0:T(8,128)(2,1)S(1)} %get-tuple-element.24.refs_1_.refs_2_, bf16[544,128]{1,0:T(8,128)(2,1)S(1)} %collective-permute-done.5.refs_2_.refs_9_, ...), custom_call_target="tpu_custom_call" | custom-call | flops 1610612736 | bytes 1048576 | tf_op jit(solution)/shard_map/forward_stats/pallas_call | solution.py:209
  31.1 4.4 %collective-permute-done.7.refs_2_.refs_9_ = bf16[544,128]{1,0:T(8,128)(2,1)S(1)} collective-permute-done((bf16[544,128]{1,0:T(8,128)(2,1)S(1)}, bf16[544,128]{1,0:T(8,128)(2,1)S(1)}, u32[]{:S(2)}, u32[]{:S(2)}) %collective-permute-start.7) | collective-permute-done | bytes 139296 | tf_op jit(solution)/shard_map/ppermute | solution.py:263
  35.5 0.9 %forward_stats.11.refs_8_ = f32[32,256]{1,0:T(8,128)S(1)} custom-call(bf16[2048,128]{1,0:T(8,128)(2,1)S(1)} %get-tuple-element.23.refs_0_.refs_1_, bf16[2048,128]{1,0:T(8,128)(2,1)S(1)} %get-tuple-element.24.refs_1_.refs_2_, bf16[544,128]{1,0:T(8,128)(2,1)S(1)} %collective-permute-done.7.refs_2_.refs_9_), custom_call_target="tpu_custom_call" | custom-call | flops 805306368 | bytes 1048576 | tf_op jit(solution)/shard_map/forward_stats/pallas_call | solution.py:209
  36.5 2.5 %backward_grads.5 = (f32[1024,256]{1,0:T(8,128)S(1)}, bf16[512,128]{1,0:T(8,128)(2,1)S(1)}) custom-call(s32[1]{0:T(128)S(6)} %copy.14.refs_0_, bf16[2048,128]{1,0:T(8,128)(2,1)S(1)} %get-tuple-element.23.refs_0_.refs_1_, bf16[2048,128]{1,0:T(8,128)(2,1)S(1)} %get-tuple-element.24.refs_1_.refs_2_, f32[32,256]{1,0:T(8,128)S(1)} %get-tuple-element.25.refs_3_, ...), custom_call_target="tpu_custom_call" | custom-call | flops 2013265920 | bytes 2097152 | tf_op jit(solution)/shard_map/backward_grads/pallas_call | solution.py:236
  39.1 3.6 %backward_grads.6 = (f32[1024,256]{1,0:T(8,128)S(1)}, f32[512,128]{1,0:T(8,128)S(1)}, bf16[512,128]{1,0:T(8,128)(2,1)S(1)}) custom-call(s32[1]{0:T(128)S(6)} %copy.14.refs_0_, bf16[2048,128]{1,0:T(8,128)(2,1)S(1)} %get-tuple-element.23.refs_0_.refs_1_, bf16[2048,128]{1,0:T(8,128)(2,1)S(1)} %get-tuple-element.24.refs_1_.refs_2_, ...), custom_call_target="tpu_custom_call" | custom-call | flops 4026531840 | bytes 2097152 | tf_op jit(solution)/shard_map/backward_grads/pallas_call | solution.py:236
  42.7 2.1 %collective-permute-start.10 = (bf16[512,128]{1,0:T(8,128)(2,1)S(1)}, bf16[512,128]{1,0:T(8,128)(2,1)S(1)}, u32[]{:S(2)}, u32[]{:S(2)}) collective-permute-start(bf16[512,128]{1,0:T(8,128)(2,1)S(1)} %get-tuple-element.30.refs_13_), channel_id=1, source_target_pairs={{0,1},{1,2},{2,3},{3,4},{4,5},{5,6},{6,7},{7,0},{8,9},{9,10},{10,1... | collective-permute-start | bytes 393224 | tf_op jit(solution)/shard_map/ppermute | solution.py:263
  45.0 1.3 %collective-permute-start.9 = (bf16[512,128]{1,0:T(8,128)(2,1)S(1)}, bf16[512,128]{1,0:T(8,128)(2,1)S(1)}, u32[]{:S(2)}, u32[]{:S(2)}) collective-permute-start(bf16[512,128]{1,0:T(8,128)(2,1)S(1)} %add_convert_fusion.4.refs_12_), channel_id=1, source_target_pairs={{0,7},{1,0},{2,1},{3,2},{4,3},{5,4},{6,5},{7,6},{8,15},{9,8},{10,9... | collective-permute-start | bytes 393224 | tf_op jit(solution)/shard_map/ppermute | solution.py:263
  46.4 3.6 %backward_grads.7 = (f32[1024,256]{1,0:T(8,128)S(1)}, f32[512,128]{1,0:T(8,128)S(1)}, f32[512,128]{1,0:T(8,128)S(1)}) custom-call(s32[1]{0:T(128)S(6)} %copy.14.refs_0_, bf16[2048,128]{1,0:T(8,128)(2,1)S(1)} %get-tuple-element.23.refs_0_.refs_1_, bf16[2048,128]{1,0:T(8,128)(2,1)S(1)} %get-tuple-element.24.refs_1_.refs_2_, ...), custom_call_target="tpu_custom_call" | custom-call | flops 4026531840 | bytes 2097152 | tf_op jit(solution)/shard_map/backward_grads/pallas_call | solution.py:236
  50.1 1.1 %collective-permute-start.12 = (bf16[512,128]{1,0:T(8,128)(2,1)S(1)}, bf16[512,128]{1,0:T(8,128)(2,1)S(1)}, u32[]{:S(2)}, u32[]{:S(2)}) collective-permute-start(bf16[512,128]{1,0:T(8,128)(2,1)S(1)} %add_convert_fusion.2.refs_13_), channel_id=1, source_target_pairs={{0,1},{1,2},{2,3},{3,4},{4,5},{5,6},{6,7},{7,0},{8,9},{9,10},{10,1... | collective-permute-start | bytes 393224 | tf_op jit(solution)/shard_map/ppermute | solution.py:263
  51.2 2.6 %collective-permute-start.11 = (bf16[512,128]{1,0:T(8,128)(2,1)S(1)}, bf16[512,128]{1,0:T(8,128)(2,1)S(1)}, u32[]{:S(2)}, u32[]{:S(2)}) collective-permute-start(bf16[512,128]{1,0:T(8,128)(2,1)S(1)} %add_convert_fusion.3.refs_12_), channel_id=1, source_target_pairs={{0,7},{1,0},{2,1},{3,2},{4,3},{5,4},{6,5},{7,6},{8,15},{9,8},{10,9... | collective-permute-start | bytes 393224 | tf_op jit(solution)/shard_map/ppermute | solution.py:263
  53.8 3.6 %backward_grads.8 = (f32[1024,256]{1,0:T(8,128)S(1)}, f32[512,128]{1,0:T(8,128)S(1)}, f32[512,128]{1,0:T(8,128)S(1)}) custom-call(s32[1]{0:T(128)S(6)} %copy.14.refs_0_, bf16[2048,128]{1,0:T(8,128)(2,1)S(1)} %get-tuple-element.23.refs_0_.refs_1_, bf16[2048,128]{1,0:T(8,128)(2,1)S(1)} %get-tuple-element.24.refs_1_.refs_2_, ...), custom_call_target="tpu_custom_call" | custom-call | flops 4026531840 | bytes 2097152 | tf_op jit(solution)/shard_map/backward_grads/pallas_call | solution.py:236
  57.4 0.3 collective-permute-done.12
  57.9 3.3 %collective-permute-start.13 = (bf16[512,128]{1,0:T(8,128)(2,1)S(1)}, bf16[512,128]{1,0:T(8,128)(2,1)S(1)}, u32[]{:S(2)}, u32[]{:S(2)}) collective-permute-start(bf16[512,128]{1,0:T(8,128)(2,1)S(1)} %add_convert_fusion.1.refs_13_), channel_id=1, source_target_pairs={{0,7},{1,0},{2,1},{3,2},{4,3},{5,4},{6,5},{7,6},{8,15},{9,8},{10,9... | collective-permute-start | bytes 393224 | tf_op jit(solution)/shard_map/ppermute | solution.py:263
  61.2 4.6 %backward_grads.9 = (f32[1,256,1024]{2,1,0:T(8,128)}, f32[512,128]{1,0:T(8,128)S(1)}, f32[1,256,128]{2,1,0:T(8,128)}, f32[1,256,128]{2,1,0:T(8,128)}) custom-call(s32[1]{0:T(128)S(6)} %copy.14.refs_0_, bf16[2048,128]{1,0:T(8,128)(2,1)S(1)} %get-tuple-element.23.refs_0_.refs_1_, bf16[2048,128]{1,0:T(8,128)(2,1)S(1)} %get-tuple-element.24.refs_1_.refs_2_, ...), custom_call_target="tpu_custom_call" | custom-call | flops 4026531840 | bytes 2097152 | tf_op jit(solution)/shard_map/backward_grads/pallas_call | solution.py:236
  65.8 1.6 %collective-permute-start.15 = (bf16[256,128]{1,0:T(8,128)(2,1)S(1)}, bf16[256,128]{1,0:T(8,128)(2,1)S(1)}, u32[]{:S(2)}, u32[]{:S(2)}) collective-permute-start(bf16[256,128]{1,0:T(8,128)(2,1)S(1)} %slice.23), channel_id=1, source_target_pairs={{0,8},{1,9},{2,10},{3,11},{4,12},{5,13},{6,14},{7,15},{8,0},{9,1},... | collective-permute-start | bytes 196616 | tf_op jit(solution)/shard_map/ppermute | solution.py:263
  67.5 2.7 %collective-permute-done.15 = bf16[256,128]{1,0:T(8,128)(2,1)S(1)} collective-permute-done((bf16[256,128]{1,0:T(8,128)(2,1)S(1)}, bf16[256,128]{1,0:T(8,128)(2,1)S(1)}, u32[]{:S(2)}, u32[]{:S(2)}) %collective-permute-start.15) | collective-permute-done | bytes 65568 | tf_op jit(solution)/shard_map/ppermute | solution.py:263
  70.2 0.7 fusion
  (35 shorter events, 0.7 us)
Async XLA Ops:
  1.3 5.2 %copy-start.4 = (bf16[128,128]{1,0:T(8,128)(2,1)S(1)}, bf16[128,128]{1,0:T(8,128)(2,1)}, u32[]{:S(2)}) copy-start(bf16[128,128]{1,0:T(8,128)(2,1)} %param.12) | copy-start | bytes 98308
  1.3 5.2 %copy-start.5 = (bf16[128,128]{1,0:T(8,128)(2,1)S(1)}, bf16[128,128]{1,0:T(8,128)(2,1)}, u32[]{:S(2)}) copy-start(bf16[128,128]{1,0:T(8,128)(2,1)} %param.11) | copy-start | bytes 98308
  2.1 4.3 %collective-permute-start = (bf16[272,128]{1,0:T(8,128)(2,1)S(1)}, bf16[272,128]{1,0:T(8,128)(2,1)S(1)}, u32[]{:S(2)}, u32[]{:S(2)}) collective-permute-start(bf16[272,128]{1,0:T(8,128)(2,1)S(1)} %pad_maximum_fusion.1.refs_3_), channel_id=1, source_target_pairs={{0,8},{1,9},{2,10},{3,11},{4,12},{5,13},{6,14},{7,15},{8,0},{9,1},... | collective-permute-start | bytes 208904 | tf_op jit(solution)/shard_map/ppermute | solution.py:263
  4.4 8.1 %copy-start.2 = (bf16[1,256,128]{2,1,0:T(8,128)(2,1)S(1)}, bf16[1,256,128]{2,1,0:T(8,128)(2,1)}, u32[]{:S(2)}) copy-start(bf16[1,256,128]{2,1,0:T(8,128)(2,1)} %refs_10_.1) | copy-start | bytes 196612
  4.4 8.1 %copy-start.3 = (bf16[1,256,128]{2,1,0:T(8,128)(2,1)S(1)}, bf16[1,256,128]{2,1,0:T(8,128)(2,1)}, u32[]{:S(2)}) copy-start(bf16[1,256,128]{2,1,0:T(8,128)(2,1)} %refs_11_.1) | copy-start | bytes 196612
  6.5 10.1 %collective-permute-start.1 = (bf16[544,128]{1,0:T(8,128)(2,1)S(1)}, bf16[544,128]{1,0:T(8,128)(2,1)S(1)}, u32[]{:S(2)}, u32[]{:S(2)}) collective-permute-start(bf16[544,128]{1,0:T(8,128)(2,1)S(1)} %pad_maximum_fusion.refs_9_), channel_id=1, source_target_pairs={{0,1},{1,2},{2,3},{3,4},{4,5},{5,6},{6,7},{7,0},{8,9},{9,10},{10,1... | collective-permute-start | bytes 417800 | tf_op jit(solution)/shard_map/ppermute | solution.py:263
  8.5 8.2 %collective-permute-start.2 = (bf16[544,128]{1,0:T(8,128)(2,1)S(1)}, bf16[544,128]{1,0:T(8,128)(2,1)S(1)}, u32[]{:S(2)}, u32[]{:S(2)}) collective-permute-start(bf16[544,128]{1,0:T(8,128)(2,1)S(1)} %pad_maximum_fusion.refs_9_), channel_id=1, source_target_pairs={{0,7},{1,0},{2,1},{3,2},{4,3},{5,4},{6,5},{7,6},{8,15},{9,8},{10,9... | collective-permute-start | bytes 417800 | tf_op jit(solution)/shard_map/ppermute | solution.py:263
  12.5 1.0 %copy-start = (bf16[1,256,1024]{2,1,0:T(8,128)(2,1)S(1)}, bf16[1,256,1024]{2,1,0:T(8,128)(2,1)}, u32[]{:S(2)}) copy-start(bf16[1,256,1024]{2,1,0:T(8,128)(2,1)} %refs_1_.1) | copy-start | bytes 1572868
  13.5 1.0 %copy-start.1 = (bf16[1,256,1024]{2,1,0:T(8,128)(2,1)S(1)}, bf16[1,256,1024]{2,1,0:T(8,128)(2,1)}, u32[]{:S(2)}) copy-start(bf16[1,256,1024]{2,1,0:T(8,128)(2,1)} %refs_2_.1) | copy-start | bytes 1572868
  16.6 6.3 %collective-permute-start.3 = (bf16[544,128]{1,0:T(8,128)(2,1)S(1)}, bf16[544,128]{1,0:T(8,128)(2,1)S(1)}, u32[]{:S(2)}, u32[]{:S(2)}) collective-permute-start(bf16[544,128]{1,0:T(8,128)(2,1)S(1)} %collective-permute-done.1.refs_2_.refs_9_), channel_id=1, source_target_pairs={{0,1},{1,2},{2,3},{3,4},{4,5},{5,6},{6,7},{7,0},{8,9},{9,10},{10,1... | collective-permute-start | bytes 417800 | tf_op jit(solution)/shard_map/ppermute | solution.py:263
  16.7 6.2 %collective-permute-start.4 = (bf16[544,128]{1,0:T(8,128)(2,1)S(1)}, bf16[544,128]{1,0:T(8,128)(2,1)S(1)}, u32[]{:S(2)}, u32[]{:S(2)}) collective-permute-start(bf16[544,128]{1,0:T(8,128)(2,1)S(1)} %collective-permute-done.2.refs_3_.refs_10_), channel_id=1, source_target_pairs={{0,7},{1,0},{2,1},{3,2},{4,3},{5,4},{6,5},{7,6},{8,15},{9,8},{10,9... | collective-permute-start | bytes 417800 | tf_op jit(solution)/shard_map/ppermute | solution.py:263
  23.0 6.3 %collective-permute-start.5 = (bf16[544,128]{1,0:T(8,128)(2,1)S(1)}, bf16[544,128]{1,0:T(8,128)(2,1)S(1)}, u32[]{:S(2)}, u32[]{:S(2)}) collective-permute-start(bf16[544,128]{1,0:T(8,128)(2,1)S(1)} %collective-permute-done.3.refs_2_.refs_9_), channel_id=1, source_target_pairs={{0,1},{1,2},{2,3},{3,4},{4,5},{5,6},{6,7},{7,0},{8,9},{9,10},{10,1... | collective-permute-start | bytes 417800 | tf_op jit(solution)/shard_map/ppermute | solution.py:263
  23.0 6.3 %collective-permute-start.6 = (bf16[544,128]{1,0:T(8,128)(2,1)S(1)}, bf16[544,128]{1,0:T(8,128)(2,1)S(1)}, u32[]{:S(2)}, u32[]{:S(2)}) collective-permute-start(bf16[544,128]{1,0:T(8,128)(2,1)S(1)} %collective-permute-done.4.refs_3_.refs_10_), channel_id=1, source_target_pairs={{0,7},{1,0},{2,1},{3,2},{4,3},{5,4},{6,5},{7,6},{8,15},{9,8},{10,9... | collective-permute-start | bytes 417800 | tf_op jit(solution)/shard_map/ppermute | solution.py:263
  29.3 6.3 %collective-permute-start.7 = (bf16[544,128]{1,0:T(8,128)(2,1)S(1)}, bf16[544,128]{1,0:T(8,128)(2,1)S(1)}, u32[]{:S(2)}, u32[]{:S(2)}) collective-permute-start(bf16[544,128]{1,0:T(8,128)(2,1)S(1)} %collective-permute-done.5.refs_2_.refs_9_), channel_id=1, source_target_pairs={{0,1},{1,2},{2,3},{3,4},{4,5},{5,6},{6,7},{7,0},{8,9},{9,10},{10,1... | collective-permute-start | bytes 417800 | tf_op jit(solution)/shard_map/ppermute | solution.py:263
  39.0 6.0 %collective-permute-start.8 = (bf16[512,128]{1,0:T(8,128)(2,1)S(1)}, bf16[512,128]{1,0:T(8,128)(2,1)S(1)}, u32[]{:S(2)}, u32[]{:S(2)}) collective-permute-start(bf16[512,128]{1,0:T(8,128)(2,1)S(1)} %get-tuple-element.28), channel_id=1, source_target_pairs={{0,7},{1,0},{2,1},{3,2},{4,3},{5,4},{6,5},{7,6},{8,15},{9,8},{10,9... | collective-permute-start | bytes 393224 | tf_op jit(solution)/shard_map/ppermute | solution.py:263
  42.7 7.3 %collective-permute-start.10 = (bf16[512,128]{1,0:T(8,128)(2,1)S(1)}, bf16[512,128]{1,0:T(8,128)(2,1)S(1)}, u32[]{:S(2)}, u32[]{:S(2)}) collective-permute-start(bf16[512,128]{1,0:T(8,128)(2,1)S(1)} %get-tuple-element.30.refs_13_), channel_id=1, source_target_pairs={{0,1},{1,2},{2,3},{3,4},{4,5},{5,6},{6,7},{7,0},{8,9},{9,10},{10,1... | collective-permute-start | bytes 393224 | tf_op jit(solution)/shard_map/ppermute | solution.py:263
  45.0 6.1 %collective-permute-start.9 = (bf16[512,128]{1,0:T(8,128)(2,1)S(1)}, bf16[512,128]{1,0:T(8,128)(2,1)S(1)}, u32[]{:S(2)}, u32[]{:S(2)}) collective-permute-start(bf16[512,128]{1,0:T(8,128)(2,1)S(1)} %add_convert_fusion.4.refs_12_), channel_id=1, source_target_pairs={{0,7},{1,0},{2,1},{3,2},{4,3},{5,4},{6,5},{7,6},{8,15},{9,8},{10,9... | collective-permute-start | bytes 393224 | tf_op jit(solution)/shard_map/ppermute | solution.py:263
  50.1 7.6 %collective-permute-start.12 = (bf16[512,128]{1,0:T(8,128)(2,1)S(1)}, bf16[512,128]{1,0:T(8,128)(2,1)S(1)}, u32[]{:S(2)}, u32[]{:S(2)}) collective-permute-start(bf16[512,128]{1,0:T(8,128)(2,1)S(1)} %add_convert_fusion.2.refs_13_), channel_id=1, source_target_pairs={{0,1},{1,2},{2,3},{3,4},{4,5},{5,6},{6,7},{7,0},{8,9},{9,10},{10,1... | collective-permute-start | bytes 393224 | tf_op jit(solution)/shard_map/ppermute | solution.py:263
  51.2 6.7 %collective-permute-start.11 = (bf16[512,128]{1,0:T(8,128)(2,1)S(1)}, bf16[512,128]{1,0:T(8,128)(2,1)S(1)}, u32[]{:S(2)}, u32[]{:S(2)}) collective-permute-start(bf16[512,128]{1,0:T(8,128)(2,1)S(1)} %add_convert_fusion.3.refs_12_), channel_id=1, source_target_pairs={{0,7},{1,0},{2,1},{3,2},{4,3},{5,4},{6,5},{7,6},{8,15},{9,8},{10,9... | collective-permute-start | bytes 393224 | tf_op jit(solution)/shard_map/ppermute | solution.py:263
  57.7 8.0 %collective-permute-start.14 = (bf16[512,128]{1,0:T(8,128)(2,1)S(1)}, bf16[512,128]{1,0:T(8,128)(2,1)S(1)}, u32[]{:S(2)}, u32[]{:S(2)}) collective-permute-start(bf16[512,128]{1,0:T(8,128)(2,1)S(1)} %add_convert_fusion.refs_14_), channel_id=1, source_target_pairs={{0,1},{1,2},{2,3},{3,4},{4,5},{5,6},{6,7},{7,0},{8,9},{9,10},{10,1... | collective-permute-start | bytes 393224 | tf_op jit(solution)/shard_map/ppermute | solution.py:263
  57.9 7.9 %collective-permute-start.13 = (bf16[512,128]{1,0:T(8,128)(2,1)S(1)}, bf16[512,128]{1,0:T(8,128)(2,1)S(1)}, u32[]{:S(2)}, u32[]{:S(2)}) collective-permute-start(bf16[512,128]{1,0:T(8,128)(2,1)S(1)} %add_convert_fusion.1.refs_13_), channel_id=1, source_target_pairs={{0,7},{1,0},{2,1},{3,2},{4,3},{5,4},{6,5},{7,6},{8,15},{9,8},{10,9... | collective-permute-start | bytes 393224 | tf_op jit(solution)/shard_map/ppermute | solution.py:263
  65.8 4.4 %collective-permute-start.15 = (bf16[256,128]{1,0:T(8,128)(2,1)S(1)}, bf16[256,128]{1,0:T(8,128)(2,1)S(1)}, u32[]{:S(2)}, u32[]{:S(2)}) collective-permute-start(bf16[256,128]{1,0:T(8,128)(2,1)S(1)} %slice.23), channel_id=1, source_target_pairs={{0,8},{1,9},{2,10},{3,11},{4,12},{5,13},{6,14},{7,15},{8,0},{9,1},... | collective-permute-start | bytes 196616 | tf_op jit(solution)/shard_map/ppermute | solution.py:263

commit v4 on v3

v4 whole, which is shorter than its diff:
```python
import functools
import math

import jax
import jax.numpy as jnp
from jax import lax
from jax.experimental import pallas as pl
from jax.experimental.pallas import tpu as pltpu
from jax.sharding import PartitionSpec as P

F32 = jnp.float32
BF16 = jnp.bfloat16
PAD = 16
RING = 8
SLICE = 64
SCOPED = 20 * 1024 * 1024

VMEM_SPEC = pl.BlockSpec(memory_space=pltpu.VMEM)
SMEM_SPEC = pl.BlockSpec(memory_space=pltpu.SMEM)
ANY_SPEC = pl.BlockSpec(memory_space=pl.ANY)


def dot_nn(left, right):
    return lax.dot_general(left, right, (((1,), (0,)), ((), ())), preferred_element_type=F32)


def dot_nt(left, right):
    return lax.dot_general(left, right, (((1,), (1,)), ((), ())), preferred_element_type=F32)


def fold_rows(values, combine):
    parts = [values[i : i + 8] for i in range(0, values.shape[0], 8)]
    while len(parts) > 1:
        parts = [
            combine(parts[i], parts[i + 1]) if i + 1 < len(parts) else parts[i]
            for i in range(0, len(parts), 2)
        ]
    return parts[0]


def pack_places(blocks, share):
    size = 2 * share + PAD
    return [(ref, at) for ref in blocks for at in range(0, ref.shape[0], size)]


def load_rows(blocks, own, k_all, v_all, share):
    places = pack_places(blocks, share)
    for i, (ref, at) in enumerate(places):
        k_all[i * share : (i + 1) * share, :] = ref[at : at + share, :]
        v_all[i * share : (i + 1) * share, :] = ref[at + share : at + 2 * share, :]
    if own:
        k_all[len(places) * share :, :] = own[0][0]
        v_all[len(places) * share :, :] = own[1][0]
    return len(places) * share


def own_mask(at, resp):
    key_at = lax.broadcasted_iota(jnp.int32, (SLICE, resp), 0) + at
    return key_at <= lax.broadcasted_iota(jnp.int32, (SLICE, resp), 1)


def forward_kernel(heads, share, count, opening, *refs):
    refs, scratch = refs[:-4], refs[-4:]
    k_all, v_all, s0, s1 = scratch
    if opening:
        len_ref, q_ref, c_ref = refs[:3]
        blocks, own = refs[3 : 3 + count], refs[3 + count : 5 + count]
        out_ref, e_all, g_all, q_rows, c_rows, copy_ref = refs[5 + count :]
        copy_ref[...] = blocks[0][...]
    else:
        q_rows, c_rows = refs[:2]
        blocks, own = refs[2 : 2 + count], ()
        out_ref, e_all, g_all = refs[2 + count :]
    width, resp = q_rows.shape[1], q_rows.shape[0] // heads
    rate = math.log2(math.e) / math.sqrt(width)
    s_buf = (s0, s1)
    prompt = load_rows(blocks, own, k_all, v_all, share)
    keys = k_all.shape[0]
    if opening:
        live = lax.broadcasted_iota(jnp.int32, (resp, width), 0) < len_ref[0]

    for t in range(heads + 1):
        if t < heads:
            rows = slice(t * resp, (t + 1) * resp)
            if opening:
                lanes = slice(t * width, (t + 1) * width)
                q_rows[rows, :] = q_ref[0, :, lanes]
                c_rows[rows, :] = jnp.where(live, c_ref[0, :, lanes], jnp.zeros((), BF16))
            s_buf[t % 2][...] = dot_nt(k_all[...], q_rows[rows, :])
            g_all[:, rows] = dot_nt(v_all[...], c_rows[rows, :])
        if t > 0:
            h = t - 1
            s_now, cols = s_buf[h % 2], slice(h * resp, (h + 1) * resp)
            top = mass = mixed = None
            for at in range(0, keys, SLICE):
                s = s_now[at : at + SLICE, :]
                if at >= prompt:
                    s = jnp.where(own_mask(at - prompt, resp), s, -jnp.inf)
                part = fold_rows(s, jnp.maximum)
                top = part if top is None else jnp.maximum(top, part)
            top = jnp.max(top, axis=0, keepdims=True)
            level = top * rate
            for at in range(0, keys, SLICE):
                here = slice(at, at + SLICE)
                e = jnp.exp2(s_now[here, :] * rate - level)
                if at >= prompt:
                    e = jnp.where(own_mask(at - prompt, resp), e, 0.0)
                e_all[here, cols] = e.astype(BF16)
                part = fold_rows(e, jnp.add)
                mass = part if mass is None else mass + part
                part = fold_rows(e * g_all[here, cols], jnp.add)
                mixed = part if mixed is None else mixed + part
            out_ref[h : h + 1, :] = top
            out_ref[heads + h : heads + h + 1, :] = jnp.sum(mass, axis=0, keepdims=True)
            out_ref[2 * heads + h : 2 * heads + h + 1, :] = jnp.sum(mixed, axis=0, keepdims=True)
    paid = jnp.zeros((1, width), F32)
    for ref, at in pack_places(blocks, share):
        paid = paid + ref[at + 2 * share : at + 2 * share + PAD, :].astype(F32)[:1]
    out_ref[3 * heads :, :] = jnp.broadcast_to(jnp.max(paid), (heads, resp))


def backward_kernel(heads, share, owners, count, stats, spans, after, more, last, *refs):
    refs, (k_t, p_all, ds_all) = refs[:-3], refs[-3:]
    pay_ref, q_rows, c_rows = refs[:3]
    refs = refs[3:]
    stat_refs, refs = refs[:stats], refs[stats:]
    e_refs, g_refs, refs = refs[: len(spans)], refs[len(spans) : 2 * len(spans)], refs[2 * len(spans) :]
    blocks, refs = refs[:count], refs[count:]
    prior, refs = (refs[0], refs[1:]) if more else (None, refs)
    dq_ref, *out_refs = refs[after:]
    width, resp = q_rows.shape[1], q_rows.shape[0] // heads
    scale = 1.0 / math.sqrt(width)
    rate = scale * math.log2(math.e)

    peaks = [ref[:heads, :] for ref in stat_refs]
    peak = functools.reduce(jnp.maximum, peaks)
    weights = [jnp.exp2((local - peak) * rate) for local in peaks]
    mass, mixed, paid = 0.0, 0.0, 0.0
    for ref, weight in zip(stat_refs, weights):
        mass = mass + ref[heads : 2 * heads, :] * weight
        mixed = mixed + ref[2 * heads : 3 * heads, :] * weight
        paid = paid + ref[3 * heads :, :]
    delta = mixed / mass
    factors = [weights[group] / mass for group, _, _ in spans]
    advantage = (pay_ref[0].astype(F32) - paid / owners)[:1, :width]

    if last:
        k_t[...] = blocks[0][0].T
    else:
        for i, (ref, at) in enumerate(pack_places(blocks, share)):
            k_t[:, i * share : (i + 1) * share] = ref[at : at + share, :].T
    half = heads // 2
    dk = dv = None
    for h in range(heads):
        cols = slice(h * resp, (h + 1) * resp)
        to = 0
        for (_, first, size), e_ref, g_ref, factor in zip(spans, e_refs, g_refs, factors):
            for at in range(first, first + size, SLICE):
                p = e_ref[at : at + SLICE, cols].astype(F32) * factor[h : h + 1]
                ds = p * (g_ref[at : at + SLICE, cols] - delta[h : h + 1])
                p_all[to : to + SLICE, cols] = p.astype(BF16)
                ds_all[to : to + SLICE, cols] = ds.astype(BF16)
                to += SLICE
        lanes = slice(h * width, (h + 1) * width)
        dq = dot_nn(k_t[...], ds_all[:, cols])
        if more:
            dq = dq + prior[lanes, :]
        if last:
            dq_ref[0, :, lanes] = dq.T * (advantage * scale)
        else:
            dq_ref[lanes, :] = dq
        if h % half == half - 1:
            block = slice((h + 1 - half) * resp, (h + 1) * resp)
            dk_part = dot_nn(ds_all[:, block], q_rows[block, :])
            dv_part = dot_nn(p_all[:, block], c_rows[block, :])
            dk = dk_part if dk is None else dk + dk_part
            dv = dv_part if dv is None else dv + dv_part
    dk, dv = dk * (advantage * scale), dv * advantage
    if last:
        out_refs[0][0] = dk
        out_refs[1][0] = dv
        return
    at = 0
    for ref in out_refs:
        for base in range(0, ref.shape[0], 2 * share):
            ref[base : base + share, :] = dk[at : at + share].astype(ref.dtype)
            ref[base + share : base + 2 * share, :] = dv[at : at + share].astype(ref.dtype)
            at += share


def count_keys(blocks, share, own):
    return share * sum(b.shape[0] // (2 * share + PAD) for b in blocks) + (
        own[0].shape[1] if own else 0
    )


def forward_stats(heads, share, blocks, rows=(), opening=()):
    if opening:
        lengths, queries, grad_out, *own = opening
        resp, width = queries.shape[1], queries.shape[2] // heads
        operands = (lengths, queries, grad_out, *blocks, *own)
        specs = [SMEM_SPEC] + [VMEM_SPEC] * (len(operands) - 1)
    else:
        own = ()
        resp, width = rows[0].shape[0] // heads, rows[0].shape[1]
        operands = (*rows, *blocks)
        specs = [VMEM_SPEC] * len(operands)
    keys = count_keys(blocks, share, own)
    outs = [
        jax.ShapeDtypeStruct((4 * heads, resp), F32),
        jax.ShapeDtypeStruct((keys, heads * resp), BF16),
        jax.ShapeDtypeStruct((keys, heads * resp), F32),
    ]
    if opening:
        outs += [jax.ShapeDtypeStruct((heads * resp, width), BF16)] * 2
        outs += [jax.ShapeDtypeStruct(blocks[0].shape, BF16)]
    return pl.pallas_call(
        functools.partial(forward_kernel, heads, share, len(blocks), bool(opening)),
        out_shape=tuple(outs),
        in_specs=specs,
        out_specs=(VMEM_SPEC,) * len(outs),
        scratch_shapes=[pltpu.VMEM((keys, width), BF16)] * 2 + [pltpu.VMEM((keys, resp), F32)] * 2,
        compiler_params=pltpu.CompilerParams(vmem_limit_bytes=SCOPED),
        cost_estimate=pl.CostEstimate(
            flops=12 * heads * resp * keys * width,
            bytes_accessed=1024 * 1024,
            transcendentals=heads * resp * keys,
        ),
        name="forward_stats",
    )(*operands)


def backward_grads(
    rewards, rows, stats, kept, parts, blocks, outs, owners, heads, share, prior, after, last=False
):
    resp, width = rows[0].shape[0] // heads, rows[0].shape[1]
    more = prior is not None
    keys = sum(size for _, _, size in parts)
    dq_shape = (1, resp, heads * width) if last else (heads * width, resp)
    outs = [jax.ShapeDtypeStruct(dq_shape, F32), *outs]
    operands = (
        *rows, *stats, *(kept[g][0] for g, _, _ in parts), *(kept[g][1] for g, _, _ in parts),
        *blocks, *((prior,) if more else ()),
    )
    return pl.pallas_call(
        functools.partial(
            backward_kernel, heads, share, owners, len(blocks), len(stats), parts, len(after),
            more, last,
        ),
        out_shape=tuple(outs),
        in_specs=[SMEM_SPEC] + [VMEM_SPEC] * len(operands) + [ANY_SPEC] * len(after),
        out_specs=(VMEM_SPEC,) * len(outs),
        scratch_shapes=[pltpu.VMEM((width, keys), BF16)]
        + [pltpu.VMEM((keys, heads * resp), BF16)] * 2,
        compiler_params=pltpu.CompilerParams(vmem_limit_bytes=SCOPED),
        cost_estimate=pl.CostEstimate(
            flops=20 * heads * resp * keys * width,
            bytes_accessed=2 * 1024 * 1024,
            transcendentals=0,
        ),
        name="backward_grads",
    )(rewards, *operands, *after)


def send(block, plane, step):
    pairs = [
        (y * RING + z, (y + plane) % 2 * RING + (z + step) % RING)
        for y in range(2)
        for z in range(RING)
    ]
    return lax.ppermute(block, "sample", pairs)


def shards(queries, resp_keys, resp_values, prompt_keys, prompt_values, grad_out, lengths, rewards):
    share, width = prompt_keys.shape
    resp = queries.shape[1]
    heads = queries.shape[2] // width
    owners = lax.axis_size("sample")
    reward_rows = jnp.broadcast_to(rewards.astype(BF16)[:, None], (PAD, width))
    packed = jnp.concatenate([prompt_keys, prompt_values, reward_rows], axis=0)

    swapped = send(packed, 1, 0)
    first, *keep, q_rows, c_rows, packed = forward_stats(
        heads, share, [packed], opening=(lengths, queries, grad_out, resp_keys, resp_values)
    )
    rows, stats, kept = (q_rows, c_rows), [first], [keep]
    pairs = {0: jnp.concatenate([packed, swapped], axis=0)}
    for step in (1, 2, 3, 4):
        pairs[step] = send(pairs[step - 1], 0, 1)
        if step < 4:
            pairs[RING - step] = send(pairs[(RING - step + 1) % RING], 0, -1)
    for blocks in ([swapped], [pairs[1], pairs[7]], [pairs[2], pairs[6]], [pairs[3], pairs[5]], [pairs[4]]):
        stat, *keep = forward_stats(heads, share, blocks, rows)
        stats.append(stat)
        kept.append(keep)

    back = functools.partial(
        backward_grads, rewards, rows, stats, kept, owners=owners, heads=heads, share=share
    )
    ready = jax.ShapeDtypeStruct((4 * share, width), BF16)
    wide = jax.ShapeDtypeStruct((4 * share, width), F32)
    grads = jax.ShapeDtypeStruct((1, resp, width), F32)

    def add(received, part):
        return (received.astype(F32) + part).astype(BF16)

    dq, down = back(((5, 0, 2 * share),), [pairs[4]], [ready], prior=None, after=())
    dq, part, up = back(
        ((4, 0, 4 * share),), [pairs[3], pairs[5]], [wide, ready], prior=dq, after=()
    )
    down = add(send(down, 0, -1), part)
    for step in (2, 1):
        dq, part_down, part_up = back(
            ((step + 1, 0, 4 * share),), [pairs[step], pairs[RING - step]], [wide, wide],
            prior=dq, after=(down, up),
        )
        down = add(send(down, 0, -1), part_down)
        up = add(send(up, 0, 1), part_up)
    dq, mine = back(
        ((0, 0, share), (1, 0, share)), [packed, swapped], [wide], prior=dq, after=(down, up)
    )
    mine = mine + send(down, 0, -1).astype(F32) + send(up, 0, 1).astype(F32)
    partner = mine[2 * share :].astype(BF16)
    grad_queries, grad_resp_keys, grad_resp_values = back(
        ((0, share, resp),), [resp_keys], [grads, grads], prior=dq, after=(partner,), last=True
    )
    theirs = send(partner, 1, 0).astype(F32)
    return (
        grad_queries, grad_resp_keys, grad_resp_values,
        mine[:share] + theirs[:share], mine[share : 2 * share] + theirs[share:],
    )


def solution(mesh):
    whole = P(("problem", "sample"), None, None)
    rows = P(("problem", "sample"), None)
    one = P(("problem", "sample"))
    return jax.shard_map(
        shards,
        mesh=mesh,
        in_specs=(whole, whole, whole, rows, rows, whole, one, one),
        out_specs=(whole, whole, whole, rows, rows),
        check_vma=False,
    )
```

time: 71.1 us -> 70 us (0.985); the launches traced: 70.9 us -> 68.9 us
  Pallas kernels: 26.4 us -> 21.2 us
  local copies, waits for them, and re-layouts: 2.78 us -> 3.8 us
  waiting for transfers between devices: 12.1 us -> 13 us
  starting transfers between devices: 26.3 us -> 27.1 us
    pallas_call x5 -> x6, Pallas kernels: 18 us -> 10.9 us  [backward_grads(): pl.pallas_call(functools.partial(backward_kernel, heads, share, owners, l...]
    pallas_call x6, Pallas kernels: 8.46 us -> 10.3 us  [forward_stats(): pl.pallas_call(functools.partial(forward_kernel, heads, share, len(blocks...]
    unnamed x12 -> x11, local copies, waits for them, and re-layouts: 2.11 us -> 3.77 us
    ppermute x16, waiting for transfers between devices: 12.1 us -> 13 us  [send(): return lax.ppermute(block, 'sample', pairs)]
    ppermute x16, starting transfers between devices: 26.3 us -> 27.1 us  [send(): return lax.ppermute(block, 'sample', pairs)]
  transfers between devices with their start and end apart: 16 -> 16, of which waited for: 7 -> 11; matrix products, arithmetic and copies ran while one was open for 0% -> 0% of each run, Pallas kernels for 32% -> 28%
where the time goes in v4:
time: 70 us; the launch traced here: 68.9 us
  starting transfers between devices  27.1 us (39%)
  Pallas kernels  21.2 us (30%)
  waiting for transfers between devices  13 us (19%)
  local copies, waits for them, and re-layouts  3.8 us (5%)
  between operations  2.14 us (3%)
  other arithmetic  1.76 us (3%)
    ppermute x16, starting transfers between devices, send(): return lax.ppermute(block, 'sample', pairs)  27.1 us
    ppermute x16, waiting for transfers between devices, send(): return lax.ppermute(block, 'sample', pairs)  13 us
    pallas_call x6, Pallas kernels, backward_grads(): pl.pallas_call(functools.partial(backward_kernel, heads, share, owners, l...  10.9 us
    pallas_call x6, Pallas kernels, forward_stats(): pl.pallas_call(functools.partial(forward_kernel, heads, share, len(blocks...  10.3 us
    unnamed x11, local copies, waits for them, and re-layouts  3.77 us
  transfers between devices with their start and end apart: 16, of which 11 were waited for; matrix products, arithmetic and copies ran while one was open for 0% of the time, Pallas kernels for 28%

profile of v4, /device:TPU:2, one launch (start us, length us, event | category | flops | bytes accessed | tf_op | source)
XLA Modules:
  0.0 68.9 jit_solution(11269252473846509228)
XLA Ops:
  1.3 0.9 %maximum_maximum_fusion.refs_3_ = bf16[272,128]{1,0:T(8,128)(2,1)S(1)} fusion(bf16[128,128]{1,0:T(8,128)(2,1)} %param.12, bf16[128,128]{1,0:T(8,128)(2,1)} %param.11, bf16[272]{0:T(512)(128)(2,1)S(1)} %pad.2.clone), kind=kLoop, calls=%fused_computation.7 | loop fusion | flops 208896 | bytes 135712 | tf_op jit(solution)/shard_map/concatenate | solution.py:280
  2.2 1.7 %collective-permute-start = (bf16[272,128]{1,0:T(8,128)(2,1)S(1)}, bf16[272,128]{1,0:T(8,128)(2,1)S(1)}, u32[]{:S(2)}, u32[]{:S(2)}) collective-permute-start(bf16[272,128]{1,0:T(8,128)(2,1)S(1)} %maximum_maximum_fusion.refs_3_), channel_id=1, source_target_pairs={{0,8},{1,9},{2,10},{3,11},{4,12},{5,13},{6,14},{7,15},{8,0},{9,1},... | collective-permute-start | bytes 208904 | tf_op jit(solution)/shard_map/ppermute | solution.py:271
  4.5 0.8 %copy-done = bf16[1,256,128]{2,1,0:T(8,128)(2,1)S(1)} copy-done((bf16[1,256,128]{2,1,0:T(8,128)(2,1)S(1)}, bf16[1,256,128]{2,1,0:T(8,128)(2,1)}, u32[]{:S(2)}) %copy-start) | copy-done | bytes 65560
  5.4 1.0 %copy-done.2 = bf16[1,256,1024]{2,1,0:T(8,128)(2,1)S(1)} copy-done((bf16[1,256,1024]{2,1,0:T(8,128)(2,1)S(1)}, bf16[1,256,1024]{2,1,0:T(8,128)(2,1)}, u32[]{:S(2)}) %copy-start.2) | copy-done | bytes 524312
  6.4 1.0 %copy-done.3 = bf16[1,256,1024]{2,1,0:T(8,128)(2,1)S(1)} copy-done((bf16[1,256,1024]{2,1,0:T(8,128)(2,1)S(1)}, bf16[1,256,1024]{2,1,0:T(8,128)(2,1)}, u32[]{:S(2)}) %copy-start.3) | copy-done | bytes 524312
  7.4 0.8 %copy-done.4 = bf16[1,256,128]{2,1,0:T(8,128)(2,1)S(1)} copy-done((bf16[1,256,128]{2,1,0:T(8,128)(2,1)S(1)}, bf16[1,256,128]{2,1,0:T(8,128)(2,1)}, u32[]{:S(2)}) %copy-start.4) | copy-done | bytes 65560
  8.3 1.5 %forward_stats.6 = (f32[32,256]{1,0:T(8,128)S(1)}, bf16[384,2048]{1,0:T(8,128)(2,1)S(1)}, f32[384,2048]{1,0:T(8,128)S(1)}, bf16[2048,128]{1,0:T(8,128)(2,1)S(1)}...) custom-call(s32[1]{0:T(128)S(6)} %copy.14.refs_0_, bf16[1,256,1024]{2,1,0:T(8,128)(2,1)S(1)} %copy-done.2, ...), custom_call_target="tpu_custom_call" | custom-call | flops 1207959552 | bytes 1048576 | tf_op jit(solution)/shard_map/forward_stats/pallas_call | solution.py:217
  9.9 2.0 %collective-permute-start.1 = (bf16[544,128]{1,0:T(8,128)(2,1)S(1)}, bf16[544,128]{1,0:T(8,128)(2,1)S(1)}, u32[]{:S(2)}, u32[]{:S(2)}) collective-permute-start(bf16[544,128]{1,0:T(8,128)(2,1)S(1)} %constant_dynamic-update-slice_fusion), channel_id=1, source_target_pairs={{0,1},{1,2},{2,3},{3,4},{4,5},{5,6},{6,7},{7,0},{8,9},{9,10},{10,1... | collective-permute-start | bytes 417800 | tf_op jit(solution)/shard_map/ppermute | solution.py:271
  11.8 4.0 %collective-permute-start.2 = (bf16[544,128]{1,0:T(8,128)(2,1)S(1)}, bf16[544,128]{1,0:T(8,128)(2,1)S(1)}, u32[]{:S(2)}, u32[]{:S(2)}) collective-permute-start(bf16[544,128]{1,0:T(8,128)(2,1)S(1)} %constant_dynamic-update-slice_fusion), channel_id=1, source_target_pairs={{0,7},{1,0},{2,1},{3,2},{4,3},{5,4},{6,5},{7,6},{8,15},{9,8},{10,9... | collective-permute-start | bytes 417800 | tf_op jit(solution)/shard_map/ppermute | solution.py:271
  16.4 2.7 %collective-permute-done.1.refs_2_.refs_11_ = bf16[544,128]{1,0:T(8,128)(2,1)S(1)} collective-permute-done((bf16[544,128]{1,0:T(8,128)(2,1)S(1)}, bf16[544,128]{1,0:T(8,128)(2,1)S(1)}, u32[]{:S(2)}, u32[]{:S(2)}) %collective-permute-start.1) | collective-permute-done | bytes 139296 | tf_op jit(solution)/shard_map/ppermute | solution.py:271
  19.2 3.2 %collective-permute-start.4 = (bf16[544,128]{1,0:T(8,128)(2,1)S(1)}, bf16[544,128]{1,0:T(8,128)(2,1)S(1)}, u32[]{:S(2)}, u32[]{:S(2)}) collective-permute-start(bf16[544,128]{1,0:T(8,128)(2,1)S(1)} %collective-permute-done.2.refs_3_.refs_12_), channel_id=1, source_target_pairs={{0,7},{1,0},{2,1},{3,2},{4,3},{5,4},{6,5},{7,6},{8,15},{9,8},{10,9... | collective-permute-start | bytes 417800 | tf_op jit(solution)/shard_map/ppermute | solution.py:271
  22.4 2.4 %forward_stats.8 = (f32[32,256]{1,0:T(8,128)S(1)}, bf16[512,2048]{1,0:T(8,128)(2,1)S(1)}, f32[512,2048]{1,0:T(8,128)S(1)}) custom-call(bf16[2048,128]{1,0:T(8,128)(2,1)S(1)} %get-tuple-element.42.refs_0_.refs_1_, bf16[2048,128]{1,0:T(8,128)(2,1)S(1)} %get-tuple-element.43.refs_1_.refs_2_, bf16[544,128]{1,0:T(8,128)(2,1)S(1)} %collective-permute-done.1.refs_2_.refs_11_, ...), custom_call_target="tpu_custom_call" | custom-call | flops 1610612736 | bytes 1048576 | tf_op jit(solution)/shard_map/forward_stats/pallas_call | solution.py:217
  25.5 3.2 %collective-permute-start.6 = (bf16[544,128]{1,0:T(8,128)(2,1)S(1)}, bf16[544,128]{1,0:T(8,128)(2,1)S(1)}, u32[]{:S(2)}, u32[]{:S(2)}) collective-permute-start(bf16[544,128]{1,0:T(8,128)(2,1)S(1)} %collective-permute-done.4.refs_3_.refs_12_), channel_id=1, source_target_pairs={{0,7},{1,0},{2,1},{3,2},{4,3},{5,4},{6,5},{7,6},{8,15},{9,8},{10,9... | collective-permute-start | bytes 417800 | tf_op jit(solution)/shard_map/ppermute | solution.py:271
  28.7 2.4 %forward_stats.9 = (f32[32,256]{1,0:T(8,128)S(1)}, bf16[512,2048]{1,0:T(8,128)(2,1)S(1)}, f32[512,2048]{1,0:T(8,128)S(1)}) custom-call(bf16[2048,128]{1,0:T(8,128)(2,1)S(1)} %get-tuple-element.42.refs_0_.refs_1_, bf16[2048,128]{1,0:T(8,128)(2,1)S(1)} %get-tuple-element.43.refs_1_.refs_2_, bf16[544,128]{1,0:T(8,128)(2,1)S(1)} %collective-permute-done.3.refs_2_.refs_11_, ...), custom_call_target="tpu_custom_call" | custom-call | flops 1610612736 | bytes 1048576 | tf_op jit(solution)/shard_map/forward_stats/pallas_call | solution.py:217
  31.7 2.4 %forward_stats.10 = (f32[32,256]{1,0:T(8,128)S(1)}, bf16[512,2048]{1,0:T(8,128)(2,1)S(1)}, f32[512,2048]{1,0:T(8,128)S(1)}) custom-call(bf16[2048,128]{1,0:T(8,128)(2,1)S(1)} %get-tuple-element.42.refs_0_.refs_1_, bf16[2048,128]{1,0:T(8,128)(2,1)S(1)} %get-tuple-element.43.refs_1_.refs_2_, bf16[544,128]{1,0:T(8,128)(2,1)S(1)} %collective-permute-done.5.refs_2_.refs_11_, ...), custom_call_target="tpu_custom_call" | custom-call | flops 1610612736 | bytes 1048576 | tf_op jit(solution)/shard_map/forward_stats/pallas_call | solution.py:217
  34.1 3.9 %collective-permute-done.7.refs_2_.refs_11_ = bf16[544,128]{1,0:T(8,128)(2,1)S(1)} collective-permute-done((bf16[544,128]{1,0:T(8,128)(2,1)S(1)}, bf16[544,128]{1,0:T(8,128)(2,1)S(1)}, u32[]{:S(2)}, u32[]{:S(2)}) %collective-permute-start.7) | collective-permute-done | bytes 139296 | tf_op jit(solution)/shard_map/ppermute | solution.py:271
  38.0 1.0 %forward_stats.11 = (f32[32,256]{1,0:T(8,128)S(1)}, bf16[256,2048]{1,0:T(8,128)(2,1)S(1)}, f32[256,2048]{1,0:T(8,128)S(1)}) custom-call(bf16[2048,128]{1,0:T(8,128)(2,1)S(1)} %get-tuple-element.42.refs_0_.refs_1_, bf16[2048,128]{1,0:T(8,128)(2,1)S(1)} %get-tuple-element.43.refs_1_.refs_2_, bf16[544,128]{1,0:T(8,128)(2,1)S(1)} %collective-permute-done.7.refs_2_.refs_11_), custom_call_target="tpu_custom_call" | custom-call | flops 805306368 | bytes 1048576 | tf_op jit(solution)/shard_map/forward_stats/pallas_call | solution.py:217
  39.0 1.2 %backward_grads.6 = (f32[1024,256]{1,0:T(8,128)S(1)}, bf16[512,128]{1,0:T(8,128)(2,1)S(1)}) custom-call(s32[1]{0:T(128)S(6)} %copy.15.refs_0_, bf16[2048,128]{1,0:T(8,128)(2,1)S(1)} %get-tuple-element.42.refs_0_.refs_1_, bf16[2048,128]{1,0:T(8,128)(2,1)S(1)} %get-tuple-element.43.refs_1_.refs_2_, f32[32,256]{1,0:T(8,128)S(1)} %get-tuple-element.44.refs_3_, ...), custom_call_target="tpu_custom_call" | custom-call | flops 1342177280 | bytes 2097152 | tf_op jit(solution)/shard_map/backward_grads/pallas_call | solution.py:245
  40.3 2.1 %backward_grads.7 = (f32[1024,256]{1,0:T(8,128)S(1)}, f32[512,128]{1,0:T(8,128)S(1)}, bf16[512,128]{1,0:T(8,128)(2,1)S(1)}) custom-call(s32[1]{0:T(128)S(6)} %copy.15.refs_0_, bf16[2048,128]{1,0:T(8,128)(2,1)S(1)} %get-tuple-element.42.refs_0_.refs_1_, bf16[2048,128]{1,0:T(8,128)(2,1)S(1)} %get-tuple-element.43.refs_1_.refs_2_, ...), custom_call_target="tpu_custom_call" | custom-call | flops 2684354560 | bytes 2097152 | tf_op jit(solution)/shard_map/backward_grads/pallas_call | solution.py:245
  42.4 2.1 %collective-permute-start.10 = (bf16[512,128]{1,0:T(8,128)(2,1)S(1)}, bf16[512,128]{1,0:T(8,128)(2,1)S(1)}, u32[]{:S(2)}, u32[]{:S(2)}) collective-permute-start(bf16[512,128]{1,0:T(8,128)(2,1)S(1)} %get-tuple-element.67.refs_15_), channel_id=1, source_target_pairs={{0,1},{1,2},{2,3},{3,4},{4,5},{5,6},{6,7},{7,0},{8,9},{9,10},{10,1... | collective-permute-start | bytes 393224 | tf_op jit(solution)/shard_map/ppermute | solution.py:271
  44.5 0.9 %collective-permute-done.8 = bf16[512,128]{1,0:T(8,128)(2,1)S(1)} collective-permute-done((bf16[512,128]{1,0:T(8,128)(2,1)S(1)}, bf16[512,128]{1,0:T(8,128)(2,1)S(1)}, u32[]{:S(2)}, u32[]{:S(2)}) %collective-permute-start.8) | collective-permute-done | bytes 131104 | tf_op jit(solution)/shard_map/ppermute | solution.py:271
  45.4 2.3 %collective-permute-start.9 = (bf16[512,128]{1,0:T(8,128)(2,1)S(1)}, bf16[512,128]{1,0:T(8,128)(2,1)S(1)}, u32[]{:S(2)}, u32[]{:S(2)}) collective-permute-start(bf16[512,128]{1,0:T(8,128)(2,1)S(1)} %add_convert_fusion.4.refs_14_), channel_id=1, source_target_pairs={{0,7},{1,0},{2,1},{3,2},{4,3},{5,4},{6,5},{7,6},{8,15},{9,8},{10,9... | collective-permute-start | bytes 393224 | tf_op jit(solution)/shard_map/ppermute | solution.py:271
  47.7 2.1 %backward_grads.8 = (f32[1024,256]{1,0:T(8,128)S(1)}, f32[512,128]{1,0:T(8,128)S(1)}, f32[512,128]{1,0:T(8,128)S(1)}) custom-call(s32[1]{0:T(128)S(6)} %copy.15.refs_0_, bf16[2048,128]{1,0:T(8,128)(2,1)S(1)} %get-tuple-element.42.refs_0_.refs_1_, bf16[2048,128]{1,0:T(8,128)(2,1)S(1)} %get-tuple-element.43.refs_1_.refs_2_, ...), custom_call_target="tpu_custom_call" | custom-call | flops 2684354560 | bytes 2097152 | tf_op jit(solution)/shard_map/backward_grads/pallas_call | solution.py:245
  50.2 0.8 %collective-permute-done.9 = bf16[512,128]{1,0:T(8,128)(2,1)S(1)} collective-permute-done((bf16[512,128]{1,0:T(8,128)(2,1)S(1)}, bf16[512,128]{1,0:T(8,128)(2,1)S(1)}, u32[]{:S(2)}, u32[]{:S(2)}) %collective-permute-start.9) | collective-permute-done | bytes 131104 | tf_op jit(solution)/shard_map/ppermute | solution.py:271
  51.0 4.0 %collective-permute-start.11 = (bf16[512,128]{1,0:T(8,128)(2,1)S(1)}, bf16[512,128]{1,0:T(8,128)(2,1)S(1)}, u32[]{:S(2)}, u32[]{:S(2)}) collective-permute-start(bf16[512,128]{1,0:T(8,128)(2,1)S(1)} %add_convert_fusion.3.refs_14_), channel_id=1, source_target_pairs={{0,7},{1,0},{2,1},{3,2},{4,3},{5,4},{6,5},{7,6},{8,15},{9,8},{10,9... | collective-permute-start | bytes 393224 | tf_op jit(solution)/shard_map/ppermute | solution.py:271
  55.0 2.1 %backward_grads.9 = (f32[1024,256]{1,0:T(8,128)S(1)}, f32[512,128]{1,0:T(8,128)S(1)}, f32[512,128]{1,0:T(8,128)S(1)}) custom-call(s32[1]{0:T(128)S(6)} %copy.15.refs_0_, bf16[2048,128]{1,0:T(8,128)(2,1)S(1)} %get-tuple-element.42.refs_0_.refs_1_, bf16[2048,128]{1,0:T(8,128)(2,1)S(1)} %get-tuple-element.43.refs_1_.refs_2_, ...), custom_call_target="tpu_custom_call" | custom-call | flops 2684354560 | bytes 2097152 | tf_op jit(solution)/shard_map/backward_grads/pallas_call | solution.py:245
  57.6 3.7 %collective-permute-start.13 = (bf16[512,128]{1,0:T(8,128)(2,1)S(1)}, bf16[512,128]{1,0:T(8,128)(2,1)S(1)}, u32[]{:S(2)}, u32[]{:S(2)}) collective-permute-start(bf16[512,128]{1,0:T(8,128)(2,1)S(1)} %add_convert_fusion.1.refs_16_), channel_id=1, source_target_pairs={{0,7},{1,0},{2,1},{3,2},{4,3},{5,4},{6,5},{7,6},{8,15},{9,8},{10,9... | collective-permute-start | bytes 393224 | tf_op jit(solution)/shard_map/ppermute | solution.py:271
  61.3 1.2 %backward_grads.10 = (f32[1024,256]{1,0:T(8,128)S(1)}, f32[512,128]{1,0:T(8,128)S(1)}) custom-call(s32[1]{0:T(128)S(6)} %copy.15.refs_0_, bf16[2048,128]{1,0:T(8,128)(2,1)S(1)} %get-tuple-element.42.refs_0_.refs_1_, bf16[2048,128]{1,0:T(8,128)(2,1)S(1)} %get-tuple-element.43.refs_1_.refs_2_, f32[32,256]{1,0:T(8,128)S(1)} %get-tuple-element.44.refs_3_, ...), custom_call_target="tpu_custom_call" | custom-call | flops 1342177280 | bytes 2097152 | tf_op jit(solution)/shard_map/backward_grads/pallas_call | solution.py:245
  62.5 1.0 %collective-permute-done.14 = bf16[512,128]{1,0:T(8,128)(2,1)S(1)} collective-permute-done((bf16[512,128]{1,0:T(8,128)(2,1)S(1)}, bf16[512,128]{1,0:T(8,128)(2,1)S(1)}, u32[]{:S(2)}, u32[]{:S(2)}) %collective-permute-start.14) | collective-permute-done | bytes 131104 | tf_op jit(solution)/shard_map/ppermute | solution.py:271
  64.4 2.1 %backward_grads.11 = (f32[1,256,1024]{2,1,0:T(8,128)}, f32[1,256,128]{2,1,0:T(8,128)}, f32[1,256,128]{2,1,0:T(8,128)}) custom-call(s32[1]{0:T(128)S(6)} %copy.15.refs_0_, bf16[2048,128]{1,0:T(8,128)(2,1)S(1)} %get-tuple-element.42.refs_0_.refs_1_, bf16[2048,128]{1,0:T(8,128)(2,1)S(1)} %get-tuple-element.43.refs_1_.refs_2_, ...), custom_call_target="tpu_custom_call" | custom-call | flops 1342177280 | bytes 2097152 | tf_op jit(solution)/shard_map/backward_grads/pallas_call | solution.py:245
  66.5 1.7 %collective-permute-done.15 = bf16[256,128]{1,0:T(8,128)(2,1)S(1)} collective-permute-done((bf16[256,128]{1,0:T(8,128)(2,1)S(1)}, bf16[256,128]{1,0:T(8,128)(2,1)S(1)}, u32[]{:S(2)}, u32[]{:S(2)}) %collective-permute-start.15) | collective-permute-done | bytes 65568 | tf_op jit(solution)/shard_map/ppermute | solution.py:271
  68.3 0.7 slice_add_fusion
  (36 shorter events, 3.7 us)
Async XLA Ops:
  2.2 7.6 %collective-permute-start = (bf16[272,128]{1,0:T(8,128)(2,1)S(1)}, bf16[272,128]{1,0:T(8,128)(2,1)S(1)}, u32[]{:S(2)}, u32[]{:S(2)}) collective-permute-start(bf16[272,128]{1,0:T(8,128)(2,1)S(1)} %maximum_maximum_fusion.refs_3_), channel_id=1, source_target_pairs={{0,8},{1,9},{2,10},{3,11},{4,12},{5,13},{6,14},{7,15},{8,0},{9,1},... | collective-permute-start | bytes 208904 | tf_op jit(solution)/shard_map/ppermute | solution.py:271
  4.5 0.8 %copy-start = (bf16[1,256,128]{2,1,0:T(8,128)(2,1)S(1)}, bf16[1,256,128]{2,1,0:T(8,128)(2,1)}, u32[]{:S(2)}) copy-start(bf16[1,256,128]{2,1,0:T(8,128)(2,1)} %refs_11_.1) | copy-start | bytes 196612
  5.3 1.0 %copy-start.2 = (bf16[1,256,1024]{2,1,0:T(8,128)(2,1)S(1)}, bf16[1,256,1024]{2,1,0:T(8,128)(2,1)}, u32[]{:S(2)}) copy-start(bf16[1,256,1024]{2,1,0:T(8,128)(2,1)} %refs_1_.1) | copy-start | bytes 1572868
  6.4 1.0 %copy-start.3 = (bf16[1,256,1024]{2,1,0:T(8,128)(2,1)S(1)}, bf16[1,256,1024]{2,1,0:T(8,128)(2,1)}, u32[]{:S(2)}) copy-start(bf16[1,256,1024]{2,1,0:T(8,128)(2,1)} %refs_2_.1) | copy-start | bytes 1572868
  7.4 0.8 %copy-start.4 = (bf16[1,256,128]{2,1,0:T(8,128)(2,1)S(1)}, bf16[1,256,128]{2,1,0:T(8,128)(2,1)}, u32[]{:S(2)}) copy-start(bf16[1,256,128]{2,1,0:T(8,128)(2,1)} %refs_5_.1) | copy-start | bytes 196612
  9.9 9.3 %collective-permute-start.1 = (bf16[544,128]{1,0:T(8,128)(2,1)S(1)}, bf16[544,128]{1,0:T(8,128)(2,1)S(1)}, u32[]{:S(2)}, u32[]{:S(2)}) collective-permute-start(bf16[544,128]{1,0:T(8,128)(2,1)S(1)} %constant_dynamic-update-slice_fusion), channel_id=1, source_target_pairs={{0,1},{1,2},{2,3},{3,4},{4,5},{5,6},{6,7},{7,0},{8,9},{9,10},{10,1... | collective-permute-start | bytes 417800 | tf_op jit(solution)/shard_map/ppermute | solution.py:271
  11.8 7.3 %collective-permute-start.2 = (bf16[544,128]{1,0:T(8,128)(2,1)S(1)}, bf16[544,128]{1,0:T(8,128)(2,1)S(1)}, u32[]{:S(2)}, u32[]{:S(2)}) collective-permute-start(bf16[544,128]{1,0:T(8,128)(2,1)S(1)} %constant_dynamic-update-slice_fusion), channel_id=1, source_target_pairs={{0,7},{1,0},{2,1},{3,2},{4,3},{5,4},{6,5},{7,6},{8,15},{9,8},{10,9... | collective-permute-start | bytes 417800 | tf_op jit(solution)/shard_map/ppermute | solution.py:271
  19.2 6.3 %collective-permute-start.3 = (bf16[544,128]{1,0:T(8,128)(2,1)S(1)}, bf16[544,128]{1,0:T(8,128)(2,1)S(1)}, u32[]{:S(2)}, u32[]{:S(2)}) collective-permute-start(bf16[544,128]{1,0:T(8,128)(2,1)S(1)} %collective-permute-done.1.refs_2_.refs_11_), channel_id=1, source_target_pairs={{0,1},{1,2},{2,3},{3,4},{4,5},{5,6},{6,7},{7,0},{8,9},{9,10},{10,1... | collective-permute-start | bytes 417800 | tf_op jit(solution)/shard_map/ppermute | solution.py:271
  19.2 6.3 %collective-permute-start.4 = (bf16[544,128]{1,0:T(8,128)(2,1)S(1)}, bf16[544,128]{1,0:T(8,128)(2,1)S(1)}, u32[]{:S(2)}, u32[]{:S(2)}) collective-permute-start(bf16[544,128]{1,0:T(8,128)(2,1)S(1)} %collective-permute-done.2.refs_3_.refs_12_), channel_id=1, source_target_pairs={{0,7},{1,0},{2,1},{3,2},{4,3},{5,4},{6,5},{7,6},{8,15},{9,8},{10,9... | collective-permute-start | bytes 417800 | tf_op jit(solution)/shard_map/ppermute | solution.py:271
  25.4 6.3 %collective-permute-start.5 = (bf16[544,128]{1,0:T(8,128)(2,1)S(1)}, bf16[544,128]{1,0:T(8,128)(2,1)S(1)}, u32[]{:S(2)}, u32[]{:S(2)}) collective-permute-start(bf16[544,128]{1,0:T(8,128)(2,1)S(1)} %collective-permute-done.3.refs_2_.refs_11_), channel_id=1, source_target_pairs={{0,1},{1,2},{2,3},{3,4},{4,5},{5,6},{6,7},{7,0},{8,9},{9,10},{10,1... | collective-permute-start | bytes 417800 | tf_op jit(solution)/shard_map/ppermute | solution.py:271
  25.5 6.3 %collective-permute-start.6 = (bf16[544,128]{1,0:T(8,128)(2,1)S(1)}, bf16[544,128]{1,0:T(8,128)(2,1)S(1)}, u32[]{:S(2)}, u32[]{:S(2)}) collective-permute-start(bf16[544,128]{1,0:T(8,128)(2,1)S(1)} %collective-permute-done.4.refs_3_.refs_12_), channel_id=1, source_target_pairs={{0,7},{1,0},{2,1},{3,2},{4,3},{5,4},{6,5},{7,6},{8,15},{9,8},{10,9... | collective-permute-start | bytes 417800 | tf_op jit(solution)/shard_map/ppermute | solution.py:271
  31.7 6.3 %collective-permute-start.7 = (bf16[544,128]{1,0:T(8,128)(2,1)S(1)}, bf16[544,128]{1,0:T(8,128)(2,1)S(1)}, u32[]{:S(2)}, u32[]{:S(2)}) collective-permute-start(bf16[544,128]{1,0:T(8,128)(2,1)S(1)} %collective-permute-done.5.refs_2_.refs_11_), channel_id=1, source_target_pairs={{0,1},{1,2},{2,3},{3,4},{4,5},{5,6},{6,7},{7,0},{8,9},{9,10},{10,1... | collective-permute-start | bytes 417800 | tf_op jit(solution)/shard_map/ppermute | solution.py:271
  40.2 5.2 %collective-permute-start.8 = (bf16[512,128]{1,0:T(8,128)(2,1)S(1)}, bf16[512,128]{1,0:T(8,128)(2,1)S(1)}, u32[]{:S(2)}, u32[]{:S(2)}) collective-permute-start(bf16[512,128]{1,0:T(8,128)(2,1)S(1)} %get-tuple-element.65), channel_id=1, source_target_pairs={{0,7},{1,0},{2,1},{3,2},{4,3},{5,4},{6,5},{7,6},{8,15},{9,8},{10,9... | collective-permute-start | bytes 393224 | tf_op jit(solution)/shard_map/ppermute | solution.py:271
  42.4 7.7 %collective-permute-start.10 = (bf16[512,128]{1,0:T(8,128)(2,1)S(1)}, bf16[512,128]{1,0:T(8,128)(2,1)S(1)}, u32[]{:S(2)}, u32[]{:S(2)}) collective-permute-start(bf16[512,128]{1,0:T(8,128)(2,1)S(1)} %get-tuple-element.67.refs_15_), channel_id=1, source_target_pairs={{0,1},{1,2},{2,3},{3,4},{4,5},{5,6},{6,7},{7,0},{8,9},{9,10},{10,1... | collective-permute-start | bytes 393224 | tf_op jit(solution)/shard_map/ppermute | solution.py:271
  45.4 5.6 %collective-permute-start.9 = (bf16[512,128]{1,0:T(8,128)(2,1)S(1)}, bf16[512,128]{1,0:T(8,128)(2,1)S(1)}, u32[]{:S(2)}, u32[]{:S(2)}) collective-permute-start(bf16[512,128]{1,0:T(8,128)(2,1)S(1)} %add_convert_fusion.4.refs_14_), channel_id=1, source_target_pairs={{0,7},{1,0},{2,1},{3,2},{4,3},{5,4},{6,5},{7,6},{8,15},{9,8},{10,9... | collective-permute-start | bytes 393224 | tf_op jit(solution)/shard_map/ppermute | solution.py:271
  50.1 7.0 %collective-permute-start.12 = (bf16[512,128]{1,0:T(8,128)(2,1)S(1)}, bf16[512,128]{1,0:T(8,128)(2,1)S(1)}, u32[]{:S(2)}, u32[]{:S(2)}) collective-permute-start(bf16[512,128]{1,0:T(8,128)(2,1)S(1)} %add_convert_fusion.2.refs_15_), channel_id=1, source_target_pairs={{0,1},{1,2},{2,3},{3,4},{4,5},{5,6},{6,7},{7,0},{8,9},{9,10},{10,1... | collective-permute-start | bytes 393224 | tf_op jit(solution)/shard_map/ppermute | solution.py:271
  51.0 6.5 %collective-permute-start.11 = (bf16[512,128]{1,0:T(8,128)(2,1)S(1)}, bf16[512,128]{1,0:T(8,128)(2,1)S(1)}, u32[]{:S(2)}, u32[]{:S(2)}) collective-permute-start(bf16[512,128]{1,0:T(8,128)(2,1)S(1)} %add_convert_fusion.3.refs_14_), channel_id=1, source_target_pairs={{0,7},{1,0},{2,1},{3,2},{4,3},{5,4},{6,5},{7,6},{8,15},{9,8},{10,9... | collective-permute-start | bytes 393224 | tf_op jit(solution)/shard_map/ppermute | solution.py:271
  57.2 6.3 %collective-permute-start.14 = (bf16[512,128]{1,0:T(8,128)(2,1)S(1)}, bf16[512,128]{1,0:T(8,128)(2,1)S(1)}, u32[]{:S(2)}, u32[]{:S(2)}) collective-permute-start(bf16[512,128]{1,0:T(8,128)(2,1)S(1)} %add_convert_fusion.refs_17_), channel_id=1, source_target_pairs={{0,1},{1,2},{2,3},{3,4},{4,5},{5,6},{6,7},{7,0},{8,9},{9,10},{10,1... | collective-permute-start | bytes 393224 | tf_op jit(solution)/shard_map/ppermute | solution.py:271
  57.6 6.3 %collective-permute-start.13 = (bf16[512,128]{1,0:T(8,128)(2,1)S(1)}, bf16[512,128]{1,0:T(8,128)(2,1)S(1)}, u32[]{:S(2)}, u32[]{:S(2)}) collective-permute-start(bf16[512,128]{1,0:T(8,128)(2,1)S(1)} %add_convert_fusion.1.refs_16_), channel_id=1, source_target_pairs={{0,7},{1,0},{2,1},{3,2},{4,3},{5,4},{6,5},{7,6},{8,15},{9,8},{10,9... | collective-permute-start | bytes 393224 | tf_op jit(solution)/shard_map/ppermute | solution.py:271
  61.3 3.1 %copy-start.1 = (bf16[1,256,128]{2,1,0:T(8,128)(2,1)S(1)}, bf16[1,256,128]{2,1,0:T(8,128)(2,1)}, u32[]{:S(2)}) copy-start(bf16[1,256,128]{2,1,0:T(8,128)(2,1)} %refs_11_.1) | copy-start | bytes 196612
  63.9 4.4 %collective-permute-start.15 = (bf16[256,128]{1,0:T(8,128)(2,1)S(1)}, bf16[256,128]{1,0:T(8,128)(2,1)S(1)}, u32[]{:S(2)}, u32[]{:S(2)}) collective-permute-start(bf16[256,128]{1,0:T(8,128)(2,1)S(1)} %slice.31.refs_13_), channel_id=1, source_target_pairs={{0,8},{1,9},{2,10},{3,11},{4,12},{5,13},{6,14},{7,15},{8,0},{9,1},... | collective-permute-start | bytes 196616 | tf_op jit(solution)/shard_map/ppermute | solution.py:271

commit v5 on v4

--- a/solution.py
+++ b/solution.py
@@ -38,20 +38,13 @@
     return parts[0]
 
 
-def pack_places(blocks, share):
+def pack_places(blocks, picks, share):
     size = 2 * share + PAD
-    return [(ref, at) for ref in blocks for at in range(0, ref.shape[0], size)]
-
-
-def load_rows(blocks, own, k_all, v_all, share):
-    places = pack_places(blocks, share)
-    for i, (ref, at) in enumerate(places):
-        k_all[i * share : (i + 1) * share, :] = ref[at : at + share, :]
-        v_all[i * share : (i + 1) * share, :] = ref[at + share : at + 2 * share, :]
-    if own:
-        k_all[len(places) * share :, :] = own[0][0]
-        v_all[len(places) * share :, :] = own[1][0]
-    return len(places) * share
+    return [
+        (ref, (first + i) * size)
+        for ref, (first, count) in zip(blocks, picks)
+        for i in range(count)
+    ]
 
 
 def own_mask(at, resp):
@@ -59,24 +52,30 @@
     return key_at <= lax.broadcasted_iota(jnp.int32, (SLICE, resp), 1)
 
 
-def forward_kernel(heads, share, count, opening, *refs):
+def forward_kernel(heads, share, picks, opening, *refs):
     refs, scratch = refs[:-4], refs[-4:]
     k_all, v_all, s0, s1 = scratch
+    count = len(picks)
     if opening:
-        len_ref, q_ref, c_ref = refs[:3]
-        blocks, own = refs[3 : 3 + count], refs[3 + count : 5 + count]
-        out_ref, e_all, g_all, q_rows, c_rows, copy_ref = refs[5 + count :]
-        copy_ref[...] = blocks[0][...]
+        len_ref, wide_ref, own_ref = refs[:3]
+        blocks = refs[3 : 3 + count]
+        out_ref, e_all, g_all, q_rows, c_rows = refs[3 + count :]
     else:
         q_rows, c_rows = refs[:2]
-        blocks, own = refs[2 : 2 + count], ()
+        blocks = refs[2 : 2 + count]
         out_ref, e_all, g_all = refs[2 + count :]
     width, resp = q_rows.shape[1], q_rows.shape[0] // heads
     rate = math.log2(math.e) / math.sqrt(width)
     s_buf = (s0, s1)
-    prompt = load_rows(blocks, own, k_all, v_all, share)
     keys = k_all.shape[0]
+    places = pack_places(blocks, picks, share)
+    prompt = len(places) * share
+    for i, (ref, at) in enumerate(places):
+        k_all[i * share : (i + 1) * share, :] = ref[at : at + share, :]
+        v_all[i * share : (i + 1) * share, :] = ref[at + share : at + 2 * share, :]
     if opening:
+        k_all[prompt:, :] = own_ref[0]
+        v_all[prompt:, :] = own_ref[1]
         live = lax.broadcasted_iota(jnp.int32, (resp, width), 0) < len_ref[0]
 
     for t in range(heads + 1):
@@ -84,8 +83,8 @@
             rows = slice(t * resp, (t + 1) * resp)
             if opening:
                 lanes = slice(t * width, (t + 1) * width)
-                q_rows[rows, :] = q_ref[0, :, lanes]
-                c_rows[rows, :] = jnp.where(live, c_ref[0, :, lanes], jnp.zeros((), BF16))
+                q_rows[rows, :] = wide_ref[0, :, lanes]
+                c_rows[rows, :] = jnp.where(live, wide_ref[1, :, lanes], jnp.zeros((), BF16))
             s_buf[t % 2][...] = dot_nt(k_all[...], q_rows[rows, :])
             g_all[:, rows] = dot_nt(v_all[...], c_rows[rows, :])
         if t > 0:
@@ -114,18 +113,19 @@
             out_ref[heads + h : heads + h + 1, :] = jnp.sum(mass, axis=0, keepdims=True)
             out_ref[2 * heads + h : 2 * heads + h + 1, :] = jnp.sum(mixed, axis=0, keepdims=True)
     paid = jnp.zeros((1, width), F32)
-    for ref, at in pack_places(blocks, share):
+    for ref, at in places:
         paid = paid + ref[at + 2 * share : at + 2 * share + PAD, :].astype(F32)[:1]
     out_ref[3 * heads :, :] = jnp.broadcast_to(jnp.max(paid), (heads, resp))
 
 
-def backward_kernel(heads, share, owners, count, stats, spans, after, more, last, *refs):
+def backward_kernel(heads, share, owners, picks, stats, spans, after, more, last, *refs):
     refs, (k_t, p_all, ds_all) = refs[:-3], refs[-3:]
     pay_ref, q_rows, c_rows = refs[:3]
     refs = refs[3:]
     stat_refs, refs = refs[:stats], refs[stats:]
     e_refs, g_refs, refs = refs[: len(spans)], refs[len(spans) : 2 * len(spans)], refs[2 * len(spans) :]
-    blocks, refs = refs[:count], refs[count:]
+    blocks, refs = refs[: len(picks)], refs[len(picks) :]
+    own_ref, refs = (refs[0], refs[1:]) if last else (None, refs)
     prior, refs = (refs[0], refs[1:]) if more else (None, refs)
     dq_ref, *out_refs = refs[after:]
     width, resp = q_rows.shape[1], q_rows.shape[0] // heads
@@ -144,11 +144,12 @@
     factors = [weights[group] / mass for group, _, _ in spans]
     advantage = (pay_ref[0].astype(F32) - paid / owners)[:1, :width]
 
+    places = pack_places(blocks, picks, share)
+    for i, (ref, at) in enumerate(places):
+        k_t[:, i * share : (i + 1) * share] = ref[at : at + share, :].T
+    prompt = len(places) * share
     if last:
-        k_t[...] = blocks[0][0].T
-    else:
-        for i, (ref, at) in enumerate(pack_places(blocks, share)):
-            k_t[:, i * share : (i + 1) * share] = ref[at : at + share, :].T
+        k_t[:, prompt:] = own_ref[0].T
     half = heads // 2
     dk = dv = None
     for h in range(heads):
@@ -177,9 +178,9 @@
             dv = dv_part if dv is None else dv + dv_part
     dk, dv = dk * (advantage * scale), dv * advantage
     if last:
-        out_refs[0][0] = dk
-        out_refs[1][0] = dv
-        return
+        *out_refs, own_keys, own_values = out_refs
+        own_keys[0] = dk[prompt:]
+        own_values[0] = dv[prompt:]
     at = 0
     for ref in out_refs:
         for base in range(0, ref.shape[0], 2 * share):
@@ -188,24 +189,18 @@
             at += share
 
 
-def count_keys(blocks, share, own):
-    return share * sum(b.shape[0] // (2 * share + PAD) for b in blocks) + (
-        own[0].shape[1] if own else 0
-    )
-
-
 def forward_stats(heads, share, blocks, rows=(), opening=()):
     if opening:
-        lengths, queries, grad_out, *own = opening
-        resp, width = queries.shape[1], queries.shape[2] // heads
-        operands = (lengths, queries, grad_out, *blocks, *own)
+        resp, width = opening[1].shape[1], blocks[0].shape[1]
+        operands = (*opening, *blocks)
         specs = [SMEM_SPEC] + [VMEM_SPEC] * (len(operands) - 1)
+        picks = ((0, 1),)
     else:
-        own = ()
         resp, width = rows[0].shape[0] // heads, rows[0].shape[1]
         operands = (*rows, *blocks)
         specs = [VMEM_SPEC] * len(operands)
-    keys = count_keys(blocks, share, own)
+        picks = tuple((0, block.shape[0] // (2 * share + PAD)) for block in blocks)
+    keys = share * sum(count for _, count in picks) + (resp if opening else 0)
     outs = [
         jax.ShapeDtypeStruct((4 * heads, resp), F32),
         jax.ShapeDtypeStruct((keys, heads * resp), BF16),
@@ -213,9 +208,8 @@
     ]
     if opening:
         outs += [jax.ShapeDtypeStruct((heads * resp, width), BF16)] * 2
-        outs += [jax.ShapeDtypeStruct(blocks[0].shape, BF16)]
     return pl.pallas_call(
-        functools.partial(forward_kernel, heads, share, len(blocks), bool(opening)),
+        functools.partial(forward_kernel, heads, share, picks, bool(opening)),
         out_shape=tuple(outs),
         in_specs=specs,
         out_specs=(VMEM_SPEC,) * len(outs),
@@ -231,8 +225,9 @@
 
 
 def backward_grads(
-    rewards, rows, stats, kept, parts, blocks, outs, owners, heads, share, prior, after, last=False
+    rewards, rows, stats, kept, parts, blocks, outs, owners, heads, share, prior, after, last=()
 ):
+    blocks, picks = [block for block, _, _ in blocks], tuple(pick for _, *pick in blocks)
     resp, width = rows[0].shape[0] // heads, rows[0].shape[1]
     more = prior is not None
     keys = sum(size for _, _, size in parts)
@@ -240,12 +235,12 @@
     outs = [jax.ShapeDtypeStruct(dq_shape, F32), *outs]
     operands = (
         *rows, *stats, *(kept[g][0] for g, _, _ in parts), *(kept[g][1] for g, _, _ in parts),
-        *blocks, *((prior,) if more else ()),
+        *blocks, *last, *((prior,) if more else ()),
     )
     return pl.pallas_call(
         functools.partial(
-            backward_kernel, heads, share, owners, len(blocks), len(stats), parts, len(after),
-            more, last,
+            backward_kernel, heads, share, owners, picks, len(stats), parts, len(after),
+            more, bool(last),
         ),
         out_shape=tuple(outs),
         in_specs=[SMEM_SPEC] + [VMEM_SPEC] * len(operands) + [ANY_SPEC] * len(after),
@@ -262,12 +257,30 @@
     )(rewards, *operands, *after)
 
 
-def send(block, plane, step):
-    pairs = [
-        (y * RING + z, (y + plane) % 2 * RING + (z + step) % RING)
-        for y in range(2)
-        for z in range(RING)
-    ]
+def tie(block, after):
+    return pl.pallas_call(
+        lambda block_ref, after_ref, out_ref: None,
+        out_shape=jax.ShapeDtypeStruct(block.shape, block.dtype),
+        in_specs=[ANY_SPEC] * 2,
+        out_specs=ANY_SPEC,
+        input_output_aliases={0: 0},
+        compiler_params=pltpu.CompilerParams(vmem_limit_bytes=1024 * 1024),
+        cost_estimate=pl.CostEstimate(flops=0, bytes_accessed=0, transcendentals=0),
+        name="tie",
+    )(block, after)
+
+
+def across(block):
+    pairs = [(i, (i + RING) % (2 * RING)) for i in range(2 * RING)]
+    return lax.ppermute(block, "sample", pairs)
+
+
+def along(block, side):
+    pairs = []
+    for y in range(2):
+        for z in range(RING):
+            other = (z + (1 if z % 2 == side else -1)) % RING
+            pairs.append((y * RING + z, y * RING + other))
     return lax.ppermute(block, "sample", pairs)
 
 
@@ -276,59 +289,93 @@
     resp = queries.shape[1]
     heads = queries.shape[2] // width
     owners = lax.axis_size("sample")
+    size = 2 * share
     reward_rows = jnp.broadcast_to(rewards.astype(BF16)[:, None], (PAD, width))
     packed = jnp.concatenate([prompt_keys, prompt_values, reward_rows], axis=0)
-
-    swapped = send(packed, 1, 0)
-    first, *keep, q_rows, c_rows, packed = forward_stats(
-        heads, share, [packed], opening=(lengths, queries, grad_out, resp_keys, resp_values)
+    own_rows = jnp.concatenate([resp_keys, resp_values], axis=0)
+    wide_rows = jnp.concatenate([queries, grad_out], axis=0)
+
+    first, *keep, q_rows, c_rows = forward_stats(
+        heads, share, [packed], opening=(lengths, wide_rows, own_rows)
     )
     rows, stats, kept = (q_rows, c_rows), [first], [keep]
-    pairs = {0: jnp.concatenate([packed, swapped], axis=0)}
-    for step in (1, 2, 3, 4):
-        pairs[step] = send(pairs[step - 1], 0, 1)
-        if step < 4:
-            pairs[RING - step] = send(pairs[(RING - step + 1) % RING], 0, -1)
-    for blocks in ([swapped], [pairs[1], pairs[7]], [pairs[2], pairs[6]], [pairs[3], pairs[5]], [pairs[4]]):
+
+    def forward(*blocks):
         stat, *keep = forward_stats(heads, share, blocks, rows)
         stats.append(stat)
         kept.append(keep)
 
+    def join(*blocks):
+        return jnp.concatenate(blocks, axis=0)
+
+    l1, r1 = along(packed, 0), along(packed, 1)
+    l2, r2 = along(r1, 0), along(l1, 1)
+    other1 = across(join(tie(packed, stats[-1]), l1, r1))
+    forward(l1, r1)
+    l2, r2 = tie(l2, stats[-1]), tie(r2, stats[-1])
+    l3, r3 = along(r2, 0), along(l2, 1)
+    other2 = across(join(l2, r2))
+    forward(l2, r2)
+    l3, r3 = tie(l3, stats[-1]), tie(r3, stats[-1])
+    l4 = along(r3, 0)
+    other3 = across(join(l3, r3))
+    forward(other1, l3, r3)
+    l4 = tie(l4, stats[-1])
+    other4 = across(l4)
+    forward(other2, l4)
+    forward(other3)
+    forward(other4)
+
     back = functools.partial(
         backward_grads, rewards, rows, stats, kept, owners=owners, heads=heads, share=share
     )
-    ready = jax.ShapeDtypeStruct((4 * share, width), BF16)
-    wide = jax.ShapeDtypeStruct((4 * share, width), F32)
+    ready = jax.ShapeDtypeStruct((size, width), BF16)
+    both_ready = jax.ShapeDtypeStruct((2 * size, width), BF16)
+    wide = jax.ShapeDtypeStruct((size, width), F32)
     grads = jax.ShapeDtypeStruct((1, resp, width), F32)
 
-    def add(received, part):
-        return (received.astype(F32) + part).astype(BF16)
-
-    dq, down = back(((5, 0, 2 * share),), [pairs[4]], [ready], prior=None, after=())
-    dq, part, up = back(
-        ((4, 0, 4 * share),), [pairs[3], pairs[5]], [wide, ready], prior=dq, after=()
-    )
-    down = add(send(down, 0, -1), part)
-    for step in (2, 1):
-        dq, part_down, part_up = back(
-            ((step + 1, 0, 4 * share),), [pairs[step], pairs[RING - step]], [wide, wide],
-            prior=dq, after=(down, up),
-        )
-        down = add(send(down, 0, -1), part_down)
-        up = add(send(up, 0, 1), part_up)
-    dq, mine = back(
-        ((0, 0, share), (1, 0, share)), [packed, swapped], [wide], prior=dq, after=(down, up)
-    )
-    mine = mine + send(down, 0, -1).astype(F32) + send(up, 0, 1).astype(F32)
-    partner = mine[2 * share :].astype(BF16)
-    grad_queries, grad_resp_keys, grad_resp_values = back(
-        ((0, share, resp),), [resp_keys], [grads, grads], prior=dq, after=(partner,), last=True
-    )
-    theirs = send(partner, 1, 0).astype(F32)
-    return (
-        grad_queries, grad_resp_keys, grad_resp_values,
-        mine[:share] + theirs[:share], mine[share : 2 * share] + theirs[share:],
-    )
+    def add(part, *received):
+        return sum((r.astype(F32) for r in received), part).astype(BF16)
+
+    dq, part = back(((6, 0, share),), [(other4, 0, 1)], [ready], prior=None, after=())
+    given = across(part)
+    dq, part, part_left = back(
+        ((5, 0, size), (4, size, share)), [(other3, 0, 2), (l4, 0, 1)], [both_ready, wide],
+        prior=dq, after=(),
+    )
+    far = add(part_left, given)
+    given = across(part)
+    dq, part, part_left, part_right = back(
+        ((4, 0, size), (3, 3 * share, size)), [(other2, 0, 2), (l3, 0, 1), (r3, 0, 1)],
+        [both_ready, wide, wide], prior=dq, after=(far,),
+    )
+    near = add(part_left, given[:size])
+    far = add(part_right, given[size:], along(far, 0))
+    given = across(part)
+    dq, part, part_left, part_right = back(
+        ((3, share, size), (2, 0, size)), [(other1, 1, 2), (l2, 0, 1), (r2, 0, 1)],
+        [both_ready, wide, wide], prior=dq, after=(far, near),
+    )
+    near = add(part_right, given[size:], along(near, 0))
+    far = add(part_left, given[:size], along(far, 1))
+    given = across(part)
+    dq, part, part_left, part_right = back(
+        ((3, 0, share), (1, 0, size)), [(other1, 0, 1), (l1, 0, 1), (r1, 0, 1)],
+        [ready, wide, wide], prior=dq, after=(far, near),
+    )
+    near = add(part_left, given[:size], along(near, 1))
+    far = add(part_right, given[size:], along(far, 0))
+    given = across(part)
+    grad_queries, mine, grad_resp_keys, grad_resp_values = back(
+        ((0, 0, share + resp),), [(packed, 0, 1)], [wide, grads, grads], prior=dq,
+        after=(far, near), last=(own_rows,),
+    )
+    near, far = along(near, 0), along(far, 1)
+    total = [
+        mine[at : at + share] + sum(r[at : at + share].astype(F32) for r in (given, near, far))
+        for at in (0, share)
+    ]
+    return grad_queries, grad_resp_keys, grad_resp_values, *total
 
 
 def solution(mesh):

time: 70 us -> 67.3 us (0.961)
  local copies, waits for them, and re-layouts: 3.8 us -> 0.88 us
  starting transfers between devices: 27.1 us -> 29.6 us
  waiting for transfers between devices: 13 us -> 10.8 us
  other arithmetic: 1.76 us -> 3.07 us
  Pallas kernels: 21.2 us -> 20.4 us
    unnamed x11 -> x4, local copies, waits for them, and re-layouts: 3.77 us -> 0.86 us
    ppermute x16 -> x23, starting transfers between devices: 27.1 us -> 29.6 us  [the longest x14 18.9 us: along(): return lax.ppermute(block, 'sample', pairs)]
    ppermute x16 -> x23, waiting for transfers between devices: 13 us -> 10.8 us  [the longest x14 8.81 us: along(): return lax.ppermute(block, 'sample', pairs)]
    concatenate x0 -> x4, other arithmetic: none -> 1.33 us  [the longest x1 1.3 us: shards(): wide_rows = jnp.concatenate([queries, grad_out], axis=0)]
    pallas_call x12 -> x19, Pallas kernels: 21.2 us -> 20.4 us  [the longest x6 11 us: backward_grads(): pl.pallas_call(functools.partial(backward_kernel, heads, share, owners, p...]
  transfers between devices with their start and end apart: 16 -> 23, of which waited for: 11 -> 10; matrix products, arithmetic and copies ran while one was open for 0% -> 4% of each run, Pallas kernels for 28% -> 29%
where the time goes in v5:
time: 67.3 us; the launch traced here: 66.9 us
  starting transfers between devices  29.6 us (44%)
  Pallas kernels  20.4 us (30%)
  waiting for transfers between devices  10.8 us (16%)
  other arithmetic  3.07 us (5%)
  between operations  2.18 us (3%)
  local copies, waits for them, and re-layouts  0.88 us (1%)
    ppermute x14, starting transfers between devices, along(): return lax.ppermute(block, 'sample', pairs)  18.9 us
    pallas_call x6, Pallas kernels, backward_grads(): pl.pallas_call(functools.partial(backward_kernel, heads, share, owners, p...  11 us
    ppermute x9, starting transfers between devices, across(): return lax.ppermute(block, 'sample', pairs)  10.7 us
    pallas_call x7, Pallas kernels, forward_stats(): pl.pallas_call(functools.partial(forward_kernel, heads, share, picks, boo...  9.44 us
    ppermute x14, waiting for transfers between devices, along(): return lax.ppermute(block, 'sample', pairs)  8.81 us
    ppermute x9, waiting for transfers between devices, across(): return lax.ppermute(block, 'sample', pairs)  1.95 us
  transfers between devices with their start and end apart: 23, of which 10 were waited for; matrix products, arithmetic and copies ran while one was open for 4% of the time, Pallas kernels for 29%

profile of v5, /device:TPU:2, one launch (start us, length us, event | category | flops | bytes accessed | tf_op | source)
XLA Modules:
  0.0 66.9 jit_solution(14002197052094843398)
XLA Ops:
  1.3 0.9 %maximum_maximum_fusion.refs_3_.refs_12_ = bf16[272,128]{1,0:T(8,128)(2,1)S(1)} fusion(bf16[128,128]{1,0:T(8,128)(2,1)} %param.12, bf16[128,128]{1,0:T(8,128)(2,1)} %param.11, bf16[272]{0:T(512)(128)(2,1)S(1)} %pad.9.clone), kind=kLoop, calls=%fused_computation.11 | loop fusion | flops 208896 | bytes 135712 | tf_op jit(solution)/shard_map/concatenate | solution.py:294
  2.2 2.0 %collective-permute-start = (bf16[272,128]{1,0:T(8,128)(2,1)S(1)}, bf16[272,128]{1,0:T(8,128)(2,1)S(1)}, u32[]{:S(2)}, u32[]{:S(2)}) collective-permute-start(bf16[272,128]{1,0:T(8,128)(2,1)S(1)} %maximum_maximum_fusion.refs_3_.refs_12_), channel_id=1, source_target_pairs={{0,1},{1,0},{2,3},{3,2},{4,5},{5,4},{6,7},{7,6},{8,9},{9,8},{10,11... | collective-permute-start | bytes 208904 | tf_op jit(solution)/shard_map/ppermute | solution.py:284
  4.2 4.9 %collective-permute-start.1 = (bf16[272,128]{1,0:T(8,128)(2,1)S(1)}, bf16[272,128]{1,0:T(8,128)(2,1)S(1)}, u32[]{:S(2)}, u32[]{:S(2)}) collective-permute-start(bf16[272,128]{1,0:T(8,128)(2,1)S(1)} %maximum_maximum_fusion.refs_3_.refs_12_), channel_id=1, source_target_pairs={{0,7},{1,2},{2,1},{3,4},{4,3},{5,6},{6,5},{7,0},{8,15},{9,10},{10,... | collective-permute-start | bytes 208904 | tf_op jit(solution)/shard_map/ppermute | solution.py:284
  9.8 0.8 %constant_dynamic-update-slice_fusion.1 = bf16[2,256,128]{2,1,0:T(8,128)(2,1)S(1)} fusion(bf16[1,256,128]{2,1,0:T(8,128)(2,1)} %param.9), kind=kLoop, calls=%fused_computation.15 | loop fusion | bytes 131072
  10.7 1.3 %pad_maximum_fusion.refs_1_ = bf16[2,256,1024]{2,1,0:T(8,128)(2,1)S(1)} fusion(bf16[1,256,1024]{2,1,0:T(8,128)(2,1)} %param.13, bf16[1,256,1024]{2,1,0:T(8,128)(2,1)} %param.8), kind=kLoop, calls=%fused_computation | loop fusion | flops 524288 | bytes 2097152 | tf_op jit(solution)/shard_map/concatenate | solution.py:296
  12.0 1.5 %forward_stats.7 = (f32[32,256]{1,0:T(8,128)S(1)}, bf16[384,2048]{1,0:T(8,128)(2,1)S(1)}, f32[384,2048]{1,0:T(8,128)S(1)}, bf16[2048,128]{1,0:T(8,128)(2,1)S(1)}, bf16[2048,128]{1,0:T(8,128)(2,1)S(1)}) custom-call(s32[1]{0:T(128)S(6)} %copy.26.refs_0_, bf16[2,256,1024]{2,1,0:T(8,128)(2,1)S(1)} %pad_maximum_fusion.refs_1_, ...), custom_call_target="tpu_custom_call" | custom-call | flops 1207959552 | bytes 1048576 | tf_op jit(solution)/shard_map/forward_stats/pallas_call | solution.py:211
  13.6 1.7 %collective-permute-start.4 = (bf16[816,128]{1,0:T(8,128)(2,1)S(1)}, bf16[816,128]{1,0:T(8,128)(2,1)S(1)}, u32[]{:S(2)}, u32[]{:S(2)}) collective-permute-start(bf16[816,128]{1,0:T(8,128)(2,1)S(1)} %pad_maximum_fusion.1), channel_id=1, source_target_pairs={{0,8},{1,9},{2,10},{3,11},{4,12},{5,13},{6,14},{7,15},{8,0},{9,1},... | collective-permute-start | bytes 626696 | tf_op jit(solution)/shard_map/ppermute | solution.py:275
  15.3 2.0 %collective-permute-start.3 = (bf16[272,128]{1,0:T(8,128)(2,1)S(1)}, bf16[272,128]{1,0:T(8,128)(2,1)S(1)}, u32[]{:S(2)}, u32[]{:S(2)}) collective-permute-start(bf16[272,128]{1,0:T(8,128)(2,1)S(1)} %collective-permute-done.refs_2_.refs_15_), channel_id=1, source_target_pairs={{0,7},{1,2},{2,1},{3,4},{4,3},{5,6},{6,5},{7,0},{8,15},{9,10},{10,... | collective-permute-start | bytes 208904 | tf_op jit(solution)/shard_map/ppermute | solution.py:284
  17.3 1.0 %forward_stats.8 = (f32[32,256]{1,0:T(8,128)S(1)}, bf16[256,2048]{1,0:T(8,128)(2,1)S(1)}, f32[256,2048]{1,0:T(8,128)S(1)}) custom-call(bf16[2048,128]{1,0:T(8,128)(2,1)S(1)} %get-tuple-element.49.refs_0_.refs_1_, bf16[2048,128]{1,0:T(8,128)(2,1)S(1)} %get-tuple-element.50.refs_1_.refs_2_, bf16[272,128]{1,0:T(8,128)(2,1)S(1)} %collective-permute-done.refs_2_.refs_15_, ...), custom_call_target="tpu_custom_call" | custom-call | flops 805306368 | bytes 1048576 | tf_op jit(solution)/shard_map/forward_stats/pallas_call | solution.py:211
  18.3 2.5 %collective-permute-done.3.block_ref = bf16[272,128]{1,0:T(8,128)(2,1)S(1)} collective-permute-done((bf16[272,128]{1,0:T(8,128)(2,1)S(1)}, bf16[272,128]{1,0:T(8,128)(2,1)S(1)}, u32[]{:S(2)}, u32[]{:S(2)}) %collective-permute-start.3) | collective-permute-done | bytes 69664 | tf_op jit(solution)/shard_map/ppermute | solution.py:284
  21.6 1.3 %collective-permute-start.6 = (bf16[272,128]{1,0:T(8,128)(2,1)S(1)}, bf16[272,128]{1,0:T(8,128)(2,1)S(1)}, u32[]{:S(2)}, u32[]{:S(2)}) collective-permute-start(bf16[272,128]{1,0:T(8,128)(2,1)S(1)} %tie.6.refs_2_.refs_15_), channel_id=1, source_target_pairs={{0,7},{1,2},{2,1},{3,4},{4,3},{5,6},{6,5},{7,0},{8,15},{9,10},{10,... | collective-permute-start | bytes 208904 | tf_op jit(solution)/shard_map/ppermute | solution.py:284
  23.5 1.0 %forward_stats.9 = (f32[32,256]{1,0:T(8,128)S(1)}, bf16[256,2048]{1,0:T(8,128)(2,1)S(1)}, f32[256,2048]{1,0:T(8,128)S(1)}) custom-call(bf16[2048,128]{1,0:T(8,128)(2,1)S(1)} %get-tuple-element.49.refs_0_.refs_1_, bf16[2048,128]{1,0:T(8,128)(2,1)S(1)} %get-tuple-element.50.refs_1_.refs_2_, bf16[272,128]{1,0:T(8,128)(2,1)S(1)} %tie.6.refs_2_.refs_15_, ...), custom_call_target="tpu_custom_call" | custom-call | flops 805306368 | bytes 1048576 | tf_op jit(solution)/shard_map/forward_stats/pallas_call | solution.py:211
  24.4 2.7 %collective-permute-done.6.block_ref = bf16[272,128]{1,0:T(8,128)(2,1)S(1)} collective-permute-done((bf16[272,128]{1,0:T(8,128)(2,1)S(1)}, bf16[272,128]{1,0:T(8,128)(2,1)S(1)}, u32[]{:S(2)}, u32[]{:S(2)}) %collective-permute-start.6) | collective-permute-done | bytes 69664 | tf_op jit(solution)/shard_map/ppermute | solution.py:284
  27.7 2.9 %forward_stats.10 = (f32[32,256]{1,0:T(8,128)S(1)}, bf16[640,2048]{1,0:T(8,128)(2,1)S(1)}, f32[640,2048]{1,0:T(8,128)S(1)}) custom-call(bf16[2048,128]{1,0:T(8,128)(2,1)S(1)} %get-tuple-element.49.refs_0_.refs_1_, bf16[2048,128]{1,0:T(8,128)(2,1)S(1)} %get-tuple-element.50.refs_1_.refs_2_, bf16[816,128]{1,0:T(8,128)(2,1)S(1)} %collective-permute-done.4.refs_2_.refs_14_, ...), custom_call_target="tpu_custom_call" | custom-call | flops 2013265920 | bytes 1048576 | tf_op jit(solution)/shard_map/forward_stats/pallas_call | solution.py:211
  31.4 1.0 %collective-permute-start.10 = (bf16[272,128]{1,0:T(8,128)(2,1)S(1)}, bf16[272,128]{1,0:T(8,128)(2,1)S(1)}, u32[]{:S(2)}, u32[]{:S(2)}) collective-permute-start(bf16[272,128]{1,0:T(8,128)(2,1)S(1)} %tie.11.refs_3_.refs_15_), channel_id=1, source_target_pairs={{0,8},{1,9},{2,10},{3,11},{4,12},{5,13},{6,14},{7,15},{8,0},{9,1},... | collective-permute-start | bytes 208904 | tf_op jit(solution)/shard_map/ppermute | solution.py:275
  32.5 1.5 %forward_stats.11 = (f32[32,256]{1,0:T(8,128)S(1)}, bf16[384,2048]{1,0:T(8,128)(2,1)S(1)}, f32[384,2048]{1,0:T(8,128)S(1)}) custom-call(bf16[2048,128]{1,0:T(8,128)(2,1)S(1)} %get-tuple-element.49.refs_0_.refs_1_, bf16[2048,128]{1,0:T(8,128)(2,1)S(1)} %get-tuple-element.50.refs_1_.refs_2_, bf16[544,128]{1,0:T(8,128)(2,1)S(1)} %collective-permute-done.7.refs_2_.refs_14_, ...), custom_call_target="tpu_custom_call" | custom-call | flops 1207959552 | bytes 1048576 | tf_op jit(solution)/shard_map/forward_stats/pallas_call | solution.py:211
  34.0 1.0 %forward_stats.12 = (f32[32,256]{1,0:T(8,128)S(1)}, bf16[256,2048]{1,0:T(8,128)(2,1)S(1)}, f32[256,2048]{1,0:T(8,128)S(1)}) custom-call(bf16[2048,128]{1,0:T(8,128)(2,1)S(1)} %get-tuple-element.49.refs_0_.refs_1_, bf16[2048,128]{1,0:T(8,128)(2,1)S(1)} %get-tuple-element.50.refs_1_.refs_2_, bf16[544,128]{1,0:T(8,128)(2,1)S(1)} %collective-permute-done.9.refs_2_.refs_14_), custom_call_target="tpu_custom_call" | custom-call | flops 805306368 | bytes 1048576 | tf_op jit(solution)/shard_map/forward_stats/pallas_call | solution.py:211
  35.0 1.5 %collective-permute-done.10.refs_2_.refs_12_ = bf16[272,128]{1,0:T(8,128)(2,1)S(1)} collective-permute-done((bf16[272,128]{1,0:T(8,128)(2,1)S(1)}, bf16[272,128]{1,0:T(8,128)(2,1)S(1)}, u32[]{:S(2)}, u32[]{:S(2)}) %collective-permute-start.10) | collective-permute-done | bytes 69664 | tf_op jit(solution)/shard_map/ppermute | solution.py:275
  38.2 1.7 %backward_grads.7 = (f32[1024,256]{1,0:T(8,128)S(1)}, bf16[512,128]{1,0:T(8,128)(2,1)S(1)}, f32[256,128]{1,0:T(8,128)S(1)}) custom-call(s32[1]{0:T(128)S(6)} %copy.27.refs_0_, bf16[2048,128]{1,0:T(8,128)(2,1)S(1)} %get-tuple-element.49.refs_0_.refs_1_, bf16[2048,128]{1,0:T(8,128)(2,1)S(1)} %get-tuple-element.50.refs_1_.refs_2_, ...), custom_call_target="tpu_custom_call" | custom-call | flops 2013265920 | bytes 2097152 | tf_op jit(solution)/shard_map/backward_grads/pallas_call | solution.py:240
  39.9 1.6 %collective-permute-start.12 = (bf16[512,128]{1,0:T(8,128)(2,1)S(1)}, bf16[512,128]{1,0:T(8,128)(2,1)S(1)}, u32[]{:S(2)}, u32[]{:S(2)}) collective-permute-start(bf16[512,128]{1,0:T(8,128)(2,1)S(1)} %get-tuple-element.78), channel_id=1, source_target_pairs={{0,8},{1,9},{2,10},{3,11},{4,12},{5,13},{6,14},{7,15},{8,0},{9,1},... | collective-permute-start | bytes 393224 | tf_op jit(solution)/shard_map/ppermute | solution.py:275
  42.1 2.0 %collective-permute-start.13 = (bf16[256,128]{1,0:T(8,128)(2,1)S(1)}, bf16[256,128]{1,0:T(8,128)(2,1)S(1)}, u32[]{:S(2)}, u32[]{:S(2)}) collective-permute-start(bf16[256,128]{1,0:T(8,128)(2,1)S(1)} %add_convert_fusion.6.refs_18_), channel_id=1, source_target_pairs={{0,1},{1,0},{2,3},{3,2},{4,5},{5,4},{6,7},{7,6},{8,9},{9,8},{10,11... | collective-permute-start | bytes 196616 | tf_op jit(solution)/shard_map/ppermute | solution.py:284
  44.0 2.2 %backward_grads.8 = (f32[1024,256]{1,0:T(8,128)S(1)}, bf16[512,128]{1,0:T(8,128)(2,1)S(1)}, f32[256,128]{1,0:T(8,128)S(1)}, f32[256,128]{1,0:T(8,128)S(1)}) custom-call(s32[1]{0:T(128)S(6)} %copy.27.refs_0_, bf16[2048,128]{1,0:T(8,128)(2,1)S(1)} %get-tuple-element.49.refs_0_.refs_1_, bf16[2048,128]{1,0:T(8,128)(2,1)S(1)} %get-tuple-element.50.refs_1_.refs_2_, ...), custom_call_target="tpu_custom_call" | custom-call | flops 2684354560 | bytes 2097152 | tf_op jit(solution)/shard_map/backward_grads/pallas_call | solution.py:240
  46.2 1.7 %collective-permute-start.14 = (bf16[512,128]{1,0:T(8,128)(2,1)S(1)}, bf16[512,128]{1,0:T(8,128)(2,1)S(1)}, u32[]{:S(2)}, u32[]{:S(2)}) collective-permute-start(bf16[512,128]{1,0:T(8,128)(2,1)S(1)} %get-tuple-element.82), channel_id=1, source_target_pairs={{0,8},{1,9},{2,10},{3,11},{4,12},{5,13},{6,14},{7,15},{8,0},{9,1},... | collective-permute-start | bytes 393224 | tf_op jit(solution)/shard_map/ppermute | solution.py:275
  48.4 1.5 %collective-permute-start.15 = (bf16[256,128]{1,0:T(8,128)(2,1)S(1)}, bf16[256,128]{1,0:T(8,128)(2,1)S(1)}, u32[]{:S(2)}, u32[]{:S(2)}) collective-permute-start(bf16[256,128]{1,0:T(8,128)(2,1)S(1)} %get-tuple-element.100.refs_18_), channel_id=1, source_target_pairs={{0,7},{1,2},{2,1},{3,4},{4,3},{5,6},{6,5},{7,0},{8,15},{9,10},{10,... | collective-permute-start | bytes 196616 | tf_op jit(solution)/shard_map/ppermute | solution.py:284
  49.9 2.1 %backward_grads.9 = (f32[1024,256]{1,0:T(8,128)S(1)}, bf16[512,128]{1,0:T(8,128)(2,1)S(1)}, f32[256,128]{1,0:T(8,128)S(1)}, f32[256,128]{1,0:T(8,128)S(1)}) custom-call(s32[1]{0:T(128)S(6)} %copy.27.refs_0_, bf16[2048,128]{1,0:T(8,128)(2,1)S(1)} %get-tuple-element.49.refs_0_.refs_1_, bf16[2048,128]{1,0:T(8,128)(2,1)S(1)} %get-tuple-element.50.refs_1_.refs_2_, ...), custom_call_target="tpu_custom_call" | custom-call | flops 2684354560 | bytes 2097152 | tf_op jit(solution)/shard_map/backward_grads/pallas_call | solution.py:240
  52.0 1.6 %collective-permute-start.17 = (bf16[512,128]{1,0:T(8,128)(2,1)S(1)}, bf16[512,128]{1,0:T(8,128)(2,1)S(1)}, u32[]{:S(2)}, u32[]{:S(2)}) collective-permute-start(bf16[512,128]{1,0:T(8,128)(2,1)S(1)} %get-tuple-element.86), channel_id=1, source_target_pairs={{0,8},{1,9},{2,10},{3,11},{4,12},{5,13},{6,14},{7,15},{8,0},{9,1},... | collective-permute-start | bytes 393224 | tf_op jit(solution)/shard_map/ppermute | solution.py:275
  54.0 2.0 %collective-permute-start.19 = (bf16[256,128]{1,0:T(8,128)(2,1)S(1)}, bf16[256,128]{1,0:T(8,128)(2,1)S(1)}, u32[]{:S(2)}, u32[]{:S(2)}) collective-permute-start(bf16[256,128]{1,0:T(8,128)(2,1)S(1)} %get-tuple-element.97.refs_19_), channel_id=1, source_target_pairs={{0,7},{1,2},{2,1},{3,4},{4,3},{5,6},{6,5},{7,0},{8,15},{9,10},{10,... | collective-permute-start | bytes 196616 | tf_op jit(solution)/shard_map/ppermute | solution.py:284
  55.9 1.7 %backward_grads.10 = (f32[1024,256]{1,0:T(8,128)S(1)}, bf16[256,128]{1,0:T(8,128)(2,1)S(1)}, f32[256,128]{1,0:T(8,128)S(1)}, f32[256,128]{1,0:T(8,128)S(1)}) custom-call(s32[1]{0:T(128)S(6)} %copy.27.refs_0_, bf16[2048,128]{1,0:T(8,128)(2,1)S(1)} %get-tuple-element.49.refs_0_.refs_1_, bf16[2048,128]{1,0:T(8,128)(2,1)S(1)} %get-tuple-element.50.refs_1_.refs_2_, ...), custom_call_target="tpu_custom_call" | custom-call | flops 2013265920 | bytes 2097152 | tf_op jit(solution)/shard_map/backward_grads/pallas_call | solution.py:240
  57.6 1.4 %collective-permute-start.20 = (bf16[256,128]{1,0:T(8,128)(2,1)S(1)}, bf16[256,128]{1,0:T(8,128)(2,1)S(1)}, u32[]{:S(2)}, u32[]{:S(2)}) collective-permute-start(bf16[256,128]{1,0:T(8,128)(2,1)S(1)} %get-tuple-element.92), channel_id=1, source_target_pairs={{0,8},{1,9},{2,10},{3,11},{4,12},{5,13},{6,14},{7,15},{8,0},{9,1},... | collective-permute-start | bytes 196616 | tf_op jit(solution)/shard_map/ppermute | solution.py:275
  60.3 1.7 %collective-permute-start.22 = (bf16[256,128]{1,0:T(8,128)(2,1)S(1)}, bf16[256,128]{1,0:T(8,128)(2,1)S(1)}, u32[]{:S(2)}, u32[]{:S(2)}) collective-permute-start(bf16[256,128]{1,0:T(8,128)(2,1)S(1)} %get-tuple-element.96.refs_15_), channel_id=1, source_target_pairs={{0,7},{1,2},{2,1},{3,4},{4,3},{5,6},{6,5},{7,0},{8,15},{9,10},{10,... | collective-permute-start | bytes 196616 | tf_op jit(solution)/shard_map/ppermute | solution.py:284
  62.2 2.7 %backward_grads.11 = (f32[1,256,1024]{2,1,0:T(8,128)}, f32[256,128]{1,0:T(8,128)S(1)}, f32[1,256,128]{2,1,0:T(8,128)}, f32[1,256,128]{2,1,0:T(8,128)}) custom-call(s32[1]{0:T(128)S(6)} %copy.27.refs_0_, bf16[2048,128]{1,0:T(8,128)(2,1)S(1)} %get-tuple-element.49.refs_0_.refs_1_, bf16[2048,128]{1,0:T(8,128)(2,1)S(1)} %get-tuple-element.50.refs_1_.refs_2_, ...), custom_call_target="tpu_custom_call" | custom-call | flops 2013265920 | bytes 2097152 | tf_op jit(solution)/shard_map/backward_grads/pallas_call | solution.py:240
  64.9 0.9 %collective-permute-done.22 = bf16[256,128]{1,0:T(8,128)(2,1)S(1)} collective-permute-done((bf16[256,128]{1,0:T(8,128)(2,1)S(1)}, bf16[256,128]{1,0:T(8,128)(2,1)S(1)}, u32[]{:S(2)}, u32[]{:S(2)}) %collective-permute-start.22) | collective-permute-done | bytes 65568 | tf_op jit(solution)/shard_map/ppermute | solution.py:284
  (50 shorter events, 8.5 us)
Async XLA Ops:
  0.6 11.4 %copy-start = (bf16[1,256,128]{2,1,0:T(8,128)(2,1)S(1)}, bf16[1,256,128]{2,1,0:T(8,128)(2,1)}, u32[]{:S(2)}) copy-start(bf16[1,256,128]{2,1,0:T(8,128)(2,1)} %param.10) | copy-start | bytes 196612
  2.2 11.3 %collective-permute-start = (bf16[272,128]{1,0:T(8,128)(2,1)S(1)}, bf16[272,128]{1,0:T(8,128)(2,1)S(1)}, u32[]{:S(2)}, u32[]{:S(2)}) collective-permute-start(bf16[272,128]{1,0:T(8,128)(2,1)S(1)} %maximum_maximum_fusion.refs_3_.refs_12_), channel_id=1, source_target_pairs={{0,1},{1,0},{2,3},{3,2},{4,5},{5,4},{6,7},{7,6},{8,9},{9,8},{10,11... | collective-permute-start | bytes 208904 | tf_op jit(solution)/shard_map/ppermute | solution.py:284
  4.2 9.3 %collective-permute-start.1 = (bf16[272,128]{1,0:T(8,128)(2,1)S(1)}, bf16[272,128]{1,0:T(8,128)(2,1)S(1)}, u32[]{:S(2)}, u32[]{:S(2)}) collective-permute-start(bf16[272,128]{1,0:T(8,128)(2,1)S(1)} %maximum_maximum_fusion.refs_3_.refs_12_), channel_id=1, source_target_pairs={{0,7},{1,2},{2,1},{3,4},{4,3},{5,6},{6,5},{7,0},{8,15},{9,10},{10,... | collective-permute-start | bytes 208904 | tf_op jit(solution)/shard_map/ppermute | solution.py:284
  13.6 14.1 %collective-permute-start.4 = (bf16[816,128]{1,0:T(8,128)(2,1)S(1)}, bf16[816,128]{1,0:T(8,128)(2,1)S(1)}, u32[]{:S(2)}, u32[]{:S(2)}) collective-permute-start(bf16[816,128]{1,0:T(8,128)(2,1)S(1)} %pad_maximum_fusion.1), channel_id=1, source_target_pairs={{0,8},{1,9},{2,10},{3,11},{4,12},{5,13},{6,14},{7,15},{8,0},{9,1},... | collective-permute-start | bytes 626696 | tf_op jit(solution)/shard_map/ppermute | solution.py:275
  15.3 6.3 %collective-permute-start.2 = (bf16[272,128]{1,0:T(8,128)(2,1)S(1)}, bf16[272,128]{1,0:T(8,128)(2,1)S(1)}, u32[]{:S(2)}, u32[]{:S(2)}) collective-permute-start(bf16[272,128]{1,0:T(8,128)(2,1)S(1)} %collective-permute-done.1.refs_3_.refs_16_), channel_id=1, source_target_pairs={{0,1},{1,0},{2,3},{3,2},{4,5},{5,4},{6,7},{7,6},{8,9},{9,8},{10,11... | collective-permute-start | bytes 208904 | tf_op jit(solution)/shard_map/ppermute | solution.py:284
  15.3 5.5 %collective-permute-start.3 = (bf16[272,128]{1,0:T(8,128)(2,1)S(1)}, bf16[272,128]{1,0:T(8,128)(2,1)S(1)}, u32[]{:S(2)}, u32[]{:S(2)}) collective-permute-start(bf16[272,128]{1,0:T(8,128)(2,1)S(1)} %collective-permute-done.refs_2_.refs_15_), channel_id=1, source_target_pairs={{0,7},{1,2},{2,1},{3,4},{4,3},{5,6},{6,5},{7,0},{8,15},{9,10},{10,... | collective-permute-start | bytes 208904 | tf_op jit(solution)/shard_map/ppermute | solution.py:284
  20.8 6.3 %collective-permute-start.5 = (bf16[272,128]{1,0:T(8,128)(2,1)S(1)}, bf16[272,128]{1,0:T(8,128)(2,1)S(1)}, u32[]{:S(2)}, u32[]{:S(2)}) collective-permute-start(bf16[272,128]{1,0:T(8,128)(2,1)S(1)} %tie.7.refs_3_.refs_16_), channel_id=1, source_target_pairs={{0,1},{1,0},{2,3},{3,2},{4,5},{5,4},{6,7},{7,6},{8,9},{9,8},{10,11... | collective-permute-start | bytes 208904 | tf_op jit(solution)/shard_map/ppermute | solution.py:284
  21.6 5.5 %collective-permute-start.6 = (bf16[272,128]{1,0:T(8,128)(2,1)S(1)}, bf16[272,128]{1,0:T(8,128)(2,1)S(1)}, u32[]{:S(2)}, u32[]{:S(2)}) collective-permute-start(bf16[272,128]{1,0:T(8,128)(2,1)S(1)} %tie.6.refs_2_.refs_15_), channel_id=1, source_target_pairs={{0,7},{1,2},{2,1},{3,4},{4,3},{5,6},{6,5},{7,0},{8,15},{9,10},{10,... | collective-permute-start | bytes 208904 | tf_op jit(solution)/shard_map/ppermute | solution.py:284
  22.9 9.6 %collective-permute-start.7 = (bf16[544,128]{1,0:T(8,128)(2,1)S(1)}, bf16[544,128]{1,0:T(8,128)(2,1)S(1)}, u32[]{:S(2)}, u32[]{:S(2)}) collective-permute-start(bf16[544,128]{1,0:T(8,128)(2,1)S(1)} %pad_maximum_fusion.2), channel_id=1, source_target_pairs={{0,8},{1,9},{2,10},{3,11},{4,12},{5,13},{6,14},{7,15},{8,0},{9,1},... | collective-permute-start | bytes 417800 | tf_op jit(solution)/shard_map/ppermute | solution.py:275
  27.1 4.3 %collective-permute-start.8 = (bf16[272,128]{1,0:T(8,128)(2,1)S(1)}, bf16[272,128]{1,0:T(8,128)(2,1)S(1)}, u32[]{:S(2)}, u32[]{:S(2)}) collective-permute-start(bf16[272,128]{1,0:T(8,128)(2,1)S(1)} %tie.10.refs_4_.refs_16_), channel_id=1, source_target_pairs={{0,1},{1,0},{2,3},{3,2},{4,5},{5,4},{6,7},{7,6},{8,9},{9,8},{10,11... | collective-permute-start | bytes 208904 | tf_op jit(solution)/shard_map/ppermute | solution.py:284
  27.2 6.8 %collective-permute-start.9 = (bf16[544,128]{1,0:T(8,128)(2,1)S(1)}, bf16[544,128]{1,0:T(8,128)(2,1)S(1)}, u32[]{:S(2)}, u32[]{:S(2)}) collective-permute-start(bf16[544,128]{1,0:T(8,128)(2,1)S(1)} %pad_maximum_fusion.3), channel_id=1, source_target_pairs={{0,8},{1,9},{2,10},{3,11},{4,12},{5,13},{6,14},{7,15},{8,0},{9,1},... | collective-permute-start | bytes 417800 | tf_op jit(solution)/shard_map/ppermute | solution.py:275
  31.4 5.0 %collective-permute-start.10 = (bf16[272,128]{1,0:T(8,128)(2,1)S(1)}, bf16[272,128]{1,0:T(8,128)(2,1)S(1)}, u32[]{:S(2)}, u32[]{:S(2)}) collective-permute-start(bf16[272,128]{1,0:T(8,128)(2,1)S(1)} %tie.11.refs_3_.refs_15_), channel_id=1, source_target_pairs={{0,8},{1,9},{2,10},{3,11},{4,12},{5,13},{6,14},{7,15},{8,0},{9,1},... | collective-permute-start | bytes 208904 | tf_op jit(solution)/shard_map/ppermute | solution.py:275
  37.7 4.4 %collective-permute-start.11 = (bf16[256,128]{1,0:T(8,128)(2,1)S(1)}, bf16[256,128]{1,0:T(8,128)(2,1)S(1)}, u32[]{:S(2)}, u32[]{:S(2)}) collective-permute-start(bf16[256,128]{1,0:T(8,128)(2,1)S(1)} %get-tuple-element.75), channel_id=1, source_target_pairs={{0,8},{1,9},{2,10},{3,11},{4,12},{5,13},{6,14},{7,15},{8,0},{9,1},... | collective-permute-start | bytes 196616 | tf_op jit(solution)/shard_map/ppermute | solution.py:275
  39.9 8.0 %collective-permute-start.12 = (bf16[512,128]{1,0:T(8,128)(2,1)S(1)}, bf16[512,128]{1,0:T(8,128)(2,1)S(1)}, u32[]{:S(2)}, u32[]{:S(2)}) collective-permute-start(bf16[512,128]{1,0:T(8,128)(2,1)S(1)} %get-tuple-element.78), channel_id=1, source_target_pairs={{0,8},{1,9},{2,10},{3,11},{4,12},{5,13},{6,14},{7,15},{8,0},{9,1},... | collective-permute-start | bytes 393224 | tf_op jit(solution)/shard_map/ppermute | solution.py:275
  42.1 5.9 %collective-permute-start.13 = (bf16[256,128]{1,0:T(8,128)(2,1)S(1)}, bf16[256,128]{1,0:T(8,128)(2,1)S(1)}, u32[]{:S(2)}, u32[]{:S(2)}) collective-permute-start(bf16[256,128]{1,0:T(8,128)(2,1)S(1)} %add_convert_fusion.6.refs_18_), channel_id=1, source_target_pairs={{0,1},{1,0},{2,3},{3,2},{4,5},{5,4},{6,7},{7,6},{8,9},{9,8},{10,11... | collective-permute-start | bytes 196616 | tf_op jit(solution)/shard_map/ppermute | solution.py:284
  46.2 7.5 %collective-permute-start.14 = (bf16[512,128]{1,0:T(8,128)(2,1)S(1)}, bf16[512,128]{1,0:T(8,128)(2,1)S(1)}, u32[]{:S(2)}, u32[]{:S(2)}) collective-permute-start(bf16[512,128]{1,0:T(8,128)(2,1)S(1)} %get-tuple-element.82), channel_id=1, source_target_pairs={{0,8},{1,9},{2,10},{3,11},{4,12},{5,13},{6,14},{7,15},{8,0},{9,1},... | collective-permute-start | bytes 393224 | tf_op jit(solution)/shard_map/ppermute | solution.py:275
  48.0 5.7 %collective-permute-start.16 = (bf16[256,128]{1,0:T(8,128)(2,1)S(1)}, bf16[256,128]{1,0:T(8,128)(2,1)S(1)}, u32[]{:S(2)}, u32[]{:S(2)}) collective-permute-start(bf16[256,128]{1,0:T(8,128)(2,1)S(1)} %get-tuple-element.99.refs_19_), channel_id=1, source_target_pairs={{0,1},{1,0},{2,3},{3,2},{4,5},{5,4},{6,7},{7,6},{8,9},{9,8},{10,11... | collective-permute-start | bytes 196616 | tf_op jit(solution)/shard_map/ppermute | solution.py:284
  48.4 5.5 %collective-permute-start.15 = (bf16[256,128]{1,0:T(8,128)(2,1)S(1)}, bf16[256,128]{1,0:T(8,128)(2,1)S(1)}, u32[]{:S(2)}, u32[]{:S(2)}) collective-permute-start(bf16[256,128]{1,0:T(8,128)(2,1)S(1)} %get-tuple-element.100.refs_18_), channel_id=1, source_target_pairs={{0,7},{1,2},{2,1},{3,4},{4,3},{5,6},{6,5},{7,0},{8,15},{9,10},{10,... | collective-permute-start | bytes 196616 | tf_op jit(solution)/shard_map/ppermute | solution.py:284
  52.0 8.2 %collective-permute-start.17 = (bf16[512,128]{1,0:T(8,128)(2,1)S(1)}, bf16[512,128]{1,0:T(8,128)(2,1)S(1)}, u32[]{:S(2)}, u32[]{:S(2)}) collective-permute-start(bf16[512,128]{1,0:T(8,128)(2,1)S(1)} %get-tuple-element.86), channel_id=1, source_target_pairs={{0,8},{1,9},{2,10},{3,11},{4,12},{5,13},{6,14},{7,15},{8,0},{9,1},... | collective-permute-start | bytes 393224 | tf_op jit(solution)/shard_map/ppermute | solution.py:275
  54.0 5.8 %collective-permute-start.19 = (bf16[256,128]{1,0:T(8,128)(2,1)S(1)}, bf16[256,128]{1,0:T(8,128)(2,1)S(1)}, u32[]{:S(2)}, u32[]{:S(2)}) collective-permute-start(bf16[256,128]{1,0:T(8,128)(2,1)S(1)} %get-tuple-element.97.refs_19_), channel_id=1, source_target_pairs={{0,7},{1,2},{2,1},{3,4},{4,3},{5,6},{6,5},{7,0},{8,15},{9,10},{10,... | collective-permute-start | bytes 196616 | tf_op jit(solution)/shard_map/ppermute | solution.py:284
  55.9 4.3 %collective-permute-start.18 = (bf16[256,128]{1,0:T(8,128)(2,1)S(1)}, bf16[256,128]{1,0:T(8,128)(2,1)S(1)}, u32[]{:S(2)}, u32[]{:S(2)}) collective-permute-start(bf16[256,128]{1,0:T(8,128)(2,1)S(1)} %get-tuple-element.98.refs_18_), channel_id=1, source_target_pairs={{0,1},{1,0},{2,3},{3,2},{4,5},{5,4},{6,7},{7,6},{8,9},{9,8},{10,11... | collective-permute-start | bytes 196616 | tf_op jit(solution)/shard_map/ppermute | solution.py:284
  57.6 7.3 %collective-permute-start.20 = (bf16[256,128]{1,0:T(8,128)(2,1)S(1)}, bf16[256,128]{1,0:T(8,128)(2,1)S(1)}, u32[]{:S(2)}, u32[]{:S(2)}) collective-permute-start(bf16[256,128]{1,0:T(8,128)(2,1)S(1)} %get-tuple-element.92), channel_id=1, source_target_pairs={{0,8},{1,9},{2,10},{3,11},{4,12},{5,13},{6,14},{7,15},{8,0},{9,1},... | collective-permute-start | bytes 196616 | tf_op jit(solution)/shard_map/ppermute | solution.py:275
  60.3 5.6 %collective-permute-start.22 = (bf16[256,128]{1,0:T(8,128)(2,1)S(1)}, bf16[256,128]{1,0:T(8,128)(2,1)S(1)}, u32[]{:S(2)}, u32[]{:S(2)}) collective-permute-start(bf16[256,128]{1,0:T(8,128)(2,1)S(1)} %get-tuple-element.96.refs_15_), channel_id=1, source_target_pairs={{0,7},{1,2},{2,1},{3,4},{4,3},{5,6},{6,5},{7,0},{8,15},{9,10},{10,... | collective-permute-start | bytes 196616 | tf_op jit(solution)/shard_map/ppermute | solution.py:284
  61.9 4.3 %collective-permute-start.21 = (bf16[256,128]{1,0:T(8,128)(2,1)S(1)}, bf16[256,128]{1,0:T(8,128)(2,1)S(1)}, u32[]{:S(2)}, u32[]{:S(2)}) collective-permute-start(bf16[256,128]{1,0:T(8,128)(2,1)S(1)} %get-tuple-element.95.refs_16_), channel_id=1, source_target_pairs={{0,1},{1,0},{2,3},{3,2},{4,5},{5,4},{6,7},{7,6},{8,9},{9,8},{10,11... | collective-permute-start | bytes 196616 | tf_op jit(solution)/shard_map/ppermute | solution.py:284

commit v6 on v5

--- a/solution.py
+++ b/solution.py
@@ -52,18 +52,18 @@
     return key_at <= lax.broadcasted_iota(jnp.int32, (SLICE, resp), 1)
 
 
-def forward_kernel(heads, share, picks, opening, *refs):
+def forward_kernel(heads, share, picks, after, opening, *refs):
     refs, scratch = refs[:-4], refs[-4:]
     k_all, v_all, s0, s1 = scratch
     count = len(picks)
     if opening:
         len_ref, wide_ref, own_ref = refs[:3]
         blocks = refs[3 : 3 + count]
-        out_ref, e_all, g_all, q_rows, c_rows = refs[3 + count :]
+        out_ref, e_all, g_all, q_rows, c_rows = refs[3 + count + after :]
     else:
         q_rows, c_rows = refs[:2]
         blocks = refs[2 : 2 + count]
-        out_ref, e_all, g_all = refs[2 + count :]
+        out_ref, e_all, g_all = refs[2 + count + after :]
     width, resp = q_rows.shape[1], q_rows.shape[0] // heads
     rate = math.log2(math.e) / math.sqrt(width)
     s_buf = (s0, s1)
@@ -189,7 +189,7 @@
             at += share
 
 
-def forward_stats(heads, share, blocks, rows=(), opening=()):
+def forward_stats(heads, share, blocks, rows=(), opening=(), after=()):
     if opening:
         resp, width = opening[1].shape[1], blocks[0].shape[1]
         operands = (*opening, *blocks)
@@ -209,9 +209,9 @@
     if opening:
         outs += [jax.ShapeDtypeStruct((heads * resp, width), BF16)] * 2
     return pl.pallas_call(
-        functools.partial(forward_kernel, heads, share, picks, bool(opening)),
+        functools.partial(forward_kernel, heads, share, picks, len(after), bool(opening)),
         out_shape=tuple(outs),
-        in_specs=specs,
+        in_specs=specs + [ANY_SPEC] * len(after),
         out_specs=(VMEM_SPEC,) * len(outs),
         scratch_shapes=[pltpu.VMEM((keys, width), BF16)] * 2 + [pltpu.VMEM((keys, resp), F32)] * 2,
         compiler_params=pltpu.CompilerParams(vmem_limit_bytes=SCOPED),
@@ -221,7 +221,7 @@
             transcendentals=heads * resp * keys,
         ),
         name="forward_stats",
-    )(*operands)
+    )(*operands, *after)
 
 
 def backward_grads(
@@ -257,17 +257,22 @@
     )(rewards, *operands, *after)
 
 
-def tie(block, after):
+def merge(part, given, first, relayed, after):
+    size = part.shape[0]
+
+    def kernel(part_ref, given_ref, relayed_ref, after_ref, out_ref):
+        total = part_ref[...] + given_ref[first : first + size, :].astype(F32)
+        out_ref[...] = (total + relayed_ref[...].astype(F32)).astype(BF16)
+
     return pl.pallas_call(
-        lambda block_ref, after_ref, out_ref: None,
-        out_shape=jax.ShapeDtypeStruct(block.shape, block.dtype),
-        in_specs=[ANY_SPEC] * 2,
-        out_specs=ANY_SPEC,
-        input_output_aliases={0: 0},
-        compiler_params=pltpu.CompilerParams(vmem_limit_bytes=1024 * 1024),
-        cost_estimate=pl.CostEstimate(flops=0, bytes_accessed=0, transcendentals=0),
-        name="tie",
-    )(block, after)
+        kernel,
+        out_shape=jax.ShapeDtypeStruct(part.shape, BF16),
+        in_specs=[VMEM_SPEC] * 3 + [ANY_SPEC],
+        out_specs=VMEM_SPEC,
+        compiler_params=pltpu.CompilerParams(vmem_limit_bytes=2 * 1024 * 1024),
+        cost_estimate=pl.CostEstimate(flops=0, bytes_accessed=part.size, transcendentals=0),
+        name="merge",
+    )(part, given, relayed, after)
 
 
 def across(block):
@@ -275,12 +280,14 @@
     return lax.ppermute(block, "sample", pairs)
 
 
-def along(block, side):
-    pairs = []
-    for y in range(2):
-        for z in range(RING):
-            other = (z + (1 if z % 2 == side else -1)) % RING
-            pairs.append((y * RING + z, y * RING + other))
+def along(block, reach, side):
+    partner = {}
+    for start in range(math.gcd(reach, RING)):
+        tour = [(start + reach * i) % RING for i in range(RING // math.gcd(reach, RING))]
+        for i in range(side, len(tour) + side, 2):
+            one, two = tour[i % len(tour)], tour[(i + 1) % len(tour)]
+            partner[one], partner[two] = two, one
+    pairs = [(y * RING + z, y * RING + partner[z]) for y in range(2) for z in range(RING)]
     return lax.ppermute(block, "sample", pairs)
 
 
@@ -295,41 +302,34 @@
     own_rows = jnp.concatenate([resp_keys, resp_values], axis=0)
     wide_rows = jnp.concatenate([queries, grad_out], axis=0)
 
-    first, *keep, q_rows, c_rows = forward_stats(
-        heads, share, [packed], opening=(lengths, wide_rows, own_rows)
-    )
-    rows, stats, kept = (q_rows, c_rows), [first], [keep]
-
-    def forward(*blocks):
-        stat, *keep = forward_stats(heads, share, blocks, rows)
+    def forward(*blocks, after=()):
+        stat, *keep = forward_stats(heads, share, blocks, rows, after=after)
         stats.append(stat)
         kept.append(keep)
 
     def join(*blocks):
         return jnp.concatenate(blocks, axis=0)
 
-    l1, r1 = along(packed, 0), along(packed, 1)
-    l2, r2 = along(r1, 0), along(l1, 1)
-    other1 = across(join(tie(packed, stats[-1]), l1, r1))
-    forward(l1, r1)
-    l2, r2 = tie(l2, stats[-1]), tie(r2, stats[-1])
-    l3, r3 = along(r2, 0), along(l2, 1)
-    other2 = across(join(l2, r2))
-    forward(l2, r2)
-    l3, r3 = tie(l3, stats[-1]), tie(r3, stats[-1])
-    l4 = along(r3, 0)
-    other3 = across(join(l3, r3))
-    forward(other1, l3, r3)
-    l4 = tie(l4, stats[-1])
-    other4 = across(l4)
-    forward(other2, l4)
-    forward(other3)
-    forward(other4)
+    n3a, n3b, other = along(packed, 3, 0), along(packed, 3, 1), across(packed)
+    both = join(packed, other)
+    n2a, n2b = along(both, 2, 0), along(both, 2, 1)
+    n1a, n1b = along(both, 1, 0), along(both, 1, 1)
+    first, *keep, q_rows, c_rows = forward_stats(
+        heads, share, [packed], opening=(lengths, wide_rows, own_rows), after=(both,)
+    )
+    rows, stats, kept = (q_rows, c_rows), [first], [keep]
+    n4 = along(n3b, 1, 0)
+    far = join(n3a, n3b, n4)
+    others = across(far)
+    forward(other, n3a, n3b)
+    forward(n1a, n1b, after=(far,))
+    forward(n2a, n2b, n4, after=(far,))
+    forward(others)
 
     back = functools.partial(
         backward_grads, rewards, rows, stats, kept, owners=owners, heads=heads, share=share
     )
-    ready = jax.ShapeDtypeStruct((size, width), BF16)
+    far_ready = jax.ShapeDtypeStruct((3 * size, width), BF16)
     both_ready = jax.ShapeDtypeStruct((2 * size, width), BF16)
     wide = jax.ShapeDtypeStruct((size, width), F32)
     grads = jax.ShapeDtypeStruct((1, resp, width), F32)
@@ -337,42 +337,37 @@
     def add(part, *received):
         return sum((r.astype(F32) for r in received), part).astype(BF16)
 
-    dq, part = back(((6, 0, share),), [(other4, 0, 1)], [ready], prior=None, after=())
+    dq, part = back(
+        ((4, 0, 3 * share),), [(others, 0, 3)], [far_ready], prior=None, after=()
+    )
     given = across(part)
-    dq, part, part_left = back(
-        ((5, 0, size), (4, size, share)), [(other3, 0, 2), (l4, 0, 1)], [both_ready, wide],
-        prior=dq, after=(),
-    )
-    far = add(part_left, given)
-    given = across(part)
-    dq, part, part_left, part_right = back(
-        ((4, 0, size), (3, 3 * share, size)), [(other2, 0, 2), (l3, 0, 1), (r3, 0, 1)],
-        [both_ready, wide, wide], prior=dq, after=(far,),
-    )
-    near = add(part_left, given[:size])
-    far = add(part_right, given[size:], along(far, 0))
-    given = across(part)
-    dq, part, part_left, part_right = back(
-        ((3, share, size), (2, 0, size)), [(other1, 1, 2), (l2, 0, 1), (r2, 0, 1)],
-        [both_ready, wide, wide], prior=dq, after=(far, near),
-    )
-    near = add(part_right, given[size:], along(near, 0))
-    far = add(part_left, given[:size], along(far, 1))
-    given = across(part)
-    dq, part, part_left, part_right = back(
-        ((3, 0, share), (1, 0, size)), [(other1, 0, 1), (l1, 0, 1), (r1, 0, 1)],
-        [ready, wide, wide], prior=dq, after=(far, near),
-    )
-    near = add(part_left, given[:size], along(near, 1))
-    far = add(part_right, given[size:], along(far, 0))
-    given = across(part)
+    dq, part_a, part_b = back(
+        ((3, 0, 2 * size),), [(n2a, 0, 2), (n2b, 0, 2)], [both_ready] * 2, prior=dq, after=()
+    )
+    came = [along(part_a, 2, 0), along(part_b, 2, 1)]
+    dq, partner, part_a, part_b, part_4 = back(
+        ((1, 0, 3 * share), (3, 2 * size, share)),
+        [(other, 0, 1), (n3a, 0, 1), (n3b, 0, 1), (n4, 0, 1)], [wide] * 4, prior=dq,
+        after=(part_a, part_b),
+    )
+    part_4 = add(part_4, given[2 * size :])
+    part_a = add(part_a, given[:size])
+    relayed, far_a = along(part_4, 1, 0), along(part_a, 3, 0)
+    dq, near_a, near_b = back(
+        ((2, 0, 2 * size),), [(n1a, 0, 2), (n1b, 0, 2)], [both_ready] * 2, prior=dq,
+        after=(part_4, part_a),
+    )
+    came += [along(near_a, 1, 0), along(near_b, 1, 1)]
+    part_b = merge(part_b, given, size, relayed, near_a)
+    far_b = along(part_b, 3, 1)
     grad_queries, mine, grad_resp_keys, grad_resp_values = back(
         ((0, 0, share + resp),), [(packed, 0, 1)], [wide, grads, grads], prior=dq,
-        after=(far, near), last=(own_rows,),
-    )
-    near, far = along(near, 0), along(far, 1)
+        after=(part_b,), last=(own_rows,),
+    )
+    partner = add(partner, *(block[size:] for block in came))
+    came += [far_a, far_b, across(partner)]
     total = [
-        mine[at : at + share] + sum(r[at : at + share].astype(F32) for r in (given, near, far))
+        mine[at : at + share] + sum(block[at : at + share].astype(F32) for block in came)
         for at in (0, share)
     ]
     return grad_queries, grad_resp_keys, grad_resp_values, *total

time: 67.3 us -> 70.3 us (1.045)
  starting transfers between devices: 29.6 us -> 31.5 us
  local copies, waits for them, and re-layouts: 0.88 us -> 1.74 us
    ppermute x14, starting transfers between devices: 18.9 us -> 27.1 us  [along(): return lax.ppermute(block, 'sample', pairs)]
    ppermute x9 -> x4, starting transfers between devices: 10.7 us -> 4.44 us  [across(): return lax.ppermute(block, 'sample', pairs)]
    ppermute x9 -> x4, waiting for transfers between devices: 1.95 us -> 0.11 us  [across(): return lax.ppermute(block, 'sample', pairs)]
    ppermute x14, waiting for transfers between devices: 8.81 us -> 10.5 us  [along(): return lax.ppermute(block, 'sample', pairs)]
    concatenate x1, local copies, waits for them, and re-layouts: 0.01 us -> 0.85 us  [shards(): own_rows = jnp.concatenate([resp_keys, resp_values], axis=0)]
    concatenate x3 -> x1, other arithmetic: 0.04 us -> 0.79 us  [join(): return jnp.concatenate(blocks, axis=0)]
    pallas_call x6 -> x5, Pallas kernels: 11 us -> 10.6 us  [backward_grads(): pl.pallas_call(functools.partial(backward_kernel, heads, share, owners, p...]
    pallas_call x13 -> x6, Pallas kernels: 9.45 us -> 9.72 us  [the longest x5 9.7 us: forward_stats(): pl.pallas_call(functools.partial(forward_kernel, heads, share, picks, len...]
  transfers between devices with their start and end apart: 23 -> 18, of which waited for: 10 -> 4; matrix products, arithmetic and copies ran while one was open for 4% -> 6% of each run, Pallas kernels for 29% -> 25%
where the time goes in v6:
time: 70.3 us; the launch traced here: 70 us
  starting transfers between devices  31.5 us (45%)
  Pallas kernels  20.3 us (29%)
  waiting for transfers between devices  10.6 us (15%)
  other arithmetic  3.67 us (5%)
  between operations  2.1 us (3%)
  local copies, waits for them, and re-layouts  1.74 us (2%)
    ppermute x14, starting transfers between devices, along(): return lax.ppermute(block, 'sample', pairs)  27.1 us
    pallas_call x5, Pallas kernels, backward_grads(): pl.pallas_call(functools.partial(backward_kernel, heads, share, owners, p...  10.6 us
    ppermute x14, waiting for transfers between devices, along(): return lax.ppermute(block, 'sample', pairs)  10.5 us
    pallas_call x5, Pallas kernels, forward_stats(): pl.pallas_call(functools.partial(forward_kernel, heads, share, picks, len...  9.7 us
    ppermute x4, starting transfers between devices, across(): return lax.ppermute(block, 'sample', pairs)  4.44 us
  transfers between devices with their start and end apart: 18, of which 4 were waited for; matrix products, arithmetic and copies ran while one was open for 6% of the time, Pallas kernels for 25%

profile of v6, /device:TPU:2, one launch (start us, length us, event | category | flops | bytes accessed | tf_op | source)
XLA Modules:
  0.0 70.0 jit_solution(4000813070394233199)
XLA Ops:
  1.3 0.8 %pad_maximum_fusion.2.refs_3_.refs_10_ = bf16[272,128]{1,0:T(8,128)(2,1)S(1)} fusion(bf16[16,128]{1,0:T(8,128)(2,1)S(1)} %broadcast_in_dim.9, bf16[128,128]{1,0:T(8,128)(2,1)} %param.12, bf16[128,128]{1,0:T(8,128)(2,1)} %param.11), kind=kLoop, calls=%fused_computation.5 | loop fusion | flops 208896 | bytes 139264 | tf_op jit(solution)/shard_map/concatenate | solution.py:301
  2.1 1.6 %collective-permute-start = (bf16[272,128]{1,0:T(8,128)(2,1)S(1)}, bf16[272,128]{1,0:T(8,128)(2,1)S(1)}, u32[]{:S(2)}, u32[]{:S(2)}) collective-permute-start(bf16[272,128]{1,0:T(8,128)(2,1)S(1)} %pad_maximum_fusion.2.refs_3_.refs_10_), channel_id=1, source_target_pairs={{0,8},{1,9},{2,10},{3,11},{4,12},{5,13},{6,14},{7,15},{8,0},{9,1},... | collective-permute-start | bytes 208904 | tf_op jit(solution)/shard_map/ppermute | solution.py:280
  3.7 4.6 %collective-permute-start.1 = (bf16[272,128]{1,0:T(8,128)(2,1)S(1)}, bf16[272,128]{1,0:T(8,128)(2,1)S(1)}, u32[]{:S(2)}, u32[]{:S(2)}) collective-permute-start(bf16[272,128]{1,0:T(8,128)(2,1)S(1)} %pad_maximum_fusion.2.refs_3_.refs_10_), channel_id=1, source_target_pairs={{0,3},{1,6},{2,5},{3,0},{4,7},{5,2},{6,1},{7,4},{8,11},{9,14},{10,... | collective-permute-start | bytes 208904 | tf_op jit(solution)/shard_map/ppermute | solution.py:291
  8.3 2.2 %collective-permute-start.2 = (bf16[272,128]{1,0:T(8,128)(2,1)S(1)}, bf16[272,128]{1,0:T(8,128)(2,1)S(1)}, u32[]{:S(2)}, u32[]{:S(2)}) collective-permute-start(bf16[272,128]{1,0:T(8,128)(2,1)S(1)} %pad_maximum_fusion.2.refs_3_.refs_10_), channel_id=1, source_target_pairs={{0,5},{1,4},{2,7},{3,6},{4,1},{5,0},{6,3},{7,2},{8,13},{9,12},{10,... | collective-permute-start | bytes 208904 | tf_op jit(solution)/shard_map/ppermute | solution.py:291
  11.2 0.8 %constant_dynamic-update-slice_fusion.1 = bf16[2,256,128]{2,1,0:T(8,128)(2,1)S(1)} fusion(bf16[1,256,128]{2,1,0:T(8,128)(2,1)} %param.9), kind=kLoop, calls=%fused_computation.9 | loop fusion | bytes 131072
  12.0 1.3 %pad_maximum_fusion.refs_1_ = bf16[2,256,1024]{2,1,0:T(8,128)(2,1)S(1)} fusion(bf16[1,256,1024]{2,1,0:T(8,128)(2,1)} %param.13, bf16[1,256,1024]{2,1,0:T(8,128)(2,1)} %param.8), kind=kLoop, calls=%fused_computation | loop fusion | flops 524288 | bytes 2097152 | tf_op jit(solution)/shard_map/concatenate | solution.py:303
  13.3 0.9 %constant_dynamic-update-slice_fusion.refs_2_.refs_11_ = bf16[2,256,128]{2,1,0:T(8,128)(2,1)S(1)} fusion(bf16[2,256,128]{2,1,0:T(8,128)(2,1)S(1)} %constant_dynamic-update-slice_fusion.1, bf16[1,256,128]{2,1,0:T(8,128)(2,1)} %param.10), kind=kLoop, calls=%fused_computation.8 | loop fusion | bytes 131072 | tf_op jit(solution)/shard_map/concatenate | solution.py:302
  14.2 0.8 %pad_maximum_fusion.1.refs_4_ = bf16[544,128]{1,0:T(8,128)(2,1)S(1)} fusion(bf16[272,128]{1,0:T(8,128)(2,1)S(1)} %collective-permute-done.refs_2_.refs_12_, bf16[16,128]{1,0:T(8,128)(2,1)S(1)} %broadcast_in_dim.9, bf16[128,128]{1,0:T(8,128)(2,1)} %param.12, bf16[128,128]{1,0:T(8,128)(2,1)} %param.11), kind=kLoop, calls=%fused_computation.1 | loop fusion | flops 557056 | bytes 278528 | tf_op jit(solution)/shard_map/concatenate | solution.py:311
  15.0 2.9 %collective-permute-start.3 = (bf16[544,128]{1,0:T(8,128)(2,1)S(1)}, bf16[544,128]{1,0:T(8,128)(2,1)S(1)}, u32[]{:S(2)}, u32[]{:S(2)}) collective-permute-start(bf16[544,128]{1,0:T(8,128)(2,1)S(1)} %pad_maximum_fusion.1.refs_4_), channel_id=1, source_target_pairs={{0,1},{1,0},{2,3},{3,2},{4,5},{5,4},{6,7},{7,6},{8,9},{9,8},{10,11... | collective-permute-start | bytes 417800 | tf_op jit(solution)/shard_map/ppermute | solution.py:291
  17.9 1.3 %collective-permute-start.4 = (bf16[544,128]{1,0:T(8,128)(2,1)S(1)}, bf16[544,128]{1,0:T(8,128)(2,1)S(1)}, u32[]{:S(2)}, u32[]{:S(2)}) collective-permute-start(bf16[544,128]{1,0:T(8,128)(2,1)S(1)} %pad_maximum_fusion.1.refs_4_), channel_id=1, source_target_pairs={{0,7},{1,2},{2,1},{3,4},{4,3},{5,6},{6,5},{7,0},{8,15},{9,10},{10,... | collective-permute-start | bytes 417800 | tf_op jit(solution)/shard_map/ppermute | solution.py:291
  19.4 3.6 %collective-permute-start.7 = (bf16[544,128]{1,0:T(8,128)(2,1)S(1)}, bf16[544,128]{1,0:T(8,128)(2,1)S(1)}, u32[]{:S(2)}, u32[]{:S(2)}) collective-permute-start(bf16[544,128]{1,0:T(8,128)(2,1)S(1)} %pad_maximum_fusion.1.refs_4_), channel_id=1, source_target_pairs={{0,6},{1,7},{2,4},{3,5},{4,2},{5,3},{6,0},{7,1},{8,14},{9,15},{10,... | collective-permute-start | bytes 417800 | tf_op jit(solution)/shard_map/ppermute | solution.py:291
  23.0 1.5 %forward_stats.5 = (f32[32,256]{1,0:T(8,128)S(1)}, bf16[384,2048]{1,0:T(8,128)(2,1)S(1)}, f32[384,2048]{1,0:T(8,128)S(1)}, bf16[2048,128]{1,0:T(8,128)(2,1)S(1)}, bf16[2048,128]{1,0:T(8,128)(2,1)S(1)}) custom-call(s32[1]{0:T(128)S(6)} %copy.16.refs_0_, bf16[2,256,1024]{2,1,0:T(8,128)(2,1)S(1)} %pad_maximum_fusion.refs_1_, ...), custom_call_target="tpu_custom_call" | custom-call | flops 1207959552 | bytes 1048576 | tf_op jit(solution)/shard_map/forward_stats/pallas_call | solution.py:211
  24.6 1.1 %collective-permute-start.5 = (bf16[272,128]{1,0:T(8,128)(2,1)S(1)}, bf16[272,128]{1,0:T(8,128)(2,1)S(1)}, u32[]{:S(2)}, u32[]{:S(2)}) collective-permute-start(bf16[272,128]{1,0:T(8,128)(2,1)S(1)} %collective-permute-done.2.refs_4_.refs_14_), channel_id=1, source_target_pairs={{0,1},{1,0},{2,3},{3,2},{4,5},{5,4},{6,7},{7,6},{8,9},{9,8},{10,11... | collective-permute-start | bytes 208904 | tf_op jit(solution)/shard_map/ppermute | solution.py:291
  25.7 1.5 %forward_stats.6 = (f32[32,256]{1,0:T(8,128)S(1)}, bf16[384,2048]{1,0:T(8,128)(2,1)S(1)}, f32[384,2048]{1,0:T(8,128)S(1)}) custom-call(bf16[2048,128]{1,0:T(8,128)(2,1)S(1)} %get-tuple-element.39.refs_0_.refs_1_, bf16[2048,128]{1,0:T(8,128)(2,1)S(1)} %get-tuple-element.40.refs_1_.refs_2_, bf16[272,128]{1,0:T(8,128)(2,1)S(1)} %collective-permute-done.refs_2_.refs_12_, ...), custom_call_target="tpu_custom_call" | custom-call | flops 1207959552 | bytes 1048576 | tf_op jit(solution)/shard_map/forward_stats/pallas_call | solution.py:211
  27.2 3.1 %collective-permute-done.5.refs_4_.refs_15_ = bf16[272,128]{1,0:T(8,128)(2,1)S(1)} collective-permute-done((bf16[272,128]{1,0:T(8,128)(2,1)S(1)}, bf16[272,128]{1,0:T(8,128)(2,1)S(1)}, u32[]{:S(2)}, u32[]{:S(2)}) %collective-permute-start.5) | collective-permute-done | bytes 69664 | tf_op jit(solution)/shard_map/ppermute | solution.py:291
  31.0 2.3 %forward_stats.7 = (f32[32,256]{1,0:T(8,128)S(1)}, bf16[512,2048]{1,0:T(8,128)(2,1)S(1)}, f32[512,2048]{1,0:T(8,128)S(1)}) custom-call(bf16[2048,128]{1,0:T(8,128)(2,1)S(1)} %get-tuple-element.39.refs_0_.refs_1_, bf16[2048,128]{1,0:T(8,128)(2,1)S(1)} %get-tuple-element.40.refs_1_.refs_2_, bf16[544,128]{1,0:T(8,128)(2,1)S(1)} %collective-permute-done.3.refs_2_.refs_10_, ...), custom_call_target="tpu_custom_call" | custom-call | flops 1610612736 | bytes 1048576 | tf_op jit(solution)/shard_map/forward_stats/pallas_call | solution.py:211
  33.3 2.9 %forward_stats.8 = (f32[32,256]{1,0:T(8,128)S(1)}, bf16[640,2048]{1,0:T(8,128)(2,1)S(1)}, f32[640,2048]{1,0:T(8,128)S(1)}) custom-call(bf16[2048,128]{1,0:T(8,128)(2,1)S(1)} %get-tuple-element.39.refs_0_.refs_1_, bf16[2048,128]{1,0:T(8,128)(2,1)S(1)} %get-tuple-element.40.refs_1_.refs_2_, bf16[544,128]{1,0:T(8,128)(2,1)S(1)} %collective-permute-done.6.refs_2_.refs_10_, ...), custom_call_target="tpu_custom_call" | custom-call | flops 2013265920 | bytes 1048576 | tf_op jit(solution)/shard_map/forward_stats/pallas_call | solution.py:211
  36.4 1.5 %forward_stats.9 = (f32[32,256]{1,0:T(8,128)S(1)}, bf16[384,2048]{1,0:T(8,128)(2,1)S(1)}, f32[384,2048]{1,0:T(8,128)S(1)}) custom-call(bf16[2048,128]{1,0:T(8,128)(2,1)S(1)} %get-tuple-element.39.refs_0_.refs_1_, bf16[2048,128]{1,0:T(8,128)(2,1)S(1)} %get-tuple-element.40.refs_1_.refs_2_, bf16[816,128]{1,0:T(8,128)(2,1)S(1)} %collective-permute-done.8.refs_2_.refs_10_), custom_call_target="tpu_custom_call" | custom-call | flops 1207959552 | bytes 1048576 | tf_op jit(solution)/shard_map/forward_stats/pallas_call | solution.py:211
  37.9 1.6 %backward_grads.5 = (f32[1024,256]{1,0:T(8,128)S(1)}, bf16[768,128]{1,0:T(8,128)(2,1)S(1)}) custom-call(s32[1]{0:T(128)S(6)} %copy.17.refs_0_, bf16[2048,128]{1,0:T(8,128)(2,1)S(1)} %get-tuple-element.39.refs_0_.refs_1_, bf16[2048,128]{1,0:T(8,128)(2,1)S(1)} %get-tuple-element.40.refs_1_.refs_2_, f32[32,256]{1,0:T(8,128)S(1)} %get-tuple-element.41.refs_3_, ...), custom_call_target="tpu_custom_call" | custom-call | flops 2013265920 | bytes 2097152 | tf_op jit(solution)/shard_map/backward_grads/pallas_call | solution.py:240
  39.5 1.6 %collective-permute-start.9 = (bf16[768,128]{1,0:T(8,128)(2,1)S(1)}, bf16[768,128]{1,0:T(8,128)(2,1)S(1)}, u32[]{:S(2)}, u32[]{:S(2)}) collective-permute-start(bf16[768,128]{1,0:T(8,128)(2,1)S(1)} %get-tuple-element.62), channel_id=1, source_target_pairs={{0,8},{1,9},{2,10},{3,11},{4,12},{5,13},{6,14},{7,15},{8,0},{9,1},... | collective-permute-start | bytes 589832 | tf_op jit(solution)/shard_map/ppermute | solution.py:280
  41.1 2.1 %backward_grads.6 = (f32[1024,256]{1,0:T(8,128)S(1)}, bf16[512,128]{1,0:T(8,128)(2,1)S(1)}, bf16[512,128]{1,0:T(8,128)(2,1)S(1)}) custom-call(s32[1]{0:T(128)S(6)} %copy.17.refs_0_, bf16[2048,128]{1,0:T(8,128)(2,1)S(1)} %get-tuple-element.39.refs_0_.refs_1_, bf16[2048,128]{1,0:T(8,128)(2,1)S(1)} %get-tuple-element.40.refs_1_.refs_2_, ...), custom_call_target="tpu_custom_call" | custom-call | flops 2684354560 | bytes 2097152 | tf_op jit(solution)/shard_map/backward_grads/pallas_call | solution.py:240
  43.2 1.4 %collective-permute-start.12 = (bf16[512,128]{1,0:T(8,128)(2,1)S(1)}, bf16[512,128]{1,0:T(8,128)(2,1)S(1)}, u32[]{:S(2)}, u32[]{:S(2)}) collective-permute-start(bf16[512,128]{1,0:T(8,128)(2,1)S(1)} %get-tuple-element.59.refs_18_), channel_id=1, source_target_pairs={{0,6},{1,7},{2,4},{3,5},{4,2},{5,3},{6,0},{7,1},{8,14},{9,15},{10,... | collective-permute-start | bytes 393224 | tf_op jit(solution)/shard_map/ppermute | solution.py:291
  44.6 2.0 %collective-permute-start.11 = (bf16[512,128]{1,0:T(8,128)(2,1)S(1)}, bf16[512,128]{1,0:T(8,128)(2,1)S(1)}, u32[]{:S(2)}, u32[]{:S(2)}) collective-permute-start(bf16[512,128]{1,0:T(8,128)(2,1)S(1)} %get-tuple-element.58.refs_17_), channel_id=1, source_target_pairs={{0,2},{1,3},{2,0},{3,1},{4,6},{5,7},{6,4},{7,5},{8,10},{9,11},{10,... | collective-permute-start | bytes 393224 | tf_op jit(solution)/shard_map/ppermute | solution.py:291
  46.6 2.1 %backward_grads.7 = (f32[1024,256]{1,0:T(8,128)S(1)}, f32[256,128]{1,0:T(8,128)S(1)}, f32[256,128]{1,0:T(8,128)S(1)}, f32[256,128]{1,0:T(8,128)S(1)}, f32[256,128]{1,0:T(8,128)S(1)}) custom-call(s32[1]{0:T(128)S(6)} %copy.17.refs_0_, bf16[2048,128]{1,0:T(8,128)(2,1)S(1)} %get-tuple-element.39.refs_0_.refs_1_, ...), custom_call_target="tpu_custom_call" | custom-call | flops 2684354560 | bytes 2097152 | tf_op jit(solution)/shard_map/backward_grads/pallas_call | solution.py:240
  48.7 2.1 %backward_grads.8 = (f32[1024,256]{1,0:T(8,128)S(1)}, bf16[512,128]{1,0:T(8,128)(2,1)S(1)}, bf16[512,128]{1,0:T(8,128)(2,1)S(1)}) custom-call(s32[1]{0:T(128)S(6)} %copy.17.refs_0_, bf16[2048,128]{1,0:T(8,128)(2,1)S(1)} %get-tuple-element.39.refs_0_.refs_1_, bf16[2048,128]{1,0:T(8,128)(2,1)S(1)} %get-tuple-element.40.refs_1_.refs_2_, ...), custom_call_target="tpu_custom_call" | custom-call | flops 2684354560 | bytes 2097152 | tf_op jit(solution)/shard_map/backward_grads/pallas_call | solution.py:240
  50.9 2.0 %collective-permute-start.14 = (bf16[512,128]{1,0:T(8,128)(2,1)S(1)}, bf16[512,128]{1,0:T(8,128)(2,1)S(1)}, u32[]{:S(2)}, u32[]{:S(2)}) collective-permute-start(bf16[512,128]{1,0:T(8,128)(2,1)S(1)} %get-tuple-element.71), channel_id=1, source_target_pairs={{0,7},{1,2},{2,1},{3,4},{4,3},{5,6},{6,5},{7,0},{8,15},{9,10},{10,... | collective-permute-start | bytes 393224 | tf_op jit(solution)/shard_map/ppermute | solution.py:291
  52.9 2.0 %collective-permute-start.10 = (bf16[256,128]{1,0:T(8,128)(2,1)S(1)}, bf16[256,128]{1,0:T(8,128)(2,1)S(1)}, u32[]{:S(2)}, u32[]{:S(2)}) collective-permute-start(bf16[256,128]{1,0:T(8,128)(2,1)S(1)} %get-tuple-element.76.refs_13_), channel_id=1, source_target_pairs={{0,1},{1,0},{2,3},{3,2},{4,5},{5,4},{6,7},{7,6},{8,9},{9,8},{10,11... | collective-permute-start | bytes 196616 | tf_op jit(solution)/shard_map/ppermute | solution.py:291
  54.9 5.0 %collective-permute-done.10.relayed_ref = bf16[256,128]{1,0:T(8,128)(2,1)S(1)} collective-permute-done((bf16[256,128]{1,0:T(8,128)(2,1)S(1)}, bf16[256,128]{1,0:T(8,128)(2,1)S(1)}, u32[]{:S(2)}, u32[]{:S(2)}) %collective-permute-start.10) | collective-permute-done | bytes 65568 | tf_op jit(solution)/shard_map/ppermute | solution.py:291
  60.0 1.9 %collective-permute-start.15 = (bf16[256,128]{1,0:T(8,128)(2,1)S(1)}, bf16[256,128]{1,0:T(8,128)(2,1)S(1)}, u32[]{:S(2)}, u32[]{:S(2)}) collective-permute-start(bf16[256,128]{1,0:T(8,128)(2,1)S(1)} %get-tuple-element.75.refs_14_), channel_id=1, source_target_pairs={{0,3},{1,6},{2,5},{3,0},{4,7},{5,2},{6,1},{7,4},{8,11},{9,14},{10,... | collective-permute-start | bytes 196616 | tf_op jit(solution)/shard_map/ppermute | solution.py:291
  61.9 1.8 %collective-permute-start.16 = (bf16[256,128]{1,0:T(8,128)(2,1)S(1)}, bf16[256,128]{1,0:T(8,128)(2,1)S(1)}, u32[]{:S(2)}, u32[]{:S(2)}) collective-permute-start(bf16[256,128]{1,0:T(8,128)(2,1)S(1)} %merge.1.refs_13_), channel_id=1, source_target_pairs={{0,5},{1,4},{2,7},{3,6},{4,1},{5,0},{6,3},{7,2},{8,13},{9,12},{10,... | collective-permute-start | bytes 196616 | tf_op jit(solution)/shard_map/ppermute | solution.py:291
  64.4 2.6 %backward_grads.9 = (f32[1,256,1024]{2,1,0:T(8,128)}, f32[256,128]{1,0:T(8,128)S(1)}, f32[1,256,128]{2,1,0:T(8,128)}, f32[1,256,128]{2,1,0:T(8,128)}) custom-call(s32[1]{0:T(128)S(6)} %copy.17.refs_0_, bf16[2048,128]{1,0:T(8,128)(2,1)S(1)} %get-tuple-element.39.refs_0_.refs_1_, bf16[2048,128]{1,0:T(8,128)(2,1)S(1)} %get-tuple-element.40.refs_1_.refs_2_, ...), custom_call_target="tpu_custom_call" | custom-call | flops 2013265920 | bytes 2097152 | tf_op jit(solution)/shard_map/backward_grads/pallas_call | solution.py:240
  67.0 2.3 %collective-permute-done.16 = bf16[256,128]{1,0:T(8,128)(2,1)S(1)} collective-permute-done((bf16[256,128]{1,0:T(8,128)(2,1)S(1)}, bf16[256,128]{1,0:T(8,128)(2,1)S(1)}, u32[]{:S(2)}, u32[]{:S(2)}) %collective-permute-start.16) | collective-permute-done | bytes 65568 | tf_op jit(solution)/shard_map/ppermute | solution.py:291
  (27 shorter events, 2.6 us)
Async XLA Ops:
  2.1 12.1 %collective-permute-start = (bf16[272,128]{1,0:T(8,128)(2,1)S(1)}, bf16[272,128]{1,0:T(8,128)(2,1)S(1)}, u32[]{:S(2)}, u32[]{:S(2)}) collective-permute-start(bf16[272,128]{1,0:T(8,128)(2,1)S(1)} %pad_maximum_fusion.2.refs_3_.refs_10_), channel_id=1, source_target_pairs={{0,8},{1,9},{2,10},{3,11},{4,12},{5,13},{6,14},{7,15},{8,0},{9,1},... | collective-permute-start | bytes 208904 | tf_op jit(solution)/shard_map/ppermute | solution.py:280
  3.7 15.8 %collective-permute-start.1 = (bf16[272,128]{1,0:T(8,128)(2,1)S(1)}, bf16[272,128]{1,0:T(8,128)(2,1)S(1)}, u32[]{:S(2)}, u32[]{:S(2)}) collective-permute-start(bf16[272,128]{1,0:T(8,128)(2,1)S(1)} %pad_maximum_fusion.2.refs_3_.refs_10_), channel_id=1, source_target_pairs={{0,3},{1,6},{2,5},{3,0},{4,7},{5,2},{6,1},{7,4},{8,11},{9,14},{10,... | collective-permute-start | bytes 208904 | tf_op jit(solution)/shard_map/ppermute | solution.py:291
  8.3 16.3 %collective-permute-start.2 = (bf16[272,128]{1,0:T(8,128)(2,1)S(1)}, bf16[272,128]{1,0:T(8,128)(2,1)S(1)}, u32[]{:S(2)}, u32[]{:S(2)}) collective-permute-start(bf16[272,128]{1,0:T(8,128)(2,1)S(1)} %pad_maximum_fusion.2.refs_3_.refs_10_), channel_id=1, source_target_pairs={{0,5},{1,4},{2,7},{3,6},{4,1},{5,0},{6,3},{7,2},{8,13},{9,12},{10,... | collective-permute-start | bytes 208904 | tf_op jit(solution)/shard_map/ppermute | solution.py:291
  15.0 16.1 %collective-permute-start.3 = (bf16[544,128]{1,0:T(8,128)(2,1)S(1)}, bf16[544,128]{1,0:T(8,128)(2,1)S(1)}, u32[]{:S(2)}, u32[]{:S(2)}) collective-permute-start(bf16[544,128]{1,0:T(8,128)(2,1)S(1)} %pad_maximum_fusion.1.refs_4_), channel_id=1, source_target_pairs={{0,1},{1,0},{2,3},{3,2},{4,5},{5,4},{6,7},{7,6},{8,9},{9,8},{10,11... | collective-permute-start | bytes 417800 | tf_op jit(solution)/shard_map/ppermute | solution.py:291
  17.9 13.1 %collective-permute-start.4 = (bf16[544,128]{1,0:T(8,128)(2,1)S(1)}, bf16[544,128]{1,0:T(8,128)(2,1)S(1)}, u32[]{:S(2)}, u32[]{:S(2)}) collective-permute-start(bf16[544,128]{1,0:T(8,128)(2,1)S(1)} %pad_maximum_fusion.1.refs_4_), channel_id=1, source_target_pairs={{0,7},{1,2},{2,1},{3,4},{4,3},{5,6},{6,5},{7,0},{8,15},{9,10},{10,... | collective-permute-start | bytes 417800 | tf_op jit(solution)/shard_map/ppermute | solution.py:291
  19.2 14.1 %collective-permute-start.6 = (bf16[544,128]{1,0:T(8,128)(2,1)S(1)}, bf16[544,128]{1,0:T(8,128)(2,1)S(1)}, u32[]{:S(2)}, u32[]{:S(2)}) collective-permute-start(bf16[544,128]{1,0:T(8,128)(2,1)S(1)} %pad_maximum_fusion.1.refs_4_), channel_id=1, source_target_pairs={{0,2},{1,3},{2,0},{3,1},{4,6},{5,7},{6,4},{7,5},{8,10},{9,11},{10,... | collective-permute-start | bytes 417800 | tf_op jit(solution)/shard_map/ppermute | solution.py:291
  19.4 13.9 %collective-permute-start.7 = (bf16[544,128]{1,0:T(8,128)(2,1)S(1)}, bf16[544,128]{1,0:T(8,128)(2,1)S(1)}, u32[]{:S(2)}, u32[]{:S(2)}) collective-permute-start(bf16[544,128]{1,0:T(8,128)(2,1)S(1)} %pad_maximum_fusion.1.refs_4_), channel_id=1, source_target_pairs={{0,6},{1,7},{2,4},{3,5},{4,2},{5,3},{6,0},{7,1},{8,14},{9,15},{10,... | collective-permute-start | bytes 417800 | tf_op jit(solution)/shard_map/ppermute | solution.py:291
  24.6 5.7 %collective-permute-start.5 = (bf16[272,128]{1,0:T(8,128)(2,1)S(1)}, bf16[272,128]{1,0:T(8,128)(2,1)S(1)}, u32[]{:S(2)}, u32[]{:S(2)}) collective-permute-start(bf16[272,128]{1,0:T(8,128)(2,1)S(1)} %collective-permute-done.2.refs_4_.refs_14_), channel_id=1, source_target_pairs={{0,1},{1,0},{2,3},{3,2},{4,5},{5,4},{6,7},{7,6},{8,9},{9,8},{10,11... | collective-permute-start | bytes 208904 | tf_op jit(solution)/shard_map/ppermute | solution.py:291
  30.3 6.1 %collective-permute-start.8 = (bf16[816,128]{1,0:T(8,128)(2,1)S(1)}, bf16[816,128]{1,0:T(8,128)(2,1)S(1)}, u32[]{:S(2)}, u32[]{:S(2)}) collective-permute-start(bf16[816,128]{1,0:T(8,128)(2,1)S(1)} %constant_dynamic-update-slice_fusion.2.refs_4_.refs_5_), channel_id=1, source_target_pairs={{0,8},{1,9},{2,10},{3,11},{4,12},{5,13},{6,14},{7,15},{8,0},{9,1},... | collective-permute-start | bytes 626696 | tf_op jit(solution)/shard_map/ppermute | solution.py:280
  39.5 9.2 %collective-permute-start.9 = (bf16[768,128]{1,0:T(8,128)(2,1)S(1)}, bf16[768,128]{1,0:T(8,128)(2,1)S(1)}, u32[]{:S(2)}, u32[]{:S(2)}) collective-permute-start(bf16[768,128]{1,0:T(8,128)(2,1)S(1)} %get-tuple-element.62), channel_id=1, source_target_pairs={{0,8},{1,9},{2,10},{3,11},{4,12},{5,13},{6,14},{7,15},{8,0},{9,1},... | collective-permute-start | bytes 589832 | tf_op jit(solution)/shard_map/ppermute | solution.py:280
  43.2 18.7 %collective-permute-start.12 = (bf16[512,128]{1,0:T(8,128)(2,1)S(1)}, bf16[512,128]{1,0:T(8,128)(2,1)S(1)}, u32[]{:S(2)}, u32[]{:S(2)}) collective-permute-start(bf16[512,128]{1,0:T(8,128)(2,1)S(1)} %get-tuple-element.59.refs_18_), channel_id=1, source_target_pairs={{0,6},{1,7},{2,4},{3,5},{4,2},{5,3},{6,0},{7,1},{8,14},{9,15},{10,... | collective-permute-start | bytes 393224 | tf_op jit(solution)/shard_map/ppermute | solution.py:291
  44.6 19.1 %collective-permute-start.11 = (bf16[512,128]{1,0:T(8,128)(2,1)S(1)}, bf16[512,128]{1,0:T(8,128)(2,1)S(1)}, u32[]{:S(2)}, u32[]{:S(2)}) collective-permute-start(bf16[512,128]{1,0:T(8,128)(2,1)S(1)} %get-tuple-element.58.refs_17_), channel_id=1, source_target_pairs={{0,2},{1,3},{2,0},{3,1},{4,6},{5,7},{6,4},{7,5},{8,10},{9,11},{10,... | collective-permute-start | bytes 393224 | tf_op jit(solution)/shard_map/ppermute | solution.py:291
  50.9 12.9 %collective-permute-start.14 = (bf16[512,128]{1,0:T(8,128)(2,1)S(1)}, bf16[512,128]{1,0:T(8,128)(2,1)S(1)}, u32[]{:S(2)}, u32[]{:S(2)}) collective-permute-start(bf16[512,128]{1,0:T(8,128)(2,1)S(1)} %get-tuple-element.71), channel_id=1, source_target_pairs={{0,7},{1,2},{2,1},{3,4},{4,3},{5,6},{6,5},{7,0},{8,15},{9,10},{10,... | collective-permute-start | bytes 393224 | tf_op jit(solution)/shard_map/ppermute | solution.py:291
  52.9 10.8 %collective-permute-start.13 = (bf16[512,128]{1,0:T(8,128)(2,1)S(1)}, bf16[512,128]{1,0:T(8,128)(2,1)S(1)}, u32[]{:S(2)}, u32[]{:S(2)}) collective-permute-start(bf16[512,128]{1,0:T(8,128)(2,1)S(1)} %get-tuple-element.66.after_ref), channel_id=1, source_target_pairs={{0,1},{1,0},{2,3},{3,2},{4,5},{5,4},{6,7},{7,6},{8,9},{9,8},{10,11... | collective-permute-start | bytes 393224 | tf_op jit(solution)/shard_map/ppermute | solution.py:291
  52.9 7.1 %collective-permute-start.10 = (bf16[256,128]{1,0:T(8,128)(2,1)S(1)}, bf16[256,128]{1,0:T(8,128)(2,1)S(1)}, u32[]{:S(2)}, u32[]{:S(2)}) collective-permute-start(bf16[256,128]{1,0:T(8,128)(2,1)S(1)} %get-tuple-element.76.refs_13_), channel_id=1, source_target_pairs={{0,1},{1,0},{2,3},{3,2},{4,5},{5,4},{6,7},{7,6},{8,9},{9,8},{10,11... | collective-permute-start | bytes 196616 | tf_op jit(solution)/shard_map/ppermute | solution.py:291
  60.0 7.0 %collective-permute-start.15 = (bf16[256,128]{1,0:T(8,128)(2,1)S(1)}, bf16[256,128]{1,0:T(8,128)(2,1)S(1)}, u32[]{:S(2)}, u32[]{:S(2)}) collective-permute-start(bf16[256,128]{1,0:T(8,128)(2,1)S(1)} %get-tuple-element.75.refs_14_), channel_id=1, source_target_pairs={{0,3},{1,6},{2,5},{3,0},{4,7},{5,2},{6,1},{7,4},{8,11},{9,14},{10,... | collective-permute-start | bytes 196616 | tf_op jit(solution)/shard_map/ppermute | solution.py:291
  61.9 7.4 %collective-permute-start.16 = (bf16[256,128]{1,0:T(8,128)(2,1)S(1)}, bf16[256,128]{1,0:T(8,128)(2,1)S(1)}, u32[]{:S(2)}, u32[]{:S(2)}) collective-permute-start(bf16[256,128]{1,0:T(8,128)(2,1)S(1)} %merge.1.refs_13_), channel_id=1, source_target_pairs={{0,5},{1,4},{2,7},{3,6},{4,1},{5,0},{6,3},{7,2},{8,13},{9,12},{10,... | collective-permute-start | bytes 196616 | tf_op jit(solution)/shard_map/ppermute | solution.py:291
  63.8 5.5 %collective-permute-start.17 = (bf16[256,128]{1,0:T(8,128)(2,1)S(1)}, bf16[256,128]{1,0:T(8,128)(2,1)S(1)}, u32[]{:S(2)}, u32[]{:S(2)}) collective-permute-start(bf16[256,128]{1,0:T(8,128)(2,1)S(1)} %add_convert_fusion), channel_id=1, source_target_pairs={{0,8},{1,9},{2,10},{3,11},{4,12},{5,13},{6,14},{7,15},{8,0},{9,1},... | collective-permute-start | bytes 196616 | tf_op jit(solution)/shard_map/ppermute | solution.py:280

commit v7 on v4

--- a/solution.py
+++ b/solution.py
@@ -43,14 +43,11 @@
     return [(ref, at) for ref in blocks for at in range(0, ref.shape[0], size)]
 
 
-def load_rows(blocks, own, k_all, v_all, share):
+def load_rows(blocks, k_all, v_all, share):
     places = pack_places(blocks, share)
     for i, (ref, at) in enumerate(places):
         k_all[i * share : (i + 1) * share, :] = ref[at : at + share, :]
         v_all[i * share : (i + 1) * share, :] = ref[at + share : at + 2 * share, :]
-    if own:
-        k_all[len(places) * share :, :] = own[0][0]
-        v_all[len(places) * share :, :] = own[1][0]
     return len(places) * share
 
 
@@ -63,20 +60,21 @@
     refs, scratch = refs[:-4], refs[-4:]
     k_all, v_all, s0, s1 = scratch
     if opening:
-        len_ref, q_ref, c_ref = refs[:3]
-        blocks, own = refs[3 : 3 + count], refs[3 + count : 5 + count]
-        out_ref, e_all, g_all, q_rows, c_rows, copy_ref = refs[5 + count :]
-        copy_ref[...] = blocks[0][...]
+        len_ref, wide_ref, own_ref = refs[:3]
+        blocks = refs[3 : 3 + count]
+        out_ref, e_all, g_all, q_rows, c_rows = refs[3 + count :]
     else:
         q_rows, c_rows = refs[:2]
-        blocks, own = refs[2 : 2 + count], ()
+        blocks = refs[2 : 2 + count]
         out_ref, e_all, g_all = refs[2 + count :]
     width, resp = q_rows.shape[1], q_rows.shape[0] // heads
     rate = math.log2(math.e) / math.sqrt(width)
     s_buf = (s0, s1)
-    prompt = load_rows(blocks, own, k_all, v_all, share)
     keys = k_all.shape[0]
+    prompt = load_rows(blocks, k_all, v_all, share)
     if opening:
+        k_all[prompt:, :] = own_ref[0]
+        v_all[prompt:, :] = own_ref[1]
         live = lax.broadcasted_iota(jnp.int32, (resp, width), 0) < len_ref[0]
 
     for t in range(heads + 1):
@@ -84,8 +82,8 @@
             rows = slice(t * resp, (t + 1) * resp)
             if opening:
                 lanes = slice(t * width, (t + 1) * width)
-                q_rows[rows, :] = q_ref[0, :, lanes]
-                c_rows[rows, :] = jnp.where(live, c_ref[0, :, lanes], jnp.zeros((), BF16))
+                q_rows[rows, :] = wide_ref[0, :, lanes]
+                c_rows[rows, :] = jnp.where(live, wide_ref[1, :, lanes], jnp.zeros((), BF16))
             s_buf[t % 2][...] = dot_nt(k_all[...], q_rows[rows, :])
             g_all[:, rows] = dot_nt(v_all[...], c_rows[rows, :])
         if t > 0:
@@ -188,24 +186,17 @@
             at += share
 
 
-def count_keys(blocks, share, own):
-    return share * sum(b.shape[0] // (2 * share + PAD) for b in blocks) + (
-        own[0].shape[1] if own else 0
-    )
-
-
 def forward_stats(heads, share, blocks, rows=(), opening=()):
     if opening:
-        lengths, queries, grad_out, *own = opening
-        resp, width = queries.shape[1], queries.shape[2] // heads
-        operands = (lengths, queries, grad_out, *blocks, *own)
+        resp, width = opening[1].shape[1], opening[2].shape[2]
+        operands = (*opening, *blocks)
         specs = [SMEM_SPEC] + [VMEM_SPEC] * (len(operands) - 1)
     else:
-        own = ()
         resp, width = rows[0].shape[0] // heads, rows[0].shape[1]
         operands = (*rows, *blocks)
         specs = [VMEM_SPEC] * len(operands)
-    keys = count_keys(blocks, share, own)
+    keys = share * sum(block.shape[0] // (2 * share + PAD) for block in blocks)
+    keys += resp if opening else 0
     outs = [
         jax.ShapeDtypeStruct((4 * heads, resp), F32),
         jax.ShapeDtypeStruct((keys, heads * resp), BF16),
@@ -213,7 +204,6 @@
     ]
     if opening:
         outs += [jax.ShapeDtypeStruct((heads * resp, width), BF16)] * 2
-        outs += [jax.ShapeDtypeStruct(blocks[0].shape, BF16)]
     return pl.pallas_call(
         functools.partial(forward_kernel, heads, share, len(blocks), bool(opening)),
         out_shape=tuple(outs),
@@ -262,12 +252,17 @@
     )(rewards, *operands, *after)
 
 
-def send(block, plane, step):
-    pairs = [
-        (y * RING + z, (y + plane) % 2 * RING + (z + step) % RING)
-        for y in range(2)
-        for z in range(RING)
-    ]
+def across(block):
+    pairs = [(i, (i + RING) % (2 * RING)) for i in range(2 * RING)]
+    return lax.ppermute(block, "sample", pairs)
+
+
+def along(block, side):
+    pairs = []
+    for y in range(2):
+        for z in range(RING):
+            other = (z + (1 if z % 2 == side else -1)) % RING
+            pairs.append((y * RING + z, y * RING + other))
     return lax.ppermute(block, "sample", pairs)
 
 
@@ -279,17 +274,20 @@
     reward_rows = jnp.broadcast_to(rewards.astype(BF16)[:, None], (PAD, width))
     packed = jnp.concatenate([prompt_keys, prompt_values, reward_rows], axis=0)
 
-    swapped = send(packed, 1, 0)
-    first, *keep, q_rows, c_rows, packed = forward_stats(
-        heads, share, [packed], opening=(lengths, queries, grad_out, resp_keys, resp_values)
+    swapped = across(packed)
+    wide_rows = jnp.concatenate([queries, grad_out], axis=0)
+    own_rows = jnp.concatenate([resp_keys, resp_values], axis=0)
+    first, *keep, q_rows, c_rows = forward_stats(
+        heads, share, [packed], opening=(lengths, wide_rows, own_rows)
     )
     rows, stats, kept = (q_rows, c_rows), [first], [keep]
-    pairs = {0: jnp.concatenate([packed, swapped], axis=0)}
+    both = jnp.concatenate([packed, swapped], axis=0)
+    far, near = [both], [both]
     for step in (1, 2, 3, 4):
-        pairs[step] = send(pairs[step - 1], 0, 1)
+        far.append(along(far[-1], (step - 1) % 2))
         if step < 4:
-            pairs[RING - step] = send(pairs[(RING - step + 1) % RING], 0, -1)
-    for blocks in ([swapped], [pairs[1], pairs[7]], [pairs[2], pairs[6]], [pairs[3], pairs[5]], [pairs[4]]):
+            near.append(along(near[-1], step % 2))
+    for blocks in ([swapped], [far[1], near[1]], [far[2], near[2]], [far[3], near[3]], [far[4]]):
         stat, *keep = forward_stats(heads, share, blocks, rows)
         stats.append(stat)
         kept.append(keep)
@@ -304,27 +302,27 @@
     def add(received, part):
         return (received.astype(F32) + part).astype(BF16)
 
-    dq, down = back(((5, 0, 2 * share),), [pairs[4]], [ready], prior=None, after=())
+    dq, down = back(((5, 0, 2 * share),), [far[4]], [ready], prior=None, after=())
     dq, part, up = back(
-        ((4, 0, 4 * share),), [pairs[3], pairs[5]], [wide, ready], prior=dq, after=()
-    )
-    down = add(send(down, 0, -1), part)
+        ((4, 0, 4 * share),), [far[3], near[3]], [wide, ready], prior=dq, after=()
+    )
+    down = add(along(down, 1), part)
     for step in (2, 1):
         dq, part_down, part_up = back(
-            ((step + 1, 0, 4 * share),), [pairs[step], pairs[RING - step]], [wide, wide],
+            ((step + 1, 0, 4 * share),), [far[step], near[step]], [wide, wide],
             prior=dq, after=(down, up),
         )
-        down = add(send(down, 0, -1), part_down)
-        up = add(send(up, 0, 1), part_up)
+        up = add(along(up, (step + 1) % 2), part_up)
+        down = add(along(down, step % 2), part_down)
     dq, mine = back(
         ((0, 0, share), (1, 0, share)), [packed, swapped], [wide], prior=dq, after=(down, up)
     )
-    mine = mine + send(down, 0, -1).astype(F32) + send(up, 0, 1).astype(F32)
+    mine = mine + along(up, 1).astype(F32) + along(down, 0).astype(F32)
     partner = mine[2 * share :].astype(BF16)
     grad_queries, grad_resp_keys, grad_resp_values = back(
-        ((0, share, resp),), [resp_keys], [grads, grads], prior=dq, after=(partner,), last=True
-    )
-    theirs = send(partner, 1, 0).astype(F32)
+        ((0, share, resp),), [own_rows], [grads, grads], prior=dq, after=(partner,), last=True
+    )
+    theirs = across(partner).astype(F32)
     return (
         grad_queries, grad_resp_keys, grad_resp_values,
         mine[:share] + theirs[:share], mine[share : 2 * share] + theirs[share:],

time: 70 us -> 66.6 us (0.951)
  local copies, waits for them, and re-layouts: 3.8 us -> 0.89 us
  other arithmetic: 1.76 us -> 2.99 us
  starting transfers between devices: 27.1 us -> 25.9 us
    unnamed x11 -> x7, local copies, waits for them, and re-layouts: 3.77 us -> 0.86 us
    concatenate x0 -> x2, other arithmetic: none -> 1.31 us  [the longest x1 1.3 us: shards(): wide_rows = jnp.concatenate([queries, grad_out], axis=0)]
    ppermute x16, starting transfers between devices: 27.1 us -> 25.9 us  [the longest x14 23.1 us: along(): return lax.ppermute(block, 'sample', pairs)]
  transfers between devices with their start and end apart: 16 -> 16, of which waited for: 11 -> 10; matrix products, arithmetic and copies ran while one was open for 0% -> 4% of each run, Pallas kernels for 28% -> 29%
where the time goes in v7:
time: 66.6 us; the launch traced here: 66 us
  starting transfers between devices  25.9 us (39%)
  Pallas kernels  21.2 us (32%)
  waiting for transfers between devices  12.8 us (19%)
  other arithmetic  2.99 us (4%)
  between operations  2.2 us (3%)
  local copies, waits for them, and re-layouts  0.89 us (1%)
    ppermute x14, starting transfers between devices, along(): return lax.ppermute(block, 'sample', pairs)  23.1 us
    ppermute x14, waiting for transfers between devices, along(): return lax.ppermute(block, 'sample', pairs)  11.8 us
    pallas_call x6, Pallas kernels, backward_grads(): pl.pallas_call(functools.partial(backward_kernel, heads, share, owners, l...  10.9 us
    pallas_call x6, Pallas kernels, forward_stats(): pl.pallas_call(functools.partial(forward_kernel, heads, share, len(blocks...  10.3 us
    ppermute x2, starting transfers between devices, across(): return lax.ppermute(block, 'sample', pairs)  2.87 us
  transfers between devices with their start and end apart: 16, of which 10 were waited for; matrix products, arithmetic and copies ran while one was open for 4% of the time, Pallas kernels for 29%

profile of v7, /device:TPU:2, one launch (start us, length us, event | category | flops | bytes accessed | tf_op | source)
XLA Modules:
  0.0 66.0 jit_solution(10188419765535521270)
XLA Ops:
  2.1 1.6 %collective-permute-start = (bf16[272,128]{1,0:T(8,128)(2,1)S(1)}, bf16[272,128]{1,0:T(8,128)(2,1)S(1)}, u32[]{:S(2)}, u32[]{:S(2)}) collective-permute-start(bf16[272,128]{1,0:T(8,128)(2,1)S(1)} %pad_maximum_fusion.2.refs_3_.refs_13_), channel_id=1, source_target_pairs={{0,8},{1,9},{2,10},{3,11},{4,12},{5,13},{6,14},{7,15},{8,0},{9,1},... | collective-permute-start | bytes 208904 | tf_op jit(solution)/shard_map/ppermute | solution.py:257
  4.4 0.8 %constant_dynamic-update-slice_fusion.1 = bf16[2,256,128]{2,1,0:T(8,128)(2,1)S(1)} fusion(bf16[1,256,128]{2,1,0:T(8,128)(2,1)} %param.9), kind=kLoop, calls=%fused_computation.13 | loop fusion | bytes 131072
  5.2 1.3 %pad_maximum_fusion.refs_1_ = bf16[2,256,1024]{2,1,0:T(8,128)(2,1)S(1)} fusion(bf16[1,256,1024]{2,1,0:T(8,128)(2,1)} %param.13, bf16[1,256,1024]{2,1,0:T(8,128)(2,1)} %param.8), kind=kLoop, calls=%fused_computation | loop fusion | flops 524288 | bytes 2097152 | tf_op jit(solution)/shard_map/concatenate | solution.py:278
  6.6 2.0 %collective-permute-start.1 = (bf16[544,128]{1,0:T(8,128)(2,1)S(1)}, bf16[544,128]{1,0:T(8,128)(2,1)S(1)}, u32[]{:S(2)}, u32[]{:S(2)}) collective-permute-start(bf16[544,128]{1,0:T(8,128)(2,1)S(1)} %pad_maximum_fusion.1), channel_id=1, source_target_pairs={{0,1},{1,0},{2,3},{3,2},{4,5},{5,4},{6,7},{7,6},{8,9},{9,8},{10,11... | collective-permute-start | bytes 417800 | tf_op jit(solution)/shard_map/ppermute | solution.py:266
  8.6 4.9 %collective-permute-start.2 = (bf16[544,128]{1,0:T(8,128)(2,1)S(1)}, bf16[544,128]{1,0:T(8,128)(2,1)S(1)}, u32[]{:S(2)}, u32[]{:S(2)}) collective-permute-start(bf16[544,128]{1,0:T(8,128)(2,1)S(1)} %pad_maximum_fusion.1), channel_id=1, source_target_pairs={{0,7},{1,2},{2,1},{3,4},{4,3},{5,6},{6,5},{7,0},{8,15},{9,10},{10,... | collective-permute-start | bytes 417800 | tf_op jit(solution)/shard_map/ppermute | solution.py:266
  13.6 1.5 %forward_stats.6 = (f32[32,256]{1,0:T(8,128)S(1)}, bf16[384,2048]{1,0:T(8,128)(2,1)S(1)}, f32[384,2048]{1,0:T(8,128)S(1)}, bf16[2048,128]{1,0:T(8,128)(2,1)S(1)}, bf16[2048,128]{1,0:T(8,128)(2,1)S(1)}) custom-call(s32[1]{0:T(128)S(6)} %copy.14.refs_0_, bf16[2,256,1024]{2,1,0:T(8,128)(2,1)S(1)} %pad_maximum_fusion.refs_1_, ...), custom_call_target="tpu_custom_call" | custom-call | flops 1207959552 | bytes 1048576 | tf_op jit(solution)/shard_map/forward_stats/pallas_call | solution.py:207
  15.7 2.0 %collective-permute-start.3 = (bf16[544,128]{1,0:T(8,128)(2,1)S(1)}, bf16[544,128]{1,0:T(8,128)(2,1)S(1)}, u32[]{:S(2)}, u32[]{:S(2)}) collective-permute-start(bf16[544,128]{1,0:T(8,128)(2,1)S(1)} %collective-permute-done.1.refs_2_.refs_11_), channel_id=1, source_target_pairs={{0,7},{1,2},{2,1},{3,4},{4,3},{5,6},{6,5},{7,0},{8,15},{9,10},{10,... | collective-permute-start | bytes 417800 | tf_op jit(solution)/shard_map/ppermute | solution.py:266
  17.7 2.4 %forward_stats.8 = (f32[32,256]{1,0:T(8,128)S(1)}, bf16[512,2048]{1,0:T(8,128)(2,1)S(1)}, f32[512,2048]{1,0:T(8,128)S(1)}) custom-call(bf16[2048,128]{1,0:T(8,128)(2,1)S(1)} %get-tuple-element.41.refs_0_.refs_1_, bf16[2048,128]{1,0:T(8,128)(2,1)S(1)} %get-tuple-element.42.refs_1_.refs_2_, bf16[544,128]{1,0:T(8,128)(2,1)S(1)} %collective-permute-done.1.refs_2_.refs_11_, ...), custom_call_target="tpu_custom_call" | custom-call | flops 1610612736 | bytes 1048576 | tf_op jit(solution)/shard_map/forward_stats/pallas_call | solution.py:207
  20.1 1.9 %collective-permute-done.3.refs_2_.refs_11_ = bf16[544,128]{1,0:T(8,128)(2,1)S(1)} collective-permute-done((bf16[544,128]{1,0:T(8,128)(2,1)S(1)}, bf16[544,128]{1,0:T(8,128)(2,1)S(1)}, u32[]{:S(2)}, u32[]{:S(2)}) %collective-permute-start.3) | collective-permute-done | bytes 139296 | tf_op jit(solution)/shard_map/ppermute | solution.py:266
  23.0 2.8 %collective-permute-start.6 = (bf16[544,128]{1,0:T(8,128)(2,1)S(1)}, bf16[544,128]{1,0:T(8,128)(2,1)S(1)}, u32[]{:S(2)}, u32[]{:S(2)}) collective-permute-start(bf16[544,128]{1,0:T(8,128)(2,1)S(1)} %collective-permute-done.4.refs_3_.refs_12_), channel_id=1, source_target_pairs={{0,7},{1,2},{2,1},{3,4},{4,3},{5,6},{6,5},{7,0},{8,15},{9,10},{10,... | collective-permute-start | bytes 417800 | tf_op jit(solution)/shard_map/ppermute | solution.py:266
  25.8 2.4 %forward_stats.9 = (f32[32,256]{1,0:T(8,128)S(1)}, bf16[512,2048]{1,0:T(8,128)(2,1)S(1)}, f32[512,2048]{1,0:T(8,128)S(1)}) custom-call(bf16[2048,128]{1,0:T(8,128)(2,1)S(1)} %get-tuple-element.41.refs_0_.refs_1_, bf16[2048,128]{1,0:T(8,128)(2,1)S(1)} %get-tuple-element.42.refs_1_.refs_2_, bf16[544,128]{1,0:T(8,128)(2,1)S(1)} %collective-permute-done.3.refs_2_.refs_11_, ...), custom_call_target="tpu_custom_call" | custom-call | flops 1610612736 | bytes 1048576 | tf_op jit(solution)/shard_map/forward_stats/pallas_call | solution.py:207
  28.2 0.8 %collective-permute-start.7 = (bf16[544,128]{1,0:T(8,128)(2,1)S(1)}, bf16[544,128]{1,0:T(8,128)(2,1)S(1)}, u32[]{:S(2)}, u32[]{:S(2)}) collective-permute-start(bf16[544,128]{1,0:T(8,128)(2,1)S(1)} %collective-permute-done.5.refs_2_.refs_11_), channel_id=1, source_target_pairs={{0,7},{1,2},{2,1},{3,4},{4,3},{5,6},{6,5},{7,0},{8,15},{9,10},{10,... | collective-permute-start | bytes 417800 | tf_op jit(solution)/shard_map/ppermute | solution.py:266
  29.0 1.5 %collective-permute-done.6.refs_3_.refs_12_ = bf16[544,128]{1,0:T(8,128)(2,1)S(1)} collective-permute-done((bf16[544,128]{1,0:T(8,128)(2,1)S(1)}, bf16[544,128]{1,0:T(8,128)(2,1)S(1)}, u32[]{:S(2)}, u32[]{:S(2)}) %collective-permute-start.6) | collective-permute-done | bytes 139296 | tf_op jit(solution)/shard_map/ppermute | solution.py:266
  30.5 2.4 %forward_stats.10 = (f32[32,256]{1,0:T(8,128)S(1)}, bf16[512,2048]{1,0:T(8,128)(2,1)S(1)}, f32[512,2048]{1,0:T(8,128)S(1)}) custom-call(bf16[2048,128]{1,0:T(8,128)(2,1)S(1)} %get-tuple-element.41.refs_0_.refs_1_, bf16[2048,128]{1,0:T(8,128)(2,1)S(1)} %get-tuple-element.42.refs_1_.refs_2_, bf16[544,128]{1,0:T(8,128)(2,1)S(1)} %collective-permute-done.5.refs_2_.refs_11_, ...), custom_call_target="tpu_custom_call" | custom-call | flops 1610612736 | bytes 1048576 | tf_op jit(solution)/shard_map/forward_stats/pallas_call | solution.py:207
  32.9 1.9 %collective-permute-done.7.refs_2_.refs_11_ = bf16[544,128]{1,0:T(8,128)(2,1)S(1)} collective-permute-done((bf16[544,128]{1,0:T(8,128)(2,1)S(1)}, bf16[544,128]{1,0:T(8,128)(2,1)S(1)}, u32[]{:S(2)}, u32[]{:S(2)}) %collective-permute-start.7) | collective-permute-done | bytes 139296 | tf_op jit(solution)/shard_map/ppermute | solution.py:266
  34.7 1.0 %forward_stats.11 = (f32[32,256]{1,0:T(8,128)S(1)}, bf16[256,2048]{1,0:T(8,128)(2,1)S(1)}, f32[256,2048]{1,0:T(8,128)S(1)}) custom-call(bf16[2048,128]{1,0:T(8,128)(2,1)S(1)} %get-tuple-element.41.refs_0_.refs_1_, bf16[2048,128]{1,0:T(8,128)(2,1)S(1)} %get-tuple-element.42.refs_1_.refs_2_, bf16[544,128]{1,0:T(8,128)(2,1)S(1)} %collective-permute-done.7.refs_2_.refs_11_), custom_call_target="tpu_custom_call" | custom-call | flops 805306368 | bytes 1048576 | tf_op jit(solution)/shard_map/forward_stats/pallas_call | solution.py:207
  35.7 1.2 %backward_grads.6 = (f32[1024,256]{1,0:T(8,128)S(1)}, bf16[512,128]{1,0:T(8,128)(2,1)S(1)}) custom-call(s32[1]{0:T(128)S(6)} %copy.15.refs_0_, bf16[2048,128]{1,0:T(8,128)(2,1)S(1)} %get-tuple-element.41.refs_0_.refs_1_, bf16[2048,128]{1,0:T(8,128)(2,1)S(1)} %get-tuple-element.42.refs_1_.refs_2_, f32[32,256]{1,0:T(8,128)S(1)} %get-tuple-element.43.refs_3_, ...), custom_call_target="tpu_custom_call" | custom-call | flops 1342177280 | bytes 2097152 | tf_op jit(solution)/shard_map/backward_grads/pallas_call | solution.py:235
  36.9 0.8 %collective-permute-start.8 = (bf16[512,128]{1,0:T(8,128)(2,1)S(1)}, bf16[512,128]{1,0:T(8,128)(2,1)S(1)}, u32[]{:S(2)}, u32[]{:S(2)}) collective-permute-start(bf16[512,128]{1,0:T(8,128)(2,1)S(1)} %get-tuple-element.63), channel_id=1, source_target_pairs={{0,7},{1,2},{2,1},{3,4},{4,3},{5,6},{6,5},{7,0},{8,15},{9,10},{10,... | collective-permute-start | bytes 393224 | tf_op jit(solution)/shard_map/ppermute | solution.py:266
  37.7 2.1 %backward_grads.7 = (f32[1024,256]{1,0:T(8,128)S(1)}, f32[512,128]{1,0:T(8,128)S(1)}, bf16[512,128]{1,0:T(8,128)(2,1)S(1)}) custom-call(s32[1]{0:T(128)S(6)} %copy.15.refs_0_, bf16[2048,128]{1,0:T(8,128)(2,1)S(1)} %get-tuple-element.41.refs_0_.refs_1_, bf16[2048,128]{1,0:T(8,128)(2,1)S(1)} %get-tuple-element.42.refs_1_.refs_2_, ...), custom_call_target="tpu_custom_call" | custom-call | flops 2684354560 | bytes 2097152 | tf_op jit(solution)/shard_map/backward_grads/pallas_call | solution.py:235
  39.9 2.6 %collective-permute-start.10 = (bf16[512,128]{1,0:T(8,128)(2,1)S(1)}, bf16[512,128]{1,0:T(8,128)(2,1)S(1)}, u32[]{:S(2)}, u32[]{:S(2)}) collective-permute-start(bf16[512,128]{1,0:T(8,128)(2,1)S(1)} %get-tuple-element.65.refs_15_), channel_id=1, source_target_pairs={{0,7},{1,2},{2,1},{3,4},{4,3},{5,6},{6,5},{7,0},{8,15},{9,10},{10,... | collective-permute-start | bytes 393224 | tf_op jit(solution)/shard_map/ppermute | solution.py:266
  42.5 1.0 %collective-permute-done.8 = bf16[512,128]{1,0:T(8,128)(2,1)S(1)} collective-permute-done((bf16[512,128]{1,0:T(8,128)(2,1)S(1)}, bf16[512,128]{1,0:T(8,128)(2,1)S(1)}, u32[]{:S(2)}, u32[]{:S(2)}) %collective-permute-start.8) | collective-permute-done | bytes 131104 | tf_op jit(solution)/shard_map/ppermute | solution.py:266
  43.7 2.1 %backward_grads.8 = (f32[1024,256]{1,0:T(8,128)S(1)}, f32[512,128]{1,0:T(8,128)S(1)}, f32[512,128]{1,0:T(8,128)S(1)}) custom-call(s32[1]{0:T(128)S(6)} %copy.15.refs_0_, bf16[2048,128]{1,0:T(8,128)(2,1)S(1)} %get-tuple-element.41.refs_0_.refs_1_, bf16[2048,128]{1,0:T(8,128)(2,1)S(1)} %get-tuple-element.42.refs_1_.refs_2_, ...), custom_call_target="tpu_custom_call" | custom-call | flops 2684354560 | bytes 2097152 | tf_op jit(solution)/shard_map/backward_grads/pallas_call | solution.py:235
  46.2 1.8 %collective-permute-start.12 = (bf16[512,128]{1,0:T(8,128)(2,1)S(1)}, bf16[512,128]{1,0:T(8,128)(2,1)S(1)}, u32[]{:S(2)}, u32[]{:S(2)}) collective-permute-start(bf16[512,128]{1,0:T(8,128)(2,1)S(1)} %add_convert_fusion.2.refs_15_), channel_id=1, source_target_pairs={{0,1},{1,0},{2,3},{3,2},{4,5},{5,4},{6,7},{7,6},{8,9},{9,8},{10,11... | collective-permute-start | bytes 393224 | tf_op jit(solution)/shard_map/ppermute | solution.py:266
  48.6 1.2 %collective-permute-start.11 = (bf16[512,128]{1,0:T(8,128)(2,1)S(1)}, bf16[512,128]{1,0:T(8,128)(2,1)S(1)}, u32[]{:S(2)}, u32[]{:S(2)}) collective-permute-start(bf16[512,128]{1,0:T(8,128)(2,1)S(1)} %add_convert_fusion.3.refs_14_), channel_id=1, source_target_pairs={{0,7},{1,2},{2,1},{3,4},{4,3},{5,6},{6,5},{7,0},{8,15},{9,10},{10,... | collective-permute-start | bytes 393224 | tf_op jit(solution)/shard_map/ppermute | solution.py:266
  49.9 2.1 %backward_grads.9 = (f32[1024,256]{1,0:T(8,128)S(1)}, f32[512,128]{1,0:T(8,128)S(1)}, f32[512,128]{1,0:T(8,128)S(1)}) custom-call(s32[1]{0:T(128)S(6)} %copy.15.refs_0_, bf16[2048,128]{1,0:T(8,128)(2,1)S(1)} %get-tuple-element.41.refs_0_.refs_1_, bf16[2048,128]{1,0:T(8,128)(2,1)S(1)} %get-tuple-element.42.refs_1_.refs_2_, ...), custom_call_target="tpu_custom_call" | custom-call | flops 2684354560 | bytes 2097152 | tf_op jit(solution)/shard_map/backward_grads/pallas_call | solution.py:235
  52.1 3.7 %collective-permute-start.13 = (bf16[512,128]{1,0:T(8,128)(2,1)S(1)}, bf16[512,128]{1,0:T(8,128)(2,1)S(1)}, u32[]{:S(2)}, u32[]{:S(2)}) collective-permute-start(bf16[512,128]{1,0:T(8,128)(2,1)S(1)} %add_convert_fusion.refs_17_), channel_id=1, source_target_pairs={{0,7},{1,2},{2,1},{3,4},{4,3},{5,6},{6,5},{7,0},{8,15},{9,10},{10,... | collective-permute-start | bytes 393224 | tf_op jit(solution)/shard_map/ppermute | solution.py:266
  55.9 1.2 %backward_grads.10 = (f32[1024,256]{1,0:T(8,128)S(1)}, f32[512,128]{1,0:T(8,128)S(1)}) custom-call(s32[1]{0:T(128)S(6)} %copy.15.refs_0_, bf16[2048,128]{1,0:T(8,128)(2,1)S(1)} %get-tuple-element.41.refs_0_.refs_1_, bf16[2048,128]{1,0:T(8,128)(2,1)S(1)} %get-tuple-element.42.refs_1_.refs_2_, f32[32,256]{1,0:T(8,128)S(1)} %get-tuple-element.43.refs_3_, ...), custom_call_target="tpu_custom_call" | custom-call | flops 1342177280 | bytes 2097152 | tf_op jit(solution)/shard_map/backward_grads/pallas_call | solution.py:235
  57.1 1.6 %collective-permute-done.13 = bf16[512,128]{1,0:T(8,128)(2,1)S(1)} collective-permute-done((bf16[512,128]{1,0:T(8,128)(2,1)S(1)}, bf16[512,128]{1,0:T(8,128)(2,1)S(1)}, u32[]{:S(2)}, u32[]{:S(2)}) %collective-permute-start.13) | collective-permute-done | bytes 131104 | tf_op jit(solution)/shard_map/ppermute | solution.py:266
  58.7 2.2 %collective-permute-done.14 = bf16[512,128]{1,0:T(8,128)(2,1)S(1)} collective-permute-done((bf16[512,128]{1,0:T(8,128)(2,1)S(1)}, bf16[512,128]{1,0:T(8,128)(2,1)S(1)}, u32[]{:S(2)}, u32[]{:S(2)}) %collective-permute-start.14) | collective-permute-done | bytes 131104 | tf_op jit(solution)/shard_map/ppermute | solution.py:266
  60.9 1.3 %collective-permute-start.15 = (bf16[256,128]{1,0:T(8,128)(2,1)S(1)}, bf16[256,128]{1,0:T(8,128)(2,1)S(1)}, u32[]{:S(2)}, u32[]{:S(2)}) collective-permute-start(bf16[256,128]{1,0:T(8,128)(2,1)S(1)} %slice.31.refs_13_), channel_id=1, source_target_pairs={{0,8},{1,9},{2,10},{3,11},{4,12},{5,13},{6,14},{7,15},{8,0},{9,1},... | collective-permute-start | bytes 196616 | tf_op jit(solution)/shard_map/ppermute | solution.py:257
  62.2 2.1 %backward_grads.11 = (f32[1,256,1024]{2,1,0:T(8,128)}, f32[1,256,128]{2,1,0:T(8,128)}, f32[1,256,128]{2,1,0:T(8,128)}) custom-call(s32[1]{0:T(128)S(6)} %copy.15.refs_0_, bf16[2048,128]{1,0:T(8,128)(2,1)S(1)} %get-tuple-element.41.refs_0_.refs_1_, bf16[2048,128]{1,0:T(8,128)(2,1)S(1)} %get-tuple-element.42.refs_1_.refs_2_, ...), custom_call_target="tpu_custom_call" | custom-call | flops 1342177280 | bytes 2097152 | tf_op jit(solution)/shard_map/backward_grads/pallas_call | solution.py:235
  64.3 0.9 %collective-permute-done.15 = bf16[256,128]{1,0:T(8,128)(2,1)S(1)} collective-permute-done((bf16[256,128]{1,0:T(8,128)(2,1)S(1)}, bf16[256,128]{1,0:T(8,128)(2,1)S(1)}, u32[]{:S(2)}, u32[]{:S(2)}) %collective-permute-start.15) | collective-permute-done | bytes 65568 | tf_op jit(solution)/shard_map/ppermute | solution.py:257
  (33 shorter events, 4.4 us)
Async XLA Ops:
  0.6 5.9 %copy-start = (bf16[128,128]{1,0:T(8,128)(2,1)S(1)}, bf16[128,128]{1,0:T(8,128)(2,1)}, u32[]{:S(2)}) copy-start(bf16[128,128]{1,0:T(8,128)(2,1)} %param.12) | copy-start | bytes 98308
  0.6 5.9 %copy-start.1 = (bf16[128,128]{1,0:T(8,128)(2,1)S(1)}, bf16[128,128]{1,0:T(8,128)(2,1)}, u32[]{:S(2)}) copy-start(bf16[128,128]{1,0:T(8,128)(2,1)} %param.11) | copy-start | bytes 98308
  0.7 5.9 %copy-start.2 = (bf16[1,256,128]{2,1,0:T(8,128)(2,1)S(1)}, bf16[1,256,128]{2,1,0:T(8,128)(2,1)}, u32[]{:S(2)}) copy-start(bf16[1,256,128]{2,1,0:T(8,128)(2,1)} %param.10) | copy-start | bytes 196612
  2.1 4.4 %collective-permute-start = (bf16[272,128]{1,0:T(8,128)(2,1)S(1)}, bf16[272,128]{1,0:T(8,128)(2,1)S(1)}, u32[]{:S(2)}, u32[]{:S(2)}) collective-permute-start(bf16[272,128]{1,0:T(8,128)(2,1)S(1)} %pad_maximum_fusion.2.refs_3_.refs_13_), channel_id=1, source_target_pairs={{0,8},{1,9},{2,10},{3,11},{4,12},{5,13},{6,14},{7,15},{8,0},{9,1},... | collective-permute-start | bytes 208904 | tf_op jit(solution)/shard_map/ppermute | solution.py:257
  6.6 9.1 %collective-permute-start.1 = (bf16[544,128]{1,0:T(8,128)(2,1)S(1)}, bf16[544,128]{1,0:T(8,128)(2,1)S(1)}, u32[]{:S(2)}, u32[]{:S(2)}) collective-permute-start(bf16[544,128]{1,0:T(8,128)(2,1)S(1)} %pad_maximum_fusion.1), channel_id=1, source_target_pairs={{0,1},{1,0},{2,3},{3,2},{4,5},{5,4},{6,7},{7,6},{8,9},{9,8},{10,11... | collective-permute-start | bytes 417800 | tf_op jit(solution)/shard_map/ppermute | solution.py:266
  8.6 9.1 %collective-permute-start.2 = (bf16[544,128]{1,0:T(8,128)(2,1)S(1)}, bf16[544,128]{1,0:T(8,128)(2,1)S(1)}, u32[]{:S(2)}, u32[]{:S(2)}) collective-permute-start(bf16[544,128]{1,0:T(8,128)(2,1)S(1)} %pad_maximum_fusion.1), channel_id=1, source_target_pairs={{0,7},{1,2},{2,1},{3,4},{4,3},{5,6},{6,5},{7,0},{8,15},{9,10},{10,... | collective-permute-start | bytes 417800 | tf_op jit(solution)/shard_map/ppermute | solution.py:266
  15.7 6.4 %collective-permute-start.3 = (bf16[544,128]{1,0:T(8,128)(2,1)S(1)}, bf16[544,128]{1,0:T(8,128)(2,1)S(1)}, u32[]{:S(2)}, u32[]{:S(2)}) collective-permute-start(bf16[544,128]{1,0:T(8,128)(2,1)S(1)} %collective-permute-done.1.refs_2_.refs_11_), channel_id=1, source_target_pairs={{0,7},{1,2},{2,1},{3,4},{4,3},{5,6},{6,5},{7,0},{8,15},{9,10},{10,... | collective-permute-start | bytes 417800 | tf_op jit(solution)/shard_map/ppermute | solution.py:266
  17.7 5.3 %collective-permute-start.4 = (bf16[544,128]{1,0:T(8,128)(2,1)S(1)}, bf16[544,128]{1,0:T(8,128)(2,1)S(1)}, u32[]{:S(2)}, u32[]{:S(2)}) collective-permute-start(bf16[544,128]{1,0:T(8,128)(2,1)S(1)} %collective-permute-done.2.refs_3_.refs_12_), channel_id=1, source_target_pairs={{0,1},{1,0},{2,3},{3,2},{4,5},{5,4},{6,7},{7,6},{8,9},{9,8},{10,11... | collective-permute-start | bytes 417800 | tf_op jit(solution)/shard_map/ppermute | solution.py:266
  22.0 6.1 %collective-permute-start.5 = (bf16[544,128]{1,0:T(8,128)(2,1)S(1)}, bf16[544,128]{1,0:T(8,128)(2,1)S(1)}, u32[]{:S(2)}, u32[]{:S(2)}) collective-permute-start(bf16[544,128]{1,0:T(8,128)(2,1)S(1)} %collective-permute-done.3.refs_2_.refs_11_), channel_id=1, source_target_pairs={{0,1},{1,0},{2,3},{3,2},{4,5},{5,4},{6,7},{7,6},{8,9},{9,8},{10,11... | collective-permute-start | bytes 417800 | tf_op jit(solution)/shard_map/ppermute | solution.py:266
  23.0 7.5 %collective-permute-start.6 = (bf16[544,128]{1,0:T(8,128)(2,1)S(1)}, bf16[544,128]{1,0:T(8,128)(2,1)S(1)}, u32[]{:S(2)}, u32[]{:S(2)}) collective-permute-start(bf16[544,128]{1,0:T(8,128)(2,1)S(1)} %collective-permute-done.4.refs_3_.refs_12_), channel_id=1, source_target_pairs={{0,7},{1,2},{2,1},{3,4},{4,3},{5,6},{6,5},{7,0},{8,15},{9,10},{10,... | collective-permute-start | bytes 417800 | tf_op jit(solution)/shard_map/ppermute | solution.py:266
  28.2 6.5 %collective-permute-start.7 = (bf16[544,128]{1,0:T(8,128)(2,1)S(1)}, bf16[544,128]{1,0:T(8,128)(2,1)S(1)}, u32[]{:S(2)}, u32[]{:S(2)}) collective-permute-start(bf16[544,128]{1,0:T(8,128)(2,1)S(1)} %collective-permute-done.5.refs_2_.refs_11_), channel_id=1, source_target_pairs={{0,7},{1,2},{2,1},{3,4},{4,3},{5,6},{6,5},{7,0},{8,15},{9,10},{10,... | collective-permute-start | bytes 417800 | tf_op jit(solution)/shard_map/ppermute | solution.py:266
  36.9 6.6 %collective-permute-start.8 = (bf16[512,128]{1,0:T(8,128)(2,1)S(1)}, bf16[512,128]{1,0:T(8,128)(2,1)S(1)}, u32[]{:S(2)}, u32[]{:S(2)}) collective-permute-start(bf16[512,128]{1,0:T(8,128)(2,1)S(1)} %get-tuple-element.63), channel_id=1, source_target_pairs={{0,7},{1,2},{2,1},{3,4},{4,3},{5,6},{6,5},{7,0},{8,15},{9,10},{10,... | collective-permute-start | bytes 393224 | tf_op jit(solution)/shard_map/ppermute | solution.py:266
  39.9 6.3 %collective-permute-start.10 = (bf16[512,128]{1,0:T(8,128)(2,1)S(1)}, bf16[512,128]{1,0:T(8,128)(2,1)S(1)}, u32[]{:S(2)}, u32[]{:S(2)}) collective-permute-start(bf16[512,128]{1,0:T(8,128)(2,1)S(1)} %get-tuple-element.65.refs_15_), channel_id=1, source_target_pairs={{0,7},{1,2},{2,1},{3,4},{4,3},{5,6},{6,5},{7,0},{8,15},{9,10},{10,... | collective-permute-start | bytes 393224 | tf_op jit(solution)/shard_map/ppermute | solution.py:266
  43.6 5.1 %collective-permute-start.9 = (bf16[512,128]{1,0:T(8,128)(2,1)S(1)}, bf16[512,128]{1,0:T(8,128)(2,1)S(1)}, u32[]{:S(2)}, u32[]{:S(2)}) collective-permute-start(bf16[512,128]{1,0:T(8,128)(2,1)S(1)} %add_convert_fusion.4.refs_14_), channel_id=1, source_target_pairs={{0,1},{1,0},{2,3},{3,2},{4,5},{5,4},{6,7},{7,6},{8,9},{9,8},{10,11... | collective-permute-start | bytes 393224 | tf_op jit(solution)/shard_map/ppermute | solution.py:266
  46.2 5.9 %collective-permute-start.12 = (bf16[512,128]{1,0:T(8,128)(2,1)S(1)}, bf16[512,128]{1,0:T(8,128)(2,1)S(1)}, u32[]{:S(2)}, u32[]{:S(2)}) collective-permute-start(bf16[512,128]{1,0:T(8,128)(2,1)S(1)} %add_convert_fusion.2.refs_15_), channel_id=1, source_target_pairs={{0,1},{1,0},{2,3},{3,2},{4,5},{5,4},{6,7},{7,6},{8,9},{9,8},{10,11... | collective-permute-start | bytes 393224 | tf_op jit(solution)/shard_map/ppermute | solution.py:266
  48.6 7.1 %collective-permute-start.11 = (bf16[512,128]{1,0:T(8,128)(2,1)S(1)}, bf16[512,128]{1,0:T(8,128)(2,1)S(1)}, u32[]{:S(2)}, u32[]{:S(2)}) collective-permute-start(bf16[512,128]{1,0:T(8,128)(2,1)S(1)} %add_convert_fusion.3.refs_14_), channel_id=1, source_target_pairs={{0,7},{1,2},{2,1},{3,4},{4,3},{5,6},{6,5},{7,0},{8,15},{9,10},{10,... | collective-permute-start | bytes 393224 | tf_op jit(solution)/shard_map/ppermute | solution.py:266
  52.1 6.6 %collective-permute-start.13 = (bf16[512,128]{1,0:T(8,128)(2,1)S(1)}, bf16[512,128]{1,0:T(8,128)(2,1)S(1)}, u32[]{:S(2)}, u32[]{:S(2)}) collective-permute-start(bf16[512,128]{1,0:T(8,128)(2,1)S(1)} %add_convert_fusion.refs_17_), channel_id=1, source_target_pairs={{0,7},{1,2},{2,1},{3,4},{4,3},{5,6},{6,5},{7,0},{8,15},{9,10},{10,... | collective-permute-start | bytes 393224 | tf_op jit(solution)/shard_map/ppermute | solution.py:266
  55.8 5.1 %collective-permute-start.14 = (bf16[512,128]{1,0:T(8,128)(2,1)S(1)}, bf16[512,128]{1,0:T(8,128)(2,1)S(1)}, u32[]{:S(2)}, u32[]{:S(2)}) collective-permute-start(bf16[512,128]{1,0:T(8,128)(2,1)S(1)} %add_convert_fusion.1.refs_16_), channel_id=1, source_target_pairs={{0,1},{1,0},{2,3},{3,2},{4,5},{5,4},{6,7},{7,6},{8,9},{9,8},{10,11... | collective-permute-start | bytes 393224 | tf_op jit(solution)/shard_map/ppermute | solution.py:266
  60.9 4.4 %collective-permute-start.15 = (bf16[256,128]{1,0:T(8,128)(2,1)S(1)}, bf16[256,128]{1,0:T(8,128)(2,1)S(1)}, u32[]{:S(2)}, u32[]{:S(2)}) collective-permute-start(bf16[256,128]{1,0:T(8,128)(2,1)S(1)} %slice.31.refs_13_), channel_id=1, source_target_pairs={{0,8},{1,9},{2,10},{3,11},{4,12},{5,13},{6,14},{7,15},{8,0},{9,1},... | collective-permute-start | bytes 196616 | tf_op jit(solution)/shard_map/ppermute | solution.py:257

commit v8 on v5

--- a/solution.py
+++ b/solution.py
@@ -118,6 +118,23 @@
     out_ref[3 * heads :, :] = jnp.broadcast_to(jnp.max(paid), (heads, resp))
 
 
+def merge_stats(stat_refs, pay_ref, merged_ref, heads, owners, width):
+    rate = math.log2(math.e) / math.sqrt(width)
+    peaks = [ref[:heads, :] for ref in stat_refs]
+    peak = functools.reduce(jnp.maximum, peaks)
+    weights = [jnp.exp2((local - peak) * rate) for local in peaks]
+    mass, mixed, paid = 0.0, 0.0, 0.0
+    for ref, weight in zip(stat_refs, weights):
+        mass = mass + ref[heads : 2 * heads, :] * weight
+        mixed = mixed + ref[2 * heads : 3 * heads, :] * weight
+        paid = paid + ref[3 * heads :, :]
+    for i, weight in enumerate(weights):
+        merged_ref[i * heads : (i + 1) * heads, :] = weight / mass
+    at = len(weights) * heads
+    merged_ref[at : at + heads, :] = mixed / mass
+    merged_ref[at + heads :, :] = pay_ref[0].astype(F32) - paid / owners
+
+
 def backward_kernel(heads, share, owners, picks, stats, spans, after, more, last, *refs):
     refs, (k_t, p_all, ds_all) = refs[:-3], refs[-3:]
     pay_ref, q_rows, c_rows = refs[:3]
@@ -130,19 +147,15 @@
     dq_ref, *out_refs = refs[after:]
     width, resp = q_rows.shape[1], q_rows.shape[0] // heads
     scale = 1.0 / math.sqrt(width)
-    rate = scale * math.log2(math.e)
-
-    peaks = [ref[:heads, :] for ref in stat_refs]
-    peak = functools.reduce(jnp.maximum, peaks)
-    weights = [jnp.exp2((local - peak) * rate) for local in peaks]
-    mass, mixed, paid = 0.0, 0.0, 0.0
-    for ref, weight in zip(stat_refs, weights):
-        mass = mass + ref[heads : 2 * heads, :] * weight
-        mixed = mixed + ref[2 * heads : 3 * heads, :] * weight
-        paid = paid + ref[3 * heads :, :]
-    delta = mixed / mass
-    factors = [weights[group] / mass for group, _, _ in spans]
-    advantage = (pay_ref[0].astype(F32) - paid / owners)[:1, :width]
+    if more:
+        (merged_ref,) = stat_refs
+    else:
+        merged_ref = out_refs.pop()
+        merge_stats(stat_refs, pay_ref, merged_ref, heads, owners, width)
+    tail = merged_ref.shape[0] - 2 * heads
+    factors = [merged_ref[group * heads : (group + 1) * heads, :] for group, _, _ in spans]
+    delta = merged_ref[tail : tail + heads, :]
+    advantage = merged_ref[tail + heads : tail + heads + 1, :width]
 
     places = pack_places(blocks, picks, share)
     for i, (ref, at) in enumerate(places):
@@ -150,7 +163,7 @@
     prompt = len(places) * share
     if last:
         k_t[:, prompt:] = own_ref[0].T
-    half = heads // 2
+    ends = [heads // 2, heads - 1, heads]
     dk = dv = None
     for h in range(heads):
         cols = slice(h * resp, (h + 1) * resp)
@@ -170,8 +183,8 @@
             dq_ref[0, :, lanes] = dq.T * (advantage * scale)
         else:
             dq_ref[lanes, :] = dq
-        if h % half == half - 1:
-            block = slice((h + 1 - half) * resp, (h + 1) * resp)
+        if h + 1 in ends:
+            block = slice(([0] + ends)[ends.index(h + 1)] * resp, (h + 1) * resp)
             dk_part = dot_nn(ds_all[:, block], q_rows[block, :])
             dv_part = dot_nn(p_all[:, block], c_rows[block, :])
             dk = dk_part if dk is None else dk + dk_part
@@ -233,6 +246,8 @@
     keys = sum(size for _, _, size in parts)
     dq_shape = (1, resp, heads * width) if last else (heads * width, resp)
     outs = [jax.ShapeDtypeStruct(dq_shape, F32), *outs]
+    if not more:
+        outs.append(jax.ShapeDtypeStruct(((len(stats) + 2) * heads, resp), F32))
     operands = (
         *rows, *stats, *(kept[g][0] for g, _, _ in parts), *(kept[g][1] for g, _, _ in parts),
         *blocks, *last, *((prior,) if more else ()),
@@ -257,19 +272,6 @@
     )(rewards, *operands, *after)
 
 
-def tie(block, after):
-    return pl.pallas_call(
-        lambda block_ref, after_ref, out_ref: None,
-        out_shape=jax.ShapeDtypeStruct(block.shape, block.dtype),
-        in_specs=[ANY_SPEC] * 2,
-        out_specs=ANY_SPEC,
-        input_output_aliases={0: 0},
-        compiler_params=pltpu.CompilerParams(vmem_limit_bytes=1024 * 1024),
-        cost_estimate=pl.CostEstimate(flops=0, bytes_accessed=0, transcendentals=0),
-        name="tie",
-    )(block, after)
-
-
 def across(block):
     pairs = [(i, (i + RING) % (2 * RING)) for i in range(2 * RING)]
     return lax.ppermute(block, "sample", pairs)
@@ -295,39 +297,24 @@
     own_rows = jnp.concatenate([resp_keys, resp_values], axis=0)
     wide_rows = jnp.concatenate([queries, grad_out], axis=0)
 
+    swapped = across(packed)
     first, *keep, q_rows, c_rows = forward_stats(
         heads, share, [packed], opening=(lengths, wide_rows, own_rows)
     )
     rows, stats, kept = (q_rows, c_rows), [first], [keep]
-
-    def forward(*blocks):
+    both = jnp.concatenate([packed, swapped], axis=0)
+    far, near = [both], [both]
+    for step in (1, 2, 3, 4):
+        far.append(along(far[-1], (step - 1) % 2))
+        if step < 4:
+            near.append(along(near[-1], step % 2))
+    for blocks in ([swapped], [far[1], near[1]], [far[2], near[2]], [far[3], near[3]], [far[4]]):
         stat, *keep = forward_stats(heads, share, blocks, rows)
         stats.append(stat)
         kept.append(keep)
 
-    def join(*blocks):
-        return jnp.concatenate(blocks, axis=0)
-
-    l1, r1 = along(packed, 0), along(packed, 1)
-    l2, r2 = along(r1, 0), along(l1, 1)
-    other1 = across(join(tie(packed, stats[-1]), l1, r1))
-    forward(l1, r1)
-    l2, r2 = tie(l2, stats[-1]), tie(r2, stats[-1])
-    l3, r3 = along(r2, 0), along(l2, 1)
-    other2 = across(join(l2, r2))
-    forward(l2, r2)
-    l3, r3 = tie(l3, stats[-1]), tie(r3, stats[-1])
-    l4 = along(r3, 0)
-    other3 = across(join(l3, r3))
-    forward(other1, l3, r3)
-    l4 = tie(l4, stats[-1])
-    other4 = across(l4)
-    forward(other2, l4)
-    forward(other3)
-    forward(other4)
-
     back = functools.partial(
-        backward_grads, rewards, rows, stats, kept, owners=owners, heads=heads, share=share
+        backward_grads, rewards, rows, kept=kept, owners=owners, heads=heads, share=share
     )
     ready = jax.ShapeDtypeStruct((size, width), BF16)
     both_ready = jax.ShapeDtypeStruct((2 * size, width), BF16)
@@ -337,40 +324,46 @@
     def add(part, *received):
         return sum((r.astype(F32) for r in received), part).astype(BF16)
 
-    dq, part = back(((6, 0, share),), [(other4, 0, 1)], [ready], prior=None, after=())
+    def planes(group, plane):
+        return ((group, plane * share, share), (group, size + plane * share, share))
+
+    dq, part, merged = back(
+        stats, parts=((5, share, share),), blocks=[(far[4], 1, 1)], outs=[ready], prior=None,
+        after=(),
+    )
+    back = functools.partial(back, (merged,))
     given = across(part)
-    dq, part, part_left = back(
-        ((5, 0, size), (4, size, share)), [(other3, 0, 2), (l4, 0, 1)], [both_ready, wide],
-        prior=dq, after=(),
-    )
-    far = add(part_left, given)
+    dq, part, part_far = back(
+        parts=(*planes(4, 1), (5, 0, share)),
+        blocks=[(far[3], 1, 1), (near[3], 1, 1), (far[4], 0, 1)],
+        outs=[both_ready, wide], prior=dq, after=(),
+    )
+    down = add(part_far, given)
     given = across(part)
-    dq, part, part_left, part_right = back(
-        ((4, 0, size), (3, 3 * share, size)), [(other2, 0, 2), (l3, 0, 1), (r3, 0, 1)],
-        [both_ready, wide, wide], prior=dq, after=(far,),
-    )
-    near = add(part_left, given[:size])
-    far = add(part_right, given[size:], along(far, 0))
-    given = across(part)
-    dq, part, part_left, part_right = back(
-        ((3, share, size), (2, 0, size)), [(other1, 1, 2), (l2, 0, 1), (r2, 0, 1)],
-        [both_ready, wide, wide], prior=dq, after=(far, near),
-    )
-    near = add(part_right, given[size:], along(near, 0))
-    far = add(part_left, given[:size], along(far, 1))
-    given = across(part)
-    dq, part, part_left, part_right = back(
-        ((3, 0, share), (1, 0, size)), [(other1, 0, 1), (l1, 0, 1), (r1, 0, 1)],
-        [ready, wide, wide], prior=dq, after=(far, near),
-    )
-    near = add(part_left, given[:size], along(near, 1))
-    far = add(part_right, given[size:], along(far, 0))
-    given = across(part)
+    up = None
+    for step in (3, 2, 1):
+        if step > 1:
+            parts = (*planes(step, 1), *planes(step + 1, 0))
+            blocks = [(far[step - 1], 1, 1), (near[step - 1], 1, 1)]
+            outs = [both_ready, wide, wide]
+        else:
+            parts = ((1, 0, share), *planes(2, 0))
+            blocks = [(swapped, 0, 1)]
+            outs = [ready, wide, wide]
+        blocks += [(far[step], 0, 1), (near[step], 0, 1)]
+        dq, part, part_far, part_near = back(
+            parts=parts, blocks=blocks, outs=outs, prior=dq,
+            after=(down,) if up is None else (down, up),
+        )
+        relayed = () if up is None else (along(up, (step + 1) % 2),)
+        up = add(part_near, given[size:], *relayed)
+        down = add(part_far, given[:size], along(down, step % 2))
+        given = across(part)
     grad_queries, mine, grad_resp_keys, grad_resp_values = back(
-        ((0, 0, share + resp),), [(packed, 0, 1)], [wide, grads, grads], prior=dq,
-        after=(far, near), last=(own_rows,),
-    )
-    near, far = along(near, 0), along(far, 1)
+        parts=((0, 0, share + resp),), blocks=[(packed, 0, 1)], outs=[wide, grads, grads],
+        prior=dq, after=(down, up), last=(own_rows,),
+    )
+    near, far = along(up, 1), along(down, 0)
     total = [
         mine[at : at + share] + sum(r[at : at + share].astype(F32) for r in (given, near, far))
         for at in (0, share)

time: 67.3 us -> 69.6 us (1.034)
  waiting for transfers between devices: 10.8 us -> 15.1 us
  starting transfers between devices: 29.6 us -> 27.7 us
    ppermute x14, waiting for transfers between devices: 8.81 us -> 13.9 us  [along(): return lax.ppermute(block, 'sample', pairs)]
    ppermute x9 -> x6, starting transfers between devices: 10.7 us -> 8.41 us  [across(): return lax.ppermute(block, 'sample', pairs)]
    ppermute x9 -> x6, waiting for transfers between devices: 1.95 us -> 1.26 us  [across(): return lax.ppermute(block, 'sample', pairs)]
    pallas_call x7 -> x6, Pallas kernels: 9.44 us -> 10.1 us  [forward_stats(): pl.pallas_call(functools.partial(forward_kernel, heads, share, picks, boo...]
  transfers between devices with their start and end apart: 23 -> 20, of which waited for: 10 -> 12; matrix products, arithmetic and copies ran while one was open for 4% -> 3% of each run, Pallas kernels for 29% -> 27%
where the time goes in v8:
time: 69.6 us; the launch traced here: 69.3 us
  starting transfers between devices  27.7 us (40%)
  Pallas kernels  20.5 us (29%)
  waiting for transfers between devices  15.1 us (22%)
  other arithmetic  2.95 us (4%)
  between operations  2.17 us (3%)
  local copies, waits for them, and re-layouts  0.88 us (1%)
    ppermute x14, starting transfers between devices, along(): return lax.ppermute(block, 'sample', pairs)  19.3 us
    ppermute x14, waiting for transfers between devices, along(): return lax.ppermute(block, 'sample', pairs)  13.9 us
    pallas_call x6, Pallas kernels, backward_grads(): pl.pallas_call(functools.partial(backward_kernel, heads, share, owners, p...  10.4 us
    pallas_call x6, Pallas kernels, forward_stats(): pl.pallas_call(functools.partial(forward_kernel, heads, share, picks, boo...  10.1 us
    ppermute x6, starting transfers between devices, across(): return lax.ppermute(block, 'sample', pairs)  8.41 us
  transfers between devices with their start and end apart: 20, of which 12 were waited for; matrix products, arithmetic and copies ran while one was open for 3% of the time, Pallas kernels for 27%

profile of v8, /device:TPU:2, one launch (start us, length us, event | category | flops | bytes accessed | tf_op | source)
XLA Modules:
  0.0 69.3 jit_solution(1323775324276086883)
XLA Ops:
  2.1 1.6 %collective-permute-start = (bf16[272,128]{1,0:T(8,128)(2,1)S(1)}, bf16[272,128]{1,0:T(8,128)(2,1)S(1)}, u32[]{:S(2)}, u32[]{:S(2)}) collective-permute-start(bf16[272,128]{1,0:T(8,128)(2,1)S(1)} %pad_maximum_fusion.2.refs_3_.refs_6_), channel_id=1, source_target_pairs={{0,8},{1,9},{2,10},{3,11},{4,12},{5,13},{6,14},{7,15},{8,0},{9,1},... | collective-permute-start | bytes 208904 | tf_op jit(solution)/shard_map/ppermute | solution.py:277
  4.4 0.8 %constant_dynamic-update-slice_fusion.1 = bf16[2,256,128]{2,1,0:T(8,128)(2,1)S(1)} fusion(bf16[1,256,128]{2,1,0:T(8,128)(2,1)} %param.9), kind=kLoop, calls=%fused_computation.13 | loop fusion | bytes 131072
  5.2 1.3 %pad_maximum_fusion.refs_1_ = bf16[2,256,1024]{2,1,0:T(8,128)(2,1)S(1)} fusion(bf16[1,256,1024]{2,1,0:T(8,128)(2,1)} %param.13, bf16[1,256,1024]{2,1,0:T(8,128)(2,1)} %param.8), kind=kLoop, calls=%fused_computation | loop fusion | flops 524288 | bytes 2097152 | tf_op jit(solution)/shard_map/concatenate | solution.py:298
  6.6 5.9 %collective-permute-start.2 = (bf16[544,128]{1,0:T(8,128)(2,1)S(1)}, bf16[544,128]{1,0:T(8,128)(2,1)S(1)}, u32[]{:S(2)}, u32[]{:S(2)}) collective-permute-start(bf16[544,128]{1,0:T(8,128)(2,1)S(1)} %pad_maximum_fusion.1), channel_id=1, source_target_pairs={{0,7},{1,2},{2,1},{3,4},{4,3},{5,6},{6,5},{7,0},{8,15},{9,10},{10,... | collective-permute-start | bytes 417800 | tf_op jit(solution)/shard_map/ppermute | solution.py:286
  12.5 1.5 %forward_stats.6 = (f32[32,256]{1,0:T(8,128)S(1)}, bf16[384,2048]{1,0:T(8,128)(2,1)S(1)}, f32[384,2048]{1,0:T(8,128)S(1)}, bf16[2048,128]{1,0:T(8,128)(2,1)S(1)}, bf16[2048,128]{1,0:T(8,128)(2,1)S(1)}) custom-call(s32[1]{0:T(128)S(6)} %copy.14.refs_0_, bf16[2,256,1024]{2,1,0:T(8,128)(2,1)S(1)} %pad_maximum_fusion.refs_1_, ...), custom_call_target="tpu_custom_call" | custom-call | flops 1207959552 | bytes 1048576 | tf_op jit(solution)/shard_map/forward_stats/pallas_call | solution.py:224
  14.7 1.2 %collective-permute-done.2.refs_3_.refs_13_.refs_12_ = bf16[544,128]{1,0:T(8,128)(2,1)S(1)} collective-permute-done((bf16[544,128]{1,0:T(8,128)(2,1)S(1)}, bf16[544,128]{1,0:T(8,128)(2,1)S(1)}, u32[]{:S(2)}, u32[]{:S(2)}) %collective-permute-start.2) | collective-permute-done | bytes 139296 | tf_op jit(solution)/shard_map/ppermute | solution.py:286
  15.9 0.9 %collective-permute-start.4 = (bf16[544,128]{1,0:T(8,128)(2,1)S(1)}, bf16[544,128]{1,0:T(8,128)(2,1)S(1)}, u32[]{:S(2)}, u32[]{:S(2)}) collective-permute-start(bf16[544,128]{1,0:T(8,128)(2,1)S(1)} %collective-permute-done.2.refs_3_.refs_13_.refs_12_), channel_id=1, source_target_pairs={{0,1},{1,0},{2,3},{3,2},{4,5},{5,4},{6,7},{7,6},{8,9},{9,8},{10,11... | collective-permute-start | bytes 417800 | tf_op jit(solution)/shard_map/ppermute | solution.py:286
  16.8 0.8 %collective-permute-done.1.refs_2_.refs_12_.refs_11_ = bf16[544,128]{1,0:T(8,128)(2,1)S(1)} collective-permute-done((bf16[544,128]{1,0:T(8,128)(2,1)S(1)}, bf16[544,128]{1,0:T(8,128)(2,1)S(1)}, u32[]{:S(2)}, u32[]{:S(2)}) %collective-permute-start.1) | collective-permute-done | bytes 139296 | tf_op jit(solution)/shard_map/ppermute | solution.py:286
  17.7 1.2 %collective-permute-start.3 = (bf16[544,128]{1,0:T(8,128)(2,1)S(1)}, bf16[544,128]{1,0:T(8,128)(2,1)S(1)}, u32[]{:S(2)}, u32[]{:S(2)}) collective-permute-start(bf16[544,128]{1,0:T(8,128)(2,1)S(1)} %collective-permute-done.1.refs_2_.refs_12_.refs_11_), channel_id=1, source_target_pairs={{0,7},{1,2},{2,1},{3,4},{4,3},{5,6},{6,5},{7,0},{8,15},{9,10},{10,... | collective-permute-start | bytes 417800 | tf_op jit(solution)/shard_map/ppermute | solution.py:286
  18.9 2.3 %forward_stats.8 = (f32[32,256]{1,0:T(8,128)S(1)}, bf16[512,2048]{1,0:T(8,128)(2,1)S(1)}, f32[512,2048]{1,0:T(8,128)S(1)}) custom-call(bf16[2048,128]{1,0:T(8,128)(2,1)S(1)} %get-tuple-element.47.refs_0_.refs_1_, bf16[2048,128]{1,0:T(8,128)(2,1)S(1)} %get-tuple-element.48.refs_1_.refs_2_, ...), custom_call_target="tpu_custom_call" | custom-call | flops 1610612736 | bytes 1048576 | tf_op jit(solution)/shard_map/forward_stats/pallas_call | solution.py:224
  21.2 2.7 %collective-permute-start.6 = (bf16[544,128]{1,0:T(8,128)(2,1)S(1)}, bf16[544,128]{1,0:T(8,128)(2,1)S(1)}, u32[]{:S(2)}, u32[]{:S(2)}) collective-permute-start(bf16[544,128]{1,0:T(8,128)(2,1)S(1)} %collective-permute-done.4.refs_3_.refs_13_.refs_15_), channel_id=1, source_target_pairs={{0,7},{1,2},{2,1},{3,4},{4,3},{5,6},{6,5},{7,0},{8,15},{9,10},{10,... | collective-permute-start | bytes 417800 | tf_op jit(solution)/shard_map/ppermute | solution.py:286
  24.4 2.3 %forward_stats.9 = (f32[32,256]{1,0:T(8,128)S(1)}, bf16[512,2048]{1,0:T(8,128)(2,1)S(1)}, f32[512,2048]{1,0:T(8,128)S(1)}) custom-call(bf16[2048,128]{1,0:T(8,128)(2,1)S(1)} %get-tuple-element.47.refs_0_.refs_1_, bf16[2048,128]{1,0:T(8,128)(2,1)S(1)} %get-tuple-element.48.refs_1_.refs_2_, ...), custom_call_target="tpu_custom_call" | custom-call | flops 1610612736 | bytes 1048576 | tf_op jit(solution)/shard_map/forward_stats/pallas_call | solution.py:224
  26.7 2.7 %collective-permute-done.5.refs_2_.refs_10_.refs_14_ = bf16[544,128]{1,0:T(8,128)(2,1)S(1)} collective-permute-done((bf16[544,128]{1,0:T(8,128)(2,1)S(1)}, bf16[544,128]{1,0:T(8,128)(2,1)S(1)}, u32[]{:S(2)}, u32[]{:S(2)}) %collective-permute-start.5) | collective-permute-done | bytes 139296 | tf_op jit(solution)/shard_map/ppermute | solution.py:286
  30.2 2.3 %forward_stats.10 = (f32[32,256]{1,0:T(8,128)S(1)}, bf16[512,2048]{1,0:T(8,128)(2,1)S(1)}, f32[512,2048]{1,0:T(8,128)S(1)}) custom-call(bf16[2048,128]{1,0:T(8,128)(2,1)S(1)} %get-tuple-element.47.refs_0_.refs_1_, bf16[2048,128]{1,0:T(8,128)(2,1)S(1)} %get-tuple-element.48.refs_1_.refs_2_, ...), custom_call_target="tpu_custom_call" | custom-call | flops 1610612736 | bytes 1048576 | tf_op jit(solution)/shard_map/forward_stats/pallas_call | solution.py:224
  32.5 3.1 %collective-permute-done.7.refs_2_.refs_11_.refs_12_ = bf16[544,128]{1,0:T(8,128)(2,1)S(1)} collective-permute-done((bf16[544,128]{1,0:T(8,128)(2,1)S(1)}, bf16[544,128]{1,0:T(8,128)(2,1)S(1)}, u32[]{:S(2)}, u32[]{:S(2)}) %collective-permute-start.7) | collective-permute-done | bytes 139296 | tf_op jit(solution)/shard_map/ppermute | solution.py:286
  35.7 1.0 %forward_stats.11 = (f32[32,256]{1,0:T(8,128)S(1)}, bf16[256,2048]{1,0:T(8,128)(2,1)S(1)}, f32[256,2048]{1,0:T(8,128)S(1)}) custom-call(bf16[2048,128]{1,0:T(8,128)(2,1)S(1)} %get-tuple-element.47.refs_0_.refs_1_, bf16[2048,128]{1,0:T(8,128)(2,1)S(1)} %get-tuple-element.48.refs_1_.refs_2_, bf16[544,128]{1,0:T(8,128)(2,1)S(1)} %collective-permute-done.7.refs_2_.refs_11_.refs_12_), custom_call_target="tpu_custom_call" | custom-call | flops 805306368 | bytes 1048576 | tf_op jit(solution)/shard_map/forward_stats/pallas_call | solution.py:224
  37.4 2.9 %collective-permute-start.8 = (bf16[256,128]{1,0:T(8,128)(2,1)S(1)}, bf16[256,128]{1,0:T(8,128)(2,1)S(1)}, u32[]{:S(2)}, u32[]{:S(2)}) collective-permute-start(bf16[256,128]{1,0:T(8,128)(2,1)S(1)} %get-tuple-element.71), channel_id=1, source_target_pairs={{0,8},{1,9},{2,10},{3,11},{4,12},{5,13},{6,14},{7,15},{8,0},{9,1},... | collective-permute-start | bytes 196616 | tf_op jit(solution)/shard_map/ppermute | solution.py:277
  40.3 1.6 %backward_grads.7 = (f32[1024,256]{1,0:T(8,128)S(1)}, bf16[512,128]{1,0:T(8,128)(2,1)S(1)}, f32[256,128]{1,0:T(8,128)S(1)}) custom-call(s32[1]{0:T(128)S(6)} %copy.15.refs_0_, bf16[2048,128]{1,0:T(8,128)(2,1)S(1)} %get-tuple-element.47.refs_0_.refs_1_, bf16[2048,128]{1,0:T(8,128)(2,1)S(1)} %get-tuple-element.48.refs_1_.refs_2_, ...), custom_call_target="tpu_custom_call" | custom-call | flops 2013265920 | bytes 2097152 | tf_op jit(solution)/shard_map/backward_grads/pallas_call | solution.py:255
  42.0 1.2 %collective-permute-done.8 = bf16[256,128]{1,0:T(8,128)(2,1)S(1)} collective-permute-done((bf16[256,128]{1,0:T(8,128)(2,1)S(1)}, bf16[256,128]{1,0:T(8,128)(2,1)S(1)}, u32[]{:S(2)}, u32[]{:S(2)}) %collective-permute-start.8) | collective-permute-done | bytes 65568 | tf_op jit(solution)/shard_map/ppermute | solution.py:277
  43.4 2.0 %backward_grads.8 = (f32[1024,256]{1,0:T(8,128)S(1)}, bf16[512,128]{1,0:T(8,128)(2,1)S(1)}, f32[256,128]{1,0:T(8,128)S(1)}, f32[256,128]{1,0:T(8,128)S(1)}) custom-call(s32[1]{0:T(128)S(6)} %copy.15.refs_0_, bf16[2048,128]{1,0:T(8,128)(2,1)S(1)} %get-tuple-element.47.refs_0_.refs_1_, bf16[2048,128]{1,0:T(8,128)(2,1)S(1)} %get-tuple-element.48.refs_1_.refs_2_, ...), custom_call_target="tpu_custom_call" | custom-call | flops 2684354560 | bytes 2097152 | tf_op jit(solution)/shard_map/backward_grads/pallas_call | solution.py:255
  45.4 2.5 %collective-permute-start.11 = (bf16[512,128]{1,0:T(8,128)(2,1)S(1)}, bf16[512,128]{1,0:T(8,128)(2,1)S(1)}, u32[]{:S(2)}, u32[]{:S(2)}) collective-permute-start(bf16[512,128]{1,0:T(8,128)(2,1)S(1)} %get-tuple-element.78), channel_id=1, source_target_pairs={{0,8},{1,9},{2,10},{3,11},{4,12},{5,13},{6,14},{7,15},{8,0},{9,1},... | collective-permute-start | bytes 393224 | tf_op jit(solution)/shard_map/ppermute | solution.py:277
  47.9 1.0 %collective-permute-done.10 = bf16[256,128]{1,0:T(8,128)(2,1)S(1)} collective-permute-done((bf16[256,128]{1,0:T(8,128)(2,1)S(1)}, bf16[256,128]{1,0:T(8,128)(2,1)S(1)}, u32[]{:S(2)}, u32[]{:S(2)}) %collective-permute-start.10) | collective-permute-done | bytes 65568 | tf_op jit(solution)/shard_map/ppermute | solution.py:286
  48.9 1.9 %collective-permute-start.13 = (bf16[256,128]{1,0:T(8,128)(2,1)S(1)}, bf16[256,128]{1,0:T(8,128)(2,1)S(1)}, u32[]{:S(2)}, u32[]{:S(2)}) collective-permute-start(bf16[256,128]{1,0:T(8,128)(2,1)S(1)} %get-tuple-element.95.refs_18_), channel_id=1, source_target_pairs={{0,7},{1,2},{2,1},{3,4},{4,3},{5,6},{6,5},{7,0},{8,15},{9,10},{10,... | collective-permute-start | bytes 196616 | tf_op jit(solution)/shard_map/ppermute | solution.py:286
  50.8 2.0 %backward_grads.9 = (f32[1024,256]{1,0:T(8,128)S(1)}, bf16[512,128]{1,0:T(8,128)(2,1)S(1)}, f32[256,128]{1,0:T(8,128)S(1)}, f32[256,128]{1,0:T(8,128)S(1)}) custom-call(s32[1]{0:T(128)S(6)} %copy.15.refs_0_, bf16[2048,128]{1,0:T(8,128)(2,1)S(1)} %get-tuple-element.47.refs_0_.refs_1_, bf16[2048,128]{1,0:T(8,128)(2,1)S(1)} %get-tuple-element.48.refs_1_.refs_2_, ...), custom_call_target="tpu_custom_call" | custom-call | flops 2684354560 | bytes 2097152 | tf_op jit(solution)/shard_map/backward_grads/pallas_call | solution.py:255
  52.8 0.9 %collective-permute-start.14 = (bf16[512,128]{1,0:T(8,128)(2,1)S(1)}, bf16[512,128]{1,0:T(8,128)(2,1)S(1)}, u32[]{:S(2)}, u32[]{:S(2)}) collective-permute-start(bf16[512,128]{1,0:T(8,128)(2,1)S(1)} %get-tuple-element.82), channel_id=1, source_target_pairs={{0,8},{1,9},{2,10},{3,11},{4,12},{5,13},{6,14},{7,15},{8,0},{9,1},... | collective-permute-start | bytes 393224 | tf_op jit(solution)/shard_map/ppermute | solution.py:277
  54.5 1.3 %collective-permute-done.12 = bf16[256,128]{1,0:T(8,128)(2,1)S(1)} collective-permute-done((bf16[256,128]{1,0:T(8,128)(2,1)S(1)}, bf16[256,128]{1,0:T(8,128)(2,1)S(1)}, u32[]{:S(2)}, u32[]{:S(2)}) %collective-permute-start.12) | collective-permute-done | bytes 65568 | tf_op jit(solution)/shard_map/ppermute | solution.py:286
  55.9 2.8 %collective-permute-start.15 = (bf16[256,128]{1,0:T(8,128)(2,1)S(1)}, bf16[256,128]{1,0:T(8,128)(2,1)S(1)}, u32[]{:S(2)}, u32[]{:S(2)}) collective-permute-start(bf16[256,128]{1,0:T(8,128)(2,1)S(1)} %get-tuple-element.94.refs_14_), channel_id=1, source_target_pairs={{0,7},{1,2},{2,1},{3,4},{4,3},{5,6},{6,5},{7,0},{8,15},{9,10},{10,... | collective-permute-start | bytes 196616 | tf_op jit(solution)/shard_map/ppermute | solution.py:286
  58.7 1.6 %backward_grads.10 = (f32[1024,256]{1,0:T(8,128)S(1)}, bf16[256,128]{1,0:T(8,128)(2,1)S(1)}, f32[256,128]{1,0:T(8,128)S(1)}, f32[256,128]{1,0:T(8,128)S(1)}) custom-call(s32[1]{0:T(128)S(6)} %copy.15.refs_0_, bf16[2048,128]{1,0:T(8,128)(2,1)S(1)} %get-tuple-element.47.refs_0_.refs_1_, bf16[2048,128]{1,0:T(8,128)(2,1)S(1)} %get-tuple-element.48.refs_1_.refs_2_, ...), custom_call_target="tpu_custom_call" | custom-call | flops 2013265920 | bytes 2097152 | tf_op jit(solution)/shard_map/backward_grads/pallas_call | solution.py:255
  60.7 0.8 %collective-permute-done.15 = bf16[256,128]{1,0:T(8,128)(2,1)S(1)} collective-permute-done((bf16[256,128]{1,0:T(8,128)(2,1)S(1)}, bf16[256,128]{1,0:T(8,128)(2,1)S(1)}, u32[]{:S(2)}, u32[]{:S(2)}) %collective-permute-start.15) | collective-permute-done | bytes 65568 | tf_op jit(solution)/shard_map/ppermute | solution.py:286
  61.5 2.8 %collective-permute-start.18 = (bf16[256,128]{1,0:T(8,128)(2,1)S(1)}, bf16[256,128]{1,0:T(8,128)(2,1)S(1)}, u32[]{:S(2)}, u32[]{:S(2)}) collective-permute-start(bf16[256,128]{1,0:T(8,128)(2,1)S(1)} %get-tuple-element.91.refs_10_), channel_id=1, source_target_pairs={{0,7},{1,2},{2,1},{3,4},{4,3},{5,6},{6,5},{7,0},{8,15},{9,10},{10,... | collective-permute-start | bytes 196616 | tf_op jit(solution)/shard_map/ppermute | solution.py:286
  64.4 2.6 %backward_grads.11 = (f32[1,256,1024]{2,1,0:T(8,128)}, f32[256,128]{1,0:T(8,128)S(1)}, f32[1,256,128]{2,1,0:T(8,128)}, f32[1,256,128]{2,1,0:T(8,128)}) custom-call(s32[1]{0:T(128)S(6)} %copy.15.refs_0_, bf16[2048,128]{1,0:T(8,128)(2,1)S(1)} %get-tuple-element.47.refs_0_.refs_1_, bf16[2048,128]{1,0:T(8,128)(2,1)S(1)} %get-tuple-element.48.refs_1_.refs_2_, ...), custom_call_target="tpu_custom_call" | custom-call | flops 2013265920 | bytes 2097152 | tf_op jit(solution)/shard_map/backward_grads/pallas_call | solution.py:255
  67.1 1.5 %collective-permute-done.19 = bf16[256,128]{1,0:T(8,128)(2,1)S(1)} collective-permute-done((bf16[256,128]{1,0:T(8,128)(2,1)S(1)}, bf16[256,128]{1,0:T(8,128)(2,1)S(1)}, u32[]{:S(2)}, u32[]{:S(2)}) %collective-permute-start.19) | collective-permute-done | bytes 65568 | tf_op jit(solution)/shard_map/ppermute | solution.py:286
  (37 shorter events, 5.8 us)
Async XLA Ops:
  0.6 5.9 %copy-start = (bf16[128,128]{1,0:T(8,128)(2,1)S(1)}, bf16[128,128]{1,0:T(8,128)(2,1)}, u32[]{:S(2)}) copy-start(bf16[128,128]{1,0:T(8,128)(2,1)} %param.12) | copy-start | bytes 98308
  0.6 5.9 %copy-start.1 = (bf16[128,128]{1,0:T(8,128)(2,1)S(1)}, bf16[128,128]{1,0:T(8,128)(2,1)}, u32[]{:S(2)}) copy-start(bf16[128,128]{1,0:T(8,128)(2,1)} %param.11) | copy-start | bytes 98308
  0.7 5.9 %copy-start.2 = (bf16[1,256,128]{2,1,0:T(8,128)(2,1)S(1)}, bf16[1,256,128]{2,1,0:T(8,128)(2,1)}, u32[]{:S(2)}) copy-start(bf16[1,256,128]{2,1,0:T(8,128)(2,1)} %param.10) | copy-start | bytes 196612
  2.1 4.4 %collective-permute-start = (bf16[272,128]{1,0:T(8,128)(2,1)S(1)}, bf16[272,128]{1,0:T(8,128)(2,1)S(1)}, u32[]{:S(2)}, u32[]{:S(2)}) collective-permute-start(bf16[272,128]{1,0:T(8,128)(2,1)S(1)} %pad_maximum_fusion.2.refs_3_.refs_6_), channel_id=1, source_target_pairs={{0,8},{1,9},{2,10},{3,11},{4,12},{5,13},{6,14},{7,15},{8,0},{9,1},... | collective-permute-start | bytes 208904 | tf_op jit(solution)/shard_map/ppermute | solution.py:277
  6.6 9.3 %collective-permute-start.2 = (bf16[544,128]{1,0:T(8,128)(2,1)S(1)}, bf16[544,128]{1,0:T(8,128)(2,1)S(1)}, u32[]{:S(2)}, u32[]{:S(2)}) collective-permute-start(bf16[544,128]{1,0:T(8,128)(2,1)S(1)} %pad_maximum_fusion.1), channel_id=1, source_target_pairs={{0,7},{1,2},{2,1},{3,4},{4,3},{5,6},{6,5},{7,0},{8,15},{9,10},{10,... | collective-permute-start | bytes 417800 | tf_op jit(solution)/shard_map/ppermute | solution.py:286
  12.5 5.1 %collective-permute-start.1 = (bf16[544,128]{1,0:T(8,128)(2,1)S(1)}, bf16[544,128]{1,0:T(8,128)(2,1)S(1)}, u32[]{:S(2)}, u32[]{:S(2)}) collective-permute-start(bf16[544,128]{1,0:T(8,128)(2,1)S(1)} %pad_maximum_fusion.1), channel_id=1, source_target_pairs={{0,1},{1,0},{2,3},{3,2},{4,5},{5,4},{6,7},{7,6},{8,9},{9,8},{10,11... | collective-permute-start | bytes 417800 | tf_op jit(solution)/shard_map/ppermute | solution.py:286
  15.9 5.3 %collective-permute-start.4 = (bf16[544,128]{1,0:T(8,128)(2,1)S(1)}, bf16[544,128]{1,0:T(8,128)(2,1)S(1)}, u32[]{:S(2)}, u32[]{:S(2)}) collective-permute-start(bf16[544,128]{1,0:T(8,128)(2,1)S(1)} %collective-permute-done.2.refs_3_.refs_13_.refs_12_), channel_id=1, source_target_pairs={{0,1},{1,0},{2,3},{3,2},{4,5},{5,4},{6,7},{7,6},{8,9},{9,8},{10,11... | collective-permute-start | bytes 417800 | tf_op jit(solution)/shard_map/ppermute | solution.py:286
  17.7 6.7 %collective-permute-start.3 = (bf16[544,128]{1,0:T(8,128)(2,1)S(1)}, bf16[544,128]{1,0:T(8,128)(2,1)S(1)}, u32[]{:S(2)}, u32[]{:S(2)}) collective-permute-start(bf16[544,128]{1,0:T(8,128)(2,1)S(1)} %collective-permute-done.1.refs_2_.refs_12_.refs_11_), channel_id=1, source_target_pairs={{0,7},{1,2},{2,1},{3,4},{4,3},{5,6},{6,5},{7,0},{8,15},{9,10},{10,... | collective-permute-start | bytes 417800 | tf_op jit(solution)/shard_map/ppermute | solution.py:286
  21.2 9.0 %collective-permute-start.6 = (bf16[544,128]{1,0:T(8,128)(2,1)S(1)}, bf16[544,128]{1,0:T(8,128)(2,1)S(1)}, u32[]{:S(2)}, u32[]{:S(2)}) collective-permute-start(bf16[544,128]{1,0:T(8,128)(2,1)S(1)} %collective-permute-done.4.refs_3_.refs_13_.refs_15_), channel_id=1, source_target_pairs={{0,7},{1,2},{2,1},{3,4},{4,3},{5,6},{6,5},{7,0},{8,15},{9,10},{10,... | collective-permute-start | bytes 417800 | tf_op jit(solution)/shard_map/ppermute | solution.py:286
  24.4 5.1 %collective-permute-start.5 = (bf16[544,128]{1,0:T(8,128)(2,1)S(1)}, bf16[544,128]{1,0:T(8,128)(2,1)S(1)}, u32[]{:S(2)}, u32[]{:S(2)}) collective-permute-start(bf16[544,128]{1,0:T(8,128)(2,1)S(1)} %collective-permute-done.3.refs_2_.refs_12_.refs_14_), channel_id=1, source_target_pairs={{0,1},{1,0},{2,3},{3,2},{4,5},{5,4},{6,7},{7,6},{8,9},{9,8},{10,11... | collective-permute-start | bytes 417800 | tf_op jit(solution)/shard_map/ppermute | solution.py:286
  29.4 6.3 %collective-permute-start.7 = (bf16[544,128]{1,0:T(8,128)(2,1)S(1)}, bf16[544,128]{1,0:T(8,128)(2,1)S(1)}, u32[]{:S(2)}, u32[]{:S(2)}) collective-permute-start(bf16[544,128]{1,0:T(8,128)(2,1)S(1)} %collective-permute-done.5.refs_2_.refs_10_.refs_14_), channel_id=1, source_target_pairs={{0,7},{1,2},{2,1},{3,4},{4,3},{5,6},{6,5},{7,0},{8,15},{9,10},{10,... | collective-permute-start | bytes 417800 | tf_op jit(solution)/shard_map/ppermute | solution.py:286
  37.4 5.9 %collective-permute-start.8 = (bf16[256,128]{1,0:T(8,128)(2,1)S(1)}, bf16[256,128]{1,0:T(8,128)(2,1)S(1)}, u32[]{:S(2)}, u32[]{:S(2)}) collective-permute-start(bf16[256,128]{1,0:T(8,128)(2,1)S(1)} %get-tuple-element.71), channel_id=1, source_target_pairs={{0,8},{1,9},{2,10},{3,11},{4,12},{5,13},{6,14},{7,15},{8,0},{9,1},... | collective-permute-start | bytes 196616 | tf_op jit(solution)/shard_map/ppermute | solution.py:277
  41.9 6.9 %collective-permute-start.9 = (bf16[512,128]{1,0:T(8,128)(2,1)S(1)}, bf16[512,128]{1,0:T(8,128)(2,1)S(1)}, u32[]{:S(2)}, u32[]{:S(2)}) collective-permute-start(bf16[512,128]{1,0:T(8,128)(2,1)S(1)} %get-tuple-element.74), channel_id=1, source_target_pairs={{0,8},{1,9},{2,10},{3,11},{4,12},{5,13},{6,14},{7,15},{8,0},{9,1},... | collective-permute-start | bytes 393224 | tf_op jit(solution)/shard_map/ppermute | solution.py:277
  43.3 5.6 %collective-permute-start.10 = (bf16[256,128]{1,0:T(8,128)(2,1)S(1)}, bf16[256,128]{1,0:T(8,128)(2,1)S(1)}, u32[]{:S(2)}, u32[]{:S(2)}) collective-permute-start(bf16[256,128]{1,0:T(8,128)(2,1)S(1)} %add_convert_fusion.6.refs_17_), channel_id=1, source_target_pairs={{0,7},{1,2},{2,1},{3,4},{4,3},{5,6},{6,5},{7,0},{8,15},{9,10},{10,... | collective-permute-start | bytes 196616 | tf_op jit(solution)/shard_map/ppermute | solution.py:286
  45.4 8.4 %collective-permute-start.11 = (bf16[512,128]{1,0:T(8,128)(2,1)S(1)}, bf16[512,128]{1,0:T(8,128)(2,1)S(1)}, u32[]{:S(2)}, u32[]{:S(2)}) collective-permute-start(bf16[512,128]{1,0:T(8,128)(2,1)S(1)} %get-tuple-element.78), channel_id=1, source_target_pairs={{0,8},{1,9},{2,10},{3,11},{4,12},{5,13},{6,14},{7,15},{8,0},{9,1},... | collective-permute-start | bytes 393224 | tf_op jit(solution)/shard_map/ppermute | solution.py:277
  48.9 5.6 %collective-permute-start.13 = (bf16[256,128]{1,0:T(8,128)(2,1)S(1)}, bf16[256,128]{1,0:T(8,128)(2,1)S(1)}, u32[]{:S(2)}, u32[]{:S(2)}) collective-permute-start(bf16[256,128]{1,0:T(8,128)(2,1)S(1)} %get-tuple-element.95.refs_18_), channel_id=1, source_target_pairs={{0,7},{1,2},{2,1},{3,4},{4,3},{5,6},{6,5},{7,0},{8,15},{9,10},{10,... | collective-permute-start | bytes 196616 | tf_op jit(solution)/shard_map/ppermute | solution.py:286
  50.8 5.0 %collective-permute-start.12 = (bf16[256,128]{1,0:T(8,128)(2,1)S(1)}, bf16[256,128]{1,0:T(8,128)(2,1)S(1)}, u32[]{:S(2)}, u32[]{:S(2)}) collective-permute-start(bf16[256,128]{1,0:T(8,128)(2,1)S(1)} %get-tuple-element.96.refs_17_), channel_id=1, source_target_pairs={{0,1},{1,0},{2,3},{3,2},{4,5},{5,4},{6,7},{7,6},{8,9},{9,8},{10,11... | collective-permute-start | bytes 196616 | tf_op jit(solution)/shard_map/ppermute | solution.py:286
  52.8 8.7 %collective-permute-start.14 = (bf16[512,128]{1,0:T(8,128)(2,1)S(1)}, bf16[512,128]{1,0:T(8,128)(2,1)S(1)}, u32[]{:S(2)}, u32[]{:S(2)}) collective-permute-start(bf16[512,128]{1,0:T(8,128)(2,1)S(1)} %get-tuple-element.82), channel_id=1, source_target_pairs={{0,8},{1,9},{2,10},{3,11},{4,12},{5,13},{6,14},{7,15},{8,0},{9,1},... | collective-permute-start | bytes 393224 | tf_op jit(solution)/shard_map/ppermute | solution.py:277
  55.8 4.8 %collective-permute-start.16 = (bf16[256,128]{1,0:T(8,128)(2,1)S(1)}, bf16[256,128]{1,0:T(8,128)(2,1)S(1)}, u32[]{:S(2)}, u32[]{:S(2)}) collective-permute-start(bf16[256,128]{1,0:T(8,128)(2,1)S(1)} %get-tuple-element.93.refs_15_), channel_id=1, source_target_pairs={{0,1},{1,0},{2,3},{3,2},{4,5},{5,4},{6,7},{7,6},{8,9},{9,8},{10,11... | collective-permute-start | bytes 196616 | tf_op jit(solution)/shard_map/ppermute | solution.py:286
  55.9 5.6 %collective-permute-start.15 = (bf16[256,128]{1,0:T(8,128)(2,1)S(1)}, bf16[256,128]{1,0:T(8,128)(2,1)S(1)}, u32[]{:S(2)}, u32[]{:S(2)}) collective-permute-start(bf16[256,128]{1,0:T(8,128)(2,1)S(1)} %get-tuple-element.94.refs_14_), channel_id=1, source_target_pairs={{0,7},{1,2},{2,1},{3,4},{4,3},{5,6},{6,5},{7,0},{8,15},{9,10},{10,... | collective-permute-start | bytes 196616 | tf_op jit(solution)/shard_map/ppermute | solution.py:286
  60.3 6.6 %collective-permute-start.17 = (bf16[256,128]{1,0:T(8,128)(2,1)S(1)}, bf16[256,128]{1,0:T(8,128)(2,1)S(1)}, u32[]{:S(2)}, u32[]{:S(2)}) collective-permute-start(bf16[256,128]{1,0:T(8,128)(2,1)S(1)} %get-tuple-element.88), channel_id=1, source_target_pairs={{0,8},{1,9},{2,10},{3,11},{4,12},{5,13},{6,14},{7,15},{8,0},{9,1},... | collective-permute-start | bytes 196616 | tf_op jit(solution)/shard_map/ppermute | solution.py:277
  61.5 5.6 %collective-permute-start.18 = (bf16[256,128]{1,0:T(8,128)(2,1)S(1)}, bf16[256,128]{1,0:T(8,128)(2,1)S(1)}, u32[]{:S(2)}, u32[]{:S(2)}) collective-permute-start(bf16[256,128]{1,0:T(8,128)(2,1)S(1)} %get-tuple-element.91.refs_10_), channel_id=1, source_target_pairs={{0,7},{1,2},{2,1},{3,4},{4,3},{5,6},{6,5},{7,0},{8,15},{9,10},{10,... | collective-permute-start | bytes 196616 | tf_op jit(solution)/shard_map/ppermute | solution.py:286
  64.3 4.3 %collective-permute-start.19 = (bf16[256,128]{1,0:T(8,128)(2,1)S(1)}, bf16[256,128]{1,0:T(8,128)(2,1)S(1)}, u32[]{:S(2)}, u32[]{:S(2)}) collective-permute-start(bf16[256,128]{1,0:T(8,128)(2,1)S(1)} %get-tuple-element.92.refs_9_), channel_id=1, source_target_pairs={{0,1},{1,0},{2,3},{3,2},{4,5},{5,4},{6,7},{7,6},{8,9},{9,8},{10,11... | collective-permute-start | bytes 196616 | tf_op jit(solution)/shard_map/ppermute | solution.py:286

commit v9 on v8

--- a/solution.py
+++ b/solution.py
@@ -47,9 +47,9 @@
     ]
 
 
-def own_mask(at, resp):
-    key_at = lax.broadcasted_iota(jnp.int32, (SLICE, resp), 0) + at
-    return key_at <= lax.broadcasted_iota(jnp.int32, (SLICE, resp), 1)
+def own_mask(at, size, resp):
+    key_at = lax.broadcasted_iota(jnp.int32, (size, resp), 0) + at
+    return key_at <= lax.broadcasted_iota(jnp.int32, (size, resp), 1)
 
 
 def forward_kernel(heads, share, picks, opening, *refs):
@@ -78,38 +78,43 @@
         v_all[prompt:, :] = own_ref[1]
         live = lax.broadcasted_iota(jnp.int32, (resp, width), 0) < len_ref[0]
 
+    tops = [None] * heads
     for t in range(heads + 1):
+        h = t - 1
         if t < heads:
             rows = slice(t * resp, (t + 1) * resp)
             if opening:
                 lanes = slice(t * width, (t + 1) * width)
                 q_rows[rows, :] = wide_ref[0, :, lanes]
                 c_rows[rows, :] = jnp.where(live, wide_ref[1, :, lanes], jnp.zeros((), BF16))
-            s_buf[t % 2][...] = dot_nt(k_all[...], q_rows[rows, :])
-            g_all[:, rows] = dot_nt(v_all[...], c_rows[rows, :])
+            top = None
         if t > 0:
-            h = t - 1
-            s_now, cols = s_buf[h % 2], slice(h * resp, (h + 1) * resp)
-            top = mass = mixed = None
-            for at in range(0, keys, SLICE):
-                s = s_now[at : at + SLICE, :]
-                if at >= prompt:
-                    s = jnp.where(own_mask(at - prompt, resp), s, -jnp.inf)
+            cols = slice(h * resp, (h + 1) * resp)
+            level = tops[h] * rate
+            mass = mixed = None
+        for first in range(0, keys, share):
+            if t < heads:
+                span = slice(first, first + share)
+                s = dot_nt(k_all[span, :], q_rows[rows, :])
+                if first >= prompt:
+                    s = jnp.where(own_mask(first - prompt, share, resp), s, -jnp.inf)
+                s_buf[t % 2][span, :] = s
                 part = fold_rows(s, jnp.maximum)
                 top = part if top is None else jnp.maximum(top, part)
-            top = jnp.max(top, axis=0, keepdims=True)
-            level = top * rate
-            for at in range(0, keys, SLICE):
-                here = slice(at, at + SLICE)
-                e = jnp.exp2(s_now[here, :] * rate - level)
-                if at >= prompt:
-                    e = jnp.where(own_mask(at - prompt, resp), e, 0.0)
-                e_all[here, cols] = e.astype(BF16)
-                part = fold_rows(e, jnp.add)
-                mass = part if mass is None else mass + part
-                part = fold_rows(e * g_all[here, cols], jnp.add)
-                mixed = part if mixed is None else mixed + part
-            out_ref[h : h + 1, :] = top
+                g_all[span, rows] = dot_nt(v_all[span, :], c_rows[rows, :])
+            if t > 0:
+                for at in range(first, first + share, SLICE):
+                    here = slice(at, at + SLICE)
+                    e = jnp.exp2(s_buf[h % 2][here, :] * rate - level)
+                    e_all[here, cols] = e.astype(BF16)
+                    part = fold_rows(e, jnp.add)
+                    mass = part if mass is None else mass + part
+                    part = fold_rows(e * g_all[here, cols], jnp.add)
+                    mixed = part if mixed is None else mixed + part
+        if t < heads:
+            tops[t] = jnp.max(top, axis=0, keepdims=True)
+        if t > 0:
+            out_ref[h : h + 1, :] = tops[h]
             out_ref[heads + h : heads + h + 1, :] = jnp.sum(mass, axis=0, keepdims=True)
             out_ref[2 * heads + h : 2 * heads + h + 1, :] = jnp.sum(mixed, axis=0, keepdims=True)
     paid = jnp.zeros((1, width), F32)
@@ -316,58 +321,41 @@
     back = functools.partial(
         backward_grads, rewards, rows, kept=kept, owners=owners, heads=heads, share=share
     )
-    ready = jax.ShapeDtypeStruct((size, width), BF16)
-    both_ready = jax.ShapeDtypeStruct((2 * size, width), BF16)
-    wide = jax.ShapeDtypeStruct((size, width), F32)
+    ready = jax.ShapeDtypeStruct((2 * size, width), BF16)
+    wide = jax.ShapeDtypeStruct((2 * size, width), F32)
     grads = jax.ShapeDtypeStruct((1, resp, width), F32)
 
-    def add(part, *received):
-        return sum((r.astype(F32) for r in received), part).astype(BF16)
-
-    def planes(group, plane):
-        return ((group, plane * share, share), (group, size + plane * share, share))
-
-    dq, part, merged = back(
-        stats, parts=((5, share, share),), blocks=[(far[4], 1, 1)], outs=[ready], prior=None,
-        after=(),
+    def add(part, received):
+        return (received.astype(F32) + part).astype(BF16)
+
+    dq, down, merged = back(
+        stats, parts=((5, 0, size),), blocks=[(far[4], 0, 2)], outs=[ready], prior=None, after=()
     )
     back = functools.partial(back, (merged,))
-    given = across(part)
-    dq, part, part_far = back(
-        parts=(*planes(4, 1), (5, 0, share)),
-        blocks=[(far[3], 1, 1), (near[3], 1, 1), (far[4], 0, 1)],
-        outs=[both_ready, wide], prior=dq, after=(),
-    )
-    down = add(part_far, given)
-    given = across(part)
-    up = None
-    for step in (3, 2, 1):
-        if step > 1:
-            parts = (*planes(step, 1), *planes(step + 1, 0))
-            blocks = [(far[step - 1], 1, 1), (near[step - 1], 1, 1)]
-            outs = [both_ready, wide, wide]
-        else:
-            parts = ((1, 0, share), *planes(2, 0))
-            blocks = [(swapped, 0, 1)]
-            outs = [ready, wide, wide]
-        blocks += [(far[step], 0, 1), (near[step], 0, 1)]
-        dq, part, part_far, part_near = back(
-            parts=parts, blocks=blocks, outs=outs, prior=dq,
-            after=(down,) if up is None else (down, up),
+    dq, part, up = back(
+        parts=((4, 0, 2 * size),), blocks=[(far[3], 0, 2), (near[3], 0, 2)], outs=[wide, ready],
+        prior=dq, after=(),
+    )
+    down = add(part, along(down, 1))
+    for step in (2, 1):
+        dq, part_down, part_up = back(
+            parts=((step + 1, 0, 2 * size),), blocks=[(far[step], 0, 2), (near[step], 0, 2)],
+            outs=[wide, wide], prior=dq, after=(down, up),
         )
-        relayed = () if up is None else (along(up, (step + 1) % 2),)
-        up = add(part_near, given[size:], *relayed)
-        down = add(part_far, given[:size], along(down, step % 2))
-        given = across(part)
-    grad_queries, mine, grad_resp_keys, grad_resp_values = back(
-        parts=((0, 0, share + resp),), blocks=[(packed, 0, 1)], outs=[wide, grads, grads],
-        prior=dq, after=(down, up), last=(own_rows,),
-    )
-    near, far = along(up, 1), along(down, 0)
-    total = [
-        mine[at : at + share] + sum(r[at : at + share].astype(F32) for r in (given, near, far))
-        for at in (0, share)
-    ]
+        up = add(part_up, along(up, (step + 1) % 2))
+        down = add(part_down, along(down, step % 2))
+    dq, mine = back(
+        parts=((0, 0, share), (1, 0, share)), blocks=[(packed, 0, 1), (swapped, 0, 1)],
+        outs=[wide], prior=dq, after=(down, up),
+    )
+    mine = mine + along(up, 1).astype(F32) + along(down, 0).astype(F32)
+    partner = mine[size:].astype(BF16)
+    grad_queries, grad_resp_keys, grad_resp_values = back(
+        parts=((0, share, resp),), blocks=[], outs=[grads, grads], prior=dq, after=(partner,),
+        last=(own_rows,),
+    )
+    theirs = across(partner).astype(F32)
+    total = [mine[at : at + share] + theirs[at : at + share] for at in (0, share)]
     return grad_queries, grad_resp_keys, grad_resp_values, *total
 
 

time: 69.6 us -> 70.1 us (level)
  starting transfers between devices: 27.7 us -> 25 us
  waiting for transfers between devices: 15.1 us -> 17.3 us
    ppermute x14, waiting for transfers between devices: 13.9 us -> 17.2 us  [along(): return lax.ppermute(block, 'sample', pairs)]
    ppermute x14, starting transfers between devices: 19.3 us -> 17.8 us  [along(): return lax.ppermute(block, 'sample', pairs)]
    ppermute x6 -> x2, starting transfers between devices: 8.41 us -> 7.21 us  [across(): return lax.ppermute(block, 'sample', pairs)]
    ppermute x6 -> x2, waiting for transfers between devices: 1.26 us -> 0.1 us  [across(): return lax.ppermute(block, 'sample', pairs)]
  transfers between devices with their start and end apart: 20 -> 16, of which waited for: 12 -> 13; matrix products, arithmetic and copies ran while one was open for 3% -> 3% of each run, Pallas kernels for 27% -> 27%
where the time goes in v9:
time: 70.1 us; the launch traced here: 69.2 us
  starting transfers between devices  25 us (36%)
  Pallas kernels  20.8 us (30%)
  waiting for transfers between devices  17.3 us (25%)
  other arithmetic  2.99 us (4%)
  between operations  2.18 us (3%)
  local copies, waits for them, and re-layouts  0.89 us (1%)
    ppermute x14, starting transfers between devices, along(): return lax.ppermute(block, 'sample', pairs)  17.8 us
    ppermute x14, waiting for transfers between devices, along(): return lax.ppermute(block, 'sample', pairs)  17.2 us
    pallas_call x6, Pallas kernels, backward_grads(): pl.pallas_call(functools.partial(backward_kernel, heads, share, owners, p...  10.5 us
    pallas_call x6, Pallas kernels, forward_stats(): pl.pallas_call(functools.partial(forward_kernel, heads, share, picks, boo...  10.4 us
    ppermute x2, starting transfers between devices, across(): return lax.ppermute(block, 'sample', pairs)  7.21 us
  transfers between devices with their start and end apart: 16, of which 13 were waited for; matrix products, arithmetic and copies ran while one was open for 3% of the time, Pallas kernels for 27%

profile of v9, /device:TPU:2, one launch (start us, length us, event | category | flops | bytes accessed | tf_op | source)
XLA Modules:
  0.0 69.2 jit_solution(5529620808942066871)
XLA Ops:
  1.4 0.8 %pad_maximum_fusion.2.refs_3_.refs_8_ = bf16[272,128]{1,0:T(8,128)(2,1)S(1)} fusion(bf16[16,128]{1,0:T(8,128)(2,1)S(1)} %broadcast_in_dim.9, bf16[128,128]{1,0:T(8,128)(2,1)} %param.12, bf16[128,128]{1,0:T(8,128)(2,1)} %param.11), kind=kLoop, calls=%fused_computation.9 | loop fusion | flops 208896 | bytes 139264 | tf_op jit(solution)/shard_map/concatenate | solution.py:301
  2.1 1.6 %collective-permute-start = (bf16[272,128]{1,0:T(8,128)(2,1)S(1)}, bf16[272,128]{1,0:T(8,128)(2,1)S(1)}, u32[]{:S(2)}, u32[]{:S(2)}) collective-permute-start(bf16[272,128]{1,0:T(8,128)(2,1)S(1)} %pad_maximum_fusion.2.refs_3_.refs_8_), channel_id=1, source_target_pairs={{0,8},{1,9},{2,10},{3,11},{4,12},{5,13},{6,14},{7,15},{8,0},{9,1},... | collective-permute-start | bytes 208904 | tf_op jit(solution)/shard_map/ppermute | solution.py:282
  4.4 0.8 %constant_dynamic-update-slice_fusion.1 = bf16[2,256,128]{2,1,0:T(8,128)(2,1)S(1)} fusion(bf16[1,256,128]{2,1,0:T(8,128)(2,1)} %param.9), kind=kLoop, calls=%fused_computation.13 | loop fusion | bytes 131072
  5.2 1.3 %pad_maximum_fusion.refs_1_ = bf16[2,256,1024]{2,1,0:T(8,128)(2,1)S(1)} fusion(bf16[1,256,1024]{2,1,0:T(8,128)(2,1)} %param.13, bf16[1,256,1024]{2,1,0:T(8,128)(2,1)} %param.8), kind=kLoop, calls=%fused_computation | loop fusion | flops 524288 | bytes 2097152 | tf_op jit(solution)/shard_map/concatenate | solution.py:303
  6.6 5.9 %collective-permute-start.2 = (bf16[544,128]{1,0:T(8,128)(2,1)S(1)}, bf16[544,128]{1,0:T(8,128)(2,1)S(1)}, u32[]{:S(2)}, u32[]{:S(2)}) collective-permute-start(bf16[544,128]{1,0:T(8,128)(2,1)S(1)} %pad_maximum_fusion.1), channel_id=1, source_target_pairs={{0,7},{1,2},{2,1},{3,4},{4,3},{5,6},{6,5},{7,0},{8,15},{9,10},{10,... | collective-permute-start | bytes 417800 | tf_op jit(solution)/shard_map/ppermute | solution.py:291
  12.5 1.5 %forward_stats.6 = (f32[32,256]{1,0:T(8,128)S(1)}, bf16[384,2048]{1,0:T(8,128)(2,1)S(1)}, f32[384,2048]{1,0:T(8,128)S(1)}, bf16[2048,128]{1,0:T(8,128)(2,1)S(1)}, bf16[2048,128]{1,0:T(8,128)(2,1)S(1)}) custom-call(s32[1]{0:T(128)S(6)} %copy.14.refs_0_, bf16[2,256,1024]{2,1,0:T(8,128)(2,1)S(1)} %pad_maximum_fusion.refs_1_, ...), custom_call_target="tpu_custom_call" | custom-call | flops 1207959552 | bytes 1048576 | tf_op jit(solution)/shard_map/forward_stats/pallas_call | solution.py:229
  14.6 1.3 %collective-permute-done.2.refs_3_.refs_7_ = bf16[544,128]{1,0:T(8,128)(2,1)S(1)} collective-permute-done((bf16[544,128]{1,0:T(8,128)(2,1)S(1)}, bf16[544,128]{1,0:T(8,128)(2,1)S(1)}, u32[]{:S(2)}, u32[]{:S(2)}) %collective-permute-start.2) | collective-permute-done | bytes 139296 | tf_op jit(solution)/shard_map/ppermute | solution.py:291
  16.7 0.9 %collective-permute-done.1.refs_2_.refs_6_ = bf16[544,128]{1,0:T(8,128)(2,1)S(1)} collective-permute-done((bf16[544,128]{1,0:T(8,128)(2,1)S(1)}, bf16[544,128]{1,0:T(8,128)(2,1)S(1)}, u32[]{:S(2)}, u32[]{:S(2)}) %collective-permute-start.1) | collective-permute-done | bytes 139296 | tf_op jit(solution)/shard_map/ppermute | solution.py:291
  17.7 1.2 %collective-permute-start.3 = (bf16[544,128]{1,0:T(8,128)(2,1)S(1)}, bf16[544,128]{1,0:T(8,128)(2,1)S(1)}, u32[]{:S(2)}, u32[]{:S(2)}) collective-permute-start(bf16[544,128]{1,0:T(8,128)(2,1)S(1)} %collective-permute-done.1.refs_2_.refs_6_), channel_id=1, source_target_pairs={{0,7},{1,2},{2,1},{3,4},{4,3},{5,6},{6,5},{7,0},{8,15},{9,10},{10,... | collective-permute-start | bytes 417800 | tf_op jit(solution)/shard_map/ppermute | solution.py:291
  18.9 2.4 %forward_stats.8 = (f32[32,256]{1,0:T(8,128)S(1)}, bf16[512,2048]{1,0:T(8,128)(2,1)S(1)}, f32[512,2048]{1,0:T(8,128)S(1)}) custom-call(bf16[2048,128]{1,0:T(8,128)(2,1)S(1)} %get-tuple-element.42.refs_0_.refs_1_, bf16[2048,128]{1,0:T(8,128)(2,1)S(1)} %get-tuple-element.43.refs_1_.refs_2_, bf16[544,128]{1,0:T(8,128)(2,1)S(1)} %collective-permute-done.1.refs_2_.refs_6_, ...), custom_call_target="tpu_custom_call" | custom-call | flops 1610612736 | bytes 1048576 | tf_op jit(solution)/shard_map/forward_stats/pallas_call | solution.py:229
  21.3 2.6 %collective-permute-start.6 = (bf16[544,128]{1,0:T(8,128)(2,1)S(1)}, bf16[544,128]{1,0:T(8,128)(2,1)S(1)}, u32[]{:S(2)}, u32[]{:S(2)}) collective-permute-start(bf16[544,128]{1,0:T(8,128)(2,1)S(1)} %collective-permute-done.4.refs_3_.refs_7_), channel_id=1, source_target_pairs={{0,7},{1,2},{2,1},{3,4},{4,3},{5,6},{6,5},{7,0},{8,15},{9,10},{10,... | collective-permute-start | bytes 417800 | tf_op jit(solution)/shard_map/ppermute | solution.py:291
  24.2 2.4 %forward_stats.9 = (f32[32,256]{1,0:T(8,128)S(1)}, bf16[512,2048]{1,0:T(8,128)(2,1)S(1)}, f32[512,2048]{1,0:T(8,128)S(1)}) custom-call(bf16[2048,128]{1,0:T(8,128)(2,1)S(1)} %get-tuple-element.42.refs_0_.refs_1_, bf16[2048,128]{1,0:T(8,128)(2,1)S(1)} %get-tuple-element.43.refs_1_.refs_2_, bf16[544,128]{1,0:T(8,128)(2,1)S(1)} %collective-permute-done.3.refs_2_.refs_6_, ...), custom_call_target="tpu_custom_call" | custom-call | flops 1610612736 | bytes 1048576 | tf_op jit(solution)/shard_map/forward_stats/pallas_call | solution.py:229
  26.7 2.6 %collective-permute-done.5.refs_2_.refs_6_ = bf16[544,128]{1,0:T(8,128)(2,1)S(1)} collective-permute-done((bf16[544,128]{1,0:T(8,128)(2,1)S(1)}, bf16[544,128]{1,0:T(8,128)(2,1)S(1)}, u32[]{:S(2)}, u32[]{:S(2)}) %collective-permute-start.5) | collective-permute-done | bytes 139296 | tf_op jit(solution)/shard_map/ppermute | solution.py:291
  29.3 0.9 %collective-permute-start.7 = (bf16[544,128]{1,0:T(8,128)(2,1)S(1)}, bf16[544,128]{1,0:T(8,128)(2,1)S(1)}, u32[]{:S(2)}, u32[]{:S(2)}) collective-permute-start(bf16[544,128]{1,0:T(8,128)(2,1)S(1)} %collective-permute-done.5.refs_2_.refs_6_), channel_id=1, source_target_pairs={{0,7},{1,2},{2,1},{3,4},{4,3},{5,6},{6,5},{7,0},{8,15},{9,10},{10,... | collective-permute-start | bytes 417800 | tf_op jit(solution)/shard_map/ppermute | solution.py:291
  30.2 2.4 %forward_stats.10 = (f32[32,256]{1,0:T(8,128)S(1)}, bf16[512,2048]{1,0:T(8,128)(2,1)S(1)}, f32[512,2048]{1,0:T(8,128)S(1)}) custom-call(bf16[2048,128]{1,0:T(8,128)(2,1)S(1)} %get-tuple-element.42.refs_0_.refs_1_, bf16[2048,128]{1,0:T(8,128)(2,1)S(1)} %get-tuple-element.43.refs_1_.refs_2_, bf16[544,128]{1,0:T(8,128)(2,1)S(1)} %collective-permute-done.5.refs_2_.refs_6_, ...), custom_call_target="tpu_custom_call" | custom-call | flops 1610612736 | bytes 1048576 | tf_op jit(solution)/shard_map/forward_stats/pallas_call | solution.py:229
  32.6 2.9 %collective-permute-done.7.refs_2_.refs_11_ = bf16[544,128]{1,0:T(8,128)(2,1)S(1)} collective-permute-done((bf16[544,128]{1,0:T(8,128)(2,1)S(1)}, bf16[544,128]{1,0:T(8,128)(2,1)S(1)}, u32[]{:S(2)}, u32[]{:S(2)}) %collective-permute-start.7) | collective-permute-done | bytes 139296 | tf_op jit(solution)/shard_map/ppermute | solution.py:291
  35.6 1.1 %forward_stats.11 = (f32[32,256]{1,0:T(8,128)S(1)}, bf16[256,2048]{1,0:T(8,128)(2,1)S(1)}, f32[256,2048]{1,0:T(8,128)S(1)}) custom-call(bf16[2048,128]{1,0:T(8,128)(2,1)S(1)} %get-tuple-element.42.refs_0_.refs_1_, bf16[2048,128]{1,0:T(8,128)(2,1)S(1)} %get-tuple-element.43.refs_1_.refs_2_, bf16[544,128]{1,0:T(8,128)(2,1)S(1)} %collective-permute-done.7.refs_2_.refs_11_), custom_call_target="tpu_custom_call" | custom-call | flops 805306368 | bytes 1048576 | tf_op jit(solution)/shard_map/forward_stats/pallas_call | solution.py:229
  36.6 1.1 %backward_grads.6 = (f32[1024,256]{1,0:T(8,128)S(1)}, bf16[512,128]{1,0:T(8,128)(2,1)S(1)}, f32[64,256]{1,0:T(8,128)S(1)}) custom-call(s32[1]{0:T(128)S(6)} %copy.15.refs_0_, bf16[2048,128]{1,0:T(8,128)(2,1)S(1)} %get-tuple-element.42.refs_0_.refs_1_, bf16[2048,128]{1,0:T(8,128)(2,1)S(1)} %get-tuple-element.43.refs_1_.refs_2_, ...), custom_call_target="tpu_custom_call" | custom-call | flops 1342177280 | bytes 2097152 | tf_op jit(solution)/shard_map/backward_grads/pallas_call | solution.py:260
  37.8 1.0 %collective-permute-start.8 = (bf16[512,128]{1,0:T(8,128)(2,1)S(1)}, bf16[512,128]{1,0:T(8,128)(2,1)S(1)}, u32[]{:S(2)}, u32[]{:S(2)}) collective-permute-start(bf16[512,128]{1,0:T(8,128)(2,1)S(1)} %get-tuple-element.65), channel_id=1, source_target_pairs={{0,7},{1,2},{2,1},{3,4},{4,3},{5,6},{6,5},{7,0},{8,15},{9,10},{10,... | collective-permute-start | bytes 393224 | tf_op jit(solution)/shard_map/ppermute | solution.py:291
  38.8 2.0 %backward_grads.7 = (f32[1024,256]{1,0:T(8,128)S(1)}, f32[512,128]{1,0:T(8,128)S(1)}, bf16[512,128]{1,0:T(8,128)(2,1)S(1)}) custom-call(s32[1]{0:T(128)S(6)} %copy.15.refs_0_, bf16[2048,128]{1,0:T(8,128)(2,1)S(1)} %get-tuple-element.42.refs_0_.refs_1_, bf16[2048,128]{1,0:T(8,128)(2,1)S(1)} %get-tuple-element.43.refs_1_.refs_2_, ...), custom_call_target="tpu_custom_call" | custom-call | flops 2684354560 | bytes 2097152 | tf_op jit(solution)/shard_map/backward_grads/pallas_call | solution.py:260
  40.8 2.4 %collective-permute-start.10 = (bf16[512,128]{1,0:T(8,128)(2,1)S(1)}, bf16[512,128]{1,0:T(8,128)(2,1)S(1)}, u32[]{:S(2)}, u32[]{:S(2)}) collective-permute-start(bf16[512,128]{1,0:T(8,128)(2,1)S(1)} %get-tuple-element.67.refs_10_), channel_id=1, source_target_pairs={{0,7},{1,2},{2,1},{3,4},{4,3},{5,6},{6,5},{7,0},{8,15},{9,10},{10,... | collective-permute-start | bytes 393224 | tf_op jit(solution)/shard_map/ppermute | solution.py:291
  43.2 0.8 %collective-permute-done.8 = bf16[512,128]{1,0:T(8,128)(2,1)S(1)} collective-permute-done((bf16[512,128]{1,0:T(8,128)(2,1)S(1)}, bf16[512,128]{1,0:T(8,128)(2,1)S(1)}, u32[]{:S(2)}, u32[]{:S(2)}) %collective-permute-start.8) | collective-permute-done | bytes 131104 | tf_op jit(solution)/shard_map/ppermute | solution.py:291
  44.2 2.0 %backward_grads.8 = (f32[1024,256]{1,0:T(8,128)S(1)}, f32[512,128]{1,0:T(8,128)S(1)}, f32[512,128]{1,0:T(8,128)S(1)}) custom-call(s32[1]{0:T(128)S(6)} %copy.15.refs_0_, bf16[2048,128]{1,0:T(8,128)(2,1)S(1)} %get-tuple-element.42.refs_0_.refs_1_, bf16[2048,128]{1,0:T(8,128)(2,1)S(1)} %get-tuple-element.43.refs_1_.refs_2_, ...), custom_call_target="tpu_custom_call" | custom-call | flops 2684354560 | bytes 2097152 | tf_op jit(solution)/shard_map/backward_grads/pallas_call | solution.py:260
  46.2 2.0 %collective-permute-done.10 = bf16[512,128]{1,0:T(8,128)(2,1)S(1)} collective-permute-done((bf16[512,128]{1,0:T(8,128)(2,1)S(1)}, bf16[512,128]{1,0:T(8,128)(2,1)S(1)}, u32[]{:S(2)}, u32[]{:S(2)}) %collective-permute-start.10) | collective-permute-done | bytes 131104 | tf_op jit(solution)/shard_map/ppermute | solution.py:291
  49.2 1.0 %collective-permute-start.11 = (bf16[512,128]{1,0:T(8,128)(2,1)S(1)}, bf16[512,128]{1,0:T(8,128)(2,1)S(1)}, u32[]{:S(2)}, u32[]{:S(2)}) collective-permute-start(bf16[512,128]{1,0:T(8,128)(2,1)S(1)} %add_convert_fusion.3.refs_9_), channel_id=1, source_target_pairs={{0,7},{1,2},{2,1},{3,4},{4,3},{5,6},{6,5},{7,0},{8,15},{9,10},{10,... | collective-permute-start | bytes 393224 | tf_op jit(solution)/shard_map/ppermute | solution.py:291
  50.2 2.0 %backward_grads.9 = (f32[1024,256]{1,0:T(8,128)S(1)}, f32[512,128]{1,0:T(8,128)S(1)}, f32[512,128]{1,0:T(8,128)S(1)}) custom-call(s32[1]{0:T(128)S(6)} %copy.15.refs_0_, bf16[2048,128]{1,0:T(8,128)(2,1)S(1)} %get-tuple-element.42.refs_0_.refs_1_, bf16[2048,128]{1,0:T(8,128)(2,1)S(1)} %get-tuple-element.43.refs_1_.refs_2_, ...), custom_call_target="tpu_custom_call" | custom-call | flops 2684354560 | bytes 2097152 | tf_op jit(solution)/shard_map/backward_grads/pallas_call | solution.py:260
  52.2 1.5 %collective-permute-done.12 = bf16[512,128]{1,0:T(8,128)(2,1)S(1)} collective-permute-done((bf16[512,128]{1,0:T(8,128)(2,1)S(1)}, bf16[512,128]{1,0:T(8,128)(2,1)S(1)}, u32[]{:S(2)}, u32[]{:S(2)}) %collective-permute-start.12) | collective-permute-done | bytes 131104 | tf_op jit(solution)/shard_map/ppermute | solution.py:291
  53.7 1.5 %collective-permute-start.13 = (bf16[512,128]{1,0:T(8,128)(2,1)S(1)}, bf16[512,128]{1,0:T(8,128)(2,1)S(1)}, u32[]{:S(2)}, u32[]{:S(2)}) collective-permute-start(bf16[512,128]{1,0:T(8,128)(2,1)S(1)} %add_convert_fusion.refs_12_), channel_id=1, source_target_pairs={{0,7},{1,2},{2,1},{3,4},{4,3},{5,6},{6,5},{7,0},{8,15},{9,10},{10,... | collective-permute-start | bytes 393224 | tf_op jit(solution)/shard_map/ppermute | solution.py:291
  55.6 1.1 %backward_grads.10 = (f32[1024,256]{1,0:T(8,128)S(1)}, f32[512,128]{1,0:T(8,128)S(1)}) custom-call(s32[1]{0:T(128)S(6)} %copy.15.refs_0_, bf16[2048,128]{1,0:T(8,128)(2,1)S(1)} %get-tuple-element.42.refs_0_.refs_1_, bf16[2048,128]{1,0:T(8,128)(2,1)S(1)} %get-tuple-element.43.refs_1_.refs_2_, f32[64,256]{1,0:T(8,128)S(1)} %get-tuple-element.52.refs_3_, ...), custom_call_target="tpu_custom_call" | custom-call | flops 1342177280 | bytes 2097152 | tf_op jit(solution)/shard_map/backward_grads/pallas_call | solution.py:260
  56.7 3.5 %collective-permute-done.13 = bf16[512,128]{1,0:T(8,128)(2,1)S(1)} collective-permute-done((bf16[512,128]{1,0:T(8,128)(2,1)S(1)}, bf16[512,128]{1,0:T(8,128)(2,1)S(1)}, u32[]{:S(2)}, u32[]{:S(2)}) %collective-permute-start.13) | collective-permute-done | bytes 131104 | tf_op jit(solution)/shard_map/ppermute | solution.py:291
  60.6 5.6 %collective-permute-start.15 = (bf16[256,128]{1,0:T(8,128)(2,1)S(1)}, bf16[256,128]{1,0:T(8,128)(2,1)S(1)}, u32[]{:S(2)}, u32[]{:S(2)}) collective-permute-start(bf16[256,128]{1,0:T(8,128)(2,1)S(1)} %slice.31.refs_8_), channel_id=1, source_target_pairs={{0,8},{1,9},{2,10},{3,11},{4,12},{5,13},{6,14},{7,15},{8,0},{9,1},... | collective-permute-start | bytes 196616 | tf_op jit(solution)/shard_map/ppermute | solution.py:282
  66.2 2.2 %backward_grads.11 = (f32[1,256,1024]{2,1,0:T(8,128)}, f32[1,256,128]{2,1,0:T(8,128)}, f32[1,256,128]{2,1,0:T(8,128)}) custom-call(s32[1]{0:T(128)S(6)} %copy.15.refs_0_, bf16[2048,128]{1,0:T(8,128)(2,1)S(1)} %get-tuple-element.42.refs_0_.refs_1_, bf16[2048,128]{1,0:T(8,128)(2,1)S(1)} %get-tuple-element.43.refs_1_.refs_2_, ...), custom_call_target="tpu_custom_call" | custom-call | flops 1342177280 | bytes 2097152 | tf_op jit(solution)/shard_map/backward_grads/pallas_call | solution.py:260
  (33 shorter events, 4.3 us)
Async XLA Ops:
  0.6 5.9 %copy-start = (bf16[128,128]{1,0:T(8,128)(2,1)S(1)}, bf16[128,128]{1,0:T(8,128)(2,1)}, u32[]{:S(2)}) copy-start(bf16[128,128]{1,0:T(8,128)(2,1)} %param.12) | copy-start | bytes 98308
  0.6 5.9 %copy-start.1 = (bf16[128,128]{1,0:T(8,128)(2,1)S(1)}, bf16[128,128]{1,0:T(8,128)(2,1)}, u32[]{:S(2)}) copy-start(bf16[128,128]{1,0:T(8,128)(2,1)} %param.11) | copy-start | bytes 98308
  0.7 5.9 %copy-start.2 = (bf16[1,256,128]{2,1,0:T(8,128)(2,1)S(1)}, bf16[1,256,128]{2,1,0:T(8,128)(2,1)}, u32[]{:S(2)}) copy-start(bf16[1,256,128]{2,1,0:T(8,128)(2,1)} %param.10) | copy-start | bytes 196612
  2.1 4.4 %collective-permute-start = (bf16[272,128]{1,0:T(8,128)(2,1)S(1)}, bf16[272,128]{1,0:T(8,128)(2,1)S(1)}, u32[]{:S(2)}, u32[]{:S(2)}) collective-permute-start(bf16[272,128]{1,0:T(8,128)(2,1)S(1)} %pad_maximum_fusion.2.refs_3_.refs_8_), channel_id=1, source_target_pairs={{0,8},{1,9},{2,10},{3,11},{4,12},{5,13},{6,14},{7,15},{8,0},{9,1},... | collective-permute-start | bytes 208904 | tf_op jit(solution)/shard_map/ppermute | solution.py:282
  6.6 9.3 %collective-permute-start.2 = (bf16[544,128]{1,0:T(8,128)(2,1)S(1)}, bf16[544,128]{1,0:T(8,128)(2,1)S(1)}, u32[]{:S(2)}, u32[]{:S(2)}) collective-permute-start(bf16[544,128]{1,0:T(8,128)(2,1)S(1)} %pad_maximum_fusion.1), channel_id=1, source_target_pairs={{0,7},{1,2},{2,1},{3,4},{4,3},{5,6},{6,5},{7,0},{8,15},{9,10},{10,... | collective-permute-start | bytes 417800 | tf_op jit(solution)/shard_map/ppermute | solution.py:291
  12.5 5.1 %collective-permute-start.1 = (bf16[544,128]{1,0:T(8,128)(2,1)S(1)}, bf16[544,128]{1,0:T(8,128)(2,1)S(1)}, u32[]{:S(2)}, u32[]{:S(2)}) collective-permute-start(bf16[544,128]{1,0:T(8,128)(2,1)S(1)} %pad_maximum_fusion.1), channel_id=1, source_target_pairs={{0,1},{1,0},{2,3},{3,2},{4,5},{5,4},{6,7},{7,6},{8,9},{9,8},{10,11... | collective-permute-start | bytes 417800 | tf_op jit(solution)/shard_map/ppermute | solution.py:291
  15.9 5.4 %collective-permute-start.4 = (bf16[544,128]{1,0:T(8,128)(2,1)S(1)}, bf16[544,128]{1,0:T(8,128)(2,1)S(1)}, u32[]{:S(2)}, u32[]{:S(2)}) collective-permute-start(bf16[544,128]{1,0:T(8,128)(2,1)S(1)} %collective-permute-done.2.refs_3_.refs_7_), channel_id=1, source_target_pairs={{0,1},{1,0},{2,3},{3,2},{4,5},{5,4},{6,7},{7,6},{8,9},{9,8},{10,11... | collective-permute-start | bytes 417800 | tf_op jit(solution)/shard_map/ppermute | solution.py:291
  17.7 6.6 %collective-permute-start.3 = (bf16[544,128]{1,0:T(8,128)(2,1)S(1)}, bf16[544,128]{1,0:T(8,128)(2,1)S(1)}, u32[]{:S(2)}, u32[]{:S(2)}) collective-permute-start(bf16[544,128]{1,0:T(8,128)(2,1)S(1)} %collective-permute-done.1.refs_2_.refs_6_), channel_id=1, source_target_pairs={{0,7},{1,2},{2,1},{3,4},{4,3},{5,6},{6,5},{7,0},{8,15},{9,10},{10,... | collective-permute-start | bytes 417800 | tf_op jit(solution)/shard_map/ppermute | solution.py:291
  21.3 8.9 %collective-permute-start.6 = (bf16[544,128]{1,0:T(8,128)(2,1)S(1)}, bf16[544,128]{1,0:T(8,128)(2,1)S(1)}, u32[]{:S(2)}, u32[]{:S(2)}) collective-permute-start(bf16[544,128]{1,0:T(8,128)(2,1)S(1)} %collective-permute-done.4.refs_3_.refs_7_), channel_id=1, source_target_pairs={{0,7},{1,2},{2,1},{3,4},{4,3},{5,6},{6,5},{7,0},{8,15},{9,10},{10,... | collective-permute-start | bytes 417800 | tf_op jit(solution)/shard_map/ppermute | solution.py:291
  24.2 5.1 %collective-permute-start.5 = (bf16[544,128]{1,0:T(8,128)(2,1)S(1)}, bf16[544,128]{1,0:T(8,128)(2,1)S(1)}, u32[]{:S(2)}, u32[]{:S(2)}) collective-permute-start(bf16[544,128]{1,0:T(8,128)(2,1)S(1)} %collective-permute-done.3.refs_2_.refs_6_), channel_id=1, source_target_pairs={{0,1},{1,0},{2,3},{3,2},{4,5},{5,4},{6,7},{7,6},{8,9},{9,8},{10,11... | collective-permute-start | bytes 417800 | tf_op jit(solution)/shard_map/ppermute | solution.py:291
  29.3 6.3 %collective-permute-start.7 = (bf16[544,128]{1,0:T(8,128)(2,1)S(1)}, bf16[544,128]{1,0:T(8,128)(2,1)S(1)}, u32[]{:S(2)}, u32[]{:S(2)}) collective-permute-start(bf16[544,128]{1,0:T(8,128)(2,1)S(1)} %collective-permute-done.5.refs_2_.refs_6_), channel_id=1, source_target_pairs={{0,7},{1,2},{2,1},{3,4},{4,3},{5,6},{6,5},{7,0},{8,15},{9,10},{10,... | collective-permute-start | bytes 417800 | tf_op jit(solution)/shard_map/ppermute | solution.py:291
  37.8 6.3 %collective-permute-start.8 = (bf16[512,128]{1,0:T(8,128)(2,1)S(1)}, bf16[512,128]{1,0:T(8,128)(2,1)S(1)}, u32[]{:S(2)}, u32[]{:S(2)}) collective-permute-start(bf16[512,128]{1,0:T(8,128)(2,1)S(1)} %get-tuple-element.65), channel_id=1, source_target_pairs={{0,7},{1,2},{2,1},{3,4},{4,3},{5,6},{6,5},{7,0},{8,15},{9,10},{10,... | collective-permute-start | bytes 393224 | tf_op jit(solution)/shard_map/ppermute | solution.py:291
  40.8 7.4 %collective-permute-start.10 = (bf16[512,128]{1,0:T(8,128)(2,1)S(1)}, bf16[512,128]{1,0:T(8,128)(2,1)S(1)}, u32[]{:S(2)}, u32[]{:S(2)}) collective-permute-start(bf16[512,128]{1,0:T(8,128)(2,1)S(1)} %get-tuple-element.67.refs_10_), channel_id=1, source_target_pairs={{0,7},{1,2},{2,1},{3,4},{4,3},{5,6},{6,5},{7,0},{8,15},{9,10},{10,... | collective-permute-start | bytes 393224 | tf_op jit(solution)/shard_map/ppermute | solution.py:291
  44.1 5.1 %collective-permute-start.9 = (bf16[512,128]{1,0:T(8,128)(2,1)S(1)}, bf16[512,128]{1,0:T(8,128)(2,1)S(1)}, u32[]{:S(2)}, u32[]{:S(2)}) collective-permute-start(bf16[512,128]{1,0:T(8,128)(2,1)S(1)} %add_convert_fusion.4.refs_9_), channel_id=1, source_target_pairs={{0,1},{1,0},{2,3},{3,2},{4,5},{5,4},{6,7},{7,6},{8,9},{9,8},{10,11... | collective-permute-start | bytes 393224 | tf_op jit(solution)/shard_map/ppermute | solution.py:291
  48.3 5.4 %collective-permute-start.12 = (bf16[512,128]{1,0:T(8,128)(2,1)S(1)}, bf16[512,128]{1,0:T(8,128)(2,1)S(1)}, u32[]{:S(2)}, u32[]{:S(2)}) collective-permute-start(bf16[512,128]{1,0:T(8,128)(2,1)S(1)} %add_convert_fusion.2.refs_10_), channel_id=1, source_target_pairs={{0,1},{1,0},{2,3},{3,2},{4,5},{5,4},{6,7},{7,6},{8,9},{9,8},{10,11... | collective-permute-start | bytes 393224 | tf_op jit(solution)/shard_map/ppermute | solution.py:291
  49.2 6.3 %collective-permute-start.11 = (bf16[512,128]{1,0:T(8,128)(2,1)S(1)}, bf16[512,128]{1,0:T(8,128)(2,1)S(1)}, u32[]{:S(2)}, u32[]{:S(2)}) collective-permute-start(bf16[512,128]{1,0:T(8,128)(2,1)S(1)} %add_convert_fusion.3.refs_9_), channel_id=1, source_target_pairs={{0,7},{1,2},{2,1},{3,4},{4,3},{5,6},{6,5},{7,0},{8,15},{9,10},{10,... | collective-permute-start | bytes 393224 | tf_op jit(solution)/shard_map/ppermute | solution.py:291
  53.7 6.5 %collective-permute-start.13 = (bf16[512,128]{1,0:T(8,128)(2,1)S(1)}, bf16[512,128]{1,0:T(8,128)(2,1)S(1)}, u32[]{:S(2)}, u32[]{:S(2)}) collective-permute-start(bf16[512,128]{1,0:T(8,128)(2,1)S(1)} %add_convert_fusion.refs_12_), channel_id=1, source_target_pairs={{0,7},{1,2},{2,1},{3,4},{4,3},{5,6},{6,5},{7,0},{8,15},{9,10},{10,... | collective-permute-start | bytes 393224 | tf_op jit(solution)/shard_map/ppermute | solution.py:291
  55.5 5.1 %collective-permute-start.14 = (bf16[512,128]{1,0:T(8,128)(2,1)S(1)}, bf16[512,128]{1,0:T(8,128)(2,1)S(1)}, u32[]{:S(2)}, u32[]{:S(2)}) collective-permute-start(bf16[512,128]{1,0:T(8,128)(2,1)S(1)} %add_convert_fusion.1.refs_11_), channel_id=1, source_target_pairs={{0,1},{1,0},{2,3},{3,2},{4,5},{5,4},{6,7},{7,6},{8,9},{9,8},{10,11... | collective-permute-start | bytes 393224 | tf_op jit(solution)/shard_map/ppermute | solution.py:291
  60.6 7.9 %collective-permute-start.15 = (bf16[256,128]{1,0:T(8,128)(2,1)S(1)}, bf16[256,128]{1,0:T(8,128)(2,1)S(1)}, u32[]{:S(2)}, u32[]{:S(2)}) collective-permute-start(bf16[256,128]{1,0:T(8,128)(2,1)S(1)} %slice.31.refs_8_), channel_id=1, source_target_pairs={{0,8},{1,9},{2,10},{3,11},{4,12},{5,13},{6,14},{7,15},{8,0},{9,1},... | collective-permute-start | bytes 196616 | tf_op jit(solution)/shard_map/ppermute | solution.py:282

commit v10 on v8

--- a/solution.py
+++ b/solution.py
@@ -308,7 +308,7 @@
         far.append(along(far[-1], (step - 1) % 2))
         if step < 4:
             near.append(along(near[-1], step % 2))
-    for blocks in ([swapped], [far[1], near[1]], [far[2], near[2]], [far[3], near[3]], [far[4]]):
+    for blocks in ([swapped], [near[1], far[1]], [near[2], far[2]], [near[3], far[3]], [far[4]]):
         stat, *keep = forward_stats(heads, share, blocks, rows)
         stats.append(stat)
         kept.append(keep)
@@ -335,7 +335,7 @@
     given = across(part)
     dq, part, part_far = back(
         parts=(*planes(4, 1), (5, 0, share)),
-        blocks=[(far[3], 1, 1), (near[3], 1, 1), (far[4], 0, 1)],
+        blocks=[(near[3], 1, 1), (far[3], 1, 1), (far[4], 0, 1)],
         outs=[both_ready, wide], prior=dq, after=(),
     )
     down = add(part_far, given)
@@ -344,20 +344,20 @@
     for step in (3, 2, 1):
         if step > 1:
             parts = (*planes(step, 1), *planes(step + 1, 0))
-            blocks = [(far[step - 1], 1, 1), (near[step - 1], 1, 1)]
+            blocks = [(near[step - 1], 1, 1), (far[step - 1], 1, 1)]
             outs = [both_ready, wide, wide]
         else:
             parts = ((1, 0, share), *planes(2, 0))
             blocks = [(swapped, 0, 1)]
             outs = [ready, wide, wide]
-        blocks += [(far[step], 0, 1), (near[step], 0, 1)]
-        dq, part, part_far, part_near = back(
+        blocks += [(near[step], 0, 1), (far[step], 0, 1)]
+        dq, part, part_near, part_far = back(
             parts=parts, blocks=blocks, outs=outs, prior=dq,
             after=(down,) if up is None else (down, up),
         )
         relayed = () if up is None else (along(up, (step + 1) % 2),)
-        up = add(part_near, given[size:], *relayed)
-        down = add(part_far, given[:size], along(down, step % 2))
+        up = add(part_near, given[:size], *relayed)
+        down = add(part_far, given[size:], along(down, step % 2))
         given = across(part)
     grad_queries, mine, grad_resp_keys, grad_resp_values = back(
         parts=((0, 0, share + resp),), blocks=[(packed, 0, 1)], outs=[wide, grads, grads],

time: 69.6 us -> 67.9 us (0.976)
  waiting for transfers between devices: 15.1 us -> 11.7 us
  starting transfers between devices: 27.7 us -> 29.5 us
    ppermute x14, starting transfers between devices: 19.3 us -> 22.3 us  [along(): return lax.ppermute(block, 'sample', pairs)]
    ppermute x14, waiting for transfers between devices: 13.9 us -> 11.1 us  [along(): return lax.ppermute(block, 'sample', pairs)]
    ppermute x6, starting transfers between devices: 8.41 us -> 7.16 us  [across(): return lax.ppermute(block, 'sample', pairs)]
  transfers between devices with their start and end apart: 20 -> 20, of which waited for: 12 -> 10; matrix products, arithmetic and copies ran while one was open for 3% -> 3% of each run, Pallas kernels for 27% -> 28%
where the time goes in v10:
time: 67.9 us; the launch traced here: 67.6 us
  starting transfers between devices  29.5 us (43%)
  Pallas kernels  20.5 us (30%)
  waiting for transfers between devices  11.7 us (17%)
  other arithmetic  2.95 us (4%)
  between operations  2.17 us (3%)
  local copies, waits for them, and re-layouts  0.88 us (1%)
    ppermute x14, starting transfers between devices, along(): return lax.ppermute(block, 'sample', pairs)  22.3 us
    ppermute x14, waiting for transfers between devices, along(): return lax.ppermute(block, 'sample', pairs)  11.1 us
    pallas_call x6, Pallas kernels, backward_grads(): pl.pallas_call(functools.partial(backward_kernel, heads, share, owners, p...  10.4 us
    pallas_call x6, Pallas kernels, forward_stats(): pl.pallas_call(functools.partial(forward_kernel, heads, share, picks, boo...  10.1 us
    ppermute x6, starting transfers between devices, across(): return lax.ppermute(block, 'sample', pairs)  7.16 us
  transfers between devices with their start and end apart: 20, of which 10 were waited for; matrix products, arithmetic and copies ran while one was open for 3% of the time, Pallas kernels for 28%

profile of v10, /device:TPU:2, one launch (start us, length us, event | category | flops | bytes accessed | tf_op | source)
XLA Modules:
  0.0 67.6 jit_solution(16277161551015368068)
XLA Ops:
  1.4 0.8 %pad_maximum_fusion.2.refs_3_.refs_6_ = bf16[272,128]{1,0:T(8,128)(2,1)S(1)} fusion(bf16[16,128]{1,0:T(8,128)(2,1)S(1)} %broadcast_in_dim.9, bf16[128,128]{1,0:T(8,128)(2,1)} %param.12, bf16[128,128]{1,0:T(8,128)(2,1)} %param.11), kind=kLoop, calls=%fused_computation.9 | loop fusion | flops 208896 | bytes 139264 | tf_op jit(solution)/shard_map/concatenate | solution.py:296
  2.1 1.6 %collective-permute-start = (bf16[272,128]{1,0:T(8,128)(2,1)S(1)}, bf16[272,128]{1,0:T(8,128)(2,1)S(1)}, u32[]{:S(2)}, u32[]{:S(2)}) collective-permute-start(bf16[272,128]{1,0:T(8,128)(2,1)S(1)} %pad_maximum_fusion.2.refs_3_.refs_6_), channel_id=1, source_target_pairs={{0,8},{1,9},{2,10},{3,11},{4,12},{5,13},{6,14},{7,15},{8,0},{9,1},... | collective-permute-start | bytes 208904 | tf_op jit(solution)/shard_map/ppermute | solution.py:277
  4.4 0.8 %constant_dynamic-update-slice_fusion.1 = bf16[2,256,128]{2,1,0:T(8,128)(2,1)S(1)} fusion(bf16[1,256,128]{2,1,0:T(8,128)(2,1)} %param.9), kind=kLoop, calls=%fused_computation.13 | loop fusion | bytes 131072
  5.2 1.3 %pad_maximum_fusion.refs_1_ = bf16[2,256,1024]{2,1,0:T(8,128)(2,1)S(1)} fusion(bf16[1,256,1024]{2,1,0:T(8,128)(2,1)} %param.13, bf16[1,256,1024]{2,1,0:T(8,128)(2,1)} %param.8), kind=kLoop, calls=%fused_computation | loop fusion | flops 524288 | bytes 2097152 | tf_op jit(solution)/shard_map/concatenate | solution.py:298
  6.6 2.0 %collective-permute-start.2 = (bf16[544,128]{1,0:T(8,128)(2,1)S(1)}, bf16[544,128]{1,0:T(8,128)(2,1)S(1)}, u32[]{:S(2)}, u32[]{:S(2)}) collective-permute-start(bf16[544,128]{1,0:T(8,128)(2,1)S(1)} %pad_maximum_fusion.1), channel_id=1, source_target_pairs={{0,1},{1,0},{2,3},{3,2},{4,5},{5,4},{6,7},{7,6},{8,9},{9,8},{10,11... | collective-permute-start | bytes 417800 | tf_op jit(solution)/shard_map/ppermute | solution.py:286
  8.6 4.9 %collective-permute-start.1 = (bf16[544,128]{1,0:T(8,128)(2,1)S(1)}, bf16[544,128]{1,0:T(8,128)(2,1)S(1)}, u32[]{:S(2)}, u32[]{:S(2)}) collective-permute-start(bf16[544,128]{1,0:T(8,128)(2,1)S(1)} %pad_maximum_fusion.1), channel_id=1, source_target_pairs={{0,7},{1,2},{2,1},{3,4},{4,3},{5,6},{6,5},{7,0},{8,15},{9,10},{10,... | collective-permute-start | bytes 417800 | tf_op jit(solution)/shard_map/ppermute | solution.py:286
  13.6 1.5 %forward_stats.6 = (f32[32,256]{1,0:T(8,128)S(1)}, bf16[384,2048]{1,0:T(8,128)(2,1)S(1)}, f32[384,2048]{1,0:T(8,128)S(1)}, bf16[2048,128]{1,0:T(8,128)(2,1)S(1)}, bf16[2048,128]{1,0:T(8,128)(2,1)S(1)}) custom-call(s32[1]{0:T(128)S(6)} %copy.14.refs_0_, bf16[2,256,1024]{2,1,0:T(8,128)(2,1)S(1)} %pad_maximum_fusion.refs_1_, ...), custom_call_target="tpu_custom_call" | custom-call | flops 1207959552 | bytes 1048576 | tf_op jit(solution)/shard_map/forward_stats/pallas_call | solution.py:224
  15.7 2.0 %collective-permute-start.4 = (bf16[544,128]{1,0:T(8,128)(2,1)S(1)}, bf16[544,128]{1,0:T(8,128)(2,1)S(1)}, u32[]{:S(2)}, u32[]{:S(2)}) collective-permute-start(bf16[544,128]{1,0:T(8,128)(2,1)S(1)} %collective-permute-done.2.refs_3_.refs_13_.refs_12_), channel_id=1, source_target_pairs={{0,7},{1,2},{2,1},{3,4},{4,3},{5,6},{6,5},{7,0},{8,15},{9,10},{10,... | collective-permute-start | bytes 417800 | tf_op jit(solution)/shard_map/ppermute | solution.py:286
  17.7 2.3 %forward_stats.8 = (f32[32,256]{1,0:T(8,128)S(1)}, bf16[512,2048]{1,0:T(8,128)(2,1)S(1)}, f32[512,2048]{1,0:T(8,128)S(1)}) custom-call(bf16[2048,128]{1,0:T(8,128)(2,1)S(1)} %get-tuple-element.47.refs_0_.refs_1_, bf16[2048,128]{1,0:T(8,128)(2,1)S(1)} %get-tuple-element.48.refs_1_.refs_2_, ...), custom_call_target="tpu_custom_call" | custom-call | flops 1610612736 | bytes 1048576 | tf_op jit(solution)/shard_map/forward_stats/pallas_call | solution.py:224
  20.0 2.1 %collective-permute-done.4.refs_3_.refs_13_.refs_15_ = bf16[544,128]{1,0:T(8,128)(2,1)S(1)} collective-permute-done((bf16[544,128]{1,0:T(8,128)(2,1)S(1)}, bf16[544,128]{1,0:T(8,128)(2,1)S(1)}, u32[]{:S(2)}, u32[]{:S(2)}) %collective-permute-start.4) | collective-permute-done | bytes 139296 | tf_op jit(solution)/shard_map/ppermute | solution.py:286
  22.1 0.8 %collective-permute-done.3.refs_2_.refs_12_.refs_14_ = bf16[544,128]{1,0:T(8,128)(2,1)S(1)} collective-permute-done((bf16[544,128]{1,0:T(8,128)(2,1)S(1)}, bf16[544,128]{1,0:T(8,128)(2,1)S(1)}, u32[]{:S(2)}, u32[]{:S(2)}) %collective-permute-start.3) | collective-permute-done | bytes 139296 | tf_op jit(solution)/shard_map/ppermute | solution.py:286
  22.9 2.8 %collective-permute-start.5 = (bf16[544,128]{1,0:T(8,128)(2,1)S(1)}, bf16[544,128]{1,0:T(8,128)(2,1)S(1)}, u32[]{:S(2)}, u32[]{:S(2)}) collective-permute-start(bf16[544,128]{1,0:T(8,128)(2,1)S(1)} %collective-permute-done.3.refs_2_.refs_12_.refs_14_), channel_id=1, source_target_pairs={{0,7},{1,2},{2,1},{3,4},{4,3},{5,6},{6,5},{7,0},{8,15},{9,10},{10,... | collective-permute-start | bytes 417800 | tf_op jit(solution)/shard_map/ppermute | solution.py:286
  25.8 2.3 %forward_stats.9 = (f32[32,256]{1,0:T(8,128)S(1)}, bf16[512,2048]{1,0:T(8,128)(2,1)S(1)}, f32[512,2048]{1,0:T(8,128)S(1)}) custom-call(bf16[2048,128]{1,0:T(8,128)(2,1)S(1)} %get-tuple-element.47.refs_0_.refs_1_, bf16[2048,128]{1,0:T(8,128)(2,1)S(1)} %get-tuple-element.48.refs_1_.refs_2_, ...), custom_call_target="tpu_custom_call" | custom-call | flops 1610612736 | bytes 1048576 | tf_op jit(solution)/shard_map/forward_stats/pallas_call | solution.py:224
  28.1 0.9 %collective-permute-start.7 = (bf16[544,128]{1,0:T(8,128)(2,1)S(1)}, bf16[544,128]{1,0:T(8,128)(2,1)S(1)}, u32[]{:S(2)}, u32[]{:S(2)}) collective-permute-start(bf16[544,128]{1,0:T(8,128)(2,1)S(1)} %collective-permute-done.6.refs_3_.refs_11_.refs_15_), channel_id=1, source_target_pairs={{0,7},{1,2},{2,1},{3,4},{4,3},{5,6},{6,5},{7,0},{8,15},{9,10},{10,... | collective-permute-start | bytes 417800 | tf_op jit(solution)/shard_map/ppermute | solution.py:286
  29.0 1.4 %collective-permute-done.5.refs_2_.refs_10_.refs_14_ = bf16[544,128]{1,0:T(8,128)(2,1)S(1)} collective-permute-done((bf16[544,128]{1,0:T(8,128)(2,1)S(1)}, bf16[544,128]{1,0:T(8,128)(2,1)S(1)}, u32[]{:S(2)}, u32[]{:S(2)}) %collective-permute-start.5) | collective-permute-done | bytes 139296 | tf_op jit(solution)/shard_map/ppermute | solution.py:286
  30.4 2.3 %forward_stats.10 = (f32[32,256]{1,0:T(8,128)S(1)}, bf16[512,2048]{1,0:T(8,128)(2,1)S(1)}, f32[512,2048]{1,0:T(8,128)S(1)}) custom-call(bf16[2048,128]{1,0:T(8,128)(2,1)S(1)} %get-tuple-element.47.refs_0_.refs_1_, bf16[2048,128]{1,0:T(8,128)(2,1)S(1)} %get-tuple-element.48.refs_1_.refs_2_, ...), custom_call_target="tpu_custom_call" | custom-call | flops 1610612736 | bytes 1048576 | tf_op jit(solution)/shard_map/forward_stats/pallas_call | solution.py:224
  32.7 1.9 %collective-permute-done.7.refs_2_.refs_11_.refs_12_ = bf16[544,128]{1,0:T(8,128)(2,1)S(1)} collective-permute-done((bf16[544,128]{1,0:T(8,128)(2,1)S(1)}, bf16[544,128]{1,0:T(8,128)(2,1)S(1)}, u32[]{:S(2)}, u32[]{:S(2)}) %collective-permute-start.7) | collective-permute-done | bytes 139296 | tf_op jit(solution)/shard_map/ppermute | solution.py:286
  34.6 1.0 %forward_stats.11 = (f32[32,256]{1,0:T(8,128)S(1)}, bf16[256,2048]{1,0:T(8,128)(2,1)S(1)}, f32[256,2048]{1,0:T(8,128)S(1)}) custom-call(bf16[2048,128]{1,0:T(8,128)(2,1)S(1)} %get-tuple-element.47.refs_0_.refs_1_, bf16[2048,128]{1,0:T(8,128)(2,1)S(1)} %get-tuple-element.48.refs_1_.refs_2_, bf16[544,128]{1,0:T(8,128)(2,1)S(1)} %collective-permute-done.7.refs_2_.refs_11_.refs_12_), custom_call_target="tpu_custom_call" | custom-call | flops 805306368 | bytes 1048576 | tf_op jit(solution)/shard_map/forward_stats/pallas_call | solution.py:224
  36.3 2.5 %collective-permute-start.8 = (bf16[256,128]{1,0:T(8,128)(2,1)S(1)}, bf16[256,128]{1,0:T(8,128)(2,1)S(1)}, u32[]{:S(2)}, u32[]{:S(2)}) collective-permute-start(bf16[256,128]{1,0:T(8,128)(2,1)S(1)} %get-tuple-element.71), channel_id=1, source_target_pairs={{0,8},{1,9},{2,10},{3,11},{4,12},{5,13},{6,14},{7,15},{8,0},{9,1},... | collective-permute-start | bytes 196616 | tf_op jit(solution)/shard_map/ppermute | solution.py:277
  38.8 1.6 %backward_grads.7 = (f32[1024,256]{1,0:T(8,128)S(1)}, bf16[512,128]{1,0:T(8,128)(2,1)S(1)}, f32[256,128]{1,0:T(8,128)S(1)}) custom-call(s32[1]{0:T(128)S(6)} %copy.15.refs_0_, bf16[2048,128]{1,0:T(8,128)(2,1)S(1)} %get-tuple-element.47.refs_0_.refs_1_, bf16[2048,128]{1,0:T(8,128)(2,1)S(1)} %get-tuple-element.48.refs_1_.refs_2_, ...), custom_call_target="tpu_custom_call" | custom-call | flops 2013265920 | bytes 2097152 | tf_op jit(solution)/shard_map/backward_grads/pallas_call | solution.py:255
  41.5 2.0 %backward_grads.8 = (f32[1024,256]{1,0:T(8,128)S(1)}, bf16[512,128]{1,0:T(8,128)(2,1)S(1)}, f32[256,128]{1,0:T(8,128)S(1)}, f32[256,128]{1,0:T(8,128)S(1)}) custom-call(s32[1]{0:T(128)S(6)} %copy.15.refs_0_, bf16[2048,128]{1,0:T(8,128)(2,1)S(1)} %get-tuple-element.47.refs_0_.refs_1_, bf16[2048,128]{1,0:T(8,128)(2,1)S(1)} %get-tuple-element.48.refs_1_.refs_2_, ...), custom_call_target="tpu_custom_call" | custom-call | flops 2684354560 | bytes 2097152 | tf_op jit(solution)/shard_map/backward_grads/pallas_call | solution.py:255
  43.5 2.3 %collective-permute-start.11 = (bf16[512,128]{1,0:T(8,128)(2,1)S(1)}, bf16[512,128]{1,0:T(8,128)(2,1)S(1)}, u32[]{:S(2)}, u32[]{:S(2)}) collective-permute-start(bf16[512,128]{1,0:T(8,128)(2,1)S(1)} %get-tuple-element.78), channel_id=1, source_target_pairs={{0,8},{1,9},{2,10},{3,11},{4,12},{5,13},{6,14},{7,15},{8,0},{9,1},... | collective-permute-start | bytes 393224 | tf_op jit(solution)/shard_map/ppermute | solution.py:277
  45.8 0.9 %collective-permute-done.10 = bf16[256,128]{1,0:T(8,128)(2,1)S(1)} collective-permute-done((bf16[256,128]{1,0:T(8,128)(2,1)S(1)}, bf16[256,128]{1,0:T(8,128)(2,1)S(1)}, u32[]{:S(2)}, u32[]{:S(2)}) %collective-permute-start.10) | collective-permute-done | bytes 65568 | tf_op jit(solution)/shard_map/ppermute | solution.py:286
  46.7 2.4 %collective-permute-start.13 = (bf16[256,128]{1,0:T(8,128)(2,1)S(1)}, bf16[256,128]{1,0:T(8,128)(2,1)S(1)}, u32[]{:S(2)}, u32[]{:S(2)}) collective-permute-start(bf16[256,128]{1,0:T(8,128)(2,1)S(1)} %get-tuple-element.95.refs_18_), channel_id=1, source_target_pairs={{0,7},{1,2},{2,1},{3,4},{4,3},{5,6},{6,5},{7,0},{8,15},{9,10},{10,... | collective-permute-start | bytes 196616 | tf_op jit(solution)/shard_map/ppermute | solution.py:286
  49.1 2.0 %backward_grads.9 = (f32[1024,256]{1,0:T(8,128)S(1)}, bf16[512,128]{1,0:T(8,128)(2,1)S(1)}, f32[256,128]{1,0:T(8,128)S(1)}, f32[256,128]{1,0:T(8,128)S(1)}) custom-call(s32[1]{0:T(128)S(6)} %copy.15.refs_0_, bf16[2048,128]{1,0:T(8,128)(2,1)S(1)} %get-tuple-element.47.refs_0_.refs_1_, bf16[2048,128]{1,0:T(8,128)(2,1)S(1)} %get-tuple-element.48.refs_1_.refs_2_, ...), custom_call_target="tpu_custom_call" | custom-call | flops 2684354560 | bytes 2097152 | tf_op jit(solution)/shard_map/backward_grads/pallas_call | solution.py:255
  52.3 1.1 %collective-permute-done.12 = bf16[256,128]{1,0:T(8,128)(2,1)S(1)} collective-permute-done((bf16[256,128]{1,0:T(8,128)(2,1)S(1)}, bf16[256,128]{1,0:T(8,128)(2,1)S(1)}, u32[]{:S(2)}, u32[]{:S(2)}) %collective-permute-start.12) | collective-permute-done | bytes 65568 | tf_op jit(solution)/shard_map/ppermute | solution.py:286
  53.9 3.1 %collective-permute-start.15 = (bf16[256,128]{1,0:T(8,128)(2,1)S(1)}, bf16[256,128]{1,0:T(8,128)(2,1)S(1)}, u32[]{:S(2)}, u32[]{:S(2)}) collective-permute-start(bf16[256,128]{1,0:T(8,128)(2,1)S(1)} %get-tuple-element.94.refs_14_), channel_id=1, source_target_pairs={{0,7},{1,2},{2,1},{3,4},{4,3},{5,6},{6,5},{7,0},{8,15},{9,10},{10,... | collective-permute-start | bytes 196616 | tf_op jit(solution)/shard_map/ppermute | solution.py:286
  57.0 1.6 %backward_grads.10 = (f32[1024,256]{1,0:T(8,128)S(1)}, bf16[256,128]{1,0:T(8,128)(2,1)S(1)}, f32[256,128]{1,0:T(8,128)S(1)}, f32[256,128]{1,0:T(8,128)S(1)}) custom-call(s32[1]{0:T(128)S(6)} %copy.15.refs_0_, bf16[2048,128]{1,0:T(8,128)(2,1)S(1)} %get-tuple-element.47.refs_0_.refs_1_, bf16[2048,128]{1,0:T(8,128)(2,1)S(1)} %get-tuple-element.48.refs_1_.refs_2_, ...), custom_call_target="tpu_custom_call" | custom-call | flops 2013265920 | bytes 2097152 | tf_op jit(solution)/shard_map/backward_grads/pallas_call | solution.py:255
  59.4 3.2 %collective-permute-start.18 = (bf16[256,128]{1,0:T(8,128)(2,1)S(1)}, bf16[256,128]{1,0:T(8,128)(2,1)S(1)}, u32[]{:S(2)}, u32[]{:S(2)}) collective-permute-start(bf16[256,128]{1,0:T(8,128)(2,1)S(1)} %get-tuple-element.91.refs_10_), channel_id=1, source_target_pairs={{0,7},{1,2},{2,1},{3,4},{4,3},{5,6},{6,5},{7,0},{8,15},{9,10},{10,... | collective-permute-start | bytes 196616 | tf_op jit(solution)/shard_map/ppermute | solution.py:286
  62.7 2.6 %backward_grads.11 = (f32[1,256,1024]{2,1,0:T(8,128)}, f32[256,128]{1,0:T(8,128)S(1)}, f32[1,256,128]{2,1,0:T(8,128)}, f32[1,256,128]{2,1,0:T(8,128)}) custom-call(s32[1]{0:T(128)S(6)} %copy.15.refs_0_, bf16[2048,128]{1,0:T(8,128)(2,1)S(1)} %get-tuple-element.47.refs_0_.refs_1_, bf16[2048,128]{1,0:T(8,128)(2,1)S(1)} %get-tuple-element.48.refs_1_.refs_2_, ...), custom_call_target="tpu_custom_call" | custom-call | flops 2013265920 | bytes 2097152 | tf_op jit(solution)/shard_map/backward_grads/pallas_call | solution.py:255
  65.2 1.7 %collective-permute-done.19 = bf16[256,128]{1,0:T(8,128)(2,1)S(1)} collective-permute-done((bf16[256,128]{1,0:T(8,128)(2,1)S(1)}, bf16[256,128]{1,0:T(8,128)(2,1)S(1)}, u32[]{:S(2)}, u32[]{:S(2)}) %collective-permute-start.19) | collective-permute-done | bytes 65568 | tf_op jit(solution)/shard_map/ppermute | solution.py:286
  66.9 0.7 %add_add_fusion = (f32[128,128]{1,0:T(8,128)}, f32[128,128]{1,0:T(8,128)}) fusion(f32[256,128]{1,0:T(8,128)S(1)} %get-tuple-element.87, bf16[256,128]{1,0:T(8,128)(2,1)S(1)} %collective-permute-done.19, bf16[256,128]{1,0:T(8,128)(2,1)S(1)} %collective-permute-done.18, bf16[256,128]{1,0:T(8,128)(2,1)S(1)} %collective-permute-done.17), kind=kLoop, calls=%fused_computation.10 | loop fusion | flops 196608 | bytes 458752 | tf_op jit(solution)/shard_map/add | solution.py:368
  (37 shorter events, 5.0 us)
Async XLA Ops:
  0.6 5.9 %copy-start = (bf16[128,128]{1,0:T(8,128)(2,1)S(1)}, bf16[128,128]{1,0:T(8,128)(2,1)}, u32[]{:S(2)}) copy-start(bf16[128,128]{1,0:T(8,128)(2,1)} %param.12) | copy-start | bytes 98308
  0.6 5.9 %copy-start.1 = (bf16[128,128]{1,0:T(8,128)(2,1)S(1)}, bf16[128,128]{1,0:T(8,128)(2,1)}, u32[]{:S(2)}) copy-start(bf16[128,128]{1,0:T(8,128)(2,1)} %param.11) | copy-start | bytes 98308
  0.7 5.9 %copy-start.2 = (bf16[1,256,128]{2,1,0:T(8,128)(2,1)S(1)}, bf16[1,256,128]{2,1,0:T(8,128)(2,1)}, u32[]{:S(2)}) copy-start(bf16[1,256,128]{2,1,0:T(8,128)(2,1)} %param.10) | copy-start | bytes 196612
  2.1 4.4 %collective-permute-start = (bf16[272,128]{1,0:T(8,128)(2,1)S(1)}, bf16[272,128]{1,0:T(8,128)(2,1)S(1)}, u32[]{:S(2)}, u32[]{:S(2)}) collective-permute-start(bf16[272,128]{1,0:T(8,128)(2,1)S(1)} %pad_maximum_fusion.2.refs_3_.refs_6_), channel_id=1, source_target_pairs={{0,8},{1,9},{2,10},{3,11},{4,12},{5,13},{6,14},{7,15},{8,0},{9,1},... | collective-permute-start | bytes 208904 | tf_op jit(solution)/shard_map/ppermute | solution.py:277
  6.6 9.1 %collective-permute-start.2 = (bf16[544,128]{1,0:T(8,128)(2,1)S(1)}, bf16[544,128]{1,0:T(8,128)(2,1)S(1)}, u32[]{:S(2)}, u32[]{:S(2)}) collective-permute-start(bf16[544,128]{1,0:T(8,128)(2,1)S(1)} %pad_maximum_fusion.1), channel_id=1, source_target_pairs={{0,1},{1,0},{2,3},{3,2},{4,5},{5,4},{6,7},{7,6},{8,9},{9,8},{10,11... | collective-permute-start | bytes 417800 | tf_op jit(solution)/shard_map/ppermute | solution.py:286
  8.6 9.1 %collective-permute-start.1 = (bf16[544,128]{1,0:T(8,128)(2,1)S(1)}, bf16[544,128]{1,0:T(8,128)(2,1)S(1)}, u32[]{:S(2)}, u32[]{:S(2)}) collective-permute-start(bf16[544,128]{1,0:T(8,128)(2,1)S(1)} %pad_maximum_fusion.1), channel_id=1, source_target_pairs={{0,7},{1,2},{2,1},{3,4},{4,3},{5,6},{6,5},{7,0},{8,15},{9,10},{10,... | collective-permute-start | bytes 417800 | tf_op jit(solution)/shard_map/ppermute | solution.py:286
  15.7 6.4 %collective-permute-start.4 = (bf16[544,128]{1,0:T(8,128)(2,1)S(1)}, bf16[544,128]{1,0:T(8,128)(2,1)S(1)}, u32[]{:S(2)}, u32[]{:S(2)}) collective-permute-start(bf16[544,128]{1,0:T(8,128)(2,1)S(1)} %collective-permute-done.2.refs_3_.refs_13_.refs_12_), channel_id=1, source_target_pairs={{0,7},{1,2},{2,1},{3,4},{4,3},{5,6},{6,5},{7,0},{8,15},{9,10},{10,... | collective-permute-start | bytes 417800 | tf_op jit(solution)/shard_map/ppermute | solution.py:286
  17.7 5.3 %collective-permute-start.3 = (bf16[544,128]{1,0:T(8,128)(2,1)S(1)}, bf16[544,128]{1,0:T(8,128)(2,1)S(1)}, u32[]{:S(2)}, u32[]{:S(2)}) collective-permute-start(bf16[544,128]{1,0:T(8,128)(2,1)S(1)} %collective-permute-done.1.refs_2_.refs_12_.refs_11_), channel_id=1, source_target_pairs={{0,1},{1,0},{2,3},{3,2},{4,5},{5,4},{6,7},{7,6},{8,9},{9,8},{10,11... | collective-permute-start | bytes 417800 | tf_op jit(solution)/shard_map/ppermute | solution.py:286
  22.1 6.0 %collective-permute-start.6 = (bf16[544,128]{1,0:T(8,128)(2,1)S(1)}, bf16[544,128]{1,0:T(8,128)(2,1)S(1)}, u32[]{:S(2)}, u32[]{:S(2)}) collective-permute-start(bf16[544,128]{1,0:T(8,128)(2,1)S(1)} %collective-permute-done.4.refs_3_.refs_13_.refs_15_), channel_id=1, source_target_pairs={{0,1},{1,0},{2,3},{3,2},{4,5},{5,4},{6,7},{7,6},{8,9},{9,8},{10,11... | collective-permute-start | bytes 417800 | tf_op jit(solution)/shard_map/ppermute | solution.py:286
  22.9 7.5 %collective-permute-start.5 = (bf16[544,128]{1,0:T(8,128)(2,1)S(1)}, bf16[544,128]{1,0:T(8,128)(2,1)S(1)}, u32[]{:S(2)}, u32[]{:S(2)}) collective-permute-start(bf16[544,128]{1,0:T(8,128)(2,1)S(1)} %collective-permute-done.3.refs_2_.refs_12_.refs_14_), channel_id=1, source_target_pairs={{0,7},{1,2},{2,1},{3,4},{4,3},{5,6},{6,5},{7,0},{8,15},{9,10},{10,... | collective-permute-start | bytes 417800 | tf_op jit(solution)/shard_map/ppermute | solution.py:286
  28.1 6.5 %collective-permute-start.7 = (bf16[544,128]{1,0:T(8,128)(2,1)S(1)}, bf16[544,128]{1,0:T(8,128)(2,1)S(1)}, u32[]{:S(2)}, u32[]{:S(2)}) collective-permute-start(bf16[544,128]{1,0:T(8,128)(2,1)S(1)} %collective-permute-done.6.refs_3_.refs_11_.refs_15_), channel_id=1, source_target_pairs={{0,7},{1,2},{2,1},{3,4},{4,3},{5,6},{6,5},{7,0},{8,15},{9,10},{10,... | collective-permute-start | bytes 417800 | tf_op jit(solution)/shard_map/ppermute | solution.py:286
  36.3 4.7 %collective-permute-start.8 = (bf16[256,128]{1,0:T(8,128)(2,1)S(1)}, bf16[256,128]{1,0:T(8,128)(2,1)S(1)}, u32[]{:S(2)}, u32[]{:S(2)}) collective-permute-start(bf16[256,128]{1,0:T(8,128)(2,1)S(1)} %get-tuple-element.71), channel_id=1, source_target_pairs={{0,8},{1,9},{2,10},{3,11},{4,12},{5,13},{6,14},{7,15},{8,0},{9,1},... | collective-permute-start | bytes 196616 | tf_op jit(solution)/shard_map/ppermute | solution.py:277
  40.4 6.3 %collective-permute-start.9 = (bf16[512,128]{1,0:T(8,128)(2,1)S(1)}, bf16[512,128]{1,0:T(8,128)(2,1)S(1)}, u32[]{:S(2)}, u32[]{:S(2)}) collective-permute-start(bf16[512,128]{1,0:T(8,128)(2,1)S(1)} %get-tuple-element.74), channel_id=1, source_target_pairs={{0,8},{1,9},{2,10},{3,11},{4,12},{5,13},{6,14},{7,15},{8,0},{9,1},... | collective-permute-start | bytes 393224 | tf_op jit(solution)/shard_map/ppermute | solution.py:277
  41.1 5.6 %collective-permute-start.10 = (bf16[256,128]{1,0:T(8,128)(2,1)S(1)}, bf16[256,128]{1,0:T(8,128)(2,1)S(1)}, u32[]{:S(2)}, u32[]{:S(2)}) collective-permute-start(bf16[256,128]{1,0:T(8,128)(2,1)S(1)} %add_convert_fusion.6.refs_17_), channel_id=1, source_target_pairs={{0,7},{1,2},{2,1},{3,4},{4,3},{5,6},{6,5},{7,0},{8,15},{9,10},{10,... | collective-permute-start | bytes 196616 | tf_op jit(solution)/shard_map/ppermute | solution.py:286
  43.5 8.3 %collective-permute-start.11 = (bf16[512,128]{1,0:T(8,128)(2,1)S(1)}, bf16[512,128]{1,0:T(8,128)(2,1)S(1)}, u32[]{:S(2)}, u32[]{:S(2)}) collective-permute-start(bf16[512,128]{1,0:T(8,128)(2,1)S(1)} %get-tuple-element.78), channel_id=1, source_target_pairs={{0,8},{1,9},{2,10},{3,11},{4,12},{5,13},{6,14},{7,15},{8,0},{9,1},... | collective-permute-start | bytes 393224 | tf_op jit(solution)/shard_map/ppermute | solution.py:277
  46.7 5.6 %collective-permute-start.13 = (bf16[256,128]{1,0:T(8,128)(2,1)S(1)}, bf16[256,128]{1,0:T(8,128)(2,1)S(1)}, u32[]{:S(2)}, u32[]{:S(2)}) collective-permute-start(bf16[256,128]{1,0:T(8,128)(2,1)S(1)} %get-tuple-element.95.refs_18_), channel_id=1, source_target_pairs={{0,7},{1,2},{2,1},{3,4},{4,3},{5,6},{6,5},{7,0},{8,15},{9,10},{10,... | collective-permute-start | bytes 196616 | tf_op jit(solution)/shard_map/ppermute | solution.py:286
  49.1 4.3 %collective-permute-start.12 = (bf16[256,128]{1,0:T(8,128)(2,1)S(1)}, bf16[256,128]{1,0:T(8,128)(2,1)S(1)}, u32[]{:S(2)}, u32[]{:S(2)}) collective-permute-start(bf16[256,128]{1,0:T(8,128)(2,1)S(1)} %get-tuple-element.96.refs_17_), channel_id=1, source_target_pairs={{0,1},{1,0},{2,3},{3,2},{4,5},{5,4},{6,7},{7,6},{8,9},{9,8},{10,11... | collective-permute-start | bytes 196616 | tf_op jit(solution)/shard_map/ppermute | solution.py:286
  51.2 8.2 %collective-permute-start.14 = (bf16[512,128]{1,0:T(8,128)(2,1)S(1)}, bf16[512,128]{1,0:T(8,128)(2,1)S(1)}, u32[]{:S(2)}, u32[]{:S(2)}) collective-permute-start(bf16[512,128]{1,0:T(8,128)(2,1)S(1)} %get-tuple-element.82), channel_id=1, source_target_pairs={{0,8},{1,9},{2,10},{3,11},{4,12},{5,13},{6,14},{7,15},{8,0},{9,1},... | collective-permute-start | bytes 393224 | tf_op jit(solution)/shard_map/ppermute | solution.py:277
  53.5 5.3 %collective-permute-start.16 = (bf16[256,128]{1,0:T(8,128)(2,1)S(1)}, bf16[256,128]{1,0:T(8,128)(2,1)S(1)}, u32[]{:S(2)}, u32[]{:S(2)}) collective-permute-start(bf16[256,128]{1,0:T(8,128)(2,1)S(1)} %get-tuple-element.93.refs_15_), channel_id=1, source_target_pairs={{0,1},{1,0},{2,3},{3,2},{4,5},{5,4},{6,7},{7,6},{8,9},{9,8},{10,11... | collective-permute-start | bytes 196616 | tf_op jit(solution)/shard_map/ppermute | solution.py:286
  53.9 5.5 %collective-permute-start.15 = (bf16[256,128]{1,0:T(8,128)(2,1)S(1)}, bf16[256,128]{1,0:T(8,128)(2,1)S(1)}, u32[]{:S(2)}, u32[]{:S(2)}) collective-permute-start(bf16[256,128]{1,0:T(8,128)(2,1)S(1)} %get-tuple-element.94.refs_14_), channel_id=1, source_target_pairs={{0,7},{1,2},{2,1},{3,4},{4,3},{5,6},{6,5},{7,0},{8,15},{9,10},{10,... | collective-permute-start | bytes 196616 | tf_op jit(solution)/shard_map/ppermute | solution.py:286
  58.6 6.6 %collective-permute-start.17 = (bf16[256,128]{1,0:T(8,128)(2,1)S(1)}, bf16[256,128]{1,0:T(8,128)(2,1)S(1)}, u32[]{:S(2)}, u32[]{:S(2)}) collective-permute-start(bf16[256,128]{1,0:T(8,128)(2,1)S(1)} %get-tuple-element.88), channel_id=1, source_target_pairs={{0,8},{1,9},{2,10},{3,11},{4,12},{5,13},{6,14},{7,15},{8,0},{9,1},... | collective-permute-start | bytes 196616 | tf_op jit(solution)/shard_map/ppermute | solution.py:277
  59.4 5.8 %collective-permute-start.18 = (bf16[256,128]{1,0:T(8,128)(2,1)S(1)}, bf16[256,128]{1,0:T(8,128)(2,1)S(1)}, u32[]{:S(2)}, u32[]{:S(2)}) collective-permute-start(bf16[256,128]{1,0:T(8,128)(2,1)S(1)} %get-tuple-element.91.refs_10_), channel_id=1, source_target_pairs={{0,7},{1,2},{2,1},{3,4},{4,3},{5,6},{6,5},{7,0},{8,15},{9,10},{10,... | collective-permute-start | bytes 196616 | tf_op jit(solution)/shard_map/ppermute | solution.py:286
  62.7 4.3 %collective-permute-start.19 = (bf16[256,128]{1,0:T(8,128)(2,1)S(1)}, bf16[256,128]{1,0:T(8,128)(2,1)S(1)}, u32[]{:S(2)}, u32[]{:S(2)}) collective-permute-start(bf16[256,128]{1,0:T(8,128)(2,1)S(1)} %get-tuple-element.92.refs_9_), channel_id=1, source_target_pairs={{0,1},{1,0},{2,3},{3,2},{4,5},{5,4},{6,7},{7,6},{8,9},{9,8},{10,11... | collective-permute-start | bytes 196616 | tf_op jit(solution)/shard_map/ppermute | solution.py:286
